TPU v7x, 32 devices: a whole 2x2x4 slice. The times are simulated.
32 devices in a mesh: rows: 4 (over z), cols: 8 (over y, x, core).
Axes of the slice: x: 2, y: 2, z: 4, core: 2. Of those that a mesh axis runs over, the one named last changes fastest.
Arguments:
- slab: bfloat16 [8192, 8192], P('rows', 'cols'), may hold values from -6 to 6
- transforms: bfloat16 [8, 16384, 512], P('cols', 'rows'), may hold values from -0.25 to 0.25
- owners: int32 [2, 4], replicated, may hold values from 0 to 7, as said below
Outputs:
- updated: bfloat16 [8192, 8192], P('rows', 'cols')
Inputs may be any that keep to these rules, and one draw needn't show every extreme that they name: For each row block, the owners of different rounds differ.
All inputs are finite; a program needn't handle non-finite values.
Results may differ from a plain program's by a relative error of at most 0.0063.
Values may be sent and summed in bfloat16 or wider, within the bound.
No kernel may reach another device: no remote copies, remote signals or barrier semaphores. Data moves between devices by JAX's collectives and lax.ppermute only.
A program may use at most 64 MiB of HBM per device.

v0:
```python
import jax
import jax.numpy as jnp
from jax import lax
from jax.experimental import pallas as pl
from jax.experimental.pallas import tpu as pltpu
from jax.sharding import PartitionSpec as P


def shifted(value, axis, steps):
    count = lax.axis_size(axis)
    initial, last = (max(0, -steps), min(count, count - steps))
    return lax.ppermute(value, axis, [(source, source + steps) for source in range(initial, last)])


def flip(value, bits):
    count = lax.axis_size("cols")
    return lax.ppermute(value, "cols", [(d, d ^ (1 << bits[d & 1])) for d in range(count)])


def after(value, done):
    return lax.optimization_barrier((value, done))[0]


def place_kernel(cut, hold, got, other_hold, other_got, out, sems):
    me = lax.axis_index("cols")
    core = me & 1
    rows = hold.shape[1]
    bit0 = (me >> cut[0]) & 1
    bit1 = (me >> cut[1]) & 1
    mine = jnp.where(core == 0, bit0, bit1)
    other = jnp.where(core == 0, bit1, bit0)
    slots = (
        (hold, core * 2 + mine),
        (got, core * 2 + 1 - mine),
        (other_hold, (1 - core) * 2 + other),
        (other_got, (1 - core) * 2 + 1 - other),
    )
    copies = [
        pltpu.make_async_copy(
            piece, out.at[:, pl.ds(pl.multiple_of(at * rows, rows), rows), :], sems.at[k]
        )
        for k, (piece, at) in enumerate(slots)
    ]
    for copy in copies:
        copy.start()
    for copy in copies:
        copy.wait()


def place(cut, hold, got, other_hold, other_got):
    n, rows, width = hold.shape
    return pl.pallas_call(
        lambda *refs: place_kernel(cut, *refs),
        out_shape=jax.ShapeDtypeStruct((n, 4 * rows, width), hold.dtype),
        in_specs=[pl.BlockSpec(memory_space=pl.ANY)] * 4,
        out_specs=pl.BlockSpec(memory_space=pl.ANY),
        scratch_shapes=[pltpu.SemaphoreType.DMA((4,))],
        compiler_params=pltpu.CompilerParams(vmem_limit_bytes=1 << 20),
        cost_estimate=pl.CostEstimate(
            flops=0, bytes_accessed=2 * n * 4 * rows * width * 2, transcendentals=0
        ),
        name="place",
    )(hold, got, other_hold, other_got)


class Spread:
    def __init__(self, slot, owners_here):
        count = lax.axis_size("cols")
        dims = count.bit_length() - 2
        self.me = lax.axis_index("cols")
        self.core = self.me & 1
        self.owners = owners_here
        self.cut = (1, dims)
        self.others = [(b, b - 1) for b in range(2, dims + 1)]
        mine = self.bit(self.me, self.cut)
        other = (self.me >> jnp.where(self.core == 0, self.cut[1], self.cut[0])) & 1
        n, _, _, rows, width = slot.shape

        def take(half, piece):
            start = (0, half, piece, 0, 0)
            return lax.dynamic_slice(slot, start, (n, 1, 1, rows, width)).reshape(n, rows, width)

        self.own = take(self.core, 1 - mine), take(self.core, mine)
        self.give = take(1 - self.core, 1 - other), take(1 - self.core, other)
        self.theirs = {}

    def bit(self, index, bits):
        return (index >> jnp.where(self.core == 0, bits[0], bits[1])) & 1

    def exchange(self, lo, hi):
        got = [flip(give[lo:hi], (0, 0)) for give in self.give]
        for m in range(lo, hi):
            self.theirs[m] = [g[m - lo] for g in got]

    def begin(self, keys, first=None):
        data = []
        for part in range(2):
            data.append(
                jnp.stack(
                    [
                        jnp.where(
                            (self.owners[r] & 1) == self.core, self.own[part][m], self.theirs[m][part]
                        )
                        for r, m in keys
                    ]
                )
            )
        out = data[0] if first is None else after(data[0], first)
        return keys[0][0], data[1], flip(out, self.cut)

    def keep(self, state, bits):
        round_index, hold, got = state
        same = self.bit(self.me, bits) == self.bit(self.owners[round_index], bits)
        return jnp.where(same, hold, got)

    def middle(self, state):
        bits = self.cut
        for other in self.others:
            hold = self.keep(state, bits)
            state = (state[0], hold, flip(hold, other))
            bits = other
        return state

    def last(self, state):
        hold = self.keep(state, self.others[-1])
        return hold, flip(hold, self.cut)

    def join(self, hold, got):
        return place(self.cut, hold, got, flip(hold, (0, 0)), flip(got, (0, 0)))

    def join_above(self, hold, got):
        both = shifted(jnp.stack([hold, got]), "rows", 1)
        other = flip(both, (0, 0))
        return place(self.cut, both[:1], both[1:], other[:1], other[1:])[0]


def apply(q, x):
    product = lax.dot_general(q, x, (((0,), (0,)), ((), ())), preferred_element_type=jnp.float32)
    return product.astype(jnp.bfloat16)


def apply_many(q, x):
    product = jnp.einsum("nab,nac->nbc", q, x, preferred_element_type=jnp.float32)
    return product.astype(jnp.bfloat16)


def local(slab, transforms, owners):
    row_block = lax.axis_index("rows")
    last_block = lax.axis_size("rows") - 1
    window = transforms.shape[2]
    border = window // 2
    local_rows, local_cols = slab.shape
    wins = local_rows // window
    rounds = owners.shape[0]
    slot = transforms[0].reshape(2 * wins, 2, 2, window // 4, window)
    spread = Spread(slot, owners[:, row_block])
    spread.exchange(0, wins)
    spread.exchange(wins, 2 * wins)

    edge = [0, wins - 1, 2 * wins - 1]
    inside = [m for m in range(2 * wins) if m not in edge]
    plans = []
    for r in range(rounds):
        if r < rounds - 1:
            plans.append([(r, m) for m in range(wins)])
            plans.append([(r, m) for m in range(wins, 2 * wins)])
        else:
            plans.append([(r, m) for m in edge])
            plans.append([(r, m) for m in inside])
    states, pairs = {}, {}
    for k in range(0, len(plans), 2):
        if k == 0:
            states[k] = spread.begin(plans[k])
            states[k + 1] = spread.begin(plans[k + 1])
        else:
            states[k] = spread.begin(plans[k], states[k - 1][2])
            states[k + 1] = spread.begin(plans[k + 1], pairs[k - 2][1])
        pairs[k] = spread.last(spread.middle(states[k]))
        pairs[k + 1] = spread.last(spread.middle(states[k + 1]))

    matrix = slab
    for r in range(rounds):
        head, tail = pairs[2 * r], pairs[2 * r + 1]
        if r < rounds - 1:
            one = spread.join(*head)
            matrix = apply_many(one, matrix.reshape(wins, window, local_cols)).reshape(local_rows, local_cols)
            begin, end = matrix[:border], matrix[local_rows - border :]
            below = shifted(begin, "rows", -1)
            above = shifted(end, "rows", 1)
            prev = spread.join_above(tail[0][-1, :, border:], tail[1][-1, :, border:])
            two = spread.join(*tail)
            cross = two[wins - 1]
            two = two[: wins - 1]
            centre = matrix[border : local_rows - border]
        else:
            edges = spread.join(*head)
            cross = edges[2]
            head_rows = apply(edges[0], matrix[:window])
            tail_rows = apply(edges[1], matrix[local_rows - window :])
            begin, end = head_rows[:border], tail_rows[border:]
            below = shifted(begin, "rows", -1)
            above = shifted(end, "rows", 1)
            prev = spread.join_above(head[0][-1, :, border:], head[1][-1, :, border:])
            rest = spread.join(*tail)
            mid = apply_many(
                rest[: wins - 2],
                matrix[window : local_rows - window].reshape(wins - 2, window, local_cols),
            ).reshape(local_rows - 2 * window, local_cols)
            two = rest[wins - 2 :]
            centre = jnp.concatenate([head_rows[border:], mid, tail_rows[:border]], 0)
        inner = apply_many(two, centre.reshape(wins - 1, window, local_cols)).reshape(
            local_rows - window, local_cols
        )
        low = apply(cross[:, :border], jnp.concatenate([end, below], 0))
        low = jnp.where(row_block == last_block, end, low)
        top = apply(prev, jnp.concatenate([above, begin], 0))
        top = jnp.where(row_block == 0, begin, top)
        matrix = jnp.concatenate([top, inner, low], 0)
    return matrix


def solution(mesh):
    return jax.shard_map(
        local,
        mesh=mesh,
        in_specs=(P("rows", "cols"), P("cols", "rows", None), P()),
        out_specs=P("rows", "cols"),
        check_vma=False,
    )
```

profile of v0, /device:TPU:8, one launch (start us, length us, event | category | flops | bytes accessed | tf_op | source)
XLA Modules:
  0.0 127.3 jit_solution(7180457698739105571)
XLA Ops:
  0.0 2.7 %dynamic-slice_bitcast_fusion.2 = (bf16[4,128,512]{2,1,0:T(8,128)(2,1)}, bf16[4,128,512]{2,1,0:T(8,128)(2,1)S(1)}, bf16[4,128,512]{2,1,0:T(8,128)(2,1)S(1)}, bf16[4,128,512]{2,1,0:T(8,128)(2,1)}) fusion(bf16[8,2,2,128,512]{4,3,2,1,0:T(8,128)(2,1)} %bitcast.152, s32[]{:T(128)S(6)} %add.35, s32[]{:T(128)S(6)} %select_n.293, s32[]{:T(128)S(6)} %select_n.294, ...), kind=kLoop, calls=%fused_computation.40 | loop fusion | bytes 4194320 | tf_op jit(solution)/shard_map/slice | solution.py:91
  20.4 1.7 %collective-permute-done.4 = bf16[4,128,512]{2,1,0:T(8,128)(2,1)S(1)} collective-permute-done((bf16[4,128,512]{2,1,0:T(8,128)(2,1)S(1)}, bf16[4,128,512]{2,1,0:T(8,128)(2,1)S(1)}, u32[]{:S(2)}, u32[]{:S(2)}) %collective-permute-start.4) | collective-permute-done | bytes 524320 | tf_op jit(solution)/shard_map/ppermute | solution.py:17
  23.7 1.6 %collective-permute-start.15 = (bf16[4,128,512]{2,1,0:T(8,128)(2,1)S(1)}, bf16[4,128,512]{2,1,0:T(8,128)(2,1)}, u32[]{:S(2)}, u32[]{:S(2)}) collective-permute-start(bf16[4,128,512]{2,1,0:T(8,128)(2,1)S(1)} %maximum_select_fusion.1), channel_id=1, source_target_pairs={{0,4},{1,3},{2,6},{3,1},{4,0},{5,7},{6,2},{7,5},{8,12},{9,11},{10,... | collective-permute-start | bytes 1572872 | tf_op jit(solution)/shard_map/ppermute | solution.py:17
  25.3 4.9 %collective-permute-done.10 = bf16[4,128,512]{2,1,0:T(8,128)(2,1)S(1)} collective-permute-done((bf16[4,128,512]{2,1,0:T(8,128)(2,1)S(1)}, bf16[4,128,512]{2,1,0:T(8,128)(2,1)S(1)}, u32[]{:S(2)}, u32[]{:S(2)}) %collective-permute-start.10) | collective-permute-done | bytes 524320 | tf_op jit(solution)/shard_map/ppermute | solution.py:17
  31.0 2.5 %collective-permute-start.11 = (bf16[4,128,512]{2,1,0:T(8,128)(2,1)}, bf16[4,128,512]{2,1,0:T(8,128)(2,1)}, u32[]{:S(2)}, u32[]{:S(2)}) collective-permute-start(bf16[4,128,512]{2,1,0:T(8,128)(2,1)} %maximum_select_fusion), channel_id=1, source_target_pairs={{0,4},{1,3},{2,6},{3,1},{4,0},{5,7},{6,2},{7,5},{8,12},{9,11},{10,... | collective-permute-start | bytes 1572872 | tf_op jit(solution)/shard_map/ppermute | solution.py:17
  34.8 3.8 %collective-permute-done.5 = bf16[3,128,512]{2,1,0:T(8,128)(2,1)S(1)} collective-permute-done((bf16[3,128,512]{2,1,0:T(8,128)(2,1)}, bf16[3,128,512]{2,1,0:T(8,128)(2,1)S(1)}, u32[]{:S(2)}, u32[]{:S(2)}) %collective-permute-start.5) | collective-permute-done | bytes 393248 | tf_op jit(solution)/shard_map/ppermute | solution.py:17
  39.4 2.5 %collective-permute-start.6 = (bf16[3,128,512]{2,1,0:T(8,128)(2,1)}, bf16[3,128,512]{2,1,0:T(8,128)(2,1)}, u32[]{:S(2)}, u32[]{:S(2)}) collective-permute-start(bf16[3,128,512]{2,1,0:T(8,128)(2,1)} %maximum_select_fusion.2), channel_id=1, source_target_pairs={{0,4},{1,3},{2,6},{3,1},{4,0},{5,7},{6,2},{7,5},{8,12},{9,11},{10,... | collective-permute-start | bytes 1179656 | tf_op jit(solution)/shard_map/ppermute | solution.py:17
  47.2 5.1 %collective-permute-done.6 = bf16[3,128,512]{2,1,0:T(8,128)(2,1)} collective-permute-done((bf16[3,128,512]{2,1,0:T(8,128)(2,1)}, bf16[3,128,512]{2,1,0:T(8,128)(2,1)}, u32[]{:S(2)}, u32[]{:S(2)}) %collective-permute-start.6) | collective-permute-done | bytes 393248 | tf_op jit(solution)/shard_map/ppermute | solution.py:17
  55.0 4.5 %collective-permute-start.17 = (bf16[2,128,256]{2,1,0:T(8,128)(2,1)S(1)}, bf16[2,128,256]{2,1,0:T(8,128)(2,1)S(1)}, u32[]{:S(2)}, u32[]{:S(2)}) collective-permute-start(bf16[2,128,256]{2,1,0:T(8,128)(2,1)S(1)} %pad_maximum_fusion.9), channel_id=1, source_target_pairs={{0,8},{8,16},{16,24},{1,9},{9,17},{17,25},{2,10},{10,18},{18,26},{... | collective-permute-start | bytes 393224 | tf_op jit(solution)/shard_map/ppermute | solution.py:12
  60.2 1.7 %collective-permute-done.17 = bf16[2,128,256]{2,1,0:T(8,128)(2,1)S(1)} collective-permute-done((bf16[2,128,256]{2,1,0:T(8,128)(2,1)S(1)}, bf16[2,128,256]{2,1,0:T(8,128)(2,1)S(1)}, u32[]{:S(2)}, u32[]{:S(2)}) %collective-permute-start.17) | collective-permute-done | bytes 131104 | tf_op jit(solution)/shard_map/ppermute | solution.py:12
  63.3 4.3 %collective-permute-start.22 = (bf16[2,128,256]{2,1,0:T(8,128)(2,1)S(1)}, bf16[2,128,256]{2,1,0:T(8,128)(2,1)S(1)}, u32[]{:S(2)}, u32[]{:S(2)}) collective-permute-start(bf16[2,128,256]{2,1,0:T(8,128)(2,1)S(1)} %pad_maximum_fusion.10), channel_id=1, source_target_pairs={{0,8},{8,16},{16,24},{1,9},{9,17},{17,25},{2,10},{10,18},{18,26},{... | collective-permute-start | bytes 393224 | tf_op jit(solution)/shard_map/ppermute | solution.py:12
  68.1 2.7 %collective-permute-done.22 = bf16[2,128,256]{2,1,0:T(8,128)(2,1)S(1)} collective-permute-done((bf16[2,128,256]{2,1,0:T(8,128)(2,1)S(1)}, bf16[2,128,256]{2,1,0:T(8,128)(2,1)S(1)}, u32[]{:S(2)}, u32[]{:S(2)}) %collective-permute-start.22) | collective-permute-done | bytes 131104 | tf_op jit(solution)/shard_map/ppermute | solution.py:12
  73.0 2.4 %convolution_convert_fusion = bf16[4,512,1024]{2,1,0:T(8,128)(2,1)S(1)} fusion(bf16[4,512,512]{2,1,0:T(8,128)(2,1)S(1)} %place.7, bf16[4,512,1024]{2,1,0:T(8,128)(2,1)S(1)} %bitcast.169), kind=kOutput, calls=%fused_computation.2 | convolution fusion | flops 2149580800 | bytes 10485760 | tf_op jit(solution)/shard_map/nab,nac->nbc/dot_general | solution.py:143
  75.9 3.5 %collective-permute-start.19 = (bf16[256,1024]{1,0:T(8,128)(2,1)S(1)}, bf16[256,1024]{1,0:T(8,128)(2,1)S(1)}, u32[]{:S(2)}, u32[]{:S(2)}) collective-permute-start(bf16[256,1024]{1,0:T(8,128)(2,1)S(1)} %get-tuple-element.41), channel_id=1, source_target_pairs={{0,8},{8,16},{16,24},{1,9},{9,17},{17,25},{2,10},{10,18},{18,26},{... | collective-permute-start | bytes 1572872 | tf_op jit(solution)/shard_map/ppermute | solution.py:12
  79.6 2.1 %convolution_convert_fusion.2 = bf16[3,512,1024]{2,1,0:T(8,128)(2,1)S(1)} fusion(bf16[4,512,512]{2,1,0:T(8,128)(2,1)S(1)} %place.9, bf16[3,512,1024]{2,1,0:T(8,128)(2,1)S(1)} %bitcast.164), kind=kOutput, calls=%fused_computation.4 | convolution fusion | flops 1612185600 | bytes 8388608 | tf_op jit(solution)/shard_map/nab,nac->nbc/dot_general | solution.py:143
  81.8 2.5 %collective-permute-start.24 = (bf16[256,1024]{1,0:T(8,128)(2,1)S(1)}, bf16[256,1024]{1,0:T(8,128)(2,1)S(1)}, u32[]{:S(2)}, u32[]{:S(2)}) collective-permute-start(bf16[256,1024]{1,0:T(8,128)(2,1)S(1)} %get-tuple-element.40), channel_id=1, source_target_pairs={{8,0},{16,8},{24,16},{9,1},{17,9},{25,17},{10,2},{18,10},{26,18},{... | collective-permute-start | bytes 1572872 | tf_op jit(solution)/shard_map/ppermute | solution.py:12
  84.8 1.6 %collective-permute-start.27 = (bf16[5,128,512]{2,1,0:T(8,128)(2,1)S(1)}, bf16[5,128,512]{2,1,0:T(8,128)(2,1)S(1)}, u32[]{:S(2)}, u32[]{:S(2)}) collective-permute-start(bf16[5,128,512]{2,1,0:T(8,128)(2,1)S(1)} %broadcast_select_fusion), channel_id=1, source_target_pairs={{0,4},{1,3},{2,6},{3,1},{4,0},{5,7},{6,2},{7,5},{8,12},{9,11},{10,... | collective-permute-start | bytes 1966088 | tf_op jit(solution)/shard_map/ppermute | solution.py:17
  86.4 11.4 %collective-permute-done.24 = bf16[256,1024]{1,0:T(8,128)(2,1)S(1)} collective-permute-done((bf16[256,1024]{1,0:T(8,128)(2,1)S(1)}, bf16[256,1024]{1,0:T(8,128)(2,1)S(1)}, u32[]{:S(2)}, u32[]{:S(2)}) %collective-permute-start.24) | collective-permute-done | bytes 524320 | tf_op jit(solution)/shard_map/ppermute | solution.py:12
  99.1 3.7 %collective-permute-start.25 = (bf16[256,1024]{1,0:T(8,128)(2,1)S(1)}, bf16[256,1024]{1,0:T(8,128)(2,1)S(1)}, u32[]{:S(2)}, u32[]{:S(2)}) collective-permute-start(bf16[256,1024]{1,0:T(8,128)(2,1)S(1)} %get-tuple-element.45), channel_id=1, source_target_pairs={{0,8},{8,16},{16,24},{1,9},{9,17},{17,25},{2,10},{10,18},{18,26},{... | collective-permute-start | bytes 1572872 | tf_op jit(solution)/shard_map/ppermute | solution.py:12
  104.7 3.4 %collective-permute-start.31 = (bf16[256,1024]{1,0:T(8,128)(2,1)S(1)}, bf16[256,1024]{1,0:T(8,128)(2,1)S(1)}, u32[]{:S(2)}, u32[]{:S(2)}) collective-permute-start(bf16[256,1024]{1,0:T(8,128)(2,1)S(1)} %get-tuple-element.43), channel_id=1, source_target_pairs={{8,0},{16,8},{24,16},{9,1},{17,9},{25,17},{10,2},{18,10},{26,18},{... | collective-permute-start | bytes 1572872 | tf_op jit(solution)/shard_map/ppermute | solution.py:12
  108.8 5.2 %collective-permute-done.28.refs_1_ = bf16[5,128,512]{2,1,0:T(8,128)(2,1)S(1)} collective-permute-done((bf16[5,128,512]{2,1,0:T(8,128)(2,1)S(1)}, bf16[5,128,512]{2,1,0:T(8,128)(2,1)S(1)}, u32[]{:S(2)}, u32[]{:S(2)}) %collective-permute-start.28) | collective-permute-done | bytes 655392 | tf_op jit(solution)/shard_map/ppermute | solution.py:17
  114.6 5.6 %collective-permute-done.31 = bf16[256,1024]{1,0:T(8,128)(2,1)S(1)} collective-permute-done((bf16[256,1024]{1,0:T(8,128)(2,1)S(1)}, bf16[256,1024]{1,0:T(8,128)(2,1)S(1)}, u32[]{:S(2)}, u32[]{:S(2)}) %collective-permute-start.31) | collective-permute-done | bytes 524320 | tf_op jit(solution)/shard_map/ppermute | solution.py:12
  122.9 2.1 %convolution_convert_fusion.1 = bf16[3,512,1024]{2,1,0:T(8,128)(2,1)S(1)} fusion(bf16[5,512,512]{2,1,0:T(8,128)(2,1)S(1)} %place.11, bf16[3,512,1024]{2,1,0:T(8,128)(2,1)S(1)} %bitcast.165), kind=kOutput, calls=%fused_computation.3 | convolution fusion | flops 1612185600 | bytes 8912896 | tf_op jit(solution)/shard_map/nab,nac->nbc/dot_general | solution.py:143
  125.0 2.3 %pad_maximum_fusion = bf16[2048,1024]{1,0:T(8,128)(2,1)} fusion(bf16[256,1024]{1,0:T(8,128)(2,1)S(1)} %fusion.3, bf16[1536,1024]{1,0:T(8,128)(2,1)S(1)} %bitcast.166, bf16[256,1024]{1,0:T(8,128)(2,1)S(1)} %fusion.2), kind=kLoop, calls=%fused_computation | loop fusion | flops 12582912 | bytes 8388608 | tf_op jit(solution)/shard_map/concatenate | solution.py:218
  (110 shorter events, 39.3 us)
Async XLA Ops:
  3.2 13.2 %collective-permute-start.1 = (bf16[4,128,512]{2,1,0:T(8,128)(2,1)}, bf16[4,128,512]{2,1,0:T(8,128)(2,1)S(1)}, u32[]{:S(2)}, u32[]{:S(2)}) collective-permute-start(bf16[4,128,512]{2,1,0:T(8,128)(2,1)} %get-tuple-element.36), channel_id=1, source_target_pairs={{0,1},{1,0},{2,3},{3,2},{4,5},{5,4},{6,7},{7,6},{8,9},{9,8},{10,11... | collective-permute-start | bytes 1572872 | tf_op jit(solution)/shard_map/ppermute | solution.py:17
  12.9 9.2 %collective-permute-start.4 = (bf16[4,128,512]{2,1,0:T(8,128)(2,1)S(1)}, bf16[4,128,512]{2,1,0:T(8,128)(2,1)S(1)}, u32[]{:S(2)}, u32[]{:S(2)}) collective-permute-start(bf16[4,128,512]{2,1,0:T(8,128)(2,1)S(1)} %pad_maximum_fusion.6), channel_id=1, source_target_pairs={{0,2},{1,5},{2,0},{3,7},{4,6},{5,1},{6,4},{7,3},{8,10},{9,13},{10,... | collective-permute-start | bytes 1572872 | tf_op jit(solution)/shard_map/ppermute | solution.py:17
  14.5 15.7 %collective-permute-start.10 = (bf16[4,128,512]{2,1,0:T(8,128)(2,1)S(1)}, bf16[4,128,512]{2,1,0:T(8,128)(2,1)S(1)}, u32[]{:S(2)}, u32[]{:S(2)}) collective-permute-start(bf16[4,128,512]{2,1,0:T(8,128)(2,1)S(1)} %pad_maximum_fusion.7), channel_id=1, source_target_pairs={{0,2},{1,5},{2,0},{3,7},{4,6},{5,1},{6,4},{7,3},{8,10},{9,13},{10,... | collective-permute-start | bytes 1572872 | tf_op jit(solution)/shard_map/ppermute | solution.py:17
  22.1 16.5 %collective-permute-start.5 = (bf16[3,128,512]{2,1,0:T(8,128)(2,1)}, bf16[3,128,512]{2,1,0:T(8,128)(2,1)S(1)}, u32[]{:S(2)}, u32[]{:S(2)}) collective-permute-start(bf16[3,128,512]{2,1,0:T(8,128)(2,1)} %pad_maximum_fusion.8), channel_id=1, source_target_pairs={{0,2},{1,5},{2,0},{3,7},{4,6},{5,1},{6,4},{7,3},{8,10},{9,13},{10,... | collective-permute-start | bytes 1179656 | tf_op jit(solution)/shard_map/ppermute | solution.py:17
  23.7 18.2 %collective-permute-start.15 = (bf16[4,128,512]{2,1,0:T(8,128)(2,1)S(1)}, bf16[4,128,512]{2,1,0:T(8,128)(2,1)}, u32[]{:S(2)}, u32[]{:S(2)}) collective-permute-start(bf16[4,128,512]{2,1,0:T(8,128)(2,1)S(1)} %maximum_select_fusion.1), channel_id=1, source_target_pairs={{0,4},{1,3},{2,6},{3,1},{4,0},{5,7},{6,2},{7,5},{8,12},{9,11},{10,... | collective-permute-start | bytes 1572872 | tf_op jit(solution)/shard_map/ppermute | solution.py:17
  31.0 13.6 %collective-permute-start.11 = (bf16[4,128,512]{2,1,0:T(8,128)(2,1)}, bf16[4,128,512]{2,1,0:T(8,128)(2,1)}, u32[]{:S(2)}, u32[]{:S(2)}) collective-permute-start(bf16[4,128,512]{2,1,0:T(8,128)(2,1)} %maximum_select_fusion), channel_id=1, source_target_pairs={{0,4},{1,3},{2,6},{3,1},{4,0},{5,7},{6,2},{7,5},{8,12},{9,11},{10,... | collective-permute-start | bytes 1572872 | tf_op jit(solution)/shard_map/ppermute | solution.py:17
  39.4 12.9 %collective-permute-start.6 = (bf16[3,128,512]{2,1,0:T(8,128)(2,1)}, bf16[3,128,512]{2,1,0:T(8,128)(2,1)}, u32[]{:S(2)}, u32[]{:S(2)}) collective-permute-start(bf16[3,128,512]{2,1,0:T(8,128)(2,1)} %maximum_select_fusion.2), channel_id=1, source_target_pairs={{0,4},{1,3},{2,6},{3,1},{4,0},{5,7},{6,2},{7,5},{8,12},{9,11},{10,... | collective-permute-start | bytes 1179656 | tf_op jit(solution)/shard_map/ppermute | solution.py:17
  43.1 11.8 %collective-permute-start.16 = (bf16[4,128,512]{2,1,0:T(8,128)(2,1)S(1)}, bf16[4,128,512]{2,1,0:T(8,128)(2,1)S(1)}, u32[]{:S(2)}, u32[]{:S(2)}) collective-permute-start(bf16[4,128,512]{2,1,0:T(8,128)(2,1)S(1)} %broadcast_select_fusion.2.refs_0_), channel_id=1, source_target_pairs={{0,2},{1,5},{2,0},{3,7},{4,6},{5,1},{6,4},{7,3},{8,10},{9,13},{10,... | collective-permute-start | bytes 1572872 | tf_op jit(solution)/shard_map/ppermute | solution.py:17
  45.9 14.2 %collective-permute-start.12 = (bf16[4,128,512]{2,1,0:T(8,128)(2,1)S(1)}, bf16[4,128,512]{2,1,0:T(8,128)(2,1)S(1)}, u32[]{:S(2)}, u32[]{:S(2)}) collective-permute-start(bf16[4,128,512]{2,1,0:T(8,128)(2,1)S(1)} %broadcast_select_fusion.3.refs_0_), channel_id=1, source_target_pairs={{0,2},{1,5},{2,0},{3,7},{4,6},{5,1},{6,4},{7,3},{8,10},{9,13},{10,... | collective-permute-start | bytes 1572872 | tf_op jit(solution)/shard_map/ppermute | solution.py:17
  53.4 9.4 %collective-permute-start.7 = (bf16[3,128,512]{2,1,0:T(8,128)(2,1)S(1)}, bf16[3,128,512]{2,1,0:T(8,128)(2,1)S(1)}, u32[]{:S(2)}, u32[]{:S(2)}) collective-permute-start(bf16[3,128,512]{2,1,0:T(8,128)(2,1)S(1)} %broadcast_select_fusion.4.refs_0_), channel_id=1, source_target_pairs={{0,2},{1,5},{2,0},{3,7},{4,6},{5,1},{6,4},{7,3},{8,10},{9,13},{10,... | collective-permute-start | bytes 1179656 | tf_op jit(solution)/shard_map/ppermute | solution.py:17
  59.5 12.7 %collective-permute-start.13 = (bf16[4,128,512]{2,1,0:T(8,128)(2,1)S(1)}, bf16[4,128,512]{2,1,0:T(8,128)(2,1)S(1)}, u32[]{:S(2)}, u32[]{:S(2)}) collective-permute-start(bf16[4,128,512]{2,1,0:T(8,128)(2,1)S(1)} %broadcast_select_fusion.3.refs_0_), channel_id=1, source_target_pairs={{0,1},{1,0},{2,3},{3,2},{4,5},{5,4},{6,7},{7,6},{8,9},{9,8},{10,11... | collective-permute-start | bytes 1572872 | tf_op jit(solution)/shard_map/ppermute | solution.py:17
  59.6 16.2 %collective-permute-start.20 = (bf16[4,128,512]{2,1,0:T(8,128)(2,1)S(1)}, bf16[4,128,512]{2,1,0:T(8,128)(2,1)S(1)}, u32[]{:S(2)}, u32[]{:S(2)}) collective-permute-start(bf16[4,128,512]{2,1,0:T(8,128)(2,1)S(1)} %broadcast_select_fusion.2.refs_0_), channel_id=1, source_target_pairs={{0,1},{1,0},{2,3},{3,2},{4,5},{5,4},{6,7},{7,6},{8,9},{9,8},{10,11... | collective-permute-start | bytes 1572872 | tf_op jit(solution)/shard_map/ppermute | solution.py:17
  60.1 21.7 %collective-permute-start.8 = (bf16[3,128,512]{2,1,0:T(8,128)(2,1)S(1)}, bf16[3,128,512]{2,1,0:T(8,128)(2,1)S(1)}, u32[]{:S(2)}, u32[]{:S(2)}) collective-permute-start(bf16[3,128,512]{2,1,0:T(8,128)(2,1)S(1)} %broadcast_select_fusion.4.refs_0_), channel_id=1, source_target_pairs={{0,1},{1,0},{2,3},{3,2},{4,5},{5,4},{6,7},{7,6},{8,9},{9,8},{10,11... | collective-permute-start | bytes 1179656 | tf_op jit(solution)/shard_map/ppermute | solution.py:17
  62.8 9.4 %collective-permute-start.14 = (bf16[4,128,512]{2,1,0:T(8,128)(2,1)S(1)}, bf16[4,128,512]{2,1,0:T(8,128)(2,1)S(1)}, u32[]{:S(2)}, u32[]{:S(2)}) collective-permute-start(bf16[4,128,512]{2,1,0:T(8,128)(2,1)S(1)} %collective-permute-done.12.refs_1_), channel_id=1, source_target_pairs={{0,1},{1,0},{2,3},{3,2},{4,5},{5,4},{6,7},{7,6},{8,9},{9,8},{10,11... | collective-permute-start | bytes 1572872 | tf_op jit(solution)/shard_map/ppermute | solution.py:17
  70.8 13.9 %collective-permute-start.26 = (bf16[5,128,512]{2,1,0:T(8,128)(2,1)}, bf16[5,128,512]{2,1,0:T(8,128)(2,1)S(1)}, u32[]{:S(2)}, u32[]{:S(2)}) collective-permute-start(bf16[5,128,512]{2,1,0:T(8,128)(2,1)} %copy-done.4), channel_id=1, source_target_pairs={{0,2},{1,5},{2,0},{3,7},{4,6},{5,1},{6,4},{7,3},{8,10},{9,13},{10,... | collective-permute-start | bytes 1966088 | tf_op jit(solution)/shard_map/ppermute | solution.py:17
  72.3 12.0 %collective-permute-start.9 = (bf16[3,128,512]{2,1,0:T(8,128)(2,1)S(1)}, bf16[3,128,512]{2,1,0:T(8,128)(2,1)S(1)}, u32[]{:S(2)}, u32[]{:S(2)}) collective-permute-start(bf16[3,128,512]{2,1,0:T(8,128)(2,1)S(1)} %collective-permute-done.7.refs_1_), channel_id=1, source_target_pairs={{0,1},{1,0},{2,3},{3,2},{4,5},{5,4},{6,7},{7,6},{8,9},{9,8},{10,11... | collective-permute-start | bytes 1179656 | tf_op jit(solution)/shard_map/ppermute | solution.py:17
  75.8 32.3 %collective-permute-start.23 = (bf16[2,128,256]{2,1,0:T(8,128)(2,1)S(1)}, bf16[2,128,256]{2,1,0:T(8,128)(2,1)S(1)}, u32[]{:S(2)}, u32[]{:S(2)}) collective-permute-start(bf16[2,128,256]{2,1,0:T(8,128)(2,1)S(1)} %collective-permute-done.22), channel_id=1, source_target_pairs={{0,1},{1,0},{2,3},{3,2},{4,5},{5,4},{6,7},{7,6},{8,9},{9,8},{10,11... | collective-permute-start | bytes 393224 | tf_op jit(solution)/shard_map/ppermute | solution.py:17
  75.9 26.8 %collective-permute-start.19 = (bf16[256,1024]{1,0:T(8,128)(2,1)S(1)}, bf16[256,1024]{1,0:T(8,128)(2,1)S(1)}, u32[]{:S(2)}, u32[]{:S(2)}) collective-permute-start(bf16[256,1024]{1,0:T(8,128)(2,1)S(1)} %get-tuple-element.41), channel_id=1, source_target_pairs={{0,8},{8,16},{16,24},{1,9},{9,17},{17,25},{2,10},{10,18},{18,26},{... | collective-permute-start | bytes 1572872 | tf_op jit(solution)/shard_map/ppermute | solution.py:12
  81.8 16.0 %collective-permute-start.24 = (bf16[256,1024]{1,0:T(8,128)(2,1)S(1)}, bf16[256,1024]{1,0:T(8,128)(2,1)S(1)}, u32[]{:S(2)}, u32[]{:S(2)}) collective-permute-start(bf16[256,1024]{1,0:T(8,128)(2,1)S(1)} %get-tuple-element.40), channel_id=1, source_target_pairs={{8,0},{16,8},{24,16},{9,1},{17,9},{25,17},{10,2},{18,10},{26,18},{... | collective-permute-start | bytes 1572872 | tf_op jit(solution)/shard_map/ppermute | solution.py:12
  84.8 18.4 %collective-permute-start.27 = (bf16[5,128,512]{2,1,0:T(8,128)(2,1)S(1)}, bf16[5,128,512]{2,1,0:T(8,128)(2,1)S(1)}, u32[]{:S(2)}, u32[]{:S(2)}) collective-permute-start(bf16[5,128,512]{2,1,0:T(8,128)(2,1)S(1)} %broadcast_select_fusion), channel_id=1, source_target_pairs={{0,4},{1,3},{2,6},{3,1},{4,0},{5,7},{6,2},{7,5},{8,12},{9,11},{10,... | collective-permute-start | bytes 1966088 | tf_op jit(solution)/shard_map/ppermute | solution.py:17
  99.1 15.0 %collective-permute-start.25 = (bf16[256,1024]{1,0:T(8,128)(2,1)S(1)}, bf16[256,1024]{1,0:T(8,128)(2,1)S(1)}, u32[]{:S(2)}, u32[]{:S(2)}) collective-permute-start(bf16[256,1024]{1,0:T(8,128)(2,1)S(1)} %get-tuple-element.45), channel_id=1, source_target_pairs={{0,8},{8,16},{16,24},{1,9},{9,17},{17,25},{2,10},{10,18},{18,26},{... | collective-permute-start | bytes 1572872 | tf_op jit(solution)/shard_map/ppermute | solution.py:12
  103.3 10.7 %collective-permute-start.28 = (bf16[5,128,512]{2,1,0:T(8,128)(2,1)S(1)}, bf16[5,128,512]{2,1,0:T(8,128)(2,1)S(1)}, u32[]{:S(2)}, u32[]{:S(2)}) collective-permute-start(bf16[5,128,512]{2,1,0:T(8,128)(2,1)S(1)} %broadcast_select_fusion.1.refs_0_), channel_id=1, source_target_pairs={{0,2},{1,5},{2,0},{3,7},{4,6},{5,1},{6,4},{7,3},{8,10},{9,13},{10,... | collective-permute-start | bytes 1966088 | tf_op jit(solution)/shard_map/ppermute | solution.py:17
  104.7 15.5 %collective-permute-start.31 = (bf16[256,1024]{1,0:T(8,128)(2,1)S(1)}, bf16[256,1024]{1,0:T(8,128)(2,1)S(1)}, u32[]{:S(2)}, u32[]{:S(2)}) collective-permute-start(bf16[256,1024]{1,0:T(8,128)(2,1)S(1)} %get-tuple-element.43), channel_id=1, source_target_pairs={{8,0},{16,8},{24,16},{9,1},{17,9},{25,17},{10,2},{18,10},{26,18},{... | collective-permute-start | bytes 1572872 | tf_op jit(solution)/shard_map/ppermute | solution.py:12
  108.7 12.0 %collective-permute-start.29 = (bf16[5,128,512]{2,1,0:T(8,128)(2,1)S(1)}, bf16[5,128,512]{2,1,0:T(8,128)(2,1)S(1)}, u32[]{:S(2)}, u32[]{:S(2)}) collective-permute-start(bf16[5,128,512]{2,1,0:T(8,128)(2,1)S(1)} %broadcast_select_fusion.1.refs_0_), channel_id=1, source_target_pairs={{0,1},{1,0},{2,3},{3,2},{4,5},{5,4},{6,7},{7,6},{8,9},{9,8},{10,11... | collective-permute-start | bytes 1966088 | tf_op jit(solution)/shard_map/ppermute | solution.py:17
  (14 other events, 75.9 us)
where the time goes:
time: 129 us; the launch traced here: 127 us
  waiting for transfers between devices  43.5 us (34%)
  starting transfers between devices  42.1 us (33%)
  other arithmetic  19.3 us (15%)
  matrix products  11.5 us (9%)
  local copies, waits for them, and re-layouts  5.06 us (4%)
  between operations  4.23 us (3%)
  Pallas kernels  1.73 us (1%)
    ppermute x26, waiting for transfers between devices, flip(): lax.ppermute(value, 'cols', [(d, d ^ 1 << bits[d & 1]) for d in range(cou...  21.9 us
    ppermute x6, starting transfers between devices, shifted(): lax.ppermute(value, axis, [(source, source + steps) for source in range(i...  21.9 us
    ppermute x6, waiting for transfers between devices, shifted(): lax.ppermute(value, axis, [(source, source + steps) for source in range(i...  21.6 us
    ppermute x26, starting transfers between devices, flip(): lax.ppermute(value, 'cols', [(d, d ^ 1 << bits[d & 1]) for d in range(cou...  20.2 us
    dot_general x4, matrix products, apply_many(): jnp.einsum('nab,nac->nbc', q, x, preferred_element_type=jnp.float32)  8.16 us
    unnamed x7, other arithmetic  7.42 us
    select_n x8, other arithmetic, keep(): return jnp.where(same, hold, got)  5.43 us
    another operation x5, other arithmetic, begin(): jnp.stack([jnp.where(self.owners[r] & 1 == self.core, self.own[part][m],...  3.67 us
  transfers between devices with their start and end apart: 32, of which 12 were waited for; matrix products, arithmetic and copies ran while one was open for 20% of the time, Pallas kernels for 1%

commit v1 on v0

v1 whole, which is shorter than its diff:
```python
import jax
import jax.numpy as jnp
from jax import lax
from jax.experimental import pallas as pl
from jax.experimental.pallas import tpu as pltpu
from jax.sharding import PartitionSpec as P


def shifted(value, axis, steps):
    count = lax.axis_size(axis)
    initial, last = (max(0, -steps), min(count, count - steps))
    return lax.ppermute(value, axis, [(source, source + steps) for source in range(initial, last)])


def flip(value, bits):
    count = lax.axis_size("cols")
    return lax.ppermute(value, "cols", [(d, d ^ (1 << bits[d & 1])) for d in range(count)])


def copy_all(copies):
    for copy in copies:
        copy.start()
    for copy in copies:
        copy.wait()


def small(flops=0, bytes_accessed=0):
    return dict(
        compiler_params=pltpu.CompilerParams(vmem_limit_bytes=1 << 20),
        cost_estimate=pl.CostEstimate(
            flops=flops, bytes_accessed=bytes_accessed, transcendentals=0
        ),
    )


ANY = pl.BlockSpec(memory_space=pl.ANY)


def after(value, done):
    def kernel(source, _, out, sem):
        copy_all([pltpu.make_async_copy(source, out, sem)])

    return pl.pallas_call(
        kernel,
        out_shape=jax.ShapeDtypeStruct(value.shape, value.dtype),
        in_specs=[ANY, ANY],
        out_specs=ANY,
        scratch_shapes=[pltpu.SemaphoreType.DMA],
        name="after",
        **small(bytes_accessed=4 * value.size),
    )(value, done)


def runs(ms):
    found = []
    for at, m in enumerate(ms):
        if found and found[-1][0] + found[-1][2] == m:
            found[-1][2] += 1
        else:
            found.append([m, at, 1])
    return found


def cut_slot(cut, groups, slot):
    _, _, _, rows, width = slot.shape
    pieces = [(group, k) for group in groups for k in range(4)]
    shapes = [jax.ShapeDtypeStruct((len(group), rows, width), slot.dtype) for group, _ in pieces]
    count = sum(len(runs(group)) for group, _ in pieces)

    def kernel(source, *refs):
        outs, sems = refs[:-1], refs[-1]
        me = lax.axis_index("cols")
        core = me & 1
        bit0 = (me >> cut[0]) & 1
        bit1 = (me >> cut[1]) & 1
        mine = jnp.where(core == 0, bit0, bit1)
        other = jnp.where(core == 0, bit1, bit0)
        places = ((1 - core, 1 - other), (core, 1 - mine), (1 - core, other), (core, mine))
        copies = []
        for (group, k), out in zip(pieces, outs):
            half, piece = places[k]
            for first, at, n in runs(group):
                copies.append(
                    pltpu.make_async_copy(
                        source.at[pl.ds(first, n), half, piece],
                        out.at[pl.ds(at, n)],
                        sems.at[len(copies)],
                    )
                )
        copy_all(copies)

    outs = pl.pallas_call(
        kernel,
        out_shape=shapes,
        in_specs=[ANY],
        out_specs=[ANY] * len(shapes),
        scratch_shapes=[pltpu.SemaphoreType.DMA((count,))],
        name="cut_slot",
        **small(bytes_accessed=4 * slot.size),
    )(slot)
    return [outs[4 * g : 4 * g + 4] for g in range(len(groups))]


def place_kernel(cut, hold, got, other_hold, other_got, out, sems):
    me = lax.axis_index("cols")
    core = me & 1
    rows = hold.shape[1]
    bit0 = (me >> cut[0]) & 1
    bit1 = (me >> cut[1]) & 1
    mine = jnp.where(core == 0, bit0, bit1)
    other = jnp.where(core == 0, bit1, bit0)
    slots = (
        (hold, core * 2 + mine),
        (got, core * 2 + 1 - mine),
        (other_hold, (1 - core) * 2 + other),
        (other_got, (1 - core) * 2 + 1 - other),
    )
    copies = [
        pltpu.make_async_copy(
            piece, out.at[:, pl.ds(pl.multiple_of(at * rows, rows), rows), :], sems.at[k]
        )
        for k, (piece, at) in enumerate(slots)
    ]
    copy_all(copies)


def place(cut, hold, got, other_hold, other_got):
    n, rows, width = hold.shape
    return pl.pallas_call(
        lambda *refs: place_kernel(cut, *refs),
        out_shape=jax.ShapeDtypeStruct((n, 4 * rows, width), hold.dtype),
        in_specs=[ANY] * 4,
        out_specs=ANY,
        scratch_shapes=[pltpu.SemaphoreType.DMA((4,))],
        name="place",
        **small(bytes_accessed=2 * n * 4 * rows * width * 2),
    )(hold, got, other_hold, other_got)


class Spread:
    def __init__(self, slot, owners_here, groups):
        count = lax.axis_size("cols")
        dims = count.bit_length() - 2
        self.me = lax.axis_index("cols")
        self.core = self.me & 1
        self.owners = owners_here
        self.cut = (1, dims)
        self.others = [(b, b - 1) for b in range(2, dims + 1)]
        self.own, self.theirs = [], []
        for give_out, own_out, give_hold, own_hold in cut_slot(self.cut, groups, slot):
            self.own.append((own_out, own_hold))
            self.theirs.append((flip(give_out, (0, 0)), flip(give_hold, (0, 0))))

    def bit(self, index, bits):
        return (index >> jnp.where(self.core == 0, bits[0], bits[1])) & 1

    def begin(self, round_index, group, first=None):
        here = (self.owners[round_index] & 1) == self.core
        out, hold = [
            jnp.where(here, own, theirs)
            for own, theirs in zip(self.own[group], self.theirs[group])
        ]
        if first is not None:
            out = after(out, first)
        return round_index, hold, flip(out, self.cut)

    def keep(self, state, bits):
        round_index, hold, got = state
        same = self.bit(self.me, bits) == self.bit(self.owners[round_index], bits)
        return jnp.where(same, hold, got)

    def middle(self, state):
        bits = self.cut
        for other in self.others:
            hold = self.keep(state, bits)
            state = (state[0], hold, flip(hold, other))
            bits = other
        return state

    def last(self, state):
        hold = self.keep(state, self.others[-1])
        return hold, flip(hold, self.cut)

    def join(self, hold, got):
        return place(self.cut, hold, got, flip(hold, (0, 0)), flip(got, (0, 0)))

    def join_above(self, hold, got):
        both = shifted(jnp.stack([hold, got]), "rows", 1)
        other = flip(both, (0, 0))
        return place(self.cut, both[:1], both[1:], other[:1], other[1:])[0]


def apply(q, x):
    product = lax.dot_general(q, x, (((0,), (0,)), ((), ())), preferred_element_type=jnp.float32)
    return product.astype(jnp.bfloat16)


def apply_many(q, x):
    product = jnp.einsum("nab,nac->nbc", q, x, preferred_element_type=jnp.float32)
    return product.astype(jnp.bfloat16)


def local(slab, transforms, owners):
    row_block = lax.axis_index("rows")
    last_block = lax.axis_size("rows") - 1
    window = transforms.shape[2]
    border = window // 2
    local_rows, local_cols = slab.shape
    wins = local_rows // window
    rounds = owners.shape[0]
    slot = transforms[0].reshape(2 * wins, 2, 2, window // 4, window)
    edge = [0, wins - 1, 2 * wins - 1]
    inside = [m for m in range(2 * wins) if m not in edge]
    spread = Spread(slot, owners[:, row_block], (edge, inside))

    states, pairs = {}, {}
    for r in range(rounds):
        for g in range(2):
            first = None if r == 0 else (states[r - 1, 1][2] if g == 0 else pairs[r - 1, 0][1])
            states[r, g] = spread.middle(spread.begin(r, g, first))
        for g in range(2):
            pairs[r, g] = spread.last(states[r, g])

    matrix = slab
    for r in range(rounds):
        head, tail = pairs[r, 0], pairs[r, 1]
        edges = spread.join(*head)
        head_rows = apply(edges[0], matrix[:window])
        tail_rows = apply(edges[1], matrix[local_rows - window :])
        begin, end = head_rows[:border], tail_rows[border:]
        below = shifted(begin, "rows", -1)
        above = shifted(end, "rows", 1)
        prev = spread.join_above(head[0][-1, :, border:], head[1][-1, :, border:])
        rest = spread.join(*tail)
        mid = apply_many(
            rest[: wins - 2],
            matrix[window : local_rows - window].reshape(wins - 2, window, local_cols),
        ).reshape(local_rows - 2 * window, local_cols)
        centre = jnp.concatenate([head_rows[border:], mid, tail_rows[:border]], 0)
        inner = apply_many(rest[wins - 2 :], centre.reshape(wins - 1, window, local_cols)).reshape(
            local_rows - window, local_cols
        )
        low = apply(edges[2, :, :border], jnp.concatenate([end, below], 0))
        low = jnp.where(row_block == last_block, end, low)
        top = apply(prev, jnp.concatenate([above, begin], 0))
        top = jnp.where(row_block == 0, begin, top)
        matrix = jnp.concatenate([top, inner, low], 0)
    return matrix


def solution(mesh):
    return jax.shard_map(
        local,
        mesh=mesh,
        in_specs=(P("rows", "cols"), P("cols", "rows", None), P()),
        out_specs=P("rows", "cols"),
        check_vma=False,
    )
```

time: 129 us -> 137 us (1.062); the launches traced: 127 us -> 137 us
  waiting for transfers between devices: 43.5 us -> 61.7 us
  other arithmetic: 19.3 us -> 10.7 us
  starting transfers between devices: 42.1 us -> 38.7 us
  Pallas kernels: 1.73 us -> 4.79 us
    ppermute x26, waiting for transfers between devices: 21.9 us -> 49.9 us  [flip(): lax.ppermute(value, 'cols', [(d, d ^ 1 << bits[d & 1]) for d in range(cou...]
    ppermute x6, waiting for transfers between devices: 21.6 us -> 11.8 us  [shifted(): lax.ppermute(value, axis, [(source, source + steps) for source in range(i...]
    unnamed x7 -> x0, other arithmetic: 7.42 us -> none
    select_n x0 -> x2, other arithmetic: none -> 3.84 us  [begin(): jnp.where(here, own, theirs)]
    another operation x5 -> x0, other arithmetic: 3.67 us -> none  [begin(): jnp.stack([jnp.where(self.owners[r] & 1 == self.core, self.own[part][m],...]
    slice x5 -> x0, local copies, waits for them, and re-layouts: 3.09 us -> none  [the longest x1 2.7 us: exchange(): got = [flip(give[lo:hi], (0, 0)) for give in self.give]]
    pallas_call x0 -> x3, Pallas kernels: none -> 2.93 us  [the longest x1 2.53 us: cut_slot(): pl.pallas_call(kernel, out_shape=shapes, in_specs=[ANY], out_specs=[ANY]...]
    ppermute x6, starting transfers between devices: 21.9 us -> 19 us  [shifted(): lax.ppermute(value, axis, [(source, source + steps) for source in range(i...]
  transfers between devices with their start and end apart: 32 -> 32, of which waited for: 12 -> 13; matrix products, arithmetic and copies ran while one was open for 20% -> 14% of each run, Pallas kernels for 1% -> 1%
where the time goes in v1:
time: 137 us
  waiting for transfers between devices  61.7 us (45%)
  starting transfers between devices  38.7 us (28%)
  matrix products  12.1 us (9%)
  other arithmetic  10.7 us (8%)
  local copies, waits for them, and re-layouts  5.03 us (4%)
  Pallas kernels  4.79 us (3%)
  between operations  3.87 us (3%)
    ppermute x26, waiting for transfers between devices, flip(): lax.ppermute(value, 'cols', [(d, d ^ 1 << bits[d & 1]) for d in range(cou...  49.9 us
    ppermute x26, starting transfers between devices, flip(): lax.ppermute(value, 'cols', [(d, d ^ 1 << bits[d & 1]) for d in range(cou...  19.8 us
    ppermute x6, starting transfers between devices, shifted(): lax.ppermute(value, axis, [(source, source + steps) for source in range(i...  19 us
    ppermute x6, waiting for transfers between devices, shifted(): lax.ppermute(value, axis, [(source, source + steps) for source in range(i...  11.8 us
    dot_general x4, matrix products, apply_many(): jnp.einsum('nab,nac->nbc', q, x, preferred_element_type=jnp.float32)  7.27 us
    dot_general x8, matrix products, apply(): lax.dot_general(q, x, (((0,), (0,)), ((), ())), preferred_element_type=jn...  4.79 us
    select_n x2, other arithmetic, begin(): jnp.where(here, own, theirs)  3.84 us
    select_n x7, other arithmetic, keep(): return jnp.where(same, hold, got)  3.13 us
  transfers between devices with their start and end apart: 32, of which 13 were waited for; matrix products, arithmetic and copies ran while one was open for 14% of the time, Pallas kernels for 1%

profile of v1, /device:TPU:8, one launch (start us, length us, event | category | flops | bytes accessed | tf_op | source)
XLA Modules:
  0.0 136.9 jit_solution(7863745073017264951)
XLA Ops:
  0.0 2.2 %copy-done.2 = bf16[1,4096,512]{2,1,0:T(8,128)(2,1)S(1)} copy-done((bf16[1,4096,512]{2,1,0:T(8,128)(2,1)S(1)}, bf16[1,4096,512]{2,1,0:T(8,128)(2,1)}, u32[]{:S(2)}) %copy-start.2) | copy-done | bytes 4194328
  2.2 2.5 %cut_slot.1 = (bf16[3,128,512]{2,1,0:T(8,128)(2,1)S(1)}, bf16[3,128,512]{2,1,0:T(8,128)(2,1)S(1)}, bf16[3,128,512]{2,1,0:T(8,128)(2,1)S(1)}, bf16[3,128,512]{2,1...) custom-call(bf16[8,2,2,128,512]{4,3,2,1,0:T(8,128)(2,1)S(1)} %bitcast.43), custom_call_target="tpu_custom_call" | custom-call | bytes 8388608 | tf_op jit(solution)/shard_map/cut_slot/pallas_call | solution.py:92
  11.7 5.9 %collective-permute-done.11 = bf16[3,128,512]{2,1,0:T(8,128)(2,1)S(1)} collective-permute-done((bf16[3,128,512]{2,1,0:T(8,128)(2,1)}, bf16[3,128,512]{2,1,0:T(8,128)(2,1)S(1)}, u32[]{:S(2)}, u32[]{:S(2)}) %collective-permute-start.11) | collective-permute-done | bytes 393248 | tf_op jit(solution)/shard_map/ppermute | solution.py:17
  20.9 5.8 %collective-permute-done.12 = bf16[3,128,512]{2,1,0:T(8,128)(2,1)} collective-permute-done((bf16[3,128,512]{2,1,0:T(8,128)(2,1)S(1)}, bf16[3,128,512]{2,1,0:T(8,128)(2,1)}, u32[]{:S(2)}, u32[]{:S(2)}) %collective-permute-start.12) | collective-permute-done | bytes 393248 | tf_op jit(solution)/shard_map/ppermute | solution.py:17
  30.8 3.7 %collective-permute-done.13.refs_1_._ = bf16[3,128,512]{2,1,0:T(8,128)(2,1)S(1)} collective-permute-done((bf16[3,128,512]{2,1,0:T(8,128)(2,1)S(1)}, bf16[3,128,512]{2,1,0:T(8,128)(2,1)S(1)}, u32[]{:S(2)}, u32[]{:S(2)}) %collective-permute-start.13) | collective-permute-done | bytes 393248 | tf_op jit(solution)/shard_map/ppermute | solution.py:17
  37.0 4.5 %collective-permute-start.16 = (bf16[2,128,256]{2,1,0:T(8,128)(2,1)}, bf16[2,128,256]{2,1,0:T(8,128)(2,1)}, u32[]{:S(2)}, u32[]{:S(2)}) collective-permute-start(bf16[2,128,256]{2,1,0:T(8,128)(2,1)} %pad_maximum_fusion.7), channel_id=1, source_target_pairs={{0,8},{8,16},{16,24},{1,9},{9,17},{17,25},{2,10},{10,18},{18,26},{... | collective-permute-start | bytes 393224 | tf_op jit(solution)/shard_map/ppermute | solution.py:12
  45.8 2.9 %collective-permute-done.26 = bf16[5,128,512]{2,1,0:T(8,128)(2,1)} collective-permute-done((bf16[5,128,512]{2,1,0:T(8,128)(2,1)S(1)}, bf16[5,128,512]{2,1,0:T(8,128)(2,1)}, u32[]{:S(2)}, u32[]{:S(2)}) %collective-permute-start.26) | collective-permute-done | bytes 655392 | tf_op jit(solution)/shard_map/ppermute | solution.py:17
  50.4 2.6 %collective-permute-start.5 = (bf16[5,128,512]{2,1,0:T(8,128)(2,1)S(1)}, bf16[5,128,512]{2,1,0:T(8,128)(2,1)S(1)}, u32[]{:S(2)}, u32[]{:S(2)}) collective-permute-start(bf16[5,128,512]{2,1,0:T(8,128)(2,1)S(1)} %get-tuple-element.22), channel_id=1, source_target_pairs={{0,4},{1,3},{2,6},{3,1},{4,0},{5,7},{6,2},{7,5},{8,12},{9,11},{10,... | collective-permute-start | bytes 1966088 | tf_op jit(solution)/shard_map/ppermute | solution.py:17
  55.2 6.3 %collective-permute-done.5._ = bf16[5,128,512]{2,1,0:T(8,128)(2,1)S(1)} collective-permute-done((bf16[5,128,512]{2,1,0:T(8,128)(2,1)S(1)}, bf16[5,128,512]{2,1,0:T(8,128)(2,1)S(1)}, u32[]{:S(2)}, u32[]{:S(2)}) %collective-permute-start.5) | collective-permute-done | bytes 655392 | tf_op jit(solution)/shard_map/ppermute | solution.py:17
  66.1 7.6 %collective-permute-done.6 = bf16[3,128,512]{2,1,0:T(8,128)(2,1)S(1)} collective-permute-done((bf16[3,128,512]{2,1,0:T(8,128)(2,1)S(1)}, bf16[3,128,512]{2,1,0:T(8,128)(2,1)S(1)}, u32[]{:S(2)}, u32[]{:S(2)}) %collective-permute-start.6) | collective-permute-done | bytes 393248 | tf_op jit(solution)/shard_map/ppermute | solution.py:17
  73.9 2.2 %collective-permute-start.7 = (bf16[3,128,512]{2,1,0:T(8,128)(2,1)S(1)}, bf16[3,128,512]{2,1,0:T(8,128)(2,1)S(1)}, u32[]{:S(2)}, u32[]{:S(2)}) collective-permute-start(bf16[3,128,512]{2,1,0:T(8,128)(2,1)S(1)} %select_select_fusion.3), channel_id=1, source_target_pairs={{0,4},{1,3},{2,6},{3,1},{4,0},{5,7},{6,2},{7,5},{8,12},{9,11},{10,... | collective-permute-start | bytes 1179656 | tf_op jit(solution)/shard_map/ppermute | solution.py:17
  76.1 2.4 %collective-permute-start.24 = (bf16[256,1024]{1,0:T(8,128)(2,1)S(1)}, bf16[256,1024]{1,0:T(8,128)(2,1)S(1)}, u32[]{:S(2)}, u32[]{:S(2)}) collective-permute-start(bf16[256,1024]{1,0:T(8,128)(2,1)S(1)} %get-tuple-element.30), channel_id=1, source_target_pairs={{8,0},{16,8},{24,16},{9,1},{17,9},{25,17},{10,2},{18,10},{26,18},{... | collective-permute-start | bytes 1572872 | tf_op jit(solution)/shard_map/ppermute | solution.py:12
  78.5 3.5 %collective-permute-start.18 = (bf16[256,1024]{1,0:T(8,128)(2,1)S(1)}, bf16[256,1024]{1,0:T(8,128)(2,1)S(1)}, u32[]{:S(2)}, u32[]{:S(2)}) collective-permute-start(bf16[256,1024]{1,0:T(8,128)(2,1)S(1)} %get-tuple-element.32), channel_id=1, source_target_pairs={{0,8},{8,16},{16,24},{1,9},{9,17},{17,25},{2,10},{10,18},{18,26},{... | collective-permute-start | bytes 1572872 | tf_op jit(solution)/shard_map/ppermute | solution.py:12
  82.1 4.9 %collective-permute-done.19.refs_1_ = bf16[5,128,512]{2,1,0:T(8,128)(2,1)S(1)} collective-permute-done((bf16[5,128,512]{2,1,0:T(8,128)(2,1)S(1)}, bf16[5,128,512]{2,1,0:T(8,128)(2,1)S(1)}, u32[]{:S(2)}, u32[]{:S(2)}) %collective-permute-start.19) | collective-permute-done | bytes 655392 | tf_op jit(solution)/shard_map/ppermute | solution.py:17
  90.2 7.4 %collective-permute-done.28.refs_1_ = bf16[5,128,512]{2,1,0:T(8,128)(2,1)S(1)} collective-permute-done((bf16[5,128,512]{2,1,0:T(8,128)(2,1)S(1)}, bf16[5,128,512]{2,1,0:T(8,128)(2,1)S(1)}, u32[]{:S(2)}, u32[]{:S(2)}) %collective-permute-start.28) | collective-permute-done | bytes 655392 | tf_op jit(solution)/shard_map/ppermute | solution.py:17
  97.6 4.2 %collective-permute-done.8.refs_1_ = bf16[3,128,512]{2,1,0:T(8,128)(2,1)S(1)} collective-permute-done((bf16[3,128,512]{2,1,0:T(8,128)(2,1)S(1)}, bf16[3,128,512]{2,1,0:T(8,128)(2,1)S(1)}, u32[]{:S(2)}, u32[]{:S(2)}) %collective-permute-start.8) | collective-permute-done | bytes 393248 | tf_op jit(solution)/shard_map/ppermute | solution.py:17
  101.9 2.8 %collective-permute-start.22 = (bf16[2,128,256]{2,1,0:T(8,128)(2,1)S(1)}, bf16[2,128,256]{2,1,0:T(8,128)(2,1)S(1)}, u32[]{:S(2)}, u32[]{:S(2)}) collective-permute-start(bf16[2,128,256]{2,1,0:T(8,128)(2,1)S(1)} %pad_maximum_fusion.8), channel_id=1, source_target_pairs={{0,8},{8,16},{16,24},{1,9},{9,17},{17,25},{2,10},{10,18},{18,26},{... | collective-permute-start | bytes 393224 | tf_op jit(solution)/shard_map/ppermute | solution.py:12
  107.2 2.1 %convolution_convert_fusion.1 = bf16[3,512,1024]{2,1,0:T(8,128)(2,1)S(1)} fusion(bf16[5,512,512]{2,1,0:T(8,128)(2,1)S(1)} %place.9, bf16[3,512,1024]{2,1,0:T(8,128)(2,1)S(1)} %bitcast.47), kind=kOutput, calls=%fused_computation.4 | convolution fusion | flops 1612185600 | bytes 8912896 | tf_op jit(solution)/shard_map/nab,nac->nbc/dot_general | solution.py:199
  115.1 3.4 %collective-permute-start.31 = (bf16[256,1024]{1,0:T(8,128)(2,1)S(1)}, bf16[256,1024]{1,0:T(8,128)(2,1)S(1)}, u32[]{:S(2)}, u32[]{:S(2)}) collective-permute-start(bf16[256,1024]{1,0:T(8,128)(2,1)S(1)} %get-tuple-element.26), channel_id=1, source_target_pairs={{8,0},{16,8},{24,16},{9,1},{17,9},{25,17},{10,2},{18,10},{26,18},{... | collective-permute-start | bytes 1572872 | tf_op jit(solution)/shard_map/ppermute | solution.py:12
  118.4 2.5 %collective-permute-start.25 = (bf16[256,1024]{1,0:T(8,128)(2,1)S(1)}, bf16[256,1024]{1,0:T(8,128)(2,1)S(1)}, u32[]{:S(2)}, u32[]{:S(2)}) collective-permute-start(bf16[256,1024]{1,0:T(8,128)(2,1)S(1)} %get-tuple-element.28), channel_id=1, source_target_pairs={{0,8},{8,16},{16,24},{1,9},{9,17},{17,25},{2,10},{10,18},{18,26},{... | collective-permute-start | bytes 1572872 | tf_op jit(solution)/shard_map/ppermute | solution.py:12
  121.4 2.1 %convolution_convert_fusion = bf16[3,512,1024]{2,1,0:T(8,128)(2,1)S(1)} fusion(bf16[5,512,512]{2,1,0:T(8,128)(2,1)S(1)} %place.11, bf16[3,512,1024]{2,1,0:T(8,128)(2,1)S(1)} %bitcast.48), kind=kOutput, calls=%fused_computation.3 | convolution fusion | flops 1612185600 | bytes 8912896 | tf_op jit(solution)/shard_map/nab,nac->nbc/dot_general | solution.py:199
  123.5 7.6 %collective-permute-done.31 = bf16[256,1024]{1,0:T(8,128)(2,1)S(1)} collective-permute-done((bf16[256,1024]{1,0:T(8,128)(2,1)S(1)}, bf16[256,1024]{1,0:T(8,128)(2,1)S(1)}, u32[]{:S(2)}, u32[]{:S(2)}) %collective-permute-start.31) | collective-permute-done | bytes 524320 | tf_op jit(solution)/shard_map/ppermute | solution.py:12
  131.5 2.6 %collective-permute-done.25 = bf16[256,1024]{1,0:T(8,128)(2,1)S(1)} collective-permute-done((bf16[256,1024]{1,0:T(8,128)(2,1)S(1)}, bf16[256,1024]{1,0:T(8,128)(2,1)S(1)}, u32[]{:S(2)}, u32[]{:S(2)}) %collective-permute-start.25) | collective-permute-done | bytes 524320 | tf_op jit(solution)/shard_map/ppermute | solution.py:12
  134.6 2.3 %pad_maximum_fusion = bf16[2048,1024]{1,0:T(8,128)(2,1)} fusion(bf16[256,1024]{1,0:T(8,128)(2,1)S(1)} %fusion.3, bf16[1536,1024]{1,0:T(8,128)(2,1)S(1)} %bitcast.49, bf16[256,1024]{1,0:T(8,128)(2,1)S(1)} %fusion.2), kind=kLoop, calls=%fused_computation | loop fusion | flops 12582912 | bytes 8388608 | tf_op jit(solution)/shard_map/concatenate | solution.py:247
  (102 shorter events, 39.1 us)
Async XLA Ops:
  9.6 8.0 %collective-permute-start.11 = (bf16[3,128,512]{2,1,0:T(8,128)(2,1)}, bf16[3,128,512]{2,1,0:T(8,128)(2,1)S(1)}, u32[]{:S(2)}, u32[]{:S(2)}) collective-permute-start(bf16[3,128,512]{2,1,0:T(8,128)(2,1)} %get-tuple-element.34), channel_id=1, source_target_pairs={{0,2},{1,5},{2,0},{3,7},{4,6},{5,1},{6,4},{7,3},{8,10},{9,13},{10,... | collective-permute-start | bytes 1179656 | tf_op jit(solution)/shard_map/ppermute | solution.py:17
  28.3 16.9 %collective-permute-start.2 = (bf16[5,128,512]{2,1,0:T(8,128)(2,1)S(1)}, bf16[5,128,512]{2,1,0:T(8,128)(2,1)}, u32[]{:S(2)}, u32[]{:S(2)}) collective-permute-start(bf16[5,128,512]{2,1,0:T(8,128)(2,1)S(1)} %get-tuple-element.18), channel_id=1, source_target_pairs={{0,1},{1,0},{2,3},{3,2},{4,5},{5,4},{6,7},{7,6},{8,9},{9,8},{10,11... | collective-permute-start | bytes 1966088 | tf_op jit(solution)/shard_map/ppermute | solution.py:17
  30.3 15.5 %collective-permute-start.4 = (bf16[5,128,512]{2,1,0:T(8,128)(2,1)}, bf16[5,128,512]{2,1,0:T(8,128)(2,1)}, u32[]{:S(2)}, u32[]{:S(2)}) collective-permute-start(bf16[5,128,512]{2,1,0:T(8,128)(2,1)} %get-tuple-element.24), channel_id=1, source_target_pairs={{0,2},{1,5},{2,0},{3,7},{4,6},{5,1},{6,4},{7,3},{8,10},{9,13},{10,... | collective-permute-start | bytes 1966088 | tf_op jit(solution)/shard_map/ppermute | solution.py:17
  34.8 13.9 %collective-permute-start.26 = (bf16[5,128,512]{2,1,0:T(8,128)(2,1)S(1)}, bf16[5,128,512]{2,1,0:T(8,128)(2,1)}, u32[]{:S(2)}, u32[]{:S(2)}) collective-permute-start(bf16[5,128,512]{2,1,0:T(8,128)(2,1)S(1)} %after.3), channel_id=1, source_target_pairs={{0,2},{1,5},{2,0},{3,7},{4,6},{5,1},{6,4},{7,3},{8,10},{9,13},{10,... | collective-permute-start | bytes 1966088 | tf_op jit(solution)/shard_map/ppermute | solution.py:17
  42.6 10.8 %collective-permute-start.14 = (bf16[3,128,512]{2,1,0:T(8,128)(2,1)S(1)}, bf16[3,128,512]{2,1,0:T(8,128)(2,1)S(1)}, u32[]{:S(2)}, u32[]{:S(2)}) collective-permute-start(bf16[3,128,512]{2,1,0:T(8,128)(2,1)S(1)} %broadcast_select_fusion.5.refs_0_), channel_id=1, source_target_pairs={{0,1},{1,0},{2,3},{3,2},{4,5},{5,4},{6,7},{7,6},{8,9},{9,8},{10,11... | collective-permute-start | bytes 1179656 | tf_op jit(solution)/shard_map/ppermute | solution.py:17
  44.3 9.1 %collective-permute-start.15 = (bf16[3,128,512]{2,1,0:T(8,128)(2,1)S(1)}, bf16[3,128,512]{2,1,0:T(8,128)(2,1)S(1)}, u32[]{:S(2)}, u32[]{:S(2)}) collective-permute-start(bf16[3,128,512]{2,1,0:T(8,128)(2,1)S(1)} %collective-permute-done.13.refs_1_._), channel_id=1, source_target_pairs={{0,1},{1,0},{2,3},{3,2},{4,5},{5,4},{6,7},{7,6},{8,9},{9,8},{10,11... | collective-permute-start | bytes 1179656 | tf_op jit(solution)/shard_map/ppermute | solution.py:17
  50.4 11.1 %collective-permute-start.5 = (bf16[5,128,512]{2,1,0:T(8,128)(2,1)S(1)}, bf16[5,128,512]{2,1,0:T(8,128)(2,1)S(1)}, u32[]{:S(2)}, u32[]{:S(2)}) collective-permute-start(bf16[5,128,512]{2,1,0:T(8,128)(2,1)S(1)} %get-tuple-element.22), channel_id=1, source_target_pairs={{0,4},{1,3},{2,6},{3,1},{4,0},{5,7},{6,2},{7,5},{8,12},{9,11},{10,... | collective-permute-start | bytes 1966088 | tf_op jit(solution)/shard_map/ppermute | solution.py:17
  61.7 12.0 %collective-permute-start.6 = (bf16[3,128,512]{2,1,0:T(8,128)(2,1)S(1)}, bf16[3,128,512]{2,1,0:T(8,128)(2,1)S(1)}, u32[]{:S(2)}, u32[]{:S(2)}) collective-permute-start(bf16[3,128,512]{2,1,0:T(8,128)(2,1)S(1)} %after.2), channel_id=1, source_target_pairs={{0,2},{1,5},{2,0},{3,7},{4,6},{5,1},{6,4},{7,3},{8,10},{9,13},{10,... | collective-permute-start | bytes 1179656 | tf_op jit(solution)/shard_map/ppermute | solution.py:17
  63.4 18.6 %collective-permute-start.27 = (bf16[5,128,512]{2,1,0:T(8,128)(2,1)S(1)}, bf16[5,128,512]{2,1,0:T(8,128)(2,1)S(1)}, u32[]{:S(2)}, u32[]{:S(2)}) collective-permute-start(bf16[5,128,512]{2,1,0:T(8,128)(2,1)S(1)} %get-tuple-element.21), channel_id=1, source_target_pairs={{0,4},{1,3},{2,6},{3,1},{4,0},{5,7},{6,2},{7,5},{8,12},{9,11},{10,... | collective-permute-start | bytes 1966088 | tf_op jit(solution)/shard_map/ppermute | solution.py:17
  65.5 21.5 %collective-permute-start.19 = (bf16[5,128,512]{2,1,0:T(8,128)(2,1)S(1)}, bf16[5,128,512]{2,1,0:T(8,128)(2,1)S(1)}, u32[]{:S(2)}, u32[]{:S(2)}) collective-permute-start(bf16[5,128,512]{2,1,0:T(8,128)(2,1)S(1)} %broadcast_select_fusion.2.refs_0_), channel_id=1, source_target_pairs={{0,2},{1,5},{2,0},{3,7},{4,6},{5,1},{6,4},{7,3},{8,10},{9,13},{10,... | collective-permute-start | bytes 1966088 | tf_op jit(solution)/shard_map/ppermute | solution.py:17
  73.9 13.7 %collective-permute-start.7 = (bf16[3,128,512]{2,1,0:T(8,128)(2,1)S(1)}, bf16[3,128,512]{2,1,0:T(8,128)(2,1)S(1)}, u32[]{:S(2)}, u32[]{:S(2)}) collective-permute-start(bf16[3,128,512]{2,1,0:T(8,128)(2,1)S(1)} %select_select_fusion.3), channel_id=1, source_target_pairs={{0,4},{1,3},{2,6},{3,1},{4,0},{5,7},{6,2},{7,5},{8,12},{9,11},{10,... | collective-permute-start | bytes 1179656 | tf_op jit(solution)/shard_map/ppermute | solution.py:17
  76.1 11.5 %collective-permute-start.24 = (bf16[256,1024]{1,0:T(8,128)(2,1)S(1)}, bf16[256,1024]{1,0:T(8,128)(2,1)S(1)}, u32[]{:S(2)}, u32[]{:S(2)}) collective-permute-start(bf16[256,1024]{1,0:T(8,128)(2,1)S(1)} %get-tuple-element.30), channel_id=1, source_target_pairs={{8,0},{16,8},{24,16},{9,1},{17,9},{25,17},{10,2},{18,10},{26,18},{... | collective-permute-start | bytes 1572872 | tf_op jit(solution)/shard_map/ppermute | solution.py:12
  78.5 11.2 %collective-permute-start.18 = (bf16[256,1024]{1,0:T(8,128)(2,1)S(1)}, bf16[256,1024]{1,0:T(8,128)(2,1)S(1)}, u32[]{:S(2)}, u32[]{:S(2)}) collective-permute-start(bf16[256,1024]{1,0:T(8,128)(2,1)S(1)} %get-tuple-element.32), channel_id=1, source_target_pairs={{0,8},{8,16},{16,24},{1,9},{9,17},{17,25},{2,10},{10,18},{18,26},{... | collective-permute-start | bytes 1572872 | tf_op jit(solution)/shard_map/ppermute | solution.py:12
  82.0 19.9 %collective-permute-start.20 = (bf16[5,128,512]{2,1,0:T(8,128)(2,1)S(1)}, bf16[5,128,512]{2,1,0:T(8,128)(2,1)S(1)}, u32[]{:S(2)}, u32[]{:S(2)}) collective-permute-start(bf16[5,128,512]{2,1,0:T(8,128)(2,1)S(1)} %broadcast_select_fusion.2.refs_0_), channel_id=1, source_target_pairs={{0,1},{1,0},{2,3},{3,2},{4,5},{5,4},{6,7},{7,6},{8,9},{9,8},{10,11... | collective-permute-start | bytes 1966088 | tf_op jit(solution)/shard_map/ppermute | solution.py:17
  87.0 10.6 %collective-permute-start.28 = (bf16[5,128,512]{2,1,0:T(8,128)(2,1)S(1)}, bf16[5,128,512]{2,1,0:T(8,128)(2,1)S(1)}, u32[]{:S(2)}, u32[]{:S(2)}) collective-permute-start(bf16[5,128,512]{2,1,0:T(8,128)(2,1)S(1)} %broadcast_select_fusion.1.refs_0_), channel_id=1, source_target_pairs={{0,2},{1,5},{2,0},{3,7},{4,6},{5,1},{6,4},{7,3},{8,10},{9,13},{10,... | collective-permute-start | bytes 1966088 | tf_op jit(solution)/shard_map/ppermute | solution.py:17
  87.6 17.1 %collective-permute-start.21 = (bf16[5,128,512]{2,1,0:T(8,128)(2,1)S(1)}, bf16[5,128,512]{2,1,0:T(8,128)(2,1)S(1)}, u32[]{:S(2)}, u32[]{:S(2)}) collective-permute-start(bf16[5,128,512]{2,1,0:T(8,128)(2,1)S(1)} %collective-permute-done.19.refs_1_), channel_id=1, source_target_pairs={{0,1},{1,0},{2,3},{3,2},{4,5},{5,4},{6,7},{7,6},{8,9},{9,8},{10,11... | collective-permute-start | bytes 1966088 | tf_op jit(solution)/shard_map/ppermute | solution.py:17
  87.7 14.2 %collective-permute-start.8 = (bf16[3,128,512]{2,1,0:T(8,128)(2,1)S(1)}, bf16[3,128,512]{2,1,0:T(8,128)(2,1)S(1)}, u32[]{:S(2)}, u32[]{:S(2)}) collective-permute-start(bf16[3,128,512]{2,1,0:T(8,128)(2,1)S(1)} %broadcast_select_fusion.7.refs_0_), channel_id=1, source_target_pairs={{0,2},{1,5},{2,0},{3,7},{4,6},{5,1},{6,4},{7,3},{8,10},{9,13},{10,... | collective-permute-start | bytes 1179656 | tf_op jit(solution)/shard_map/ppermute | solution.py:17
  90.2 19.3 %collective-permute-start.29 = (bf16[5,128,512]{2,1,0:T(8,128)(2,1)S(1)}, bf16[5,128,512]{2,1,0:T(8,128)(2,1)S(1)}, u32[]{:S(2)}, u32[]{:S(2)}) collective-permute-start(bf16[5,128,512]{2,1,0:T(8,128)(2,1)S(1)} %broadcast_select_fusion.1.refs_0_), channel_id=1, source_target_pairs={{0,1},{1,0},{2,3},{3,2},{4,5},{5,4},{6,7},{7,6},{8,9},{9,8},{10,11... | collective-permute-start | bytes 1966088 | tf_op jit(solution)/shard_map/ppermute | solution.py:17
  97.6 11.9 %collective-permute-start.30 = (bf16[5,128,512]{2,1,0:T(8,128)(2,1)S(1)}, bf16[5,128,512]{2,1,0:T(8,128)(2,1)S(1)}, u32[]{:S(2)}, u32[]{:S(2)}) collective-permute-start(bf16[5,128,512]{2,1,0:T(8,128)(2,1)S(1)} %collective-permute-done.28.refs_1_), channel_id=1, source_target_pairs={{0,1},{1,0},{2,3},{3,2},{4,5},{5,4},{6,7},{7,6},{8,9},{9,8},{10,11... | collective-permute-start | bytes 1966088 | tf_op jit(solution)/shard_map/ppermute | solution.py:17
  101.8 11.3 %collective-permute-start.9 = (bf16[3,128,512]{2,1,0:T(8,128)(2,1)S(1)}, bf16[3,128,512]{2,1,0:T(8,128)(2,1)S(1)}, u32[]{:S(2)}, u32[]{:S(2)}) collective-permute-start(bf16[3,128,512]{2,1,0:T(8,128)(2,1)S(1)} %broadcast_select_fusion.7.refs_0_), channel_id=1, source_target_pairs={{0,1},{1,0},{2,3},{3,2},{4,5},{5,4},{6,7},{7,6},{8,9},{9,8},{10,11... | collective-permute-start | bytes 1179656 | tf_op jit(solution)/shard_map/ppermute | solution.py:17
  101.9 9.4 %collective-permute-start.22 = (bf16[2,128,256]{2,1,0:T(8,128)(2,1)S(1)}, bf16[2,128,256]{2,1,0:T(8,128)(2,1)S(1)}, u32[]{:S(2)}, u32[]{:S(2)}) collective-permute-start(bf16[2,128,256]{2,1,0:T(8,128)(2,1)S(1)} %pad_maximum_fusion.8), channel_id=1, source_target_pairs={{0,8},{8,16},{16,24},{1,9},{9,17},{17,25},{2,10},{10,18},{18,26},{... | collective-permute-start | bytes 393224 | tf_op jit(solution)/shard_map/ppermute | solution.py:12
  104.7 8.4 %collective-permute-start.10 = (bf16[3,128,512]{2,1,0:T(8,128)(2,1)S(1)}, bf16[3,128,512]{2,1,0:T(8,128)(2,1)S(1)}, u32[]{:S(2)}, u32[]{:S(2)}) collective-permute-start(bf16[3,128,512]{2,1,0:T(8,128)(2,1)S(1)} %collective-permute-done.8.refs_1_), channel_id=1, source_target_pairs={{0,1},{1,0},{2,3},{3,2},{4,5},{5,4},{6,7},{7,6},{8,9},{9,8},{10,11... | collective-permute-start | bytes 1179656 | tf_op jit(solution)/shard_map/ppermute | solution.py:17
  115.1 16.0 %collective-permute-start.31 = (bf16[256,1024]{1,0:T(8,128)(2,1)S(1)}, bf16[256,1024]{1,0:T(8,128)(2,1)S(1)}, u32[]{:S(2)}, u32[]{:S(2)}) collective-permute-start(bf16[256,1024]{1,0:T(8,128)(2,1)S(1)} %get-tuple-element.26), channel_id=1, source_target_pairs={{8,0},{16,8},{24,16},{9,1},{17,9},{25,17},{10,2},{18,10},{26,18},{... | collective-permute-start | bytes 1572872 | tf_op jit(solution)/shard_map/ppermute | solution.py:12
  118.4 15.7 %collective-permute-start.25 = (bf16[256,1024]{1,0:T(8,128)(2,1)S(1)}, bf16[256,1024]{1,0:T(8,128)(2,1)S(1)}, u32[]{:S(2)}, u32[]{:S(2)}) collective-permute-start(bf16[256,1024]{1,0:T(8,128)(2,1)S(1)} %get-tuple-element.28), channel_id=1, source_target_pairs={{0,8},{8,16},{16,24},{1,9},{9,17},{17,25},{2,10},{10,18},{18,26},{... | collective-permute-start | bytes 1572872 | tf_op jit(solution)/shard_map/ppermute | solution.py:12
  (14 other events, 68.3 us)

commit v2 on v1

--- a/solution.py
+++ b/solution.py
@@ -24,9 +24,9 @@
         copy.wait()
 
 
-def small(flops=0, bytes_accessed=0):
+def small(flops=0, bytes_accessed=0, limit=1 << 20):
     return dict(
-        compiler_params=pltpu.CompilerParams(vmem_limit_bytes=1 << 20),
+        compiler_params=pltpu.CompilerParams(vmem_limit_bytes=limit),
         cost_estimate=pl.CostEstimate(
             flops=flops, bytes_accessed=bytes_accessed, transcendentals=0
         ),
@@ -61,11 +61,10 @@
     return found
 
 
-def cut_slot(cut, groups, slot):
+def cut_slot(cut, order, kinds, slot):
     _, _, _, rows, width = slot.shape
-    pieces = [(group, k) for group in groups for k in range(4)]
-    shapes = [jax.ShapeDtypeStruct((len(group), rows, width), slot.dtype) for group, _ in pieces]
-    count = sum(len(runs(group)) for group, _ in pieces)
+    shapes = [jax.ShapeDtypeStruct((len(order), rows, width), slot.dtype) for _ in kinds]
+    spans = runs(order)
 
     def kernel(source, *refs):
         outs, sems = refs[:-1], refs[-1]
@@ -75,11 +74,12 @@
         bit1 = (me >> cut[1]) & 1
         mine = jnp.where(core == 0, bit0, bit1)
         other = jnp.where(core == 0, bit1, bit0)
-        places = ((1 - core, 1 - other), (core, 1 - mine), (1 - core, other), (core, mine))
         copies = []
-        for (group, k), out in zip(pieces, outs):
-            half, piece = places[k]
-            for first, at, n in runs(group):
+        for (own, hold), out in zip(kinds, outs):
+            half = core if own else 1 - core
+            piece = mine if own else other
+            piece = piece if hold else 1 - piece
+            for first, at, n in spans:
                 copies.append(
                     pltpu.make_async_copy(
                         source.at[pl.ds(first, n), half, piece],
@@ -89,16 +89,15 @@
                 )
         copy_all(copies)
 
-    outs = pl.pallas_call(
+    return pl.pallas_call(
         kernel,
         out_shape=shapes,
-        in_specs=[ANY],
+        in_specs=[pl.BlockSpec(memory_space=pltpu.HBM)],
         out_specs=[ANY] * len(shapes),
-        scratch_shapes=[pltpu.SemaphoreType.DMA((count,))],
+        scratch_shapes=[pltpu.SemaphoreType.DMA((len(spans) * len(kinds),))],
         name="cut_slot",
-        **small(bytes_accessed=4 * slot.size),
+        **small(bytes_accessed=len(kinds) * slot.size, limit=(60 if len(kinds) == 1 else 1) << 20),
     )(slot)
-    return [outs[4 * g : 4 * g + 4] for g in range(len(groups))]
 
 
 def place_kernel(cut, hold, got, other_hold, other_got, out, sems):
@@ -146,10 +145,17 @@
         self.owners = owners_here
         self.cut = (1, dims)
         self.others = [(b, b - 1) for b in range(2, dims + 1)]
-        self.own, self.theirs = [], []
-        for give_out, own_out, give_hold, own_hold in cut_slot(self.cut, groups, slot):
-            self.own.append((own_out, own_hold))
-            self.theirs.append((flip(give_out, (0, 0)), flip(give_hold, (0, 0))))
+        order = [m for group in groups for m in group]
+        self.spans, at = [], 0
+        for group in groups:
+            self.spans.append(slice(at, at + len(group)))
+            at += len(group)
+        (give_out,) = cut_slot(self.cut, order, [(False, False)], slot)
+        own_out, give_hold, own_hold = cut_slot(
+            self.cut, order, [(True, False), (False, True), (True, True)], slot
+        )
+        self.own = own_out, own_hold
+        self.theirs = flip(give_out, (0, 0)), flip(give_hold, (0, 0))
 
     def bit(self, index, bits):
         return (index >> jnp.where(self.core == 0, bits[0], bits[1])) & 1
@@ -157,8 +163,8 @@
     def begin(self, round_index, group, first=None):
         here = (self.owners[round_index] & 1) == self.core
         out, hold = [
-            jnp.where(here, own, theirs)
-            for own, theirs in zip(self.own[group], self.theirs[group])
+            jnp.where(here, own[self.spans[group]], theirs[self.spans[group]])
+            for own, theirs in zip(self.own, self.theirs)
         ]
         if first is not None:
             out = after(out, first)
@@ -216,7 +222,7 @@
     states, pairs = {}, {}
     for r in range(rounds):
         for g in range(2):
-            first = None if r == 0 else (states[r - 1, 1][2] if g == 0 else pairs[r - 1, 0][1])
+            first = None if r == 0 else pairs[r - 1, g][1]
             states[r, g] = spread.middle(spread.begin(r, g, first))
         for g in range(2):
             pairs[r, g] = spread.last(states[r, g])

time: 137 us -> 154 us (1.12)
  Pallas kernels: 4.79 us -> 36.9 us
  waiting for transfers between devices: 61.7 us -> 51.1 us
  starting transfers between devices: 38.7 us -> 29.8 us
  other arithmetic: 10.7 us -> 13.5 us
    pallas_call x1 -> x2, Pallas kernels: 2.53 us -> 34.6 us  [cut_slot(): pl.pallas_call(kernel, out_shape=shapes, in_specs=[pl.BlockSpec(memory_sp...]
    ppermute x26 -> x24, waiting for transfers between devices: 49.9 us -> 36.5 us  [flip(): lax.ppermute(value, 'cols', [(d, d ^ 1 << bits[d & 1]) for d in range(cou...]
    ppermute x26 -> x24, starting transfers between devices: 19.8 us -> 14.4 us  [flip(): lax.ppermute(value, 'cols', [(d, d ^ 1 << bits[d & 1]) for d in range(cou...]
    select_n x7 -> x8, other arithmetic: 3.13 us -> 7.28 us  [keep(): return jnp.where(same, hold, got)]
    ppermute x6, starting transfers between devices: 19 us -> 15.4 us  [shifted(): lax.ppermute(value, axis, [(source, source + steps) for source in range(i...]
    ppermute x6, waiting for transfers between devices: 11.8 us -> 14.6 us  [shifted(): lax.ppermute(value, axis, [(source, source + steps) for source in range(i...]
  transfers between devices with their start and end apart: 32 -> 30, of which waited for: 13 -> 12; matrix products, arithmetic and copies ran while one was open for 14% -> 13% of each run, Pallas kernels for 1% -> 2%
where the time goes in v2:
time: 154 us; the launch traced here: 153 us
  waiting for transfers between devices  51.1 us (33%)
  Pallas kernels  36.9 us (24%)
  starting transfers between devices  29.8 us (19%)
  other arithmetic  13.5 us (9%)
  matrix products  12 us (8%)
  local copies, waits for them, and re-layouts  5.41 us (4%)
  between operations  4.49 us (3%)
    ppermute x24, waiting for transfers between devices, flip(): lax.ppermute(value, 'cols', [(d, d ^ 1 << bits[d & 1]) for d in range(cou...  36.5 us
    pallas_call x2, Pallas kernels, cut_slot(): pl.pallas_call(kernel, out_shape=shapes, in_specs=[pl.BlockSpec(memory_sp...  34.6 us
    ppermute x6, starting transfers between devices, shifted(): lax.ppermute(value, axis, [(source, source + steps) for source in range(i...  15.4 us
    ppermute x6, waiting for transfers between devices, shifted(): lax.ppermute(value, axis, [(source, source + steps) for source in range(i...  14.6 us
    ppermute x24, starting transfers between devices, flip(): lax.ppermute(value, 'cols', [(d, d ^ 1 << bits[d & 1]) for d in range(cou...  14.4 us
    select_n x8, other arithmetic, keep(): return jnp.where(same, hold, got)  7.28 us
    dot_general x4, matrix products, apply_many(): jnp.einsum('nab,nac->nbc', q, x, preferred_element_type=jnp.float32)  7.27 us
    dot_general x8, matrix products, apply(): lax.dot_general(q, x, (((0,), (0,)), ((), ())), preferred_element_type=jn...  4.76 us
  transfers between devices with their start and end apart: 30, of which 12 were waited for; matrix products, arithmetic and copies ran while one was open for 13% of the time, Pallas kernels for 2%

profile of v2, /device:TPU:8, one launch (start us, length us, event | category | flops | bytes accessed | tf_op | source)
XLA Modules:
  0.0 153.1 jit_solution(6400193705985377793)
XLA Ops:
  0.0 32.9 %cut_slot.3 = bf16[8,128,512]{2,1,0:T(8,128)(2,1)} custom-call(bf16[8,2,2,128,512]{4,3,2,1,0:T(8,128)(2,1)} %bitcast.43), custom_call_target="tpu_custom_call" | custom-call | bytes 2097152 | tf_op jit(solution)/shard_map/cut_slot/pallas_call | solution.py:92
  33.0 2.2 %copy-done.2 = bf16[1,4096,512]{2,1,0:T(8,128)(2,1)S(1)} copy-done((bf16[1,4096,512]{2,1,0:T(8,128)(2,1)S(1)}, bf16[1,4096,512]{2,1,0:T(8,128)(2,1)}, u32[]{:S(2)}) %copy-start.2) | copy-done | bytes 4194328
  43.0 2.0 %broadcast_select_fusion = (bf16[5,128,512]{2,1,0:T(8,128)(2,1)S(1)}, bf16[5,128,512]{2,1,0:T(8,128)(2,1)}) fusion(pred[]{:T(512)S(6)} %eq.22, bf16[8,128,512]{2,1,0:T(8,128)(2,1)} %copy-done.4, bf16[8,128,512]{2,1,0:T(8,128)(2,1)S(1)} %get-tuple-element.10, pred[]{:T(512)S(6)} %eq.25), kind=kLoop, calls=%fused_computation.39 | loop fusion | flops 655360 | bytes 2621442 | tf_op jit(solution)/shard_map/jit(_where)/select_n | solution.py:166
  46.2 3.2 %collective-permute-done.2 = bf16[3,128,512]{2,1,0:T(8,128)(2,1)} collective-permute-done((bf16[3,128,512]{2,1,0:T(8,128)(2,1)S(1)}, bf16[3,128,512]{2,1,0:T(8,128)(2,1)}, u32[]{:S(2)}, u32[]{:S(2)}) %collective-permute-start.2) | collective-permute-done | bytes 393248 | tf_op jit(solution)/shard_map/ppermute | solution.py:17
  52.8 7.4 %collective-permute-done.15 = bf16[5,128,512]{2,1,0:T(8,128)(2,1)} collective-permute-done((bf16[5,128,512]{2,1,0:T(8,128)(2,1)}, bf16[5,128,512]{2,1,0:T(8,128)(2,1)}, u32[]{:S(2)}, u32[]{:S(2)}) %collective-permute-start.15) | collective-permute-done | bytes 655392 | tf_op jit(solution)/shard_map/ppermute | solution.py:17
  61.7 1.7 %collective-permute-start.16 = (bf16[5,128,512]{2,1,0:T(8,128)(2,1)S(1)}, bf16[5,128,512]{2,1,0:T(8,128)(2,1)}, u32[]{:S(2)}, u32[]{:S(2)}) collective-permute-start(bf16[5,128,512]{2,1,0:T(8,128)(2,1)S(1)} %select_select_fusion.1), channel_id=1, source_target_pairs={{0,4},{1,3},{2,6},{3,1},{4,0},{5,7},{6,2},{7,5},{8,12},{9,11},{10,... | collective-permute-start | bytes 1966088 | tf_op jit(solution)/shard_map/ppermute | solution.py:17
  67.2 5.0 %collective-permute-done.4._.refs_1_ = bf16[3,128,512]{2,1,0:T(8,128)(2,1)S(1)} collective-permute-done((bf16[3,128,512]{2,1,0:T(8,128)(2,1)S(1)}, bf16[3,128,512]{2,1,0:T(8,128)(2,1)S(1)}, u32[]{:S(2)}, u32[]{:S(2)}) %collective-permute-start.4) | collective-permute-done | bytes 393248 | tf_op jit(solution)/shard_map/ppermute | solution.py:17
  73.9 3.9 %collective-permute-start.12 = (bf16[2,128,256]{2,1,0:T(8,128)(2,1)S(1)}, bf16[2,128,256]{2,1,0:T(8,128)(2,1)S(1)}, u32[]{:S(2)}, u32[]{:S(2)}) collective-permute-start(bf16[2,128,256]{2,1,0:T(8,128)(2,1)S(1)} %pad_maximum_fusion.7), channel_id=1, source_target_pairs={{0,8},{8,16},{16,24},{1,9},{9,17},{17,25},{2,10},{10,18},{18,26},{... | collective-permute-start | bytes 393224 | tf_op jit(solution)/shard_map/ppermute | solution.py:12
  86.0 1.9 %collective-permute-start.22 = (bf16[256,1024]{1,0:T(8,128)(2,1)S(1)}, bf16[256,1024]{1,0:T(8,128)(2,1)S(1)}, u32[]{:S(2)}, u32[]{:S(2)}) collective-permute-start(bf16[256,1024]{1,0:T(8,128)(2,1)S(1)} %get-tuple-element.20), channel_id=1, source_target_pairs={{8,0},{16,8},{24,16},{9,1},{17,9},{25,17},{10,2},{18,10},{26,18},{... | collective-permute-start | bytes 1572872 | tf_op jit(solution)/shard_map/ppermute | solution.py:12
  88.0 4.2 %collective-permute-done.17.refs_1_._ = bf16[5,128,512]{2,1,0:T(8,128)(2,1)S(1)} collective-permute-done((bf16[5,128,512]{2,1,0:T(8,128)(2,1)S(1)}, bf16[5,128,512]{2,1,0:T(8,128)(2,1)S(1)}, u32[]{:S(2)}, u32[]{:S(2)}) %collective-permute-start.17) | collective-permute-done | bytes 655392 | tf_op jit(solution)/shard_map/ppermute | solution.py:17
  92.2 2.6 %collective-permute-start.14 = (bf16[256,1024]{1,0:T(8,128)(2,1)S(1)}, bf16[256,1024]{1,0:T(8,128)(2,1)S(1)}, u32[]{:S(2)}, u32[]{:S(2)}) collective-permute-start(bf16[256,1024]{1,0:T(8,128)(2,1)S(1)} %get-tuple-element.22), channel_id=1, source_target_pairs={{0,8},{8,16},{16,24},{1,9},{9,17},{17,25},{2,10},{10,18},{18,26},{... | collective-permute-start | bytes 1572872 | tf_op jit(solution)/shard_map/ppermute | solution.py:12
  95.2 2.1 %collective-permute-start.7 = (bf16[3,128,512]{2,1,0:T(8,128)(2,1)S(1)}, bf16[3,128,512]{2,1,0:T(8,128)(2,1)S(1)}, u32[]{:S(2)}, u32[]{:S(2)}) collective-permute-start(bf16[3,128,512]{2,1,0:T(8,128)(2,1)S(1)} %broadcast_select_fusion.7.refs_0_), channel_id=1, source_target_pairs={{0,2},{1,5},{2,0},{3,7},{4,6},{5,1},{6,4},{7,3},{8,10},{9,13},{10,... | collective-permute-start | bytes 1179656 | tf_op jit(solution)/shard_map/ppermute | solution.py:17
  97.7 3.5 %collective-permute-done.22 = bf16[256,1024]{1,0:T(8,128)(2,1)S(1)} collective-permute-done((bf16[256,1024]{1,0:T(8,128)(2,1)S(1)}, bf16[256,1024]{1,0:T(8,128)(2,1)S(1)}, u32[]{:S(2)}, u32[]{:S(2)}) %collective-permute-start.22) | collective-permute-done | bytes 524320 | tf_op jit(solution)/shard_map/ppermute | solution.py:12
  101.6 8.3 %collective-permute-done.7.refs_1_ = bf16[3,128,512]{2,1,0:T(8,128)(2,1)S(1)} collective-permute-done((bf16[3,128,512]{2,1,0:T(8,128)(2,1)S(1)}, bf16[3,128,512]{2,1,0:T(8,128)(2,1)S(1)}, u32[]{:S(2)}, u32[]{:S(2)}) %collective-permute-start.7) | collective-permute-done | bytes 393248 | tf_op jit(solution)/shard_map/ppermute | solution.py:17
  110.0 1.9 %collective-permute-start.20 = (bf16[2,128,256]{2,1,0:T(8,128)(2,1)S(1)}, bf16[2,128,256]{2,1,0:T(8,128)(2,1)S(1)}, u32[]{:S(2)}, u32[]{:S(2)}) collective-permute-start(bf16[2,128,256]{2,1,0:T(8,128)(2,1)S(1)} %pad_maximum_fusion.8), channel_id=1, source_target_pairs={{0,8},{8,16},{16,24},{1,9},{9,17},{17,25},{2,10},{10,18},{18,26},{... | collective-permute-start | bytes 393224 | tf_op jit(solution)/shard_map/ppermute | solution.py:12
  112.4 5.4 %collective-permute-done.20 = bf16[2,128,256]{2,1,0:T(8,128)(2,1)S(1)} collective-permute-done((bf16[2,128,256]{2,1,0:T(8,128)(2,1)S(1)}, bf16[2,128,256]{2,1,0:T(8,128)(2,1)S(1)}, u32[]{:S(2)}, u32[]{:S(2)}) %collective-permute-start.20) | collective-permute-done | bytes 131104 | tf_op jit(solution)/shard_map/ppermute | solution.py:12
  123.1 2.1 %convolution_convert_fusion.1 = bf16[3,512,1024]{2,1,0:T(8,128)(2,1)S(1)} fusion(bf16[5,512,512]{2,1,0:T(8,128)(2,1)S(1)} %place.9, bf16[3,512,1024]{2,1,0:T(8,128)(2,1)S(1)} %bitcast.48), kind=kOutput, calls=%fused_computation.4 | convolution fusion | flops 1612185600 | bytes 8912896 | tf_op jit(solution)/shard_map/nab,nac->nbc/dot_general | solution.py:205
  126.3 1.9 %collective-permute-start.29 = (bf16[256,1024]{1,0:T(8,128)(2,1)S(1)}, bf16[256,1024]{1,0:T(8,128)(2,1)S(1)}, u32[]{:S(2)}, u32[]{:S(2)}) collective-permute-start(bf16[256,1024]{1,0:T(8,128)(2,1)S(1)} %get-tuple-element.16), channel_id=1, source_target_pairs={{8,0},{16,8},{24,16},{9,1},{17,9},{25,17},{10,2},{18,10},{26,18},{... | collective-permute-start | bytes 1572872 | tf_op jit(solution)/shard_map/ppermute | solution.py:12
  128.3 1.9 %collective-permute-done.25 = bf16[5,128,512]{2,1,0:T(8,128)(2,1)S(1)} collective-permute-done((bf16[5,128,512]{2,1,0:T(8,128)(2,1)S(1)}, bf16[5,128,512]{2,1,0:T(8,128)(2,1)S(1)}, u32[]{:S(2)}, u32[]{:S(2)}) %collective-permute-start.25) | collective-permute-done | bytes 655392 | tf_op jit(solution)/shard_map/ppermute | solution.py:17
  131.2 3.1 %collective-permute-start.23 = (bf16[256,1024]{1,0:T(8,128)(2,1)S(1)}, bf16[256,1024]{1,0:T(8,128)(2,1)S(1)}, u32[]{:S(2)}, u32[]{:S(2)}) collective-permute-start(bf16[256,1024]{1,0:T(8,128)(2,1)S(1)} %get-tuple-element.18), channel_id=1, source_target_pairs={{0,8},{8,16},{16,24},{1,9},{9,17},{17,25},{2,10},{10,18},{18,26},{... | collective-permute-start | bytes 1572872 | tf_op jit(solution)/shard_map/ppermute | solution.py:12
  134.5 6.4 %collective-permute-done.26.refs_1_ = bf16[5,128,512]{2,1,0:T(8,128)(2,1)S(1)} collective-permute-done((bf16[5,128,512]{2,1,0:T(8,128)(2,1)S(1)}, bf16[5,128,512]{2,1,0:T(8,128)(2,1)S(1)}, u32[]{:S(2)}, u32[]{:S(2)}) %collective-permute-start.26) | collective-permute-done | bytes 655392 | tf_op jit(solution)/shard_map/ppermute | solution.py:17
  142.5 3.5 %collective-permute-done.23 = bf16[256,1024]{1,0:T(8,128)(2,1)S(1)} collective-permute-done((bf16[256,1024]{1,0:T(8,128)(2,1)S(1)}, bf16[256,1024]{1,0:T(8,128)(2,1)S(1)}, u32[]{:S(2)}, u32[]{:S(2)}) %collective-permute-start.23) | collective-permute-done | bytes 524320 | tf_op jit(solution)/shard_map/ppermute | solution.py:12
  148.7 2.1 %convolution_convert_fusion = bf16[3,512,1024]{2,1,0:T(8,128)(2,1)S(1)} fusion(bf16[5,512,512]{2,1,0:T(8,128)(2,1)S(1)} %place.11, bf16[3,512,1024]{2,1,0:T(8,128)(2,1)S(1)} %bitcast.49), kind=kOutput, calls=%fused_computation.3 | convolution fusion | flops 1612185600 | bytes 8912896 | tf_op jit(solution)/shard_map/nab,nac->nbc/dot_general | solution.py:205
  150.8 2.3 %pad_maximum_fusion = bf16[2048,1024]{1,0:T(8,128)(2,1)} fusion(bf16[256,1024]{1,0:T(8,128)(2,1)S(1)} %fusion.3, bf16[1536,1024]{1,0:T(8,128)(2,1)S(1)} %bitcast.50, bf16[256,1024]{1,0:T(8,128)(2,1)S(1)} %fusion.2), kind=kLoop, calls=%fused_computation | loop fusion | flops 12582912 | bytes 8388608 | tf_op jit(solution)/shard_map/concatenate | solution.py:253
  (100 shorter events, 37.1 us)
Async XLA Ops:
  36.9 9.3 %collective-permute-start = (bf16[8,128,512]{2,1,0:T(8,128)(2,1)}, bf16[8,128,512]{2,1,0:T(8,128)(2,1)}, u32[]{:S(2)}, u32[]{:S(2)}) collective-permute-start(bf16[8,128,512]{2,1,0:T(8,128)(2,1)} %get-tuple-element.9), channel_id=1, source_target_pairs={{0,1},{1,0},{2,3},{3,2},{4,5},{5,4},{6,7},{7,6},{8,9},{9,8},{10,11... | collective-permute-start | bytes 3145736 | tf_op jit(solution)/shard_map/ppermute | solution.py:17
  41.5 7.9 %collective-permute-start.2 = (bf16[3,128,512]{2,1,0:T(8,128)(2,1)S(1)}, bf16[3,128,512]{2,1,0:T(8,128)(2,1)}, u32[]{:S(2)}, u32[]{:S(2)}) collective-permute-start(bf16[3,128,512]{2,1,0:T(8,128)(2,1)S(1)} %get-tuple-element.14), channel_id=1, source_target_pairs={{0,2},{1,5},{2,0},{3,7},{4,6},{5,1},{6,4},{7,3},{8,10},{9,13},{10,... | collective-permute-start | bytes 1179656 | tf_op jit(solution)/shard_map/ppermute | solution.py:17
  45.0 15.2 %collective-permute-start.15 = (bf16[5,128,512]{2,1,0:T(8,128)(2,1)}, bf16[5,128,512]{2,1,0:T(8,128)(2,1)}, u32[]{:S(2)}, u32[]{:S(2)}) collective-permute-start(bf16[5,128,512]{2,1,0:T(8,128)(2,1)} %get-tuple-element.12), channel_id=1, source_target_pairs={{0,2},{1,5},{2,0},{3,7},{4,6},{5,1},{6,4},{7,3},{8,10},{9,13},{10,... | collective-permute-start | bytes 1966088 | tf_op jit(solution)/shard_map/ppermute | solution.py:17
  50.6 12.8 %collective-permute-start.3 = (bf16[3,128,512]{2,1,0:T(8,128)(2,1)S(1)}, bf16[3,128,512]{2,1,0:T(8,128)(2,1)}, u32[]{:S(2)}, u32[]{:S(2)}) collective-permute-start(bf16[3,128,512]{2,1,0:T(8,128)(2,1)S(1)} %select_select_fusion.2), channel_id=1, source_target_pairs={{0,4},{1,3},{2,6},{3,1},{4,0},{5,7},{6,2},{7,5},{8,12},{9,11},{10,... | collective-permute-start | bytes 1179656 | tf_op jit(solution)/shard_map/ppermute | solution.py:17
  61.7 16.2 %collective-permute-start.16 = (bf16[5,128,512]{2,1,0:T(8,128)(2,1)S(1)}, bf16[5,128,512]{2,1,0:T(8,128)(2,1)}, u32[]{:S(2)}, u32[]{:S(2)}) collective-permute-start(bf16[5,128,512]{2,1,0:T(8,128)(2,1)S(1)} %select_select_fusion.1), channel_id=1, source_target_pairs={{0,4},{1,3},{2,6},{3,1},{4,0},{5,7},{6,2},{7,5},{8,12},{9,11},{10,... | collective-permute-start | bytes 1966088 | tf_op jit(solution)/shard_map/ppermute | solution.py:17
  64.4 7.8 %collective-permute-start.4 = (bf16[3,128,512]{2,1,0:T(8,128)(2,1)S(1)}, bf16[3,128,512]{2,1,0:T(8,128)(2,1)S(1)}, u32[]{:S(2)}, u32[]{:S(2)}) collective-permute-start(bf16[3,128,512]{2,1,0:T(8,128)(2,1)S(1)} %broadcast_select_fusion.5.refs_0_), channel_id=1, source_target_pairs={{0,2},{1,5},{2,0},{3,7},{4,6},{5,1},{6,4},{7,3},{8,10},{9,13},{10,... | collective-permute-start | bytes 1179656 | tf_op jit(solution)/shard_map/ppermute | solution.py:17
  67.1 13.9 %collective-permute-start.10 = (bf16[3,128,512]{2,1,0:T(8,128)(2,1)S(1)}, bf16[3,128,512]{2,1,0:T(8,128)(2,1)S(1)}, u32[]{:S(2)}, u32[]{:S(2)}) collective-permute-start(bf16[3,128,512]{2,1,0:T(8,128)(2,1)S(1)} %broadcast_select_fusion.5.refs_0_), channel_id=1, source_target_pairs={{0,1},{1,0},{2,3},{3,2},{4,5},{5,4},{6,7},{7,6},{8,9},{9,8},{10,11... | collective-permute-start | bytes 1179656 | tf_op jit(solution)/shard_map/ppermute | solution.py:17
  72.5 11.0 %collective-permute-start.5 = (bf16[3,128,512]{2,1,0:T(8,128)(2,1)S(1)}, bf16[3,128,512]{2,1,0:T(8,128)(2,1)S(1)}, u32[]{:S(2)}, u32[]{:S(2)}) collective-permute-start(bf16[3,128,512]{2,1,0:T(8,128)(2,1)S(1)} %after.2), channel_id=1, source_target_pairs={{0,2},{1,5},{2,0},{3,7},{4,6},{5,1},{6,4},{7,3},{8,10},{9,13},{10,... | collective-permute-start | bytes 1179656 | tf_op jit(solution)/shard_map/ppermute | solution.py:17
  79.1 13.1 %collective-permute-start.17 = (bf16[5,128,512]{2,1,0:T(8,128)(2,1)S(1)}, bf16[5,128,512]{2,1,0:T(8,128)(2,1)S(1)}, u32[]{:S(2)}, u32[]{:S(2)}) collective-permute-start(bf16[5,128,512]{2,1,0:T(8,128)(2,1)S(1)} %broadcast_select_fusion.3.refs_0_), channel_id=1, source_target_pairs={{0,2},{1,5},{2,0},{3,7},{4,6},{5,1},{6,4},{7,3},{8,10},{9,13},{10,... | collective-permute-start | bytes 1966088 | tf_op jit(solution)/shard_map/ppermute | solution.py:17
  81.0 38.5 %collective-permute-start.18 = (bf16[5,128,512]{2,1,0:T(8,128)(2,1)S(1)}, bf16[5,128,512]{2,1,0:T(8,128)(2,1)S(1)}, u32[]{:S(2)}, u32[]{:S(2)}) collective-permute-start(bf16[5,128,512]{2,1,0:T(8,128)(2,1)S(1)} %broadcast_select_fusion.3.refs_0_), channel_id=1, source_target_pairs={{0,1},{1,0},{2,3},{3,2},{4,5},{5,4},{6,7},{7,6},{8,9},{9,8},{10,11... | collective-permute-start | bytes 1966088 | tf_op jit(solution)/shard_map/ppermute | solution.py:17
  81.1 14.1 %collective-permute-start.13 = (bf16[2,128,256]{2,1,0:T(8,128)(2,1)S(1)}, bf16[2,128,256]{2,1,0:T(8,128)(2,1)S(1)}, u32[]{:S(2)}, u32[]{:S(2)}) collective-permute-start(bf16[2,128,256]{2,1,0:T(8,128)(2,1)S(1)} %collective-permute-done.12), channel_id=1, source_target_pairs={{0,1},{1,0},{2,3},{3,2},{4,5},{5,4},{6,7},{7,6},{8,9},{9,8},{10,11... | collective-permute-start | bytes 393224 | tf_op jit(solution)/shard_map/ppermute | solution.py:17
  84.5 10.5 %collective-permute-start.6 = (bf16[3,128,512]{2,1,0:T(8,128)(2,1)S(1)}, bf16[3,128,512]{2,1,0:T(8,128)(2,1)S(1)}, u32[]{:S(2)}, u32[]{:S(2)}) collective-permute-start(bf16[3,128,512]{2,1,0:T(8,128)(2,1)S(1)} %select_select_fusion.3), channel_id=1, source_target_pairs={{0,4},{1,3},{2,6},{3,1},{4,0},{5,7},{6,2},{7,5},{8,12},{9,11},{10,... | collective-permute-start | bytes 1179656 | tf_op jit(solution)/shard_map/ppermute | solution.py:17
  86.0 15.2 %collective-permute-start.22 = (bf16[256,1024]{1,0:T(8,128)(2,1)S(1)}, bf16[256,1024]{1,0:T(8,128)(2,1)S(1)}, u32[]{:S(2)}, u32[]{:S(2)}) collective-permute-start(bf16[256,1024]{1,0:T(8,128)(2,1)S(1)} %get-tuple-element.20), channel_id=1, source_target_pairs={{8,0},{16,8},{24,16},{9,1},{17,9},{25,17},{10,2},{18,10},{26,18},{... | collective-permute-start | bytes 1572872 | tf_op jit(solution)/shard_map/ppermute | solution.py:12
  92.2 17.8 %collective-permute-start.14 = (bf16[256,1024]{1,0:T(8,128)(2,1)S(1)}, bf16[256,1024]{1,0:T(8,128)(2,1)S(1)}, u32[]{:S(2)}, u32[]{:S(2)}) collective-permute-start(bf16[256,1024]{1,0:T(8,128)(2,1)S(1)} %get-tuple-element.22), channel_id=1, source_target_pairs={{0,8},{8,16},{16,24},{1,9},{9,17},{17,25},{2,10},{10,18},{18,26},{... | collective-permute-start | bytes 1572872 | tf_op jit(solution)/shard_map/ppermute | solution.py:12
  95.0 22.7 %collective-permute-start.24 = (bf16[5,128,512]{2,1,0:T(8,128)(2,1)S(1)}, bf16[5,128,512]{2,1,0:T(8,128)(2,1)S(1)}, u32[]{:S(2)}, u32[]{:S(2)}) collective-permute-start(bf16[5,128,512]{2,1,0:T(8,128)(2,1)S(1)} %after.3), channel_id=1, source_target_pairs={{0,2},{1,5},{2,0},{3,7},{4,6},{5,1},{6,4},{7,3},{8,10},{9,13},{10,... | collective-permute-start | bytes 1966088 | tf_op jit(solution)/shard_map/ppermute | solution.py:17
  95.2 14.7 %collective-permute-start.7 = (bf16[3,128,512]{2,1,0:T(8,128)(2,1)S(1)}, bf16[3,128,512]{2,1,0:T(8,128)(2,1)S(1)}, u32[]{:S(2)}, u32[]{:S(2)}) collective-permute-start(bf16[3,128,512]{2,1,0:T(8,128)(2,1)S(1)} %broadcast_select_fusion.7.refs_0_), channel_id=1, source_target_pairs={{0,2},{1,5},{2,0},{3,7},{4,6},{5,1},{6,4},{7,3},{8,10},{9,13},{10,... | collective-permute-start | bytes 1179656 | tf_op jit(solution)/shard_map/ppermute | solution.py:17
  101.2 18.7 %collective-permute-start.19 = (bf16[5,128,512]{2,1,0:T(8,128)(2,1)S(1)}, bf16[5,128,512]{2,1,0:T(8,128)(2,1)S(1)}, u32[]{:S(2)}, u32[]{:S(2)}) collective-permute-start(bf16[5,128,512]{2,1,0:T(8,128)(2,1)S(1)} %collective-permute-done.17.refs_1_._), channel_id=1, source_target_pairs={{0,1},{1,0},{2,3},{3,2},{4,5},{5,4},{6,7},{7,6},{8,9},{9,8},{10,11... | collective-permute-start | bytes 1966088 | tf_op jit(solution)/shard_map/ppermute | solution.py:17
  109.9 15.3 %collective-permute-start.8 = (bf16[3,128,512]{2,1,0:T(8,128)(2,1)S(1)}, bf16[3,128,512]{2,1,0:T(8,128)(2,1)S(1)}, u32[]{:S(2)}, u32[]{:S(2)}) collective-permute-start(bf16[3,128,512]{2,1,0:T(8,128)(2,1)S(1)} %broadcast_select_fusion.7.refs_0_), channel_id=1, source_target_pairs={{0,1},{1,0},{2,3},{3,2},{4,5},{5,4},{6,7},{7,6},{8,9},{9,8},{10,11... | collective-permute-start | bytes 1179656 | tf_op jit(solution)/shard_map/ppermute | solution.py:17
  117.8 23.2 %collective-permute-start.21 = (bf16[2,128,256]{2,1,0:T(8,128)(2,1)S(1)}, bf16[2,128,256]{2,1,0:T(8,128)(2,1)S(1)}, u32[]{:S(2)}, u32[]{:S(2)}) collective-permute-start(bf16[2,128,256]{2,1,0:T(8,128)(2,1)S(1)} %collective-permute-done.20), channel_id=1, source_target_pairs={{0,1},{1,0},{2,3},{3,2},{4,5},{5,4},{6,7},{7,6},{8,9},{9,8},{10,11... | collective-permute-start | bytes 393224 | tf_op jit(solution)/shard_map/ppermute | solution.py:17
  119.5 10.7 %collective-permute-start.25 = (bf16[5,128,512]{2,1,0:T(8,128)(2,1)S(1)}, bf16[5,128,512]{2,1,0:T(8,128)(2,1)S(1)}, u32[]{:S(2)}, u32[]{:S(2)}) collective-permute-start(bf16[5,128,512]{2,1,0:T(8,128)(2,1)S(1)} %select_select_fusion), channel_id=1, source_target_pairs={{0,4},{1,3},{2,6},{3,1},{4,0},{5,7},{6,2},{7,5},{8,12},{9,11},{10,... | collective-permute-start | bytes 1966088 | tf_op jit(solution)/shard_map/ppermute | solution.py:17
  126.3 15.7 %collective-permute-start.29 = (bf16[256,1024]{1,0:T(8,128)(2,1)S(1)}, bf16[256,1024]{1,0:T(8,128)(2,1)S(1)}, u32[]{:S(2)}, u32[]{:S(2)}) collective-permute-start(bf16[256,1024]{1,0:T(8,128)(2,1)S(1)} %get-tuple-element.16), channel_id=1, source_target_pairs={{8,0},{16,8},{24,16},{9,1},{17,9},{25,17},{10,2},{18,10},{26,18},{... | collective-permute-start | bytes 1572872 | tf_op jit(solution)/shard_map/ppermute | solution.py:12
  130.3 10.7 %collective-permute-start.26 = (bf16[5,128,512]{2,1,0:T(8,128)(2,1)S(1)}, bf16[5,128,512]{2,1,0:T(8,128)(2,1)S(1)}, u32[]{:S(2)}, u32[]{:S(2)}) collective-permute-start(bf16[5,128,512]{2,1,0:T(8,128)(2,1)S(1)} %broadcast_select_fusion.1.refs_0_), channel_id=1, source_target_pairs={{0,2},{1,5},{2,0},{3,7},{4,6},{5,1},{6,4},{7,3},{8,10},{9,13},{10,... | collective-permute-start | bytes 1966088 | tf_op jit(solution)/shard_map/ppermute | solution.py:17
  131.2 14.9 %collective-permute-start.23 = (bf16[256,1024]{1,0:T(8,128)(2,1)S(1)}, bf16[256,1024]{1,0:T(8,128)(2,1)S(1)}, u32[]{:S(2)}, u32[]{:S(2)}) collective-permute-start(bf16[256,1024]{1,0:T(8,128)(2,1)S(1)} %get-tuple-element.18), channel_id=1, source_target_pairs={{0,8},{8,16},{16,24},{1,9},{9,17},{17,25},{2,10},{10,18},{18,26},{... | collective-permute-start | bytes 1572872 | tf_op jit(solution)/shard_map/ppermute | solution.py:12
  134.4 12.1 %collective-permute-start.27 = (bf16[5,128,512]{2,1,0:T(8,128)(2,1)S(1)}, bf16[5,128,512]{2,1,0:T(8,128)(2,1)S(1)}, u32[]{:S(2)}, u32[]{:S(2)}) collective-permute-start(bf16[5,128,512]{2,1,0:T(8,128)(2,1)S(1)} %broadcast_select_fusion.1.refs_0_), channel_id=1, source_target_pairs={{0,1},{1,0},{2,3},{3,2},{4,5},{5,4},{6,7},{7,6},{8,9},{9,8},{10,11... | collective-permute-start | bytes 1966088 | tf_op jit(solution)/shard_map/ppermute | solution.py:17
  (12 other events, 90.8 us)

commit v3 on v2

--- a/solution.py
+++ b/solution.py
@@ -10,6 +10,19 @@
     count = lax.axis_size(axis)
     initial, last = (max(0, -steps), min(count, count - steps))
     return lax.ppermute(value, axis, [(source, source + steps) for source in range(initial, last)])
+
+
+def swap_rows(up, down):
+    count = lax.axis_size("rows")
+    even = (lax.axis_index("rows") & 1) == 0
+
+    def swap(value, start):
+        pairs = [(low, low + 1) for low in range(start, count - 1, 2)]
+        return lax.ppermute(value, "rows", pairs + [(b, a) for a, b in pairs])
+
+    first = swap(jnp.where(even, down, up), 0)
+    second = swap(jnp.where(even, up, down), 1)
+    return jnp.where(even, second, first), jnp.where(even, first, second)
 
 
 def flip(value, bits):
@@ -96,7 +109,7 @@
         out_specs=[ANY] * len(shapes),
         scratch_shapes=[pltpu.SemaphoreType.DMA((len(spans) * len(kinds),))],
         name="cut_slot",
-        **small(bytes_accessed=len(kinds) * slot.size, limit=(60 if len(kinds) == 1 else 1) << 20),
+        **small(bytes_accessed=len(kinds) * slot.size, limit=(48 if len(kinds) == 1 else 1) << 20),
     )(slot)
 
 
@@ -222,7 +235,7 @@
     states, pairs = {}, {}
     for r in range(rounds):
         for g in range(2):
-            first = None if r == 0 else pairs[r - 1, g][1]
+            first = None if r == 0 else (states[r - 1, 0][2] if g == 0 else pairs[r - 1, 0][1])
             states[r, g] = spread.middle(spread.begin(r, g, first))
         for g in range(2):
             pairs[r, g] = spread.last(states[r, g])
@@ -234,8 +247,7 @@
         head_rows = apply(edges[0], matrix[:window])
         tail_rows = apply(edges[1], matrix[local_rows - window :])
         begin, end = head_rows[:border], tail_rows[border:]
-        below = shifted(begin, "rows", -1)
-        above = shifted(end, "rows", 1)
+        above, below = swap_rows(begin, end)
         prev = spread.join_above(head[0][-1, :, border:], head[1][-1, :, border:])
         rest = spread.join(*tail)
         mid = apply_many(

time: 154 us -> 137 us (0.89)
  Pallas kernels: 36.9 us -> 4.55 us
  waiting for transfers between devices: 51.1 us -> 70.6 us
  other arithmetic: 13.5 us -> 9.55 us
  local copies, waits for them, and re-layouts: 5.41 us -> 3.11 us
  starting transfers between devices: 29.8 us -> 31.4 us
    pallas_call x2, Pallas kernels: 34.6 us -> 2.31 us  [cut_slot(): pl.pallas_call(kernel, out_shape=shapes, in_specs=[pl.BlockSpec(memory_sp...]
    ppermute x24, waiting for transfers between devices: 36.5 us -> 55.7 us  [flip(): lax.ppermute(value, 'cols', [(d, d ^ 1 << bits[d & 1]) for d in range(cou...]
    ppermute x0 -> x4, waiting for transfers between devices: none -> 9.99 us  [swap(): return lax.ppermute(value, 'rows', pairs + [(b, a) for a, b in pairs])]
    ppermute x6 -> x2, waiting for transfers between devices: 14.6 us -> 4.89 us  [shifted(): lax.ppermute(value, axis, [(source, source + steps) for source in range(i...]
    ppermute x6 -> x2, starting transfers between devices: 15.4 us -> 6.85 us  [shifted(): lax.ppermute(value, axis, [(source, source + steps) for source in range(i...]
    ppermute x0 -> x4, starting transfers between devices: none -> 5.84 us  [swap(): return lax.ppermute(value, 'rows', pairs + [(b, a) for a, b in pairs])]
    ppermute x24, starting transfers between devices: 14.4 us -> 18.7 us  [flip(): lax.ppermute(value, 'cols', [(d, d ^ 1 << bits[d & 1]) for d in range(cou...]
    select_n x8 -> x7, other arithmetic: 7.28 us -> 3.69 us  [keep(): return jnp.where(same, hold, got)]
  transfers between devices with their start and end apart: 30 -> 30, of which waited for: 12 -> 14; matrix products, arithmetic and copies ran while one was open for 13% -> 13% of each run, Pallas kernels for 2% -> 3%
where the time goes in v3:
time: 137 us; the launch traced here: 135 us
  waiting for transfers between devices  70.6 us (52%)
  starting transfers between devices  31.4 us (23%)
  matrix products  12 us (9%)
  other arithmetic  9.55 us (7%)
  Pallas kernels  4.55 us (3%)
  between operations  4.13 us (3%)
  local copies, waits for them, and re-layouts  3.11 us (2%)
    ppermute x24, waiting for transfers between devices, flip(): lax.ppermute(value, 'cols', [(d, d ^ 1 << bits[d & 1]) for d in range(cou...  55.7 us
    ppermute x24, starting transfers between devices, flip(): lax.ppermute(value, 'cols', [(d, d ^ 1 << bits[d & 1]) for d in range(cou...  18.7 us
    ppermute x4, waiting for transfers between devices, swap(): return lax.ppermute(value, 'rows', pairs + [(b, a) for a, b in pairs])  9.99 us
    dot_general x4, matrix products, apply_many(): jnp.einsum('nab,nac->nbc', q, x, preferred_element_type=jnp.float32)  7.28 us
    ppermute x2, starting transfers between devices, shifted(): lax.ppermute(value, axis, [(source, source + steps) for source in range(i...  6.85 us
    ppermute x4, starting transfers between devices, swap(): return lax.ppermute(value, 'rows', pairs + [(b, a) for a, b in pairs])  5.84 us
    ppermute x2, waiting for transfers between devices, shifted(): lax.ppermute(value, axis, [(source, source + steps) for source in range(i...  4.89 us
    dot_general x8, matrix products, apply(): lax.dot_general(q, x, (((0,), (0,)), ((), ())), preferred_element_type=jn...  4.76 us
  transfers between devices with their start and end apart: 30, of which 14 were waited for; matrix products, arithmetic and copies ran while one was open for 13% of the time, Pallas kernels for 3%

profile of v3, /device:TPU:8, one launch (start us, length us, event | category | flops | bytes accessed | tf_op | source)
XLA Modules:
  0.0 135.4 jit_solution(9130391184572089047)
XLA Ops:
  0.0 2.2 %copy-done.2 = bf16[1,4096,512]{2,1,0:T(8,128)(2,1)S(1)} copy-done((bf16[1,4096,512]{2,1,0:T(8,128)(2,1)S(1)}, bf16[1,4096,512]{2,1,0:T(8,128)(2,1)}, u32[]{:S(2)}) %copy-start.2) | copy-done | bytes 4194328
  2.9 1.7 %cut_slot.2 = (bf16[8,128,512]{2,1,0:T(8,128)(2,1)S(1)}, bf16[8,128,512]{2,1,0:T(8,128)(2,1)}, bf16[8,128,512]{2,1,0:T(8,128)(2,1)S(1)}) custom-call(bf16[8,2,2,128,512]{4,3,2,1,0:T(8,128)(2,1)S(1)} %bitcast.44), custom_call_target="tpu_custom_call" | custom-call | bytes 6291456 | tf_op jit(solution)/shard_map/cut_slot/pallas_call | solution.py:105
  10.2 5.7 %collective-permute-done.2 = bf16[3,128,512]{2,1,0:T(8,128)(2,1)S(1)} collective-permute-done((bf16[3,128,512]{2,1,0:T(8,128)(2,1)S(1)}, bf16[3,128,512]{2,1,0:T(8,128)(2,1)S(1)}, u32[]{:S(2)}, u32[]{:S(2)}) %collective-permute-start.2) | collective-permute-done | bytes 393248 | tf_op jit(solution)/shard_map/ppermute | solution.py:30
  17.0 1.6 %collective-permute-start.3 = (bf16[3,128,512]{2,1,0:T(8,128)(2,1)S(1)}, bf16[3,128,512]{2,1,0:T(8,128)(2,1)S(1)}, u32[]{:S(2)}, u32[]{:S(2)}) collective-permute-start(bf16[3,128,512]{2,1,0:T(8,128)(2,1)S(1)} %select_select_fusion.2), channel_id=1, source_target_pairs={{0,4},{1,3},{2,6},{3,1},{4,0},{5,7},{6,2},{7,5},{8,12},{9,11},{10,... | collective-permute-start | bytes 1179656 | tf_op jit(solution)/shard_map/ppermute | solution.py:30
  18.6 6.3 %collective-permute-done.3._ = bf16[3,128,512]{2,1,0:T(8,128)(2,1)S(1)} collective-permute-done((bf16[3,128,512]{2,1,0:T(8,128)(2,1)S(1)}, bf16[3,128,512]{2,1,0:T(8,128)(2,1)S(1)}, u32[]{:S(2)}, u32[]{:S(2)}) %collective-permute-start.3) | collective-permute-done | bytes 393248 | tf_op jit(solution)/shard_map/ppermute | solution.py:30
  29.1 3.9 %collective-permute-done.4 = bf16[3,128,512]{2,1,0:T(8,128)(2,1)} collective-permute-done((bf16[3,128,512]{2,1,0:T(8,128)(2,1)S(1)}, bf16[3,128,512]{2,1,0:T(8,128)(2,1)}, u32[]{:S(2)}, u32[]{:S(2)}) %collective-permute-start.4) | collective-permute-done | bytes 393248 | tf_op jit(solution)/shard_map/ppermute | solution.py:30
  34.0 1.6 %collective-permute-start.5 = (bf16[3,128,512]{2,1,0:T(8,128)(2,1)S(1)}, bf16[3,128,512]{2,1,0:T(8,128)(2,1)S(1)}, u32[]{:S(2)}, u32[]{:S(2)}) collective-permute-start(bf16[3,128,512]{2,1,0:T(8,128)(2,1)S(1)} %select_select_fusion.3), channel_id=1, source_target_pairs={{0,4},{1,3},{2,6},{3,1},{4,0},{5,7},{6,2},{7,5},{8,12},{9,11},{10,... | collective-permute-start | bytes 1179656 | tf_op jit(solution)/shard_map/ppermute | solution.py:30
  35.6 4.3 %collective-permute-done.9.refs_1_._ = bf16[3,128,512]{2,1,0:T(8,128)(2,1)S(1)} collective-permute-done((bf16[3,128,512]{2,1,0:T(8,128)(2,1)S(1)}, bf16[3,128,512]{2,1,0:T(8,128)(2,1)S(1)}, u32[]{:S(2)}, u32[]{:S(2)}) %collective-permute-start.9) | collective-permute-done | bytes 393248 | tf_op jit(solution)/shard_map/ppermute | solution.py:30
  39.9 3.5 %collective-permute-start.12 = (bf16[2,128,256]{2,1,0:T(8,128)(2,1)S(1)}, bf16[2,128,256]{2,1,0:T(8,128)(2,1)S(1)}, u32[]{:S(2)}, u32[]{:S(2)}) collective-permute-start(bf16[2,128,256]{2,1,0:T(8,128)(2,1)S(1)} %pad_maximum_fusion.7), channel_id=1, source_target_pairs={{0,8},{8,16},{16,24},{1,9},{9,17},{17,25},{2,10},{10,18},{18,26},{... | collective-permute-start | bytes 393224 | tf_op jit(solution)/shard_map/ppermute | solution.py:12
  51.2 4.0 %collective-permute-done.16 = bf16[5,128,512]{2,1,0:T(8,128)(2,1)S(1)} collective-permute-done((bf16[5,128,512]{2,1,0:T(8,128)(2,1)S(1)}, bf16[5,128,512]{2,1,0:T(8,128)(2,1)S(1)}, u32[]{:S(2)}, u32[]{:S(2)}) %collective-permute-start.16) | collective-permute-done | bytes 655392 | tf_op jit(solution)/shard_map/ppermute | solution.py:30
  55.3 8.6 %collective-permute-done.25 = bf16[5,128,512]{2,1,0:T(8,128)(2,1)S(1)} collective-permute-done((bf16[5,128,512]{2,1,0:T(8,128)(2,1)S(1)}, bf16[5,128,512]{2,1,0:T(8,128)(2,1)S(1)}, u32[]{:S(2)}, u32[]{:S(2)}) %collective-permute-start.25) | collective-permute-done | bytes 655392 | tf_op jit(solution)/shard_map/ppermute | solution.py:30
  66.8 3.6 %collective-permute-start.14 = (bf16[256,1024]{1,0:T(8,128)(2,1)S(1)}, bf16[256,1024]{1,0:T(8,128)(2,1)S(1)}, u32[]{:S(2)}, u32[]{:S(2)}) collective-permute-start(bf16[256,1024]{1,0:T(8,128)(2,1)S(1)} %get-tuple-element.19), channel_id=1, source_target_pairs={{8,16},{16,8},{9,17},{17,9},{10,18},{18,10},{11,19},{19,11},{12,20... | collective-permute-start | bytes 1572872 | tf_op jit(solution)/shard_map/ppermute | solution.py:21
  70.5 1.8 %collective-permute-done.6.refs_1_ = bf16[3,128,512]{2,1,0:T(8,128)(2,1)S(1)} collective-permute-done((bf16[3,128,512]{2,1,0:T(8,128)(2,1)S(1)}, bf16[3,128,512]{2,1,0:T(8,128)(2,1)S(1)}, u32[]{:S(2)}, u32[]{:S(2)}) %collective-permute-start.6) | collective-permute-done | bytes 393248 | tf_op jit(solution)/shard_map/ppermute | solution.py:30
  72.3 3.4 %collective-permute-start.21 = (bf16[2,128,256]{2,1,0:T(8,128)(2,1)S(1)}, bf16[2,128,256]{2,1,0:T(8,128)(2,1)S(1)}, u32[]{:S(2)}, u32[]{:S(2)}) collective-permute-start(bf16[2,128,256]{2,1,0:T(8,128)(2,1)S(1)} %pad_maximum_fusion.8), channel_id=1, source_target_pairs={{0,8},{8,16},{16,24},{1,9},{9,17},{17,25},{2,10},{10,18},{18,26},{... | collective-permute-start | bytes 393224 | tf_op jit(solution)/shard_map/ppermute | solution.py:12
  76.2 4.9 %collective-permute-done.21 = bf16[2,128,256]{2,1,0:T(8,128)(2,1)S(1)} collective-permute-done((bf16[2,128,256]{2,1,0:T(8,128)(2,1)S(1)}, bf16[2,128,256]{2,1,0:T(8,128)(2,1)S(1)}, u32[]{:S(2)}, u32[]{:S(2)}) %collective-permute-start.21) | collective-permute-done | bytes 131104 | tf_op jit(solution)/shard_map/ppermute | solution.py:12
  81.6 2.0 %collective-permute-start.18 = (bf16[5,128,512]{2,1,0:T(8,128)(2,1)S(1)}, bf16[5,128,512]{2,1,0:T(8,128)(2,1)S(1)}, u32[]{:S(2)}, u32[]{:S(2)}) collective-permute-start(bf16[5,128,512]{2,1,0:T(8,128)(2,1)S(1)} %broadcast_select_fusion.3.refs_0_), channel_id=1, source_target_pairs={{0,2},{1,5},{2,0},{3,7},{4,6},{5,1},{6,4},{7,3},{8,10},{9,13},{10,... | collective-permute-start | bytes 1966088 | tf_op jit(solution)/shard_map/ppermute | solution.py:30
  84.2 14.4 %collective-permute-done.26 = bf16[5,128,512]{2,1,0:T(8,128)(2,1)S(1)} collective-permute-done((bf16[5,128,512]{2,1,0:T(8,128)(2,1)S(1)}, bf16[5,128,512]{2,1,0:T(8,128)(2,1)S(1)}, u32[]{:S(2)}, u32[]{:S(2)}) %collective-permute-start.26) | collective-permute-done | bytes 655392 | tf_op jit(solution)/shard_map/ppermute | solution.py:30
  98.7 2.2 %collective-permute-start.27 = (bf16[5,128,512]{2,1,0:T(8,128)(2,1)S(1)}, bf16[5,128,512]{2,1,0:T(8,128)(2,1)S(1)}, u32[]{:S(2)}, u32[]{:S(2)}) collective-permute-start(bf16[5,128,512]{2,1,0:T(8,128)(2,1)S(1)} %broadcast_select_fusion.1.refs_0_), channel_id=1, source_target_pairs={{0,2},{1,5},{2,0},{3,7},{4,6},{5,1},{6,4},{7,3},{8,10},{9,13},{10,... | collective-permute-start | bytes 1966088 | tf_op jit(solution)/shard_map/ppermute | solution.py:30
  104.1 5.4 %collective-permute-done.27.refs_1_ = bf16[5,128,512]{2,1,0:T(8,128)(2,1)S(1)} collective-permute-done((bf16[5,128,512]{2,1,0:T(8,128)(2,1)S(1)}, bf16[5,128,512]{2,1,0:T(8,128)(2,1)S(1)}, u32[]{:S(2)}, u32[]{:S(2)}) %collective-permute-start.27) | collective-permute-done | bytes 655392 | tf_op jit(solution)/shard_map/ppermute | solution.py:30
  111.6 2.1 %convolution_convert_fusion.1 = bf16[3,512,1024]{2,1,0:T(8,128)(2,1)S(1)} fusion(bf16[5,512,512]{2,1,0:T(8,128)(2,1)S(1)} %place.9, bf16[3,512,1024]{2,1,0:T(8,128)(2,1)S(1)} %bitcast.48), kind=kOutput, calls=%fused_computation.4 | convolution fusion | flops 1612185600 | bytes 8912896 | tf_op jit(solution)/shard_map/nab,nac->nbc/dot_general | solution.py:218
  115.6 2.1 %collective-permute-start.23 = (bf16[256,1024]{1,0:T(8,128)(2,1)S(1)}, bf16[256,1024]{1,0:T(8,128)(2,1)S(1)}, u32[]{:S(2)}, u32[]{:S(2)}) collective-permute-start(bf16[256,1024]{1,0:T(8,128)(2,1)S(1)} %get-tuple-element.15), channel_id=1, source_target_pairs={{8,16},{16,8},{9,17},{17,9},{10,18},{18,10},{11,19},{19,11},{12,20... | collective-permute-start | bytes 1572872 | tf_op jit(solution)/shard_map/ppermute | solution.py:21
  120.0 2.1 %convolution_convert_fusion = bf16[3,512,1024]{2,1,0:T(8,128)(2,1)S(1)} fusion(bf16[5,512,512]{2,1,0:T(8,128)(2,1)S(1)} %place.11, bf16[3,512,1024]{2,1,0:T(8,128)(2,1)S(1)} %bitcast.49), kind=kOutput, calls=%fused_computation.3 | convolution fusion | flops 1612185600 | bytes 8912896 | tf_op jit(solution)/shard_map/nab,nac->nbc/dot_general | solution.py:218
  122.1 9.7 %collective-permute-done.23 = bf16[256,1024]{1,0:T(8,128)(2,1)S(1)} collective-permute-done((bf16[256,1024]{1,0:T(8,128)(2,1)S(1)}, bf16[256,1024]{1,0:T(8,128)(2,1)S(1)}, u32[]{:S(2)}, u32[]{:S(2)}) %collective-permute-start.23) | collective-permute-done | bytes 524320 | tf_op jit(solution)/shard_map/ppermute | solution.py:21
  133.1 2.3 %pad_maximum_fusion = bf16[2048,1024]{1,0:T(8,128)(2,1)} fusion(bf16[256,1024]{1,0:T(8,128)(2,1)S(1)} %fusion.3, bf16[1536,1024]{1,0:T(8,128)(2,1)S(1)} %bitcast.50, bf16[256,1024]{1,0:T(8,128)(2,1)S(1)} %fusion.2), kind=kLoop, calls=%fused_computation | loop fusion | flops 12582912 | bytes 8388608 | tf_op jit(solution)/shard_map/concatenate | solution.py:265
  (99 shorter events, 32.1 us)
Async XLA Ops:
  8.0 7.8 %collective-permute-start.2 = (bf16[3,128,512]{2,1,0:T(8,128)(2,1)S(1)}, bf16[3,128,512]{2,1,0:T(8,128)(2,1)S(1)}, u32[]{:S(2)}, u32[]{:S(2)}) collective-permute-start(bf16[3,128,512]{2,1,0:T(8,128)(2,1)S(1)} %get-tuple-element.18), channel_id=1, source_target_pairs={{0,2},{1,5},{2,0},{3,7},{4,6},{5,1},{6,4},{7,3},{8,10},{9,13},{10,... | collective-permute-start | bytes 1179656 | tf_op jit(solution)/shard_map/ppermute | solution.py:30
  17.0 7.8 %collective-permute-start.3 = (bf16[3,128,512]{2,1,0:T(8,128)(2,1)S(1)}, bf16[3,128,512]{2,1,0:T(8,128)(2,1)S(1)}, u32[]{:S(2)}, u32[]{:S(2)}) collective-permute-start(bf16[3,128,512]{2,1,0:T(8,128)(2,1)S(1)} %select_select_fusion.2), channel_id=1, source_target_pairs={{0,4},{1,3},{2,6},{3,1},{4,0},{5,7},{6,2},{7,5},{8,12},{9,11},{10,... | collective-permute-start | bytes 1179656 | tf_op jit(solution)/shard_map/ppermute | solution.py:30
  25.0 7.9 %collective-permute-start.4 = (bf16[3,128,512]{2,1,0:T(8,128)(2,1)S(1)}, bf16[3,128,512]{2,1,0:T(8,128)(2,1)}, u32[]{:S(2)}, u32[]{:S(2)}) collective-permute-start(bf16[3,128,512]{2,1,0:T(8,128)(2,1)S(1)} %after.2), channel_id=1, source_target_pairs={{0,2},{1,5},{2,0},{3,7},{4,6},{5,1},{6,4},{7,3},{8,10},{9,13},{10,... | collective-permute-start | bytes 1179656 | tf_op jit(solution)/shard_map/ppermute | solution.py:30
  27.2 12.7 %collective-permute-start.9 = (bf16[3,128,512]{2,1,0:T(8,128)(2,1)S(1)}, bf16[3,128,512]{2,1,0:T(8,128)(2,1)S(1)}, u32[]{:S(2)}, u32[]{:S(2)}) collective-permute-start(bf16[3,128,512]{2,1,0:T(8,128)(2,1)S(1)} %broadcast_select_fusion.12.refs_0_), channel_id=1, source_target_pairs={{0,2},{1,5},{2,0},{3,7},{4,6},{5,1},{6,4},{7,3},{8,10},{9,13},{10,... | collective-permute-start | bytes 1179656 | tf_op jit(solution)/shard_map/ppermute | solution.py:30
  34.0 14.1 %collective-permute-start.5 = (bf16[3,128,512]{2,1,0:T(8,128)(2,1)S(1)}, bf16[3,128,512]{2,1,0:T(8,128)(2,1)S(1)}, u32[]{:S(2)}, u32[]{:S(2)}) collective-permute-start(bf16[3,128,512]{2,1,0:T(8,128)(2,1)S(1)} %select_select_fusion.3), channel_id=1, source_target_pairs={{0,4},{1,3},{2,6},{3,1},{4,0},{5,7},{6,2},{7,5},{8,12},{9,11},{10,... | collective-permute-start | bytes 1179656 | tf_op jit(solution)/shard_map/ppermute | solution.py:30
  44.6 10.7 %collective-permute-start.16 = (bf16[5,128,512]{2,1,0:T(8,128)(2,1)S(1)}, bf16[5,128,512]{2,1,0:T(8,128)(2,1)S(1)}, u32[]{:S(2)}, u32[]{:S(2)}) collective-permute-start(bf16[5,128,512]{2,1,0:T(8,128)(2,1)S(1)} %get-tuple-element.14), channel_id=1, source_target_pairs={{0,2},{1,5},{2,0},{3,7},{4,6},{5,1},{6,4},{7,3},{8,10},{9,13},{10,... | collective-permute-start | bytes 1966088 | tf_op jit(solution)/shard_map/ppermute | solution.py:30
  46.4 17.5 %collective-permute-start.25 = (bf16[5,128,512]{2,1,0:T(8,128)(2,1)S(1)}, bf16[5,128,512]{2,1,0:T(8,128)(2,1)S(1)}, u32[]{:S(2)}, u32[]{:S(2)}) collective-permute-start(bf16[5,128,512]{2,1,0:T(8,128)(2,1)S(1)} %after.3), channel_id=1, source_target_pairs={{0,2},{1,5},{2,0},{3,7},{4,6},{5,1},{6,4},{7,3},{8,10},{9,13},{10,... | collective-permute-start | bytes 1966088 | tf_op jit(solution)/shard_map/ppermute | solution.py:30
  48.1 27.6 %collective-permute-start.13 = (bf16[2,128,256]{2,1,0:T(8,128)(2,1)S(1)}, bf16[2,128,256]{2,1,0:T(8,128)(2,1)S(1)}, u32[]{:S(2)}, u32[]{:S(2)}) collective-permute-start(bf16[2,128,256]{2,1,0:T(8,128)(2,1)S(1)} %collective-permute-done.12), channel_id=1, source_target_pairs={{0,1},{1,0},{2,3},{3,2},{4,5},{5,4},{6,7},{7,6},{8,9},{9,8},{10,11... | collective-permute-start | bytes 393224 | tf_op jit(solution)/shard_map/ppermute | solution.py:30
  48.3 24.0 %collective-permute-start.6 = (bf16[3,128,512]{2,1,0:T(8,128)(2,1)S(1)}, bf16[3,128,512]{2,1,0:T(8,128)(2,1)S(1)}, u32[]{:S(2)}, u32[]{:S(2)}) collective-permute-start(bf16[3,128,512]{2,1,0:T(8,128)(2,1)S(1)} %broadcast_select_fusion.15.refs_0_), channel_id=1, source_target_pairs={{0,2},{1,5},{2,0},{3,7},{4,6},{5,1},{6,4},{7,3},{8,10},{9,13},{10,... | collective-permute-start | bytes 1179656 | tf_op jit(solution)/shard_map/ppermute | solution.py:30
  65.1 16.3 %collective-permute-start.17 = (bf16[5,128,512]{2,1,0:T(8,128)(2,1)S(1)}, bf16[5,128,512]{2,1,0:T(8,128)(2,1)S(1)}, u32[]{:S(2)}, u32[]{:S(2)}) collective-permute-start(bf16[5,128,512]{2,1,0:T(8,128)(2,1)S(1)} %get-tuple-element.12), channel_id=1, source_target_pairs={{0,4},{1,3},{2,6},{3,1},{4,0},{5,7},{6,2},{7,5},{8,12},{9,11},{10,... | collective-permute-start | bytes 1966088 | tf_op jit(solution)/shard_map/ppermute | solution.py:30
  66.8 14.7 %collective-permute-start.14 = (bf16[256,1024]{1,0:T(8,128)(2,1)S(1)}, bf16[256,1024]{1,0:T(8,128)(2,1)S(1)}, u32[]{:S(2)}, u32[]{:S(2)}) collective-permute-start(bf16[256,1024]{1,0:T(8,128)(2,1)S(1)} %get-tuple-element.19), channel_id=1, source_target_pairs={{8,16},{16,8},{9,17},{17,9},{10,18},{18,10},{11,19},{19,11},{12,20... | collective-permute-start | bytes 1572872 | tf_op jit(solution)/shard_map/ppermute | solution.py:21
  70.4 13.1 %collective-permute-start.15 = (bf16[256,1024]{1,0:T(8,128)(2,1)S(1)}, bf16[256,1024]{1,0:T(8,128)(2,1)S(1)}, u32[]{:S(2)}, u32[]{:S(2)}) collective-permute-start(bf16[256,1024]{1,0:T(8,128)(2,1)S(1)} %get-tuple-element.20), channel_id=1, source_target_pairs={{0,8},{16,24},{8,0},{24,16},{1,9},{17,25},{9,1},{25,17},{2,10},{18... | collective-permute-start | bytes 1572872 | tf_op jit(solution)/shard_map/ppermute | solution.py:21
  72.3 8.8 %collective-permute-start.21 = (bf16[2,128,256]{2,1,0:T(8,128)(2,1)S(1)}, bf16[2,128,256]{2,1,0:T(8,128)(2,1)S(1)}, u32[]{:S(2)}, u32[]{:S(2)}) collective-permute-start(bf16[2,128,256]{2,1,0:T(8,128)(2,1)S(1)} %pad_maximum_fusion.8), channel_id=1, source_target_pairs={{0,8},{8,16},{16,24},{1,9},{9,17},{17,25},{2,10},{10,18},{18,26},{... | collective-permute-start | bytes 393224 | tf_op jit(solution)/shard_map/ppermute | solution.py:12
  76.1 26.3 %collective-permute-start.7 = (bf16[3,128,512]{2,1,0:T(8,128)(2,1)S(1)}, bf16[3,128,512]{2,1,0:T(8,128)(2,1)S(1)}, u32[]{:S(2)}, u32[]{:S(2)}) collective-permute-start(bf16[3,128,512]{2,1,0:T(8,128)(2,1)S(1)} %broadcast_select_fusion.15.refs_0_), channel_id=1, source_target_pairs={{0,1},{1,0},{2,3},{3,2},{4,5},{5,4},{6,7},{7,6},{8,9},{9,8},{10,11... | collective-permute-start | bytes 1179656 | tf_op jit(solution)/shard_map/ppermute | solution.py:30
  81.1 17.5 %collective-permute-start.26 = (bf16[5,128,512]{2,1,0:T(8,128)(2,1)S(1)}, bf16[5,128,512]{2,1,0:T(8,128)(2,1)S(1)}, u32[]{:S(2)}, u32[]{:S(2)}) collective-permute-start(bf16[5,128,512]{2,1,0:T(8,128)(2,1)S(1)} %get-tuple-element.11), channel_id=1, source_target_pairs={{0,4},{1,3},{2,6},{3,1},{4,0},{5,7},{6,2},{7,5},{8,12},{9,11},{10,... | collective-permute-start | bytes 1966088 | tf_op jit(solution)/shard_map/ppermute | solution.py:30
  81.5 19.9 %collective-permute-start.22 = (bf16[2,128,256]{2,1,0:T(8,128)(2,1)S(1)}, bf16[2,128,256]{2,1,0:T(8,128)(2,1)S(1)}, u32[]{:S(2)}, u32[]{:S(2)}) collective-permute-start(bf16[2,128,256]{2,1,0:T(8,128)(2,1)S(1)} %collective-permute-done.21), channel_id=1, source_target_pairs={{0,1},{1,0},{2,3},{3,2},{4,5},{5,4},{6,7},{7,6},{8,9},{9,8},{10,11... | collective-permute-start | bytes 393224 | tf_op jit(solution)/shard_map/ppermute | solution.py:30
  81.6 19.3 %collective-permute-start.18 = (bf16[5,128,512]{2,1,0:T(8,128)(2,1)S(1)}, bf16[5,128,512]{2,1,0:T(8,128)(2,1)S(1)}, u32[]{:S(2)}, u32[]{:S(2)}) collective-permute-start(bf16[5,128,512]{2,1,0:T(8,128)(2,1)S(1)} %broadcast_select_fusion.3.refs_0_), channel_id=1, source_target_pairs={{0,2},{1,5},{2,0},{3,7},{4,6},{5,1},{6,4},{7,3},{8,10},{9,13},{10,... | collective-permute-start | bytes 1966088 | tf_op jit(solution)/shard_map/ppermute | solution.py:30
  84.1 25.3 %collective-permute-start.19 = (bf16[5,128,512]{2,1,0:T(8,128)(2,1)S(1)}, bf16[5,128,512]{2,1,0:T(8,128)(2,1)S(1)}, u32[]{:S(2)}, u32[]{:S(2)}) collective-permute-start(bf16[5,128,512]{2,1,0:T(8,128)(2,1)S(1)} %broadcast_select_fusion.3.refs_0_), channel_id=1, source_target_pairs={{0,1},{1,0},{2,3},{3,2},{4,5},{5,4},{6,7},{7,6},{8,9},{9,8},{10,11... | collective-permute-start | bytes 1966088 | tf_op jit(solution)/shard_map/ppermute | solution.py:30
  98.7 10.8 %collective-permute-start.27 = (bf16[5,128,512]{2,1,0:T(8,128)(2,1)S(1)}, bf16[5,128,512]{2,1,0:T(8,128)(2,1)S(1)}, u32[]{:S(2)}, u32[]{:S(2)}) collective-permute-start(bf16[5,128,512]{2,1,0:T(8,128)(2,1)S(1)} %broadcast_select_fusion.1.refs_0_), channel_id=1, source_target_pairs={{0,2},{1,5},{2,0},{3,7},{4,6},{5,1},{6,4},{7,3},{8,10},{9,13},{10,... | collective-permute-start | bytes 1966088 | tf_op jit(solution)/shard_map/ppermute | solution.py:30
  100.9 8.6 %collective-permute-start.20 = (bf16[5,128,512]{2,1,0:T(8,128)(2,1)S(1)}, bf16[5,128,512]{2,1,0:T(8,128)(2,1)S(1)}, u32[]{:S(2)}, u32[]{:S(2)}) collective-permute-start(bf16[5,128,512]{2,1,0:T(8,128)(2,1)S(1)} %collective-permute-done.18.refs_1_), channel_id=1, source_target_pairs={{0,1},{1,0},{2,3},{3,2},{4,5},{5,4},{6,7},{7,6},{8,9},{9,8},{10,11... | collective-permute-start | bytes 1966088 | tf_op jit(solution)/shard_map/ppermute | solution.py:30
  103.8 14.0 %collective-permute-start.28 = (bf16[5,128,512]{2,1,0:T(8,128)(2,1)S(1)}, bf16[5,128,512]{2,1,0:T(8,128)(2,1)S(1)}, u32[]{:S(2)}, u32[]{:S(2)}) collective-permute-start(bf16[5,128,512]{2,1,0:T(8,128)(2,1)S(1)} %broadcast_select_fusion.1.refs_0_), channel_id=1, source_target_pairs={{0,1},{1,0},{2,3},{3,2},{4,5},{5,4},{6,7},{7,6},{8,9},{9,8},{10,11... | collective-permute-start | bytes 1966088 | tf_op jit(solution)/shard_map/ppermute | solution.py:30
  109.4 8.4 %collective-permute-start.29 = (bf16[5,128,512]{2,1,0:T(8,128)(2,1)S(1)}, bf16[5,128,512]{2,1,0:T(8,128)(2,1)S(1)}, u32[]{:S(2)}, u32[]{:S(2)}) collective-permute-start(bf16[5,128,512]{2,1,0:T(8,128)(2,1)S(1)} %collective-permute-done.27.refs_1_), channel_id=1, source_target_pairs={{0,1},{1,0},{2,3},{3,2},{4,5},{5,4},{6,7},{7,6},{8,9},{9,8},{10,11... | collective-permute-start | bytes 1966088 | tf_op jit(solution)/shard_map/ppermute | solution.py:30
  115.6 16.2 %collective-permute-start.23 = (bf16[256,1024]{1,0:T(8,128)(2,1)S(1)}, bf16[256,1024]{1,0:T(8,128)(2,1)S(1)}, u32[]{:S(2)}, u32[]{:S(2)}) collective-permute-start(bf16[256,1024]{1,0:T(8,128)(2,1)S(1)} %get-tuple-element.15), channel_id=1, source_target_pairs={{8,16},{16,8},{9,17},{17,9},{10,18},{18,10},{11,19},{19,11},{12,20... | collective-permute-start | bytes 1572872 | tf_op jit(solution)/shard_map/ppermute | solution.py:21
  117.7 14.4 %collective-permute-start.24 = (bf16[256,1024]{1,0:T(8,128)(2,1)S(1)}, bf16[256,1024]{1,0:T(8,128)(2,1)S(1)}, u32[]{:S(2)}, u32[]{:S(2)}) collective-permute-start(bf16[256,1024]{1,0:T(8,128)(2,1)S(1)} %get-tuple-element.16), channel_id=1, source_target_pairs={{0,8},{16,24},{8,0},{24,16},{1,9},{17,25},{9,1},{25,17},{2,10},{18... | collective-permute-start | bytes 1572872 | tf_op jit(solution)/shard_map/ppermute | solution.py:21
  (12 other events, 50.4 us)

commit v4 on v3

--- a/solution.py
+++ b/solution.py
@@ -49,19 +49,19 @@
 ANY = pl.BlockSpec(memory_space=pl.ANY)
 
 
-def after(value, done):
-    def kernel(source, _, out, sem):
-        copy_all([pltpu.make_async_copy(source, out, sem)])
+def after(value, *done):
+    def kernel(source, *refs):
+        copy_all([pltpu.make_async_copy(source, refs[-2], refs[-1])])
 
     return pl.pallas_call(
         kernel,
         out_shape=jax.ShapeDtypeStruct(value.shape, value.dtype),
-        in_specs=[ANY, ANY],
+        in_specs=[ANY] * (1 + len(done)),
         out_specs=ANY,
         scratch_shapes=[pltpu.SemaphoreType.DMA],
         name="after",
         **small(bytes_accessed=4 * value.size),
-    )(value, done)
+    )(value, *done)
 
 
 def runs(ms):
@@ -150,7 +150,7 @@
 
 
 class Spread:
-    def __init__(self, slot, owners_here, groups):
+    def __init__(self, slot, owners_here, order):
         count = lax.axis_size("cols")
         dims = count.bit_length() - 2
         self.me = lax.axis_index("cols")
@@ -158,11 +158,6 @@
         self.owners = owners_here
         self.cut = (1, dims)
         self.others = [(b, b - 1) for b in range(2, dims + 1)]
-        order = [m for group in groups for m in group]
-        self.spans, at = [], 0
-        for group in groups:
-            self.spans.append(slice(at, at + len(group)))
-            at += len(group)
         (give_out,) = cut_slot(self.cut, order, [(False, False)], slot)
         own_out, give_hold, own_hold = cut_slot(
             self.cut, order, [(True, False), (False, True), (True, True)], slot
@@ -173,31 +168,44 @@
     def bit(self, index, bits):
         return (index >> jnp.where(self.core == 0, bits[0], bits[1])) & 1
 
-    def begin(self, round_index, group, first=None):
-        here = (self.owners[round_index] & 1) == self.core
+    def choose(self, rounds, test, yes, no):
+        holds = [test(self.owners[r]) for r in rounds]
+        mask = holds[0]
+        for at in range(1, len(rounds)):
+            if rounds[at] != rounds[at - 1]:
+                row = lax.broadcasted_iota(jnp.int32, yes.shape, 0)
+                mask = jnp.where(row < at, mask, holds[at])
+        return jnp.where(mask, yes, no)
+
+    def begin(self, rounds, rows, *first):
         out, hold = [
-            jnp.where(here, own[self.spans[group]], theirs[self.spans[group]])
+            self.choose(rounds, lambda owner: (owner & 1) == self.core, own[rows], theirs[rows])
             for own, theirs in zip(self.own, self.theirs)
         ]
-        if first is not None:
-            out = after(out, first)
-        return round_index, hold, flip(out, self.cut)
+        if first:
+            out = after(out, *first)
+        return rounds, hold, flip(out, self.cut)
 
     def keep(self, state, bits):
-        round_index, hold, got = state
-        same = self.bit(self.me, bits) == self.bit(self.owners[round_index], bits)
-        return jnp.where(same, hold, got)
-
-    def middle(self, state):
+        rounds, hold, got = state
+        mine = self.bit(self.me, bits)
+        return self.choose(rounds, lambda owner: mine == self.bit(owner, bits), hold, got)
+
+    def middle(self, state, *first):
         bits = self.cut
         for other in self.others:
             hold = self.keep(state, bits)
+            if first:
+                hold = after(hold, *first)
+                first = ()
             state = (state[0], hold, flip(hold, other))
             bits = other
         return state
 
-    def last(self, state):
+    def last(self, state, *first):
         hold = self.keep(state, self.others[-1])
+        if first:
+            hold = after(hold, *first)
         return hold, flip(hold, self.cut)
 
     def join(self, hold, got):
@@ -206,7 +214,7 @@
     def join_above(self, hold, got):
         both = shifted(jnp.stack([hold, got]), "rows", 1)
         other = flip(both, (0, 0))
-        return place(self.cut, both[:1], both[1:], other[:1], other[1:])[0]
+        return place(self.cut, both[0], both[1], other[0], other[1])
 
 
 def apply(q, x):
@@ -228,27 +236,47 @@
     wins = local_rows // window
     rounds = owners.shape[0]
     slot = transforms[0].reshape(2 * wins, 2, 2, window // 4, window)
-    edge = [0, wins - 1, 2 * wins - 1]
-    inside = [m for m in range(2 * wins) if m not in edge]
-    spread = Spread(slot, owners[:, row_block], (edge, inside))
-
-    states, pairs = {}, {}
+    crossing = 2 * wins - 1
+    inside = [m for m in range(crossing) if m not in (0, wins - 1)]
+    spread = Spread(slot, owners[:, row_block], [0, wins - 1, crossing, crossing] + inside)
+
+    heads, tails = [], []
     for r in range(rounds):
-        for g in range(2):
-            first = None if r == 0 else (states[r - 1, 0][2] if g == 0 else pairs[r - 1, 0][1])
-            states[r, g] = spread.middle(spread.begin(r, g, first))
-        for g in range(2):
-            pairs[r, g] = spread.last(states[r, g])
+        across = ([r] if r == 0 else []) + ([r + 1] if r + 1 < rounds else [])
+        edge_rounds = [r, r] + across
+        edge_rows = slice(0, len(edge_rounds))
+        rest_rounds = [r] * len(inside)
+        rest_rows = slice(4, 4 + len(inside))
+        if r == 0:
+            head = spread.middle(spread.begin(edge_rounds, edge_rows))
+            tail_one = spread.begin(rest_rounds, rest_rows)
+            tail_two = spread.middle(tail_one)
+            head_end = spread.last(head)
+            tail_end = spread.last(tail_two)
+        else:
+            head_one = spread.begin(edge_rounds, edge_rows, tail_one[2])
+            head_two = spread.middle(head_one, tail_two[2])
+            tail_one = spread.begin(rest_rounds, rest_rows, head_end[1])
+            tail_two = spread.middle(tail_one)
+            head_end = spread.last(head_two, tail_end[1], tail_one[2])
+            tail_end = spread.last(tail_two)
+        heads.append(head_end)
+        tails.append(tail_end)
 
     matrix = slab
+    crosses, above_crosses = [], []
     for r in range(rounds):
-        head, tail = pairs[r, 0], pairs[r, 1]
+        head, tail = heads[r], tails[r]
         edges = spread.join(*head)
+        crosses += [edges[k] for k in range(2, edges.shape[0])]
+        if edges.shape[0] > 2:
+            from_above = spread.join_above(head[0][2:, :, border:], head[1][2:, :, border:])
+            above_crosses += [from_above[k] for k in range(from_above.shape[0])]
+        prev, cross = above_crosses[r], crosses[r]
         head_rows = apply(edges[0], matrix[:window])
         tail_rows = apply(edges[1], matrix[local_rows - window :])
         begin, end = head_rows[:border], tail_rows[border:]
         above, below = swap_rows(begin, end)
-        prev = spread.join_above(head[0][-1, :, border:], head[1][-1, :, border:])
         rest = spread.join(*tail)
         mid = apply_many(
             rest[: wins - 2],
@@ -258,7 +286,7 @@
         inner = apply_many(rest[wins - 2 :], centre.reshape(wins - 1, window, local_cols)).reshape(
             local_rows - window, local_cols
         )
-        low = apply(edges[2, :, :border], jnp.concatenate([end, below], 0))
+        low = apply(cross[:, :border], jnp.concatenate([end, below], 0))
         low = jnp.where(row_block == last_block, end, low)
         top = apply(prev, jnp.concatenate([above, begin], 0))
         top = jnp.where(row_block == 0, begin, top)

time: 137 us -> 134 us (0.978)
  waiting for transfers between devices: 70.6 us -> 60.5 us
  other arithmetic: 9.55 us -> 12.7 us
  local copies, waits for them, and re-layouts: 3.11 us -> 5.46 us
  Pallas kernels: 4.55 us -> 6.01 us
    ppermute x24 -> x23, waiting for transfers between devices: 55.7 us -> 47.2 us  [flip(): lax.ppermute(value, 'cols', [(d, d ^ 1 << bits[d & 1]) for d in range(cou...]
    ppermute x2 -> x1, starting transfers between devices: 6.85 us -> 3.47 us  [shifted(): lax.ppermute(value, axis, [(source, source + steps) for source in range(i...]
    select_n x9 -> x13, other arithmetic: 5.92 us -> 8.34 us  [the longest x10 8.33 us: choose(): return jnp.where(mask, yes, no)]
    ppermute x4, starting transfers between devices: 5.84 us -> 7.74 us  [swap(): return lax.ppermute(value, 'rows', pairs + [(b, a) for a, b in pairs])]
    ppermute x2 -> x1, waiting for transfers between devices: 4.89 us -> 4.02 us  [shifted(): lax.ppermute(value, axis, [(source, source + steps) for source in range(i...]
    ppermute x24 -> x23, starting transfers between devices: 18.7 us -> 19.5 us  [flip(): lax.ppermute(value, 'cols', [(d, d ^ 1 << bits[d & 1]) for d in range(cou...]
  transfers between devices with their start and end apart: 30 -> 28, of which waited for: 14 -> 11; matrix products, arithmetic and copies ran while one was open for 13% -> 17% of each run, Pallas kernels for 3% -> 4%
where the time goes in v4:
time: 134 us; the launch traced here: 132 us
  waiting for transfers between devices  60.5 us (45%)
  starting transfers between devices  30.8 us (23%)
  other arithmetic  12.7 us (9%)
  matrix products  12 us (9%)
  Pallas kernels  6.01 us (4%)
  local copies, waits for them, and re-layouts  5.46 us (4%)
  between operations  4.36 us (3%)
    ppermute x23, waiting for transfers between devices, flip(): lax.ppermute(value, 'cols', [(d, d ^ 1 << bits[d & 1]) for d in range(cou...  47.2 us
    ppermute x23, starting transfers between devices, flip(): lax.ppermute(value, 'cols', [(d, d ^ 1 << bits[d & 1]) for d in range(cou...  19.5 us
    ppermute x4, waiting for transfers between devices, swap(): return lax.ppermute(value, 'rows', pairs + [(b, a) for a, b in pairs])  9.24 us
    select_n x10, other arithmetic, choose(): return jnp.where(mask, yes, no)  8.33 us
    ppermute x4, starting transfers between devices, swap(): return lax.ppermute(value, 'rows', pairs + [(b, a) for a, b in pairs])  7.74 us
    dot_general x4, matrix products, apply_many(): jnp.einsum('nab,nac->nbc', q, x, preferred_element_type=jnp.float32)  7.28 us
    dot_general x8, matrix products, apply(): lax.dot_general(q, x, (((0,), (0,)), ((), ())), preferred_element_type=jn...  4.75 us
    ppermute x1, waiting for transfers between devices, shifted(): lax.ppermute(value, axis, [(source, source + steps) for source in range(i...  4.02 us
  transfers between devices with their start and end apart: 28, of which 11 were waited for; matrix products, arithmetic and copies ran while one was open for 17% of the time, Pallas kernels for 4%

profile of v4, /device:TPU:8, one launch (start us, length us, event | category | flops | bytes accessed | tf_op | source)
XLA Modules:
  0.0 131.8 jit_solution(10009261388577133182)
XLA Ops:
  0.0 2.2 %copy-done.2 = bf16[1,4096,512]{2,1,0:T(8,128)(2,1)S(1)} copy-done((bf16[1,4096,512]{2,1,0:T(8,128)(2,1)S(1)}, bf16[1,4096,512]{2,1,0:T(8,128)(2,1)}, u32[]{:S(2)}) %copy-start.2) | copy-done | bytes 4194328
  3.1 1.9 %cut_slot.2 = (bf16[9,128,512]{2,1,0:T(8,128)(2,1)S(1)}, bf16[9,128,512]{2,1,0:T(8,128)(2,1)}, bf16[9,128,512]{2,1,0:T(8,128)(2,1)S(1)}) custom-call(bf16[8,2,2,128,512]{4,3,2,1,0:T(8,128)(2,1)S(1)} %bitcast.54), custom_call_target="tpu_custom_call" | custom-call | bytes 6291456 | tf_op jit(solution)/shard_map/cut_slot/pallas_call | solution.py:105
  11.6 6.4 %collective-permute-done.7 = bf16[4,128,512]{2,1,0:T(8,128)(2,1)S(1)} collective-permute-done((bf16[4,128,512]{2,1,0:T(8,128)(2,1)S(1)}, bf16[4,128,512]{2,1,0:T(8,128)(2,1)S(1)}, u32[]{:S(2)}, u32[]{:S(2)}) %collective-permute-start.7) | collective-permute-done | bytes 524320 | tf_op jit(solution)/shard_map/ppermute | solution.py:30
  19.2 1.6 %collective-permute-start.8 = (bf16[4,128,512]{2,1,0:T(8,128)(2,1)S(1)}, bf16[4,128,512]{2,1,0:T(8,128)(2,1)}, u32[]{:S(2)}, u32[]{:S(2)}) collective-permute-start(bf16[4,128,512]{2,1,0:T(8,128)(2,1)S(1)} %fusion.20), channel_id=1, source_target_pairs={{0,4},{1,3},{2,6},{3,1},{4,0},{5,7},{6,2},{7,5},{8,12},{9,11},{10,... | collective-permute-start | bytes 1572872 | tf_op jit(solution)/shard_map/ppermute | solution.py:30
  24.8 7.1 %collective-permute-done.8 = bf16[4,128,512]{2,1,0:T(8,128)(2,1)} collective-permute-done((bf16[4,128,512]{2,1,0:T(8,128)(2,1)S(1)}, bf16[4,128,512]{2,1,0:T(8,128)(2,1)}, u32[]{:S(2)}, u32[]{:S(2)}) %collective-permute-start.8) | collective-permute-done | bytes 524320 | tf_op jit(solution)/shard_map/ppermute | solution.py:30
  33.1 2.6 %collective-permute-start.9 = (bf16[4,128,512]{2,1,0:T(8,128)(2,1)S(1)}, bf16[4,128,512]{2,1,0:T(8,128)(2,1)S(1)}, u32[]{:S(2)}, u32[]{:S(2)}) collective-permute-start(bf16[4,128,512]{2,1,0:T(8,128)(2,1)S(1)} %broadcast_select_fusion.4.refs_0_), channel_id=1, source_target_pairs={{0,2},{1,5},{2,0},{3,7},{4,6},{5,1},{6,4},{7,3},{8,10},{9,13},{10,... | collective-permute-start | bytes 1572872 | tf_op jit(solution)/shard_map/ppermute | solution.py:30
  37.6 5.2 %collective-permute-done.9.refs_0_.refs_1_ = bf16[4,128,512]{2,1,0:T(8,128)(2,1)S(1)} collective-permute-done((bf16[4,128,512]{2,1,0:T(8,128)(2,1)S(1)}, bf16[4,128,512]{2,1,0:T(8,128)(2,1)S(1)}, u32[]{:S(2)}, u32[]{:S(2)}) %collective-permute-start.9) | collective-permute-done | bytes 524320 | tf_op jit(solution)/shard_map/ppermute | solution.py:30
  43.5 3.5 %collective-permute-start.16 = (bf16[2,2,128,256]{3,2,1,0:T(8,128)(2,1)}, bf16[2,2,128,256]{3,2,1,0:T(8,128)(2,1)}, u32[]{:S(2)}, u32[]{:S(2)}) collective-permute-start(bf16[2,2,128,256]{3,2,1,0:T(8,128)(2,1)} %pad_maximum_fusion.7), channel_id=1, source_target_pairs={{0,8},{8,16},{16,24},{1,9},{9,17},{17,25},{2,10},{10,18},{18,26},{... | collective-permute-start | bytes 786440 | tf_op jit(solution)/shard_map/ppermute | solution.py:12
  47.3 2.1 %collective-permute-start.10 = (bf16[5,128,512]{2,1,0:T(8,128)(2,1)S(1)}, bf16[5,128,512]{2,1,0:T(8,128)(2,1)S(1)}, u32[]{:S(2)}, u32[]{:S(2)}) collective-permute-start(bf16[5,128,512]{2,1,0:T(8,128)(2,1)S(1)} %after.6), channel_id=1, source_target_pairs={{0,2},{1,5},{2,0},{3,7},{4,6},{5,1},{6,4},{7,3},{8,10},{9,13},{10,... | collective-permute-start | bytes 1966088 | tf_op jit(solution)/shard_map/ppermute | solution.py:30
  50.4 4.0 %collective-permute-done.16 = bf16[2,2,128,256]{3,2,1,0:T(8,128)(2,1)} collective-permute-done((bf16[2,2,128,256]{3,2,1,0:T(8,128)(2,1)}, bf16[2,2,128,256]{3,2,1,0:T(8,128)(2,1)}, u32[]{:S(2)}, u32[]{:S(2)}) %collective-permute-start.16) | collective-permute-done | bytes 262176 | tf_op jit(solution)/shard_map/ppermute | solution.py:12
  59.2 1.6 %collective-permute-start.4 = (bf16[5,128,512]{2,1,0:T(8,128)(2,1)S(1)}, bf16[5,128,512]{2,1,0:T(8,128)(2,1)S(1)}, u32[]{:S(2)}, u32[]{:S(2)}) collective-permute-start(bf16[5,128,512]{2,1,0:T(8,128)(2,1)S(1)} %get-tuple-element.12), channel_id=1, source_target_pairs={{0,4},{1,3},{2,6},{3,1},{4,0},{5,7},{6,2},{7,5},{8,12},{9,11},{10,... | collective-permute-start | bytes 1966088 | tf_op jit(solution)/shard_map/ppermute | solution.py:30
  61.7 3.5 %collective-permute-start.18 = (bf16[256,1024]{1,0:T(8,128)(2,1)S(1)}, bf16[256,1024]{1,0:T(8,128)(2,1)S(1)}, u32[]{:S(2)}, u32[]{:S(2)}) collective-permute-start(bf16[256,1024]{1,0:T(8,128)(2,1)S(1)} %get-tuple-element.19), channel_id=1, source_target_pairs={{8,16},{16,8},{9,17},{17,9},{10,18},{18,10},{11,19},{19,11},{12,20... | collective-permute-start | bytes 1572872 | tf_op jit(solution)/shard_map/ppermute | solution.py:21
  65.9 3.9 %collective-permute-done.4.refs_0_ = bf16[5,128,512]{2,1,0:T(8,128)(2,1)S(1)} collective-permute-done((bf16[5,128,512]{2,1,0:T(8,128)(2,1)S(1)}, bf16[5,128,512]{2,1,0:T(8,128)(2,1)S(1)}, u32[]{:S(2)}, u32[]{:S(2)}) %collective-permute-start.4) | collective-permute-done | bytes 655392 | tf_op jit(solution)/shard_map/ppermute | solution.py:30
  69.9 2.1 %collective-permute-start.6 = (bf16[5,128,512]{2,1,0:T(8,128)(2,1)S(1)}, bf16[5,128,512]{2,1,0:T(8,128)(2,1)S(1)}, u32[]{:S(2)}, u32[]{:S(2)}) collective-permute-start(bf16[5,128,512]{2,1,0:T(8,128)(2,1)S(1)} %broadcast_select_fusion.2.refs_0_), channel_id=1, source_target_pairs={{0,2},{1,5},{2,0},{3,7},{4,6},{5,1},{6,4},{7,3},{8,10},{9,13},{10,... | collective-permute-start | bytes 1966088 | tf_op jit(solution)/shard_map/ppermute | solution.py:30
  72.5 9.0 %collective-permute-done.24 = bf16[5,128,512]{2,1,0:T(8,128)(2,1)S(1)} collective-permute-done((bf16[5,128,512]{2,1,0:T(8,128)(2,1)S(1)}, bf16[5,128,512]{2,1,0:T(8,128)(2,1)S(1)}, u32[]{:S(2)}, u32[]{:S(2)}) %collective-permute-start.24) | collective-permute-done | bytes 655392 | tf_op jit(solution)/shard_map/ppermute | solution.py:30
  83.1 4.8 %collective-permute-done.5 = bf16[2,128,512]{2,1,0:T(8,128)(2,1)S(1)} collective-permute-done((bf16[2,128,512]{2,1,0:T(8,128)(2,1)S(1)}, bf16[2,128,512]{2,1,0:T(8,128)(2,1)S(1)}, u32[]{:S(2)}, u32[]{:S(2)}) %collective-permute-start.5) | collective-permute-done | bytes 262176 | tf_op jit(solution)/shard_map/ppermute | solution.py:30
  87.9 2.3 %collective-permute-start.25 = (bf16[5,128,512]{2,1,0:T(8,128)(2,1)S(1)}, bf16[5,128,512]{2,1,0:T(8,128)(2,1)S(1)}, u32[]{:S(2)}, u32[]{:S(2)}) collective-permute-start(bf16[5,128,512]{2,1,0:T(8,128)(2,1)S(1)} %broadcast_select_fusion.refs_0_), channel_id=1, source_target_pairs={{0,2},{1,5},{2,0},{3,7},{4,6},{5,1},{6,4},{7,3},{8,10},{9,13},{10,... | collective-permute-start | bytes 1966088 | tf_op jit(solution)/shard_map/ppermute | solution.py:30
  91.1 10.5 %collective-permute-done.11.refs_1_ = bf16[2,128,512]{2,1,0:T(8,128)(2,1)S(1)} collective-permute-done((bf16[2,128,512]{2,1,0:T(8,128)(2,1)S(1)}, bf16[2,128,512]{2,1,0:T(8,128)(2,1)S(1)}, u32[]{:S(2)}, u32[]{:S(2)}) %collective-permute-start.11) | collective-permute-done | bytes 262176 | tf_op jit(solution)/shard_map/ppermute | solution.py:30
  106.8 2.1 %convolution_convert_fusion.1 = bf16[3,512,1024]{2,1,0:T(8,128)(2,1)S(1)} fusion(bf16[5,512,512]{2,1,0:T(8,128)(2,1)S(1)} %place.8, bf16[3,512,1024]{2,1,0:T(8,128)(2,1)S(1)} %bitcast.58), kind=kOutput, calls=%fused_computation.4 | convolution fusion | flops 1612185600 | bytes 8912896 | tf_op jit(solution)/shard_map/nab,nac->nbc/dot_general | solution.py:226
  110.8 3.7 %collective-permute-start.22 = (bf16[256,1024]{1,0:T(8,128)(2,1)S(1)}, bf16[256,1024]{1,0:T(8,128)(2,1)S(1)}, u32[]{:S(2)}, u32[]{:S(2)}) collective-permute-start(bf16[256,1024]{1,0:T(8,128)(2,1)S(1)} %get-tuple-element.17), channel_id=1, source_target_pairs={{8,16},{16,8},{9,17},{17,9},{10,18},{18,10},{11,19},{19,11},{12,20... | collective-permute-start | bytes 1572872 | tf_op jit(solution)/shard_map/ppermute | solution.py:21
  117.2 2.1 %convolution_convert_fusion = bf16[3,512,1024]{2,1,0:T(8,128)(2,1)S(1)} fusion(bf16[5,512,512]{2,1,0:T(8,128)(2,1)S(1)} %place.9, bf16[3,512,1024]{2,1,0:T(8,128)(2,1)S(1)} %bitcast.59), kind=kOutput, calls=%fused_computation.3 | convolution fusion | flops 1612185600 | bytes 8912896 | tf_op jit(solution)/shard_map/nab,nac->nbc/dot_general | solution.py:226
  119.3 7.7 %collective-permute-done.22 = bf16[256,1024]{1,0:T(8,128)(2,1)S(1)} collective-permute-done((bf16[256,1024]{1,0:T(8,128)(2,1)S(1)}, bf16[256,1024]{1,0:T(8,128)(2,1)S(1)}, u32[]{:S(2)}, u32[]{:S(2)}) %collective-permute-start.22) | collective-permute-done | bytes 524320 | tf_op jit(solution)/shard_map/ppermute | solution.py:21
  126.9 1.6 %collective-permute-done.23 = bf16[256,1024]{1,0:T(8,128)(2,1)S(1)} collective-permute-done((bf16[256,1024]{1,0:T(8,128)(2,1)S(1)}, bf16[256,1024]{1,0:T(8,128)(2,1)S(1)}, u32[]{:S(2)}, u32[]{:S(2)}) %collective-permute-start.23) | collective-permute-done | bytes 524320 | tf_op jit(solution)/shard_map/ppermute | solution.py:21
  129.5 2.3 %pad_maximum_fusion = bf16[2048,1024]{1,0:T(8,128)(2,1)} fusion(bf16[256,1024]{1,0:T(8,128)(2,1)S(1)} %fusion.3, bf16[1536,1024]{1,0:T(8,128)(2,1)S(1)} %bitcast.60, bf16[256,1024]{1,0:T(8,128)(2,1)S(1)} %fusion.2), kind=kLoop, calls=%fused_computation | loop fusion | flops 12582912 | bytes 8388608 | tf_op jit(solution)/shard_map/concatenate | solution.py:293
  (96 shorter events, 33.9 us)
Async XLA Ops:
  8.7 9.2 %collective-permute-start.7 = (bf16[4,128,512]{2,1,0:T(8,128)(2,1)S(1)}, bf16[4,128,512]{2,1,0:T(8,128)(2,1)S(1)}, u32[]{:S(2)}, u32[]{:S(2)}) collective-permute-start(bf16[4,128,512]{2,1,0:T(8,128)(2,1)S(1)} %slice_select_fusion), channel_id=1, source_target_pairs={{0,2},{1,5},{2,0},{3,7},{4,6},{5,1},{6,4},{7,3},{8,10},{9,13},{10,... | collective-permute-start | bytes 1572872 | tf_op jit(solution)/shard_map/ppermute | solution.py:30
  19.2 12.8 %collective-permute-start.8 = (bf16[4,128,512]{2,1,0:T(8,128)(2,1)S(1)}, bf16[4,128,512]{2,1,0:T(8,128)(2,1)}, u32[]{:S(2)}, u32[]{:S(2)}) collective-permute-start(bf16[4,128,512]{2,1,0:T(8,128)(2,1)S(1)} %fusion.20), channel_id=1, source_target_pairs={{0,4},{1,3},{2,6},{3,1},{4,0},{5,7},{6,2},{7,5},{8,12},{9,11},{10,... | collective-permute-start | bytes 1572872 | tf_op jit(solution)/shard_map/ppermute | solution.py:30
  23.2 13.5 %collective-permute-start.2 = (bf16[5,128,512]{2,1,0:T(8,128)(2,1)S(1)}, bf16[5,128,512]{2,1,0:T(8,128)(2,1)S(1)}, u32[]{:S(2)}, u32[]{:S(2)}) collective-permute-start(bf16[5,128,512]{2,1,0:T(8,128)(2,1)S(1)} %get-tuple-element.14), channel_id=1, source_target_pairs={{0,2},{1,5},{2,0},{3,7},{4,6},{5,1},{6,4},{7,3},{8,10},{9,13},{10,... | collective-permute-start | bytes 1966088 | tf_op jit(solution)/shard_map/ppermute | solution.py:30
  33.1 9.7 %collective-permute-start.9 = (bf16[4,128,512]{2,1,0:T(8,128)(2,1)S(1)}, bf16[4,128,512]{2,1,0:T(8,128)(2,1)S(1)}, u32[]{:S(2)}, u32[]{:S(2)}) collective-permute-start(bf16[4,128,512]{2,1,0:T(8,128)(2,1)S(1)} %broadcast_select_fusion.4.refs_0_), channel_id=1, source_target_pairs={{0,2},{1,5},{2,0},{3,7},{4,6},{5,1},{6,4},{7,3},{8,10},{9,13},{10,... | collective-permute-start | bytes 1572872 | tf_op jit(solution)/shard_map/ppermute | solution.py:30
  37.4 11.9 %collective-permute-start.3 = (bf16[2,128,512]{2,1,0:T(8,128)(2,1)}, bf16[2,128,512]{2,1,0:T(8,128)(2,1)}, u32[]{:S(2)}, u32[]{:S(2)}) collective-permute-start(bf16[2,128,512]{2,1,0:T(8,128)(2,1)} %after.4), channel_id=1, source_target_pairs={{0,2},{1,5},{2,0},{3,7},{4,6},{5,1},{6,4},{7,3},{8,10},{9,13},{10,... | collective-permute-start | bytes 786440 | tf_op jit(solution)/shard_map/ppermute | solution.py:30
  37.5 17.9 %collective-permute-start.14 = (bf16[4,128,512]{2,1,0:T(8,128)(2,1)S(1)}, bf16[4,128,512]{2,1,0:T(8,128)(2,1)}, u32[]{:S(2)}, u32[]{:S(2)}) collective-permute-start(bf16[4,128,512]{2,1,0:T(8,128)(2,1)S(1)} %broadcast_select_fusion.4.refs_0_), channel_id=1, source_target_pairs={{0,1},{1,0},{2,3},{3,2},{4,5},{5,4},{6,7},{7,6},{8,9},{9,8},{10,11... | collective-permute-start | bytes 1572872 | tf_op jit(solution)/shard_map/ppermute | solution.py:30
  42.8 12.7 %collective-permute-start.15 = (bf16[4,128,512]{2,1,0:T(8,128)(2,1)S(1)}, bf16[4,128,512]{2,1,0:T(8,128)(2,1)}, u32[]{:S(2)}, u32[]{:S(2)}) collective-permute-start(bf16[4,128,512]{2,1,0:T(8,128)(2,1)S(1)} %collective-permute-done.9.refs_0_.refs_1_), channel_id=1, source_target_pairs={{0,1},{1,0},{2,3},{3,2},{4,5},{5,4},{6,7},{7,6},{8,9},{9,8},{10,11... | collective-permute-start | bytes 1572872 | tf_op jit(solution)/shard_map/ppermute | solution.py:30
  43.5 10.9 %collective-permute-start.16 = (bf16[2,2,128,256]{3,2,1,0:T(8,128)(2,1)}, bf16[2,2,128,256]{3,2,1,0:T(8,128)(2,1)}, u32[]{:S(2)}, u32[]{:S(2)}) collective-permute-start(bf16[2,2,128,256]{3,2,1,0:T(8,128)(2,1)} %pad_maximum_fusion.7), channel_id=1, source_target_pairs={{0,8},{8,16},{16,24},{1,9},{9,17},{17,25},{2,10},{10,18},{18,26},{... | collective-permute-start | bytes 786440 | tf_op jit(solution)/shard_map/ppermute | solution.py:12
  47.3 10.7 %collective-permute-start.10 = (bf16[5,128,512]{2,1,0:T(8,128)(2,1)S(1)}, bf16[5,128,512]{2,1,0:T(8,128)(2,1)S(1)}, u32[]{:S(2)}, u32[]{:S(2)}) collective-permute-start(bf16[5,128,512]{2,1,0:T(8,128)(2,1)S(1)} %after.6), channel_id=1, source_target_pairs={{0,2},{1,5},{2,0},{3,7},{4,6},{5,1},{6,4},{7,3},{8,10},{9,13},{10,... | collective-permute-start | bytes 1966088 | tf_op jit(solution)/shard_map/ppermute | solution.py:30
  54.5 17.5 %collective-permute-start.17 = (bf16[2,2,128,256]{3,2,1,0:T(8,128)(2,1)}, bf16[2,2,128,256]{3,2,1,0:T(8,128)(2,1)S(1)}, u32[]{:S(2)}, u32[]{:S(2)}) collective-permute-start(bf16[2,2,128,256]{3,2,1,0:T(8,128)(2,1)} %collective-permute-done.16), channel_id=1, source_target_pairs={{0,1},{1,0},{2,3},{3,2},{4,5},{5,4},{6,7},{7,6},{8,9},{9,8},{10,11... | collective-permute-start | bytes 786440 | tf_op jit(solution)/shard_map/ppermute | solution.py:30
  59.2 10.7 %collective-permute-start.4 = (bf16[5,128,512]{2,1,0:T(8,128)(2,1)S(1)}, bf16[5,128,512]{2,1,0:T(8,128)(2,1)S(1)}, u32[]{:S(2)}, u32[]{:S(2)}) collective-permute-start(bf16[5,128,512]{2,1,0:T(8,128)(2,1)S(1)} %get-tuple-element.12), channel_id=1, source_target_pairs={{0,4},{1,3},{2,6},{3,1},{4,0},{5,7},{6,2},{7,5},{8,12},{9,11},{10,... | collective-permute-start | bytes 1966088 | tf_op jit(solution)/shard_map/ppermute | solution.py:30
  61.7 28.6 %collective-permute-start.18 = (bf16[256,1024]{1,0:T(8,128)(2,1)S(1)}, bf16[256,1024]{1,0:T(8,128)(2,1)S(1)}, u32[]{:S(2)}, u32[]{:S(2)}) collective-permute-start(bf16[256,1024]{1,0:T(8,128)(2,1)S(1)} %get-tuple-element.19), channel_id=1, source_target_pairs={{8,16},{16,8},{9,17},{17,9},{10,18},{18,10},{11,19},{19,11},{12,20... | collective-permute-start | bytes 1572872 | tf_op jit(solution)/shard_map/ppermute | solution.py:21
  65.2 25.2 %collective-permute-start.19 = (bf16[256,1024]{1,0:T(8,128)(2,1)S(1)}, bf16[256,1024]{1,0:T(8,128)(2,1)S(1)}, u32[]{:S(2)}, u32[]{:S(2)}) collective-permute-start(bf16[256,1024]{1,0:T(8,128)(2,1)S(1)} %get-tuple-element.20), channel_id=1, source_target_pairs={{0,8},{16,24},{8,0},{24,16},{1,9},{17,25},{9,1},{25,17},{2,10},{18... | collective-permute-start | bytes 1572872 | tf_op jit(solution)/shard_map/ppermute | solution.py:21
  65.3 16.2 %collective-permute-start.24 = (bf16[5,128,512]{2,1,0:T(8,128)(2,1)S(1)}, bf16[5,128,512]{2,1,0:T(8,128)(2,1)S(1)}, u32[]{:S(2)}, u32[]{:S(2)}) collective-permute-start(bf16[5,128,512]{2,1,0:T(8,128)(2,1)S(1)} %get-tuple-element.11), channel_id=1, source_target_pairs={{0,4},{1,3},{2,6},{3,1},{4,0},{5,7},{6,2},{7,5},{8,12},{9,11},{10,... | collective-permute-start | bytes 1966088 | tf_op jit(solution)/shard_map/ppermute | solution.py:30
  69.9 20.3 %collective-permute-start.6 = (bf16[5,128,512]{2,1,0:T(8,128)(2,1)S(1)}, bf16[5,128,512]{2,1,0:T(8,128)(2,1)S(1)}, u32[]{:S(2)}, u32[]{:S(2)}) collective-permute-start(bf16[5,128,512]{2,1,0:T(8,128)(2,1)S(1)} %broadcast_select_fusion.2.refs_0_), channel_id=1, source_target_pairs={{0,2},{1,5},{2,0},{3,7},{4,6},{5,1},{6,4},{7,3},{8,10},{9,13},{10,... | collective-permute-start | bytes 1966088 | tf_op jit(solution)/shard_map/ppermute | solution.py:30
  72.4 30.9 %collective-permute-start.20 = (bf16[5,128,512]{2,1,0:T(8,128)(2,1)S(1)}, bf16[5,128,512]{2,1,0:T(8,128)(2,1)S(1)}, u32[]{:S(2)}, u32[]{:S(2)}) collective-permute-start(bf16[5,128,512]{2,1,0:T(8,128)(2,1)S(1)} %broadcast_select_fusion.2.refs_0_), channel_id=1, source_target_pairs={{0,1},{1,0},{2,3},{3,2},{4,5},{5,4},{6,7},{7,6},{8,9},{9,8},{10,11... | collective-permute-start | bytes 1966088 | tf_op jit(solution)/shard_map/ppermute | solution.py:30
  87.9 14.6 %collective-permute-start.25 = (bf16[5,128,512]{2,1,0:T(8,128)(2,1)S(1)}, bf16[5,128,512]{2,1,0:T(8,128)(2,1)S(1)}, u32[]{:S(2)}, u32[]{:S(2)}) collective-permute-start(bf16[5,128,512]{2,1,0:T(8,128)(2,1)S(1)} %broadcast_select_fusion.refs_0_), channel_id=1, source_target_pairs={{0,2},{1,5},{2,0},{3,7},{4,6},{5,1},{6,4},{7,3},{8,10},{9,13},{10,... | collective-permute-start | bytes 1966088 | tf_op jit(solution)/shard_map/ppermute | solution.py:30
  90.3 11.3 %collective-permute-start.11 = (bf16[2,128,512]{2,1,0:T(8,128)(2,1)S(1)}, bf16[2,128,512]{2,1,0:T(8,128)(2,1)S(1)}, u32[]{:S(2)}, u32[]{:S(2)}) collective-permute-start(bf16[2,128,512]{2,1,0:T(8,128)(2,1)S(1)} %after.7.refs_0_), channel_id=1, source_target_pairs={{0,2},{1,5},{2,0},{3,7},{4,6},{5,1},{6,4},{7,3},{8,10},{9,13},{10,... | collective-permute-start | bytes 786440 | tf_op jit(solution)/shard_map/ppermute | solution.py:30
  90.3 13.0 %collective-permute-start.21 = (bf16[5,128,512]{2,1,0:T(8,128)(2,1)S(1)}, bf16[5,128,512]{2,1,0:T(8,128)(2,1)S(1)}, u32[]{:S(2)}, u32[]{:S(2)}) collective-permute-start(bf16[5,128,512]{2,1,0:T(8,128)(2,1)S(1)} %collective-permute-done.6.refs_0_.refs_1_), channel_id=1, source_target_pairs={{0,1},{1,0},{2,3},{3,2},{4,5},{5,4},{6,7},{7,6},{8,9},{9,8},{10,11... | collective-permute-start | bytes 1966088 | tf_op jit(solution)/shard_map/ppermute | solution.py:30
  90.5 12.6 %collective-permute-start.12 = (bf16[2,128,512]{2,1,0:T(8,128)(2,1)S(1)}, bf16[2,128,512]{2,1,0:T(8,128)(2,1)S(1)}, u32[]{:S(2)}, u32[]{:S(2)}) collective-permute-start(bf16[2,128,512]{2,1,0:T(8,128)(2,1)S(1)} %after.7.refs_0_), channel_id=1, source_target_pairs={{0,1},{1,0},{2,3},{3,2},{4,5},{5,4},{6,7},{7,6},{8,9},{9,8},{10,11... | collective-permute-start | bytes 786440 | tf_op jit(solution)/shard_map/ppermute | solution.py:30
  102.5 12.5 %collective-permute-start.26 = (bf16[5,128,512]{2,1,0:T(8,128)(2,1)S(1)}, bf16[5,128,512]{2,1,0:T(8,128)(2,1)S(1)}, u32[]{:S(2)}, u32[]{:S(2)}) collective-permute-start(bf16[5,128,512]{2,1,0:T(8,128)(2,1)S(1)} %broadcast_select_fusion.refs_0_), channel_id=1, source_target_pairs={{0,1},{1,0},{2,3},{3,2},{4,5},{5,4},{6,7},{7,6},{8,9},{9,8},{10,11... | collective-permute-start | bytes 1966088 | tf_op jit(solution)/shard_map/ppermute | solution.py:30
  103.1 11.9 %collective-permute-start.27 = (bf16[5,128,512]{2,1,0:T(8,128)(2,1)S(1)}, bf16[5,128,512]{2,1,0:T(8,128)(2,1)S(1)}, u32[]{:S(2)}, u32[]{:S(2)}) collective-permute-start(bf16[5,128,512]{2,1,0:T(8,128)(2,1)S(1)} %collective-permute-done.25.refs_1_), channel_id=1, source_target_pairs={{0,1},{1,0},{2,3},{3,2},{4,5},{5,4},{6,7},{7,6},{8,9},{9,8},{10,11... | collective-permute-start | bytes 1966088 | tf_op jit(solution)/shard_map/ppermute | solution.py:30
  110.8 16.2 %collective-permute-start.22 = (bf16[256,1024]{1,0:T(8,128)(2,1)S(1)}, bf16[256,1024]{1,0:T(8,128)(2,1)S(1)}, u32[]{:S(2)}, u32[]{:S(2)}) collective-permute-start(bf16[256,1024]{1,0:T(8,128)(2,1)S(1)} %get-tuple-element.17), channel_id=1, source_target_pairs={{8,16},{16,8},{9,17},{17,9},{10,18},{18,10},{11,19},{19,11},{12,20... | collective-permute-start | bytes 1572872 | tf_op jit(solution)/shard_map/ppermute | solution.py:21
  114.5 14.1 %collective-permute-start.23 = (bf16[256,1024]{1,0:T(8,128)(2,1)S(1)}, bf16[256,1024]{1,0:T(8,128)(2,1)S(1)}, u32[]{:S(2)}, u32[]{:S(2)}) collective-permute-start(bf16[256,1024]{1,0:T(8,128)(2,1)S(1)} %get-tuple-element.18), channel_id=1, source_target_pairs={{0,8},{16,24},{8,0},{24,16},{1,9},{17,25},{9,1},{25,17},{2,10},{18... | collective-permute-start | bytes 1572872 | tf_op jit(solution)/shard_map/ppermute | solution.py:21
  (10 other events, 55.2 us)

commit v5 on v4

--- a/solution.py
+++ b/solution.py
@@ -237,53 +237,52 @@
     rounds = owners.shape[0]
     slot = transforms[0].reshape(2 * wins, 2, 2, window // 4, window)
     crossing = 2 * wins - 1
-    inside = [m for m in range(crossing) if m not in (0, wins - 1)]
-    spread = Spread(slot, owners[:, row_block], [0, wins - 1, crossing, crossing] + inside)
+    middle_one, middle_two = list(range(1, wins - 1)), list(range(wins, crossing))
+    order = [crossing, crossing, 0, wins - 1] + middle_one + middle_two
+    spread = Spread(slot, owners[:, row_block], order)
+    cut_one, cut_two = 4 + len(middle_one), len(order)
 
     heads, tails = [], []
     for r in range(rounds):
-        across = ([r] if r == 0 else []) + ([r + 1] if r + 1 < rounds else [])
-        edge_rounds = [r, r] + across
-        edge_rows = slice(0, len(edge_rounds))
-        rest_rounds = [r] * len(inside)
-        rest_rows = slice(4, 4 + len(inside))
+        across = ([r + 1] if r + 1 < rounds else []) + ([r] if r == 0 else [])
         if r == 0:
-            head = spread.middle(spread.begin(edge_rounds, edge_rows))
-            tail_one = spread.begin(rest_rounds, rest_rows)
-            tail_two = spread.middle(tail_one)
-            head_end = spread.last(head)
-            tail_end = spread.last(tail_two)
+            head = spread.begin(across + [r, r], slice(2 - len(across), 4))
+            tail = spread.begin([r] * (cut_two - 4), slice(4, cut_two))
         else:
-            head_one = spread.begin(edge_rounds, edge_rows, tail_one[2])
-            head_two = spread.middle(head_one, tail_two[2])
-            tail_one = spread.begin(rest_rounds, rest_rows, head_end[1])
-            tail_two = spread.middle(tail_one)
-            head_end = spread.last(head_two, tail_end[1], tail_one[2])
-            tail_end = spread.last(tail_two)
-        heads.append(head_end)
-        tails.append(tail_end)
+            head = spread.begin(across + [r] * wins, slice(2 - len(across), cut_one), head[2])
+            tail = spread.begin([r] * (cut_two - cut_one), slice(cut_one, cut_two), tail[2])
+        head, tail = spread.middle(head), spread.middle(tail)
+        heads.append(spread.last(head))
+        tails.append(spread.last(tail))
 
     matrix = slab
-    crosses, above_crosses = [], []
+    crosses, above_crosses = {}, {}
     for r in range(rounds):
         head, tail = heads[r], tails[r]
         edges = spread.join(*head)
-        crosses += [edges[k] for k in range(2, edges.shape[0])]
-        if edges.shape[0] > 2:
-            from_above = spread.join_above(head[0][2:, :, border:], head[1][2:, :, border:])
-            above_crosses += [from_above[k] for k in range(from_above.shape[0])]
+        across = ([r + 1] if r + 1 < rounds else []) + ([r] if r == 0 else [])
+        if across:
+            n = len(across)
+            from_above = spread.join_above(head[0][:n, :, border:], head[1][:n, :, border:])
+            for k, q in enumerate(across):
+                crosses[q], above_crosses[q] = edges[k], from_above[k]
+            edges = edges[n:]
         prev, cross = above_crosses[r], crosses[r]
         head_rows = apply(edges[0], matrix[:window])
         tail_rows = apply(edges[1], matrix[local_rows - window :])
         begin, end = head_rows[:border], tail_rows[border:]
         above, below = swap_rows(begin, end)
         rest = spread.join(*tail)
+        if r == 0:
+            ones, twos = rest[: wins - 2], rest[wins - 2 :]
+        else:
+            ones, twos = edges[2:], rest
         mid = apply_many(
-            rest[: wins - 2],
+            ones,
             matrix[window : local_rows - window].reshape(wins - 2, window, local_cols),
         ).reshape(local_rows - 2 * window, local_cols)
         centre = jnp.concatenate([head_rows[border:], mid, tail_rows[:border]], 0)
-        inner = apply_many(rest[wins - 2 :], centre.reshape(wins - 1, window, local_cols)).reshape(
+        inner = apply_many(twos, centre.reshape(wins - 1, window, local_cols)).reshape(
             local_rows - window, local_cols
         )
         low = apply(cross[:, :border], jnp.concatenate([end, below], 0))

time: 134 us -> 118 us (0.88)
  waiting for transfers between devices: 60.5 us -> 51.1 us
  starting transfers between devices: 30.8 us -> 26 us
  Pallas kernels: 6.01 us -> 4.3 us
    ppermute x23, waiting for transfers between devices: 47.2 us -> 36.8 us  [flip(): lax.ppermute(value, 'cols', [(d, d ^ 1 << bits[d & 1]) for d in range(cou...]
    ppermute x4, waiting for transfers between devices: 9.24 us -> 12.7 us  [swap(): return lax.ppermute(value, 'rows', pairs + [(b, a) for a, b in pairs])]
    ppermute x23, starting transfers between devices: 19.5 us -> 16.6 us  [flip(): lax.ppermute(value, 'cols', [(d, d ^ 1 << bits[d & 1]) for d in range(cou...]
    ppermute x1, waiting for transfers between devices: 4.02 us -> 1.62 us  [shifted(): lax.ppermute(value, axis, [(source, source + steps) for source in range(i...]
    ppermute x4, starting transfers between devices: 7.74 us -> 6.17 us  [swap(): return lax.ppermute(value, 'rows', pairs + [(b, a) for a, b in pairs])]
    unnamed x10 -> x8, local copies, waits for them, and re-layouts: 2.22 us -> 3.52 us
    select_n x10 -> x11, other arithmetic: 8.33 us -> 9.52 us  [choose(): return jnp.where(mask, yes, no)]
  transfers between devices with their start and end apart: 28 -> 28, of which waited for: 11 -> 12; matrix products, arithmetic and copies ran while one was open for 17% -> 17% of each run, Pallas kernels for 4% -> 3%
where the time goes in v5:
time: 118 us; the launch traced here: 117 us
  waiting for transfers between devices  51.1 us (43%)
  starting transfers between devices  26 us (22%)
  other arithmetic  13.2 us (11%)
  matrix products  11.8 us (10%)
  local copies, waits for them, and re-layouts  5.73 us (5%)
  Pallas kernels  4.3 us (4%)
  between operations  4.27 us (4%)
    ppermute x23, waiting for transfers between devices, flip(): lax.ppermute(value, 'cols', [(d, d ^ 1 << bits[d & 1]) for d in range(cou...  36.8 us
    ppermute x23, starting transfers between devices, flip(): lax.ppermute(value, 'cols', [(d, d ^ 1 << bits[d & 1]) for d in range(cou...  16.6 us
    ppermute x4, waiting for transfers between devices, swap(): return lax.ppermute(value, 'rows', pairs + [(b, a) for a, b in pairs])  12.7 us
    select_n x11, other arithmetic, choose(): return jnp.where(mask, yes, no)  9.52 us
    dot_general x4, matrix products, apply_many(): jnp.einsum('nab,nac->nbc', q, x, preferred_element_type=jnp.float32)  7.04 us
    ppermute x4, starting transfers between devices, swap(): return lax.ppermute(value, 'rows', pairs + [(b, a) for a, b in pairs])  6.17 us
    dot_general x8, matrix products, apply(): lax.dot_general(q, x, (((0,), (0,)), ((), ())), preferred_element_type=jn...  4.8 us
    unnamed x8, local copies, waits for them, and re-layouts  3.52 us
  transfers between devices with their start and end apart: 28, of which 12 were waited for; matrix products, arithmetic and copies ran while one was open for 17% of the time, Pallas kernels for 3%

profile of v5, /device:TPU:8, one launch (start us, length us, event | category | flops | bytes accessed | tf_op | source)
XLA Modules:
  0.0 116.5 jit_solution(9760641200908237248)
XLA Ops:
  0.0 2.2 %copy-done.2 = bf16[1,4096,512]{2,1,0:T(8,128)(2,1)S(1)} copy-done((bf16[1,4096,512]{2,1,0:T(8,128)(2,1)S(1)}, bf16[1,4096,512]{2,1,0:T(8,128)(2,1)}, u32[]{:S(2)}) %copy-start.2) | copy-done | bytes 4194328
  3.1 1.9 %cut_slot.2 = (bf16[9,128,512]{2,1,0:T(8,128)(2,1)S(1)}, bf16[9,128,512]{2,1,0:T(8,128)(2,1)}, bf16[9,128,512]{2,1,0:T(8,128)(2,1)S(1)}) custom-call(bf16[8,2,2,128,512]{4,3,2,1,0:T(8,128)(2,1)S(1)} %bitcast.54), custom_call_target="tpu_custom_call" | custom-call | bytes 6291456 | tf_op jit(solution)/shard_map/cut_slot/pallas_call | solution.py:105
  7.5 2.2 %slice_select_fusion.4 = (bf16[4,128,512]{2,1,0:T(8,128)(2,1)S(1)}, bf16[4,128,512]{2,1,0:T(8,128)(2,1)}) fusion(bf16[9,128,512]{2,1,0:T(8,128)(2,1)} %collective-permute-done.1, bf16[9,128,512]{2,1,0:T(8,128)(2,1)S(1)} %get-tuple-element.10, pred[]{:T(512)S(6)} %eq.24, pred[4]{0:T(512)(128)(4,1)S(1)} %broadcast_select_fusion.13), kind=kLoop, calls=%fused_computation.50 | loop fusion | flops 524288 | bytes 3145733 | tf_op jit(solution)/shard_map/jit(_where)/select_n | solution.py:178
  9.6 1.5 %collective-permute-start.2 = (bf16[4,128,512]{2,1,0:T(8,128)(2,1)}, bf16[4,128,512]{2,1,0:T(8,128)(2,1)}, u32[]{:S(2)}, u32[]{:S(2)}) collective-permute-start(bf16[4,128,512]{2,1,0:T(8,128)(2,1)} %get-tuple-element.12), channel_id=1, source_target_pairs={{0,2},{1,5},{2,0},{3,7},{4,6},{5,1},{6,4},{7,3},{8,10},{9,13},{10,... | collective-permute-start | bytes 1572872 | tf_op jit(solution)/shard_map/ppermute | solution.py:30
  15.5 3.7 %collective-permute-done.2 = bf16[4,128,512]{2,1,0:T(8,128)(2,1)} collective-permute-done((bf16[4,128,512]{2,1,0:T(8,128)(2,1)}, bf16[4,128,512]{2,1,0:T(8,128)(2,1)}, u32[]{:S(2)}, u32[]{:S(2)}) %collective-permute-start.2) | collective-permute-done | bytes 524320 | tf_op jit(solution)/shard_map/ppermute | solution.py:30
  20.5 1.6 %collective-permute-start.3 = (bf16[4,128,512]{2,1,0:T(8,128)(2,1)S(1)}, bf16[4,128,512]{2,1,0:T(8,128)(2,1)S(1)}, u32[]{:S(2)}, u32[]{:S(2)}) collective-permute-start(bf16[4,128,512]{2,1,0:T(8,128)(2,1)S(1)} %fusion.21), channel_id=1, source_target_pairs={{0,4},{1,3},{2,6},{3,1},{4,0},{5,7},{6,2},{7,5},{8,12},{9,11},{10,... | collective-permute-start | bytes 1572872 | tf_op jit(solution)/shard_map/ppermute | solution.py:30
  22.1 7.7 %collective-permute-done.16 = bf16[5,128,512]{2,1,0:T(8,128)(2,1)} collective-permute-done((bf16[5,128,512]{2,1,0:T(8,128)(2,1)S(1)}, bf16[5,128,512]{2,1,0:T(8,128)(2,1)}, u32[]{:S(2)}, u32[]{:S(2)}) %collective-permute-start.16) | collective-permute-done | bytes 655392 | tf_op jit(solution)/shard_map/ppermute | solution.py:30
  31.2 1.6 %collective-permute-start.17 = (bf16[5,128,512]{2,1,0:T(8,128)(2,1)S(1)}, bf16[5,128,512]{2,1,0:T(8,128)(2,1)S(1)}, u32[]{:S(2)}, u32[]{:S(2)}) collective-permute-start(bf16[5,128,512]{2,1,0:T(8,128)(2,1)S(1)} %fusion.20), channel_id=1, source_target_pairs={{0,4},{1,3},{2,6},{3,1},{4,0},{5,7},{6,2},{7,5},{8,12},{9,11},{10,... | collective-permute-start | bytes 1966088 | tf_op jit(solution)/shard_map/ppermute | solution.py:30
  36.3 12.6 %collective-permute-done.17.refs_0_ = bf16[5,128,512]{2,1,0:T(8,128)(2,1)S(1)} collective-permute-done((bf16[5,128,512]{2,1,0:T(8,128)(2,1)S(1)}, bf16[5,128,512]{2,1,0:T(8,128)(2,1)S(1)}, u32[]{:S(2)}, u32[]{:S(2)}) %collective-permute-start.17) | collective-permute-done | bytes 655392 | tf_op jit(solution)/shard_map/ppermute | solution.py:30
  52.4 1.6 %collective-permute-start.5 = (bf16[4,128,512]{2,1,0:T(8,128)(2,1)S(1)}, bf16[4,128,512]{2,1,0:T(8,128)(2,1)S(1)}, u32[]{:S(2)}, u32[]{:S(2)}) collective-permute-start(bf16[4,128,512]{2,1,0:T(8,128)(2,1)S(1)} %fusion.22), channel_id=1, source_target_pairs={{0,4},{1,3},{2,6},{3,1},{4,0},{5,7},{6,2},{7,5},{8,12},{9,11},{10,... | collective-permute-start | bytes 1572872 | tf_op jit(solution)/shard_map/ppermute | solution.py:30
  54.0 3.2 %collective-permute-start.12 = (bf16[2,2,128,256]{3,2,1,0:T(8,128)(2,1)S(1)}, bf16[2,2,128,256]{3,2,1,0:T(8,128)(2,1)S(1)}, u32[]{:S(2)}, u32[]{:S(2)}) collective-permute-start(bf16[2,2,128,256]{3,2,1,0:T(8,128)(2,1)S(1)} %pad_maximum_fusion.7), channel_id=1, source_target_pairs={{0,8},{8,16},{16,24},{1,9},{9,17},{17,25},{2,10},{10,18},{18,26},{... | collective-permute-start | bytes 786440 | tf_op jit(solution)/shard_map/ppermute | solution.py:12
  57.3 2.5 %collective-permute-done.23 = bf16[3,128,512]{2,1,0:T(8,128)(2,1)S(1)} collective-permute-done((bf16[3,128,512]{2,1,0:T(8,128)(2,1)S(1)}, bf16[3,128,512]{2,1,0:T(8,128)(2,1)S(1)}, u32[]{:S(2)}, u32[]{:S(2)}) %collective-permute-start.23) | collective-permute-done | bytes 393248 | tf_op jit(solution)/shard_map/ppermute | solution.py:30
  60.8 1.6 %collective-permute-done.12 = bf16[2,2,128,256]{3,2,1,0:T(8,128)(2,1)S(1)} collective-permute-done((bf16[2,2,128,256]{3,2,1,0:T(8,128)(2,1)S(1)}, bf16[2,2,128,256]{3,2,1,0:T(8,128)(2,1)S(1)}, u32[]{:S(2)}, u32[]{:S(2)}) %collective-permute-start.12) | collective-permute-done | bytes 262176 | tf_op jit(solution)/shard_map/ppermute | solution.py:12
  62.5 4.8 %collective-permute-done.5 = bf16[4,128,512]{2,1,0:T(8,128)(2,1)S(1)} collective-permute-done((bf16[4,128,512]{2,1,0:T(8,128)(2,1)S(1)}, bf16[4,128,512]{2,1,0:T(8,128)(2,1)S(1)}, u32[]{:S(2)}, u32[]{:S(2)}) %collective-permute-start.5) | collective-permute-done | bytes 524320 | tf_op jit(solution)/shard_map/ppermute | solution.py:30
  67.3 1.5 %collective-permute-start.24 = (bf16[3,128,512]{2,1,0:T(8,128)(2,1)S(1)}, bf16[3,128,512]{2,1,0:T(8,128)(2,1)S(1)}, u32[]{:S(2)}, u32[]{:S(2)}) collective-permute-start(bf16[3,128,512]{2,1,0:T(8,128)(2,1)S(1)} %fusion.23), channel_id=1, source_target_pairs={{0,4},{1,3},{2,6},{3,1},{4,0},{5,7},{6,2},{7,5},{8,12},{9,11},{10,... | collective-permute-start | bytes 1179656 | tf_op jit(solution)/shard_map/ppermute | solution.py:30
  71.8 4.5 %collective-permute-done.24 = bf16[3,128,512]{2,1,0:T(8,128)(2,1)S(1)} collective-permute-done((bf16[3,128,512]{2,1,0:T(8,128)(2,1)S(1)}, bf16[3,128,512]{2,1,0:T(8,128)(2,1)S(1)}, u32[]{:S(2)}, u32[]{:S(2)}) %collective-permute-start.24) | collective-permute-done | bytes 393248 | tf_op jit(solution)/shard_map/ppermute | solution.py:30
  80.0 3.2 %collective-permute-start.14 = (bf16[256,1024]{1,0:T(8,128)(2,1)S(1)}, bf16[256,1024]{1,0:T(8,128)(2,1)S(1)}, u32[]{:S(2)}, u32[]{:S(2)}) collective-permute-start(bf16[256,1024]{1,0:T(8,128)(2,1)S(1)} %get-tuple-element.17), channel_id=1, source_target_pairs={{8,16},{16,8},{9,17},{17,9},{10,18},{18,10},{11,19},{19,11},{12,20... | collective-permute-start | bytes 1572872 | tf_op jit(solution)/shard_map/ppermute | solution.py:21
  84.8 1.5 %convolution_convert_fusion.2 = bf16[2,512,1024]{2,1,0:T(8,128)(2,1)S(1)} fusion(bf16[5,512,512]{2,1,0:T(8,128)(2,1)S(1)} %place.8, bf16[2,512,1024]{2,1,0:T(8,128)(2,1)S(1)} %bitcast.63), kind=kOutput, calls=%fused_computation.5 | convolution fusion | flops 1074790400 | bytes 6815744 | tf_op jit(solution)/shard_map/nab,nac->nbc/dot_general | solution.py:226
  86.7 2.1 %convolution_convert_fusion = bf16[3,512,1024]{2,1,0:T(8,128)(2,1)S(1)} fusion(bf16[5,512,512]{2,1,0:T(8,128)(2,1)S(1)} %place.8, bf16[3,512,1024]{2,1,0:T(8,128)(2,1)S(1)} %bitcast.58), kind=kOutput, calls=%fused_computation.3 | convolution fusion | flops 1612185600 | bytes 8912896 | tf_op jit(solution)/shard_map/nab,nac->nbc/dot_general | solution.py:226
  95.7 1.5 %convolution_convert_fusion.3 = bf16[2,512,1024]{2,1,0:T(8,128)(2,1)S(1)} fusion(bf16[4,512,512]{2,1,0:T(8,128)(2,1)S(1)} %place.5, bf16[2,512,1024]{2,1,0:T(8,128)(2,1)S(1)} %bitcast.64), kind=kOutput, calls=%fused_computation.6 | convolution fusion | flops 1074790400 | bytes 6291456 | tf_op jit(solution)/shard_map/nab,nac->nbc/dot_general | solution.py:226
  97.5 2.9 %collective-permute-start.21 = (bf16[256,1024]{1,0:T(8,128)(2,1)S(1)}, bf16[256,1024]{1,0:T(8,128)(2,1)S(1)}, u32[]{:S(2)}, u32[]{:S(2)}) collective-permute-start(bf16[256,1024]{1,0:T(8,128)(2,1)S(1)} %get-tuple-element.15), channel_id=1, source_target_pairs={{8,16},{16,8},{9,17},{17,9},{10,18},{18,10},{11,19},{19,11},{12,20... | collective-permute-start | bytes 1572872 | tf_op jit(solution)/shard_map/ppermute | solution.py:21
  100.8 1.9 %convolution_convert_fusion.1 = bf16[3,512,1024]{2,1,0:T(8,128)(2,1)S(1)} fusion(bf16[3,512,512]{2,1,0:T(8,128)(2,1)S(1)} %place.9, bf16[3,512,1024]{2,1,0:T(8,128)(2,1)S(1)} %bitcast.59), kind=kOutput, calls=%fused_computation.4 | convolution fusion | flops 1612185600 | bytes 7864320 | tf_op jit(solution)/shard_map/nab,nac->nbc/dot_general | solution.py:226
  102.7 9.6 %collective-permute-done.21 = bf16[256,1024]{1,0:T(8,128)(2,1)S(1)} collective-permute-done((bf16[256,1024]{1,0:T(8,128)(2,1)S(1)}, bf16[256,1024]{1,0:T(8,128)(2,1)S(1)}, u32[]{:S(2)}, u32[]{:S(2)}) %collective-permute-start.21) | collective-permute-done | bytes 524320 | tf_op jit(solution)/shard_map/ppermute | solution.py:21
  114.2 2.3 %pad_maximum_fusion = bf16[2048,1024]{1,0:T(8,128)(2,1)} fusion(bf16[256,1024]{1,0:T(8,128)(2,1)S(1)} %fusion.3, bf16[1536,1024]{1,0:T(8,128)(2,1)S(1)} %bitcast.60, bf16[256,1024]{1,0:T(8,128)(2,1)S(1)} %fusion.2), kind=kLoop, calls=%fused_computation | loop fusion | flops 12582912 | bytes 8388608 | tf_op jit(solution)/shard_map/concatenate | solution.py:292
  (93 shorter events, 32.5 us)
Async XLA Ops:
  5.0 10.4 %collective-permute-start = (bf16[9,128,512]{2,1,0:T(8,128)(2,1)}, bf16[9,128,512]{2,1,0:T(8,128)(2,1)}, u32[]{:S(2)}, u32[]{:S(2)}) collective-permute-start(bf16[9,128,512]{2,1,0:T(8,128)(2,1)} %get-tuple-element.9), channel_id=1, source_target_pairs={{0,1},{1,0},{2,3},{3,2},{4,5},{5,4},{6,7},{7,6},{8,9},{9,8},{10,11... | collective-permute-start | bytes 3538952 | tf_op jit(solution)/shard_map/ppermute | solution.py:30
  9.6 9.5 %collective-permute-start.2 = (bf16[4,128,512]{2,1,0:T(8,128)(2,1)}, bf16[4,128,512]{2,1,0:T(8,128)(2,1)}, u32[]{:S(2)}, u32[]{:S(2)}) collective-permute-start(bf16[4,128,512]{2,1,0:T(8,128)(2,1)} %get-tuple-element.12), channel_id=1, source_target_pairs={{0,2},{1,5},{2,0},{3,7},{4,6},{5,1},{6,4},{7,3},{8,10},{9,13},{10,... | collective-permute-start | bytes 1572872 | tf_op jit(solution)/shard_map/ppermute | solution.py:30
  12.3 17.5 %collective-permute-start.16 = (bf16[5,128,512]{2,1,0:T(8,128)(2,1)S(1)}, bf16[5,128,512]{2,1,0:T(8,128)(2,1)}, u32[]{:S(2)}, u32[]{:S(2)}) collective-permute-start(bf16[5,128,512]{2,1,0:T(8,128)(2,1)S(1)} %slice_select_fusion), channel_id=1, source_target_pairs={{0,2},{1,5},{2,0},{3,7},{4,6},{5,1},{6,4},{7,3},{8,10},{9,13},{10,... | collective-permute-start | bytes 1966088 | tf_op jit(solution)/shard_map/ppermute | solution.py:30
  20.5 13.3 %collective-permute-start.3 = (bf16[4,128,512]{2,1,0:T(8,128)(2,1)S(1)}, bf16[4,128,512]{2,1,0:T(8,128)(2,1)S(1)}, u32[]{:S(2)}, u32[]{:S(2)}) collective-permute-start(bf16[4,128,512]{2,1,0:T(8,128)(2,1)S(1)} %fusion.21), channel_id=1, source_target_pairs={{0,4},{1,3},{2,6},{3,1},{4,0},{5,7},{6,2},{7,5},{8,12},{9,11},{10,... | collective-permute-start | bytes 1572872 | tf_op jit(solution)/shard_map/ppermute | solution.py:30
  31.2 17.6 %collective-permute-start.17 = (bf16[5,128,512]{2,1,0:T(8,128)(2,1)S(1)}, bf16[5,128,512]{2,1,0:T(8,128)(2,1)S(1)}, u32[]{:S(2)}, u32[]{:S(2)}) collective-permute-start(bf16[5,128,512]{2,1,0:T(8,128)(2,1)S(1)} %fusion.20), channel_id=1, source_target_pairs={{0,4},{1,3},{2,6},{3,1},{4,0},{5,7},{6,2},{7,5},{8,12},{9,11},{10,... | collective-permute-start | bytes 1966088 | tf_op jit(solution)/shard_map/ppermute | solution.py:30
  33.9 17.4 %collective-permute-start.4 = (bf16[4,128,512]{2,1,0:T(8,128)(2,1)S(1)}, bf16[4,128,512]{2,1,0:T(8,128)(2,1)S(1)}, u32[]{:S(2)}, u32[]{:S(2)}) collective-permute-start(bf16[4,128,512]{2,1,0:T(8,128)(2,1)S(1)} %after.2), channel_id=1, source_target_pairs={{0,2},{1,5},{2,0},{3,7},{4,6},{5,1},{6,4},{7,3},{8,10},{9,13},{10,... | collective-permute-start | bytes 1572872 | tf_op jit(solution)/shard_map/ppermute | solution.py:30
  35.4 33.5 %collective-permute-start.10 = (bf16[4,128,512]{2,1,0:T(8,128)(2,1)S(1)}, bf16[4,128,512]{2,1,0:T(8,128)(2,1)S(1)}, u32[]{:S(2)}, u32[]{:S(2)}) collective-permute-start(bf16[4,128,512]{2,1,0:T(8,128)(2,1)S(1)} %broadcast_select_fusion.1.refs_0_), channel_id=1, source_target_pairs={{0,1},{1,0},{2,3},{3,2},{4,5},{5,4},{6,7},{7,6},{8,9},{9,8},{10,11... | collective-permute-start | bytes 1572872 | tf_op jit(solution)/shard_map/ppermute | solution.py:30
  35.4 18.5 %collective-permute-start.9 = (bf16[4,128,512]{2,1,0:T(8,128)(2,1)S(1)}, bf16[4,128,512]{2,1,0:T(8,128)(2,1)S(1)}, u32[]{:S(2)}, u32[]{:S(2)}) collective-permute-start(bf16[4,128,512]{2,1,0:T(8,128)(2,1)S(1)} %broadcast_select_fusion.1.refs_0_), channel_id=1, source_target_pairs={{0,2},{1,5},{2,0},{3,7},{4,6},{5,1},{6,4},{7,3},{8,10},{9,13},{10,... | collective-permute-start | bytes 1572872 | tf_op jit(solution)/shard_map/ppermute | solution.py:30
  49.0 10.8 %collective-permute-start.23 = (bf16[3,128,512]{2,1,0:T(8,128)(2,1)S(1)}, bf16[3,128,512]{2,1,0:T(8,128)(2,1)S(1)}, u32[]{:S(2)}, u32[]{:S(2)}) collective-permute-start(bf16[3,128,512]{2,1,0:T(8,128)(2,1)S(1)} %after.3), channel_id=1, source_target_pairs={{0,2},{1,5},{2,0},{3,7},{4,6},{5,1},{6,4},{7,3},{8,10},{9,13},{10,... | collective-permute-start | bytes 1179656 | tf_op jit(solution)/shard_map/ppermute | solution.py:30
  50.4 18.6 %collective-permute-start.18 = (bf16[5,128,512]{2,1,0:T(8,128)(2,1)S(1)}, bf16[5,128,512]{2,1,0:T(8,128)(2,1)S(1)}, u32[]{:S(2)}, u32[]{:S(2)}) collective-permute-start(bf16[5,128,512]{2,1,0:T(8,128)(2,1)S(1)} %broadcast_select_fusion.refs_0_), channel_id=1, source_target_pairs={{0,2},{1,5},{2,0},{3,7},{4,6},{5,1},{6,4},{7,3},{8,10},{9,13},{10,... | collective-permute-start | bytes 1966088 | tf_op jit(solution)/shard_map/ppermute | solution.py:30
  52.4 14.9 %collective-permute-start.5 = (bf16[4,128,512]{2,1,0:T(8,128)(2,1)S(1)}, bf16[4,128,512]{2,1,0:T(8,128)(2,1)S(1)}, u32[]{:S(2)}, u32[]{:S(2)}) collective-permute-start(bf16[4,128,512]{2,1,0:T(8,128)(2,1)S(1)} %fusion.22), channel_id=1, source_target_pairs={{0,4},{1,3},{2,6},{3,1},{4,0},{5,7},{6,2},{7,5},{8,12},{9,11},{10,... | collective-permute-start | bytes 1572872 | tf_op jit(solution)/shard_map/ppermute | solution.py:30
  54.0 8.4 %collective-permute-start.12 = (bf16[2,2,128,256]{3,2,1,0:T(8,128)(2,1)S(1)}, bf16[2,2,128,256]{3,2,1,0:T(8,128)(2,1)S(1)}, u32[]{:S(2)}, u32[]{:S(2)}) collective-permute-start(bf16[2,2,128,256]{3,2,1,0:T(8,128)(2,1)S(1)} %pad_maximum_fusion.7), channel_id=1, source_target_pairs={{0,8},{8,16},{16,24},{1,9},{9,17},{17,25},{2,10},{10,18},{18,26},{... | collective-permute-start | bytes 786440 | tf_op jit(solution)/shard_map/ppermute | solution.py:12
  59.8 9.7 %collective-permute-start.11 = (bf16[4,128,512]{2,1,0:T(8,128)(2,1)S(1)}, bf16[4,128,512]{2,1,0:T(8,128)(2,1)S(1)}, u32[]{:S(2)}, u32[]{:S(2)}) collective-permute-start(bf16[4,128,512]{2,1,0:T(8,128)(2,1)S(1)} %collective-permute-done.9.refs_1_), channel_id=1, source_target_pairs={{0,1},{1,0},{2,3},{3,2},{4,5},{5,4},{6,7},{7,6},{8,9},{9,8},{10,11... | collective-permute-start | bytes 1572872 | tf_op jit(solution)/shard_map/ppermute | solution.py:30
  62.4 17.5 %collective-permute-start.19 = (bf16[5,128,512]{2,1,0:T(8,128)(2,1)S(1)}, bf16[5,128,512]{2,1,0:T(8,128)(2,1)S(1)}, u32[]{:S(2)}, u32[]{:S(2)}) collective-permute-start(bf16[5,128,512]{2,1,0:T(8,128)(2,1)S(1)} %broadcast_select_fusion.refs_0_), channel_id=1, source_target_pairs={{0,1},{1,0},{2,3},{3,2},{4,5},{5,4},{6,7},{7,6},{8,9},{9,8},{10,11... | collective-permute-start | bytes 1966088 | tf_op jit(solution)/shard_map/ppermute | solution.py:30
  67.3 9.1 %collective-permute-start.24 = (bf16[3,128,512]{2,1,0:T(8,128)(2,1)S(1)}, bf16[3,128,512]{2,1,0:T(8,128)(2,1)S(1)}, u32[]{:S(2)}, u32[]{:S(2)}) collective-permute-start(bf16[3,128,512]{2,1,0:T(8,128)(2,1)S(1)} %fusion.23), channel_id=1, source_target_pairs={{0,4},{1,3},{2,6},{3,1},{4,0},{5,7},{6,2},{7,5},{8,12},{9,11},{10,... | collective-permute-start | bytes 1179656 | tf_op jit(solution)/shard_map/ppermute | solution.py:30
  68.9 8.6 %collective-permute-start.13 = (bf16[2,2,128,256]{3,2,1,0:T(8,128)(2,1)S(1)}, bf16[2,2,128,256]{3,2,1,0:T(8,128)(2,1)S(1)}, u32[]{:S(2)}, u32[]{:S(2)}) collective-permute-start(bf16[2,2,128,256]{3,2,1,0:T(8,128)(2,1)S(1)} %collective-permute-done.12), channel_id=1, source_target_pairs={{0,1},{1,0},{2,3},{3,2},{4,5},{5,4},{6,7},{7,6},{8,9},{9,8},{10,11... | collective-permute-start | bytes 786440 | tf_op jit(solution)/shard_map/ppermute | solution.py:30
  69.0 14.2 %collective-permute-start.20 = (bf16[5,128,512]{2,1,0:T(8,128)(2,1)S(1)}, bf16[5,128,512]{2,1,0:T(8,128)(2,1)S(1)}, u32[]{:S(2)}, u32[]{:S(2)}) collective-permute-start(bf16[5,128,512]{2,1,0:T(8,128)(2,1)S(1)} %collective-permute-done.18.refs_1_), channel_id=1, source_target_pairs={{0,1},{1,0},{2,3},{3,2},{4,5},{5,4},{6,7},{7,6},{8,9},{9,8},{10,11... | collective-permute-start | bytes 1966088 | tf_op jit(solution)/shard_map/ppermute | solution.py:30
  69.5 24.5 %collective-permute-start.7 = (bf16[4,128,512]{2,1,0:T(8,128)(2,1)S(1)}, bf16[4,128,512]{2,1,0:T(8,128)(2,1)S(1)}, u32[]{:S(2)}, u32[]{:S(2)}) collective-permute-start(bf16[4,128,512]{2,1,0:T(8,128)(2,1)S(1)} %broadcast_select_fusion.10.refs_0_), channel_id=1, source_target_pairs={{0,1},{1,0},{2,3},{3,2},{4,5},{5,4},{6,7},{7,6},{8,9},{9,8},{10,11... | collective-permute-start | bytes 1572872 | tf_op jit(solution)/shard_map/ppermute | solution.py:30
  76.4 13.4 %collective-permute-start.6 = (bf16[4,128,512]{2,1,0:T(8,128)(2,1)S(1)}, bf16[4,128,512]{2,1,0:T(8,128)(2,1)S(1)}, u32[]{:S(2)}, u32[]{:S(2)}) collective-permute-start(bf16[4,128,512]{2,1,0:T(8,128)(2,1)S(1)} %broadcast_select_fusion.10.refs_0_), channel_id=1, source_target_pairs={{0,2},{1,5},{2,0},{3,7},{4,6},{5,1},{6,4},{7,3},{8,10},{9,13},{10,... | collective-permute-start | bytes 1572872 | tf_op jit(solution)/shard_map/ppermute | solution.py:30
  77.5 12.3 %collective-permute-start.25 = (bf16[3,128,512]{2,1,0:T(8,128)(2,1)S(1)}, bf16[3,128,512]{2,1,0:T(8,128)(2,1)S(1)}, u32[]{:S(2)}, u32[]{:S(2)}) collective-permute-start(bf16[3,128,512]{2,1,0:T(8,128)(2,1)S(1)} %broadcast_select_fusion.11.refs_0_), channel_id=1, source_target_pairs={{0,2},{1,5},{2,0},{3,7},{4,6},{5,1},{6,4},{7,3},{8,10},{9,13},{10,... | collective-permute-start | bytes 1179656 | tf_op jit(solution)/shard_map/ppermute | solution.py:30
  80.0 11.1 %collective-permute-start.14 = (bf16[256,1024]{1,0:T(8,128)(2,1)S(1)}, bf16[256,1024]{1,0:T(8,128)(2,1)S(1)}, u32[]{:S(2)}, u32[]{:S(2)}) collective-permute-start(bf16[256,1024]{1,0:T(8,128)(2,1)S(1)} %get-tuple-element.17), channel_id=1, source_target_pairs={{8,16},{16,8},{9,17},{17,9},{10,18},{18,10},{11,19},{19,11},{12,20... | collective-permute-start | bytes 1572872 | tf_op jit(solution)/shard_map/ppermute | solution.py:21
  83.2 9.2 %collective-permute-start.15 = (bf16[256,1024]{1,0:T(8,128)(2,1)S(1)}, bf16[256,1024]{1,0:T(8,128)(2,1)S(1)}, u32[]{:S(2)}, u32[]{:S(2)}) collective-permute-start(bf16[256,1024]{1,0:T(8,128)(2,1)S(1)} %get-tuple-element.18), channel_id=1, source_target_pairs={{0,8},{16,24},{8,0},{24,16},{1,9},{17,25},{9,1},{25,17},{2,10},{18... | collective-permute-start | bytes 1572872 | tf_op jit(solution)/shard_map/ppermute | solution.py:21
  97.5 14.9 %collective-permute-start.21 = (bf16[256,1024]{1,0:T(8,128)(2,1)S(1)}, bf16[256,1024]{1,0:T(8,128)(2,1)S(1)}, u32[]{:S(2)}, u32[]{:S(2)}) collective-permute-start(bf16[256,1024]{1,0:T(8,128)(2,1)S(1)} %get-tuple-element.15), channel_id=1, source_target_pairs={{8,16},{16,8},{9,17},{17,9},{10,18},{18,10},{11,19},{19,11},{12,20... | collective-permute-start | bytes 1572872 | tf_op jit(solution)/shard_map/ppermute | solution.py:21
  100.3 12.9 %collective-permute-start.22 = (bf16[256,1024]{1,0:T(8,128)(2,1)S(1)}, bf16[256,1024]{1,0:T(8,128)(2,1)S(1)}, u32[]{:S(2)}, u32[]{:S(2)}) collective-permute-start(bf16[256,1024]{1,0:T(8,128)(2,1)S(1)} %get-tuple-element.16), channel_id=1, source_target_pairs={{0,8},{16,24},{8,0},{24,16},{1,9},{17,25},{9,1},{25,17},{2,10},{18... | collective-permute-start | bytes 1572872 | tf_op jit(solution)/shard_map/ppermute | solution.py:21
  (9 other events, 29.0 us)

commit v6 on v5

--- a/solution.py
+++ b/solution.py
@@ -22,7 +22,7 @@
 
     first = swap(jnp.where(even, down, up), 0)
     second = swap(jnp.where(even, up, down), 1)
-    return jnp.where(even, second, first), jnp.where(even, first, second)
+    return (jnp.where(even, second, first), jnp.where(even, first, second)), (first, second)
 
 
 def flip(value, bits):
@@ -49,13 +49,15 @@
 ANY = pl.BlockSpec(memory_space=pl.ANY)
 
 
-def after(value, *done):
+def after(value, *done, rows=None):
+    start, count = (0, value.shape[0]) if rows is None else (rows.start, rows.stop - rows.start)
+
     def kernel(source, *refs):
-        copy_all([pltpu.make_async_copy(source, refs[-2], refs[-1])])
+        copy_all([pltpu.make_async_copy(source.at[pl.ds(start, count)], refs[-2], refs[-1])])
 
     return pl.pallas_call(
         kernel,
-        out_shape=jax.ShapeDtypeStruct(value.shape, value.dtype),
+        out_shape=jax.ShapeDtypeStruct((count,) + value.shape[1:], value.dtype),
         in_specs=[ANY] * (1 + len(done)),
         out_specs=ANY,
         scratch_shapes=[pltpu.SemaphoreType.DMA],
@@ -178,13 +180,13 @@
         return jnp.where(mask, yes, no)
 
     def begin(self, rounds, rows, *first):
-        out, hold = [
-            self.choose(rounds, lambda owner: (owner & 1) == self.core, own[rows], theirs[rows])
-            for own, theirs in zip(self.own, self.theirs)
-        ]
-        if first:
-            out = after(out, *first)
-        return rounds, hold, flip(out, self.cut)
+        parts = []
+        for own, theirs in zip(self.own, self.theirs):
+            theirs = after(theirs, *first, rows=rows) if first else theirs[rows]
+            parts.append(
+                self.choose(rounds, lambda owner: (owner & 1) == self.core, own[rows], theirs)
+            )
+        return rounds, parts[1], flip(parts[0], self.cut)
 
     def keep(self, state, bits):
         rounds, hold, got = state
@@ -242,28 +244,25 @@
     spread = Spread(slot, owners[:, row_block], order)
     cut_one, cut_two = 4 + len(middle_one), len(order)
 
-    heads, tails = [], []
-    for r in range(rounds):
-        across = ([r + 1] if r + 1 < rounds else []) + ([r] if r == 0 else [])
-        if r == 0:
-            head = spread.begin(across + [r, r], slice(2 - len(across), 4))
-            tail = spread.begin([r] * (cut_two - 4), slice(4, cut_two))
-        else:
-            head = spread.begin(across + [r] * wins, slice(2 - len(across), cut_one), head[2])
-            tail = spread.begin([r] * (cut_two - cut_one), slice(cut_one, cut_two), tail[2])
-        head, tail = spread.middle(head), spread.middle(tail)
-        heads.append(spread.last(head))
-        tails.append(spread.last(tail))
-
     matrix = slab
     crosses, above_crosses = {}, {}
     for r in range(rounds):
-        head, tail = heads[r], tails[r]
-        edges = spread.join(*head)
         across = ([r + 1] if r + 1 < rounds else []) + ([r] if r == 0 else [])
-        if across:
-            n = len(across)
-            from_above = spread.join_above(head[0][:n, :, border:], head[1][:n, :, border:])
+        n = len(across)
+        if r == 0:
+            head = spread.middle(spread.begin(across + [r, r], slice(2 - n, 4)))
+            tail = spread.middle(spread.begin([r] * (cut_two - 4), slice(4, cut_two)))
+            head_pair, tail_pair = spread.last(head), spread.last(tail)
+        else:
+            head = spread.begin(across + [r] * wins, slice(2 - n, cut_one), head[2])
+            tail = spread.begin([r] * (cut_two - cut_one), slice(cut_one, cut_two), tail[2])
+            head, tail = spread.middle(head, head_rows, tail_rows), spread.middle(tail)
+            head_pair, tail_pair = spread.last(head), spread.last(tail, *swapped)
+        edges = spread.join(*head_pair)
+        if n:
+            from_above = spread.join_above(
+                head_pair[0][:n, :, border:], head_pair[1][:n, :, border:]
+            )
             for k, q in enumerate(across):
                 crosses[q], above_crosses[q] = edges[k], from_above[k]
             edges = edges[n:]
@@ -271,8 +270,8 @@
         head_rows = apply(edges[0], matrix[:window])
         tail_rows = apply(edges[1], matrix[local_rows - window :])
         begin, end = head_rows[:border], tail_rows[border:]
-        above, below = swap_rows(begin, end)
-        rest = spread.join(*tail)
+        (above, below), swapped = swap_rows(begin, end)
+        rest = spread.join(*tail_pair)
         if r == 0:
             ones, twos = rest[: wins - 2], rest[wins - 2 :]
         else:

time: 118 us -> 134 us (1.14)
  waiting for transfers between devices: 51.1 us -> 66.3 us
  starting transfers between devices: 26 us -> 30.2 us
  other arithmetic: 13.2 us -> 9.45 us
    ppermute x4, waiting for transfers between devices: 12.7 us -> 18.6 us  [swap(): return lax.ppermute(value, 'rows', pairs + [(b, a) for a, b in pairs])]
    ppermute x1, waiting for transfers between devices: 1.62 us -> 7.08 us  [shifted(): lax.ppermute(value, axis, [(source, source + steps) for source in range(i...]
    ppermute x23, waiting for transfers between devices: 36.8 us -> 40.7 us  [flip(): lax.ppermute(value, 'cols', [(d, d ^ 1 << bits[d & 1]) for d in range(cou...]
    select_n x11 -> x12, other arithmetic: 9.52 us -> 5.78 us  [choose(): return jnp.where(mask, yes, no)]
    ppermute x23, starting transfers between devices: 16.6 us -> 19.5 us  [flip(): lax.ppermute(value, 'cols', [(d, d ^ 1 << bits[d & 1]) for d in range(cou...]
    unnamed x8 -> x16, local copies, waits for them, and re-layouts: 3.52 us -> 4.64 us
  transfers between devices with their start and end apart: 28 -> 28, of which waited for: 12 -> 15; matrix products, arithmetic and copies ran while one was open for 17% -> 12% of each run, Pallas kernels for 3% -> 3%
where the time goes in v6:
time: 134 us; the launch traced here: 133 us
  waiting for transfers between devices  66.3 us (49%)
  starting transfers between devices  30.2 us (23%)
  matrix products  11.7 us (9%)
  other arithmetic  9.45 us (7%)
  local copies, waits for them, and re-layouts  5.7 us (4%)
  Pallas kernels  5.04 us (4%)
  between operations  4.29 us (3%)
    ppermute x23, waiting for transfers between devices, flip(): lax.ppermute(value, 'cols', [(d, d ^ 1 << bits[d & 1]) for d in range(cou...  40.7 us
    ppermute x23, starting transfers between devices, flip(): lax.ppermute(value, 'cols', [(d, d ^ 1 << bits[d & 1]) for d in range(cou...  19.5 us
    ppermute x4, waiting for transfers between devices, swap(): return lax.ppermute(value, 'rows', pairs + [(b, a) for a, b in pairs])  18.6 us
    ppermute x4, starting transfers between devices, swap(): return lax.ppermute(value, 'rows', pairs + [(b, a) for a, b in pairs])  7.21 us
    ppermute x1, waiting for transfers between devices, shifted(): lax.ppermute(value, axis, [(source, source + steps) for source in range(i...  7.08 us
    dot_general x4, matrix products, apply_many(): jnp.einsum('nab,nac->nbc', q, x, preferred_element_type=jnp.float32)  6.92 us
    select_n x12, other arithmetic, choose(): return jnp.where(mask, yes, no)  5.78 us
    dot_general x8, matrix products, apply(): lax.dot_general(q, x, (((0,), (0,)), ((), ())), preferred_element_type=jn...  4.76 us
  transfers between devices with their start and end apart: 28, of which 15 were waited for; matrix products, arithmetic and copies ran while one was open for 12% of the time, Pallas kernels for 3%

profile of v6, /device:TPU:8, one launch (start us, length us, event | category | flops | bytes accessed | tf_op | source)
XLA Modules:
  0.0 132.6 jit_solution(9623159599348363745)
XLA Ops:
  0.0 2.2 %copy-done.2 = bf16[1,4096,512]{2,1,0:T(8,128)(2,1)S(1)} copy-done((bf16[1,4096,512]{2,1,0:T(8,128)(2,1)S(1)}, bf16[1,4096,512]{2,1,0:T(8,128)(2,1)}, u32[]{:S(2)}) %copy-start.2) | copy-done | bytes 4194328
  3.3 2.0 %cut_slot.2 = (bf16[9,128,512]{2,1,0:T(8,128)(2,1)S(1)}, bf16[9,128,512]{2,1,0:T(8,128)(2,1)}, bf16[9,128,512]{2,1,0:T(8,128)(2,1)S(1)}) custom-call(bf16[8,2,2,128,512]{4,3,2,1,0:T(8,128)(2,1)S(1)} %bitcast.54), custom_call_target="tpu_custom_call" | custom-call | bytes 6291456 | tf_op jit(solution)/shard_map/cut_slot/pallas_call | solution.py:107
  13.9 5.3 %collective-permute-done.2 = bf16[4,128,512]{2,1,0:T(8,128)(2,1)} collective-permute-done((bf16[4,128,512]{2,1,0:T(8,128)(2,1)}, bf16[4,128,512]{2,1,0:T(8,128)(2,1)}, u32[]{:S(2)}, u32[]{:S(2)}) %collective-permute-start.2) | collective-permute-done | bytes 524320 | tf_op jit(solution)/shard_map/ppermute | solution.py:30
  19.2 2.2 %fusion.21 = bf16[4,128,512]{2,1,0:T(8,128)(2,1)} fusion(bf16[4,128,512]{2,1,0:T(8,128)(2,1)} %collective-permute-done.2, bf16[9,128,512]{2,1,0:T(8,128)(2,1)S(1)} %collective-permute-done.source, bf16[9,128,512]{2,1,0:T(8,128)(2,1)} %copy-done.5, pred[4]{0:T(512)(128)(4,1)S(1)} %broadcast_select_fusion.13, pred[4]{0:T(512)(128)(4,1)S(1)} %broadcast_select_fusion.14), kind=kLoop, calls=%fused_computation.49 | loop fusion | flops 524288 | bytes 2097160 | tf_op jit(solution)/shard_map/jit(_where)/select_n | solution.py:180
  24.1 4.6 %collective-permute-done.16 = bf16[5,128,512]{2,1,0:T(8,128)(2,1)} collective-permute-done((bf16[5,128,512]{2,1,0:T(8,128)(2,1)}, bf16[5,128,512]{2,1,0:T(8,128)(2,1)}, u32[]{:S(2)}, u32[]{:S(2)}) %collective-permute-start.16) | collective-permute-done | bytes 655392 | tf_op jit(solution)/shard_map/ppermute | solution.py:30
  28.8 1.6 %collective-permute-start.17 = (bf16[5,128,512]{2,1,0:T(8,128)(2,1)S(1)}, bf16[5,128,512]{2,1,0:T(8,128)(2,1)S(1)}, u32[]{:S(2)}, u32[]{:S(2)}) collective-permute-start(bf16[5,128,512]{2,1,0:T(8,128)(2,1)S(1)} %fusion.20), channel_id=1, source_target_pairs={{0,4},{1,3},{2,6},{3,1},{4,0},{5,7},{6,2},{7,5},{8,12},{9,11},{10,... | collective-permute-start | bytes 1966088 | tf_op jit(solution)/shard_map/ppermute | solution.py:30
  32.8 1.5 %collective-permute-start.5 = (bf16[4,128,512]{2,1,0:T(8,128)(2,1)S(1)}, bf16[4,128,512]{2,1,0:T(8,128)(2,1)S(1)}, u32[]{:S(2)}, u32[]{:S(2)}) collective-permute-start(bf16[4,128,512]{2,1,0:T(8,128)(2,1)S(1)} %broadcast_select_fusion.1.refs_0_), channel_id=1, source_target_pairs={{0,2},{1,5},{2,0},{3,7},{4,6},{5,1},{6,4},{7,3},{8,10},{9,13},{10,... | collective-permute-start | bytes 1572872 | tf_op jit(solution)/shard_map/ppermute | solution.py:30
  35.1 8.4 %collective-permute-done.17.refs_0_ = bf16[5,128,512]{2,1,0:T(8,128)(2,1)S(1)} collective-permute-done((bf16[5,128,512]{2,1,0:T(8,128)(2,1)S(1)}, bf16[5,128,512]{2,1,0:T(8,128)(2,1)S(1)}, u32[]{:S(2)}, u32[]{:S(2)}) %collective-permute-start.17) | collective-permute-done | bytes 655392 | tf_op jit(solution)/shard_map/ppermute | solution.py:30
  43.6 3.3 %collective-permute-start.18 = (bf16[5,128,512]{2,1,0:T(8,128)(2,1)S(1)}, bf16[5,128,512]{2,1,0:T(8,128)(2,1)S(1)}, u32[]{:S(2)}, u32[]{:S(2)}) collective-permute-start(bf16[5,128,512]{2,1,0:T(8,128)(2,1)S(1)} %broadcast_select_fusion.refs_0_), channel_id=1, source_target_pairs={{0,2},{1,5},{2,0},{3,7},{4,6},{5,1},{6,4},{7,3},{8,10},{9,13},{10,... | collective-permute-start | bytes 1966088 | tf_op jit(solution)/shard_map/ppermute | solution.py:30
  47.4 2.6 %collective-permute-done.4 = bf16[4,128,512]{2,1,0:T(8,128)(2,1)S(1)} collective-permute-done((bf16[4,128,512]{2,1,0:T(8,128)(2,1)S(1)}, bf16[4,128,512]{2,1,0:T(8,128)(2,1)S(1)}, u32[]{:S(2)}, u32[]{:S(2)}) %collective-permute-start.4) | collective-permute-done | bytes 524320 | tf_op jit(solution)/shard_map/ppermute | solution.py:30
  52.2 9.0 %collective-permute-done.23 = bf16[3,128,512]{2,1,0:T(8,128)(2,1)S(1)} collective-permute-done((bf16[3,128,512]{2,1,0:T(8,128)(2,1)S(1)}, bf16[3,128,512]{2,1,0:T(8,128)(2,1)S(1)}, u32[]{:S(2)}, u32[]{:S(2)}) %collective-permute-start.23) | collective-permute-done | bytes 393248 | tf_op jit(solution)/shard_map/ppermute | solution.py:30
  61.2 3.5 %collective-permute-start.12 = (bf16[2,2,128,256]{3,2,1,0:T(8,128)(2,1)S(1)}, bf16[2,2,128,256]{3,2,1,0:T(8,128)(2,1)S(1)}, u32[]{:S(2)}, u32[]{:S(2)}) collective-permute-start(bf16[2,2,128,256]{3,2,1,0:T(8,128)(2,1)S(1)} %pad_maximum_fusion.7), channel_id=1, source_target_pairs={{0,8},{8,16},{16,24},{1,9},{9,17},{17,25},{2,10},{10,18},{18,26},{... | collective-permute-start | bytes 786440 | tf_op jit(solution)/shard_map/ppermute | solution.py:12
  64.8 7.1 %collective-permute-done.12 = bf16[2,2,128,256]{3,2,1,0:T(8,128)(2,1)S(1)} collective-permute-done((bf16[2,2,128,256]{3,2,1,0:T(8,128)(2,1)S(1)}, bf16[2,2,128,256]{3,2,1,0:T(8,128)(2,1)S(1)}, u32[]{:S(2)}, u32[]{:S(2)}) %collective-permute-start.12) | collective-permute-done | bytes 262176 | tf_op jit(solution)/shard_map/ppermute | solution.py:12
  77.9 3.4 %collective-permute-start.14 = (bf16[256,1024]{1,0:T(8,128)(2,1)S(1)}, bf16[256,1024]{1,0:T(8,128)(2,1)S(1)}, u32[]{:S(2)}, u32[]{:S(2)}) collective-permute-start(bf16[256,1024]{1,0:T(8,128)(2,1)S(1)} %get-tuple-element.15), channel_id=1, source_target_pairs={{8,16},{16,8},{9,17},{17,9},{10,18},{18,10},{11,19},{19,11},{12,20... | collective-permute-start | bytes 1572872 | tf_op jit(solution)/shard_map/ppermute | solution.py:21
  82.0 4.4 %collective-permute-done.8 = bf16[4,128,512]{2,1,0:T(8,128)(2,1)S(1)} collective-permute-done((bf16[4,128,512]{2,1,0:T(8,128)(2,1)S(1)}, bf16[4,128,512]{2,1,0:T(8,128)(2,1)S(1)}, u32[]{:S(2)}, u32[]{:S(2)}) %collective-permute-start.8) | collective-permute-done | bytes 524320 | tf_op jit(solution)/shard_map/ppermute | solution.py:30
  86.5 6.6 %collective-permute-done.14.refs_1_ = bf16[256,1024]{1,0:T(8,128)(2,1)S(1)} collective-permute-done((bf16[256,1024]{1,0:T(8,128)(2,1)S(1)}, bf16[256,1024]{1,0:T(8,128)(2,1)S(1)}, u32[]{:S(2)}, u32[]{:S(2)}) %collective-permute-start.14) | collective-permute-done | bytes 524320 | tf_op jit(solution)/shard_map/ppermute | solution.py:21
  93.1 1.6 %collective-permute-start.9 = (bf16[4,128,512]{2,1,0:T(8,128)(2,1)S(1)}, bf16[4,128,512]{2,1,0:T(8,128)(2,1)S(1)}, u32[]{:S(2)}, u32[]{:S(2)}) collective-permute-start(bf16[4,128,512]{2,1,0:T(8,128)(2,1)S(1)} %broadcast_select_fusion.10.refs_0_), channel_id=1, source_target_pairs={{0,2},{1,5},{2,0},{3,7},{4,6},{5,1},{6,4},{7,3},{8,10},{9,13},{10,... | collective-permute-start | bytes 1572872 | tf_op jit(solution)/shard_map/ppermute | solution.py:30
  99.0 2.1 %convolution_convert_fusion = bf16[3,512,1024]{2,1,0:T(8,128)(2,1)S(1)} fusion(bf16[5,512,512]{2,1,0:T(8,128)(2,1)S(1)} %place.8, bf16[3,512,1024]{2,1,0:T(8,128)(2,1)S(1)} %bitcast.58), kind=kOutput, calls=%fused_computation.3 | convolution fusion | flops 1612185600 | bytes 8912896 | tf_op jit(solution)/shard_map/nab,nac->nbc/dot_general | solution.py:228
  102.6 4.0 %collective-permute-done.25.refs_1_ = bf16[3,128,512]{2,1,0:T(8,128)(2,1)S(1)} collective-permute-done((bf16[3,128,512]{2,1,0:T(8,128)(2,1)S(1)}, bf16[3,128,512]{2,1,0:T(8,128)(2,1)S(1)}, u32[]{:S(2)}, u32[]{:S(2)}) %collective-permute-start.25) | collective-permute-done | bytes 393248 | tf_op jit(solution)/shard_map/ppermute | solution.py:30
  111.9 3.6 %collective-permute-start.21 = (bf16[256,1024]{1,0:T(8,128)(2,1)S(1)}, bf16[256,1024]{1,0:T(8,128)(2,1)S(1)}, u32[]{:S(2)}, u32[]{:S(2)}) collective-permute-start(bf16[256,1024]{1,0:T(8,128)(2,1)S(1)} %get-tuple-element.13), channel_id=1, source_target_pairs={{8,16},{16,8},{9,17},{17,9},{10,18},{18,10},{11,19},{19,11},{12,20... | collective-permute-start | bytes 1572872 | tf_op jit(solution)/shard_map/ppermute | solution.py:21
  116.1 1.8 %convolution_convert_fusion.1 = bf16[3,512,1024]{2,1,0:T(8,128)(2,1)S(1)} fusion(bf16[3,512,512]{2,1,0:T(8,128)(2,1)S(1)} %place.9, bf16[3,512,1024]{2,1,0:T(8,128)(2,1)S(1)} %bitcast.59), kind=kOutput, calls=%fused_computation.4 | convolution fusion | flops 1612185600 | bytes 7864320 | tf_op jit(solution)/shard_map/nab,nac->nbc/dot_general | solution.py:228
  117.9 9.9 %collective-permute-done.21 = bf16[256,1024]{1,0:T(8,128)(2,1)S(1)} collective-permute-done((bf16[256,1024]{1,0:T(8,128)(2,1)S(1)}, bf16[256,1024]{1,0:T(8,128)(2,1)S(1)}, u32[]{:S(2)}, u32[]{:S(2)}) %collective-permute-start.21) | collective-permute-done | bytes 524320 | tf_op jit(solution)/shard_map/ppermute | solution.py:21
  127.8 1.5 %collective-permute-done.22 = bf16[256,1024]{1,0:T(8,128)(2,1)S(1)} collective-permute-done((bf16[256,1024]{1,0:T(8,128)(2,1)S(1)}, bf16[256,1024]{1,0:T(8,128)(2,1)S(1)}, u32[]{:S(2)}, u32[]{:S(2)}) %collective-permute-start.22) | collective-permute-done | bytes 524320 | tf_op jit(solution)/shard_map/ppermute | solution.py:21
  130.4 2.3 %pad_maximum_fusion = bf16[2048,1024]{1,0:T(8,128)(2,1)} fusion(bf16[256,1024]{1,0:T(8,128)(2,1)S(1)} %fusion.3, bf16[1536,1024]{1,0:T(8,128)(2,1)S(1)} %bitcast.60, bf16[256,1024]{1,0:T(8,128)(2,1)S(1)} %fusion.2), kind=kLoop, calls=%fused_computation | loop fusion | flops 12582912 | bytes 8388608 | tf_op jit(solution)/shard_map/concatenate | solution.py:291
  (106 shorter events, 33.9 us)
Async XLA Ops:
  6.4 7.5 %collective-permute-start = (bf16[9,128,512]{2,1,0:T(8,128)(2,1)}, bf16[9,128,512]{2,1,0:T(8,128)(2,1)S(1)}, u32[]{:S(2)}, u32[]{:S(2)}) collective-permute-start(bf16[9,128,512]{2,1,0:T(8,128)(2,1)} %get-tuple-element.9), channel_id=1, source_target_pairs={{0,1},{1,0},{2,3},{3,2},{4,5},{5,4},{6,7},{7,6},{8,9},{9,8},{10,11... | collective-permute-start | bytes 3538952 | tf_op jit(solution)/shard_map/ppermute | solution.py:30
  9.7 9.5 %collective-permute-start.2 = (bf16[4,128,512]{2,1,0:T(8,128)(2,1)}, bf16[4,128,512]{2,1,0:T(8,128)(2,1)}, u32[]{:S(2)}, u32[]{:S(2)}) collective-permute-start(bf16[4,128,512]{2,1,0:T(8,128)(2,1)} %slice_select_fusion.2), channel_id=1, source_target_pairs={{0,2},{1,5},{2,0},{3,7},{4,6},{5,1},{6,4},{7,3},{8,10},{9,13},{10,... | collective-permute-start | bytes 1572872 | tf_op jit(solution)/shard_map/ppermute | solution.py:30
  12.1 16.6 %collective-permute-start.16 = (bf16[5,128,512]{2,1,0:T(8,128)(2,1)}, bf16[5,128,512]{2,1,0:T(8,128)(2,1)}, u32[]{:S(2)}, u32[]{:S(2)}) collective-permute-start(bf16[5,128,512]{2,1,0:T(8,128)(2,1)} %slice_select_fusion), channel_id=1, source_target_pairs={{0,2},{1,5},{2,0},{3,7},{4,6},{5,1},{6,4},{7,3},{8,10},{9,13},{10,... | collective-permute-start | bytes 1966088 | tf_op jit(solution)/shard_map/ppermute | solution.py:30
  21.3 9.6 %collective-permute-start.3 = (bf16[4,128,512]{2,1,0:T(8,128)(2,1)}, bf16[4,128,512]{2,1,0:T(8,128)(2,1)S(1)}, u32[]{:S(2)}, u32[]{:S(2)}) collective-permute-start(bf16[4,128,512]{2,1,0:T(8,128)(2,1)} %fusion.21), channel_id=1, source_target_pairs={{0,4},{1,3},{2,6},{3,1},{4,0},{5,7},{6,2},{7,5},{8,12},{9,11},{10,... | collective-permute-start | bytes 1572872 | tf_op jit(solution)/shard_map/ppermute | solution.py:30
  28.8 14.6 %collective-permute-start.17 = (bf16[5,128,512]{2,1,0:T(8,128)(2,1)S(1)}, bf16[5,128,512]{2,1,0:T(8,128)(2,1)S(1)}, u32[]{:S(2)}, u32[]{:S(2)}) collective-permute-start(bf16[5,128,512]{2,1,0:T(8,128)(2,1)S(1)} %fusion.20), channel_id=1, source_target_pairs={{0,4},{1,3},{2,6},{3,1},{4,0},{5,7},{6,2},{7,5},{8,12},{9,11},{10,... | collective-permute-start | bytes 1966088 | tf_op jit(solution)/shard_map/ppermute | solution.py:30
  32.1 41.3 %collective-permute-start.6 = (bf16[4,128,512]{2,1,0:T(8,128)(2,1)S(1)}, bf16[4,128,512]{2,1,0:T(8,128)(2,1)S(1)}, u32[]{:S(2)}, u32[]{:S(2)}) collective-permute-start(bf16[4,128,512]{2,1,0:T(8,128)(2,1)S(1)} %broadcast_select_fusion.1.refs_0_), channel_id=1, source_target_pairs={{0,1},{1,0},{2,3},{3,2},{4,5},{5,4},{6,7},{7,6},{8,9},{9,8},{10,11... | collective-permute-start | bytes 1572872 | tf_op jit(solution)/shard_map/ppermute | solution.py:30
  32.8 18.7 %collective-permute-start.5 = (bf16[4,128,512]{2,1,0:T(8,128)(2,1)S(1)}, bf16[4,128,512]{2,1,0:T(8,128)(2,1)S(1)}, u32[]{:S(2)}, u32[]{:S(2)}) collective-permute-start(bf16[4,128,512]{2,1,0:T(8,128)(2,1)S(1)} %broadcast_select_fusion.1.refs_0_), channel_id=1, source_target_pairs={{0,2},{1,5},{2,0},{3,7},{4,6},{5,1},{6,4},{7,3},{8,10},{9,13},{10,... | collective-permute-start | bytes 1572872 | tf_op jit(solution)/shard_map/ppermute | solution.py:30
  34.4 15.5 %collective-permute-start.4 = (bf16[4,128,512]{2,1,0:T(8,128)(2,1)S(1)}, bf16[4,128,512]{2,1,0:T(8,128)(2,1)S(1)}, u32[]{:S(2)}, u32[]{:S(2)}) collective-permute-start(bf16[4,128,512]{2,1,0:T(8,128)(2,1)S(1)} %slice_select_fusion.4), channel_id=1, source_target_pairs={{0,2},{1,5},{2,0},{3,7},{4,6},{5,1},{6,4},{7,3},{8,10},{9,13},{10,... | collective-permute-start | bytes 1572872 | tf_op jit(solution)/shard_map/ppermute | solution.py:30
  43.5 52.1 %collective-permute-start.19 = (bf16[5,128,512]{2,1,0:T(8,128)(2,1)S(1)}, bf16[5,128,512]{2,1,0:T(8,128)(2,1)S(1)}, u32[]{:S(2)}, u32[]{:S(2)}) collective-permute-start(bf16[5,128,512]{2,1,0:T(8,128)(2,1)S(1)} %broadcast_select_fusion.refs_0_), channel_id=1, source_target_pairs={{0,1},{1,0},{2,3},{3,2},{4,5},{5,4},{6,7},{7,6},{8,9},{9,8},{10,11... | collective-permute-start | bytes 1966088 | tf_op jit(solution)/shard_map/ppermute | solution.py:30
  43.6 29.9 %collective-permute-start.18 = (bf16[5,128,512]{2,1,0:T(8,128)(2,1)S(1)}, bf16[5,128,512]{2,1,0:T(8,128)(2,1)S(1)}, u32[]{:S(2)}, u32[]{:S(2)}) collective-permute-start(bf16[5,128,512]{2,1,0:T(8,128)(2,1)S(1)} %broadcast_select_fusion.refs_0_), channel_id=1, source_target_pairs={{0,2},{1,5},{2,0},{3,7},{4,6},{5,1},{6,4},{7,3},{8,10},{9,13},{10,... | collective-permute-start | bytes 1966088 | tf_op jit(solution)/shard_map/ppermute | solution.py:30
  49.9 11.2 %collective-permute-start.23 = (bf16[3,128,512]{2,1,0:T(8,128)(2,1)S(1)}, bf16[3,128,512]{2,1,0:T(8,128)(2,1)S(1)}, u32[]{:S(2)}, u32[]{:S(2)}) collective-permute-start(bf16[3,128,512]{2,1,0:T(8,128)(2,1)S(1)} %slice_select_fusion.5), channel_id=1, source_target_pairs={{0,2},{1,5},{2,0},{3,7},{4,6},{5,1},{6,4},{7,3},{8,10},{9,13},{10,... | collective-permute-start | bytes 1179656 | tf_op jit(solution)/shard_map/ppermute | solution.py:30
  51.4 22.6 %collective-permute-start.7 = (bf16[4,128,512]{2,1,0:T(8,128)(2,1)S(1)}, bf16[4,128,512]{2,1,0:T(8,128)(2,1)S(1)}, u32[]{:S(2)}, u32[]{:S(2)}) collective-permute-start(bf16[4,128,512]{2,1,0:T(8,128)(2,1)S(1)} %collective-permute-done.5.refs_1_), channel_id=1, source_target_pairs={{0,1},{1,0},{2,3},{3,2},{4,5},{5,4},{6,7},{7,6},{8,9},{9,8},{10,11... | collective-permute-start | bytes 1572872 | tf_op jit(solution)/shard_map/ppermute | solution.py:30
  61.2 10.7 %collective-permute-start.12 = (bf16[2,2,128,256]{3,2,1,0:T(8,128)(2,1)S(1)}, bf16[2,2,128,256]{3,2,1,0:T(8,128)(2,1)S(1)}, u32[]{:S(2)}, u32[]{:S(2)}) collective-permute-start(bf16[2,2,128,256]{3,2,1,0:T(8,128)(2,1)S(1)} %pad_maximum_fusion.7), channel_id=1, source_target_pairs={{0,8},{8,16},{16,24},{1,9},{9,17},{17,25},{2,10},{10,18},{18,26},{... | collective-permute-start | bytes 786440 | tf_op jit(solution)/shard_map/ppermute | solution.py:12
  71.8 9.9 %collective-permute-start.24 = (bf16[3,128,512]{2,1,0:T(8,128)(2,1)S(1)}, bf16[3,128,512]{2,1,0:T(8,128)(2,1)S(1)}, u32[]{:S(2)}, u32[]{:S(2)}) collective-permute-start(bf16[3,128,512]{2,1,0:T(8,128)(2,1)S(1)} %select_select_fusion.1), channel_id=1, source_target_pairs={{0,4},{1,3},{2,6},{3,1},{4,0},{5,7},{6,2},{7,5},{8,12},{9,11},{10,... | collective-permute-start | bytes 1179656 | tf_op jit(solution)/shard_map/ppermute | solution.py:30
  73.5 23.2 %collective-permute-start.20 = (bf16[5,128,512]{2,1,0:T(8,128)(2,1)S(1)}, bf16[5,128,512]{2,1,0:T(8,128)(2,1)S(1)}, u32[]{:S(2)}, u32[]{:S(2)}) collective-permute-start(bf16[5,128,512]{2,1,0:T(8,128)(2,1)S(1)} %collective-permute-done.18.refs_1_), channel_id=1, source_target_pairs={{0,1},{1,0},{2,3},{3,2},{4,5},{5,4},{6,7},{7,6},{8,9},{9,8},{10,11... | collective-permute-start | bytes 1966088 | tf_op jit(solution)/shard_map/ppermute | solution.py:30
  77.1 9.2 %collective-permute-start.8 = (bf16[4,128,512]{2,1,0:T(8,128)(2,1)S(1)}, bf16[4,128,512]{2,1,0:T(8,128)(2,1)S(1)}, u32[]{:S(2)}, u32[]{:S(2)}) collective-permute-start(bf16[4,128,512]{2,1,0:T(8,128)(2,1)S(1)} %after.8), channel_id=1, source_target_pairs={{0,4},{1,3},{2,6},{3,1},{4,0},{5,7},{6,2},{7,5},{8,12},{9,11},{10,... | collective-permute-start | bytes 1572872 | tf_op jit(solution)/shard_map/ppermute | solution.py:30
  77.9 15.2 %collective-permute-start.14 = (bf16[256,1024]{1,0:T(8,128)(2,1)S(1)}, bf16[256,1024]{1,0:T(8,128)(2,1)S(1)}, u32[]{:S(2)}, u32[]{:S(2)}) collective-permute-start(bf16[256,1024]{1,0:T(8,128)(2,1)S(1)} %get-tuple-element.15), channel_id=1, source_target_pairs={{8,16},{16,8},{9,17},{17,9},{10,18},{18,10},{11,19},{19,11},{12,20... | collective-permute-start | bytes 1572872 | tf_op jit(solution)/shard_map/ppermute | solution.py:21
  81.8 13.5 %collective-permute-start.15 = (bf16[256,1024]{1,0:T(8,128)(2,1)S(1)}, bf16[256,1024]{1,0:T(8,128)(2,1)S(1)}, u32[]{:S(2)}, u32[]{:S(2)}) collective-permute-start(bf16[256,1024]{1,0:T(8,128)(2,1)S(1)} %get-tuple-element.16), channel_id=1, source_target_pairs={{0,8},{16,24},{8,0},{24,16},{1,9},{17,25},{9,1},{25,17},{2,10},{18... | collective-permute-start | bytes 1572872 | tf_op jit(solution)/shard_map/ppermute | solution.py:21
  86.4 22.1 %collective-permute-start.10 = (bf16[4,128,512]{2,1,0:T(8,128)(2,1)S(1)}, bf16[4,128,512]{2,1,0:T(8,128)(2,1)S(1)}, u32[]{:S(2)}, u32[]{:S(2)}) collective-permute-start(bf16[4,128,512]{2,1,0:T(8,128)(2,1)S(1)} %broadcast_select_fusion.10.refs_0_), channel_id=1, source_target_pairs={{0,1},{1,0},{2,3},{3,2},{4,5},{5,4},{6,7},{7,6},{8,9},{9,8},{10,11... | collective-permute-start | bytes 1572872 | tf_op jit(solution)/shard_map/ppermute | solution.py:30
  93.1 9.2 %collective-permute-start.9 = (bf16[4,128,512]{2,1,0:T(8,128)(2,1)S(1)}, bf16[4,128,512]{2,1,0:T(8,128)(2,1)S(1)}, u32[]{:S(2)}, u32[]{:S(2)}) collective-permute-start(bf16[4,128,512]{2,1,0:T(8,128)(2,1)S(1)} %broadcast_select_fusion.10.refs_0_), channel_id=1, source_target_pairs={{0,2},{1,5},{2,0},{3,7},{4,6},{5,1},{6,4},{7,3},{8,10},{9,13},{10,... | collective-permute-start | bytes 1572872 | tf_op jit(solution)/shard_map/ppermute | solution.py:30
  95.5 12.0 %collective-permute-start.26 = (bf16[3,128,512]{2,1,0:T(8,128)(2,1)S(1)}, bf16[3,128,512]{2,1,0:T(8,128)(2,1)S(1)}, u32[]{:S(2)}, u32[]{:S(2)}) collective-permute-start(bf16[3,128,512]{2,1,0:T(8,128)(2,1)S(1)} %after.11.refs_0_), channel_id=1, source_target_pairs={{0,1},{1,0},{2,3},{3,2},{4,5},{5,4},{6,7},{7,6},{8,9},{9,8},{10,11... | collective-permute-start | bytes 1179656 | tf_op jit(solution)/shard_map/ppermute | solution.py:30
  95.6 10.9 %collective-permute-start.25 = (bf16[3,128,512]{2,1,0:T(8,128)(2,1)S(1)}, bf16[3,128,512]{2,1,0:T(8,128)(2,1)S(1)}, u32[]{:S(2)}, u32[]{:S(2)}) collective-permute-start(bf16[3,128,512]{2,1,0:T(8,128)(2,1)S(1)} %after.11.refs_0_), channel_id=1, source_target_pairs={{0,2},{1,5},{2,0},{3,7},{4,6},{5,1},{6,4},{7,3},{8,10},{9,13},{10,... | collective-permute-start | bytes 1179656 | tf_op jit(solution)/shard_map/ppermute | solution.py:30
  111.9 15.9 %collective-permute-start.21 = (bf16[256,1024]{1,0:T(8,128)(2,1)S(1)}, bf16[256,1024]{1,0:T(8,128)(2,1)S(1)}, u32[]{:S(2)}, u32[]{:S(2)}) collective-permute-start(bf16[256,1024]{1,0:T(8,128)(2,1)S(1)} %get-tuple-element.13), channel_id=1, source_target_pairs={{8,16},{16,8},{9,17},{17,9},{10,18},{18,10},{11,19},{19,11},{12,20... | collective-permute-start | bytes 1572872 | tf_op jit(solution)/shard_map/ppermute | solution.py:21
  115.6 13.8 %collective-permute-start.22 = (bf16[256,1024]{1,0:T(8,128)(2,1)S(1)}, bf16[256,1024]{1,0:T(8,128)(2,1)S(1)}, u32[]{:S(2)}, u32[]{:S(2)}) collective-permute-start(bf16[256,1024]{1,0:T(8,128)(2,1)S(1)} %get-tuple-element.14), channel_id=1, source_target_pairs={{0,8},{16,24},{8,0},{24,16},{1,9},{17,25},{9,1},{25,17},{2,10},{18... | collective-permute-start | bytes 1572872 | tf_op jit(solution)/shard_map/ppermute | solution.py:21
  (13 other events, 56.9 us)

commit v7 on v6

--- a/solution.py
+++ b/solution.py
@@ -22,7 +22,7 @@
 
     first = swap(jnp.where(even, down, up), 0)
     second = swap(jnp.where(even, up, down), 1)
-    return (jnp.where(even, second, first), jnp.where(even, first, second)), (first, second)
+    return jnp.where(even, second, first), jnp.where(even, first, second)
 
 
 def flip(value, bits):
@@ -49,15 +49,13 @@
 ANY = pl.BlockSpec(memory_space=pl.ANY)
 
 
-def after(value, *done, rows=None):
-    start, count = (0, value.shape[0]) if rows is None else (rows.start, rows.stop - rows.start)
-
+def after(value, *done):
     def kernel(source, *refs):
-        copy_all([pltpu.make_async_copy(source.at[pl.ds(start, count)], refs[-2], refs[-1])])
+        copy_all([pltpu.make_async_copy(source, refs[-2], refs[-1])])
 
     return pl.pallas_call(
         kernel,
-        out_shape=jax.ShapeDtypeStruct((count,) + value.shape[1:], value.dtype),
+        out_shape=jax.ShapeDtypeStruct(value.shape, value.dtype),
         in_specs=[ANY] * (1 + len(done)),
         out_specs=ANY,
         scratch_shapes=[pltpu.SemaphoreType.DMA],
@@ -180,13 +178,13 @@
         return jnp.where(mask, yes, no)
 
     def begin(self, rounds, rows, *first):
-        parts = []
-        for own, theirs in zip(self.own, self.theirs):
-            theirs = after(theirs, *first, rows=rows) if first else theirs[rows]
-            parts.append(
-                self.choose(rounds, lambda owner: (owner & 1) == self.core, own[rows], theirs)
-            )
-        return rounds, parts[1], flip(parts[0], self.cut)
+        out, hold = [
+            self.choose(rounds, lambda owner: (owner & 1) == self.core, own[rows], theirs[rows])
+            for own, theirs in zip(self.own, self.theirs)
+        ]
+        if first:
+            out = after(out, *first)
+        return rounds, hold, flip(out, self.cut)
 
     def keep(self, state, bits):
         rounds, hold, got = state
@@ -213,8 +211,8 @@
     def join(self, hold, got):
         return place(self.cut, hold, got, flip(hold, (0, 0)), flip(got, (0, 0)))
 
-    def join_above(self, hold, got):
-        both = shifted(jnp.stack([hold, got]), "rows", 1)
+    def join_above(self, hold, got, *first):
+        both = shifted(after(jnp.stack([hold, got]), *first), "rows", 1)
         other = flip(both, (0, 0))
         return place(self.cut, both[0], both[1], other[0], other[1])
 
@@ -252,25 +250,24 @@
         if r == 0:
             head = spread.middle(spread.begin(across + [r, r], slice(2 - n, 4)))
             tail = spread.middle(spread.begin([r] * (cut_two - 4), slice(4, cut_two)))
-            head_pair, tail_pair = spread.last(head), spread.last(tail)
         else:
             head = spread.begin(across + [r] * wins, slice(2 - n, cut_one), head[2])
             tail = spread.begin([r] * (cut_two - cut_one), slice(cut_one, cut_two), tail[2])
-            head, tail = spread.middle(head, head_rows, tail_rows), spread.middle(tail)
-            head_pair, tail_pair = spread.last(head), spread.last(tail, *swapped)
+            head, tail = spread.middle(head), spread.middle(tail, head_rows, tail_rows)
+        head_pair, tail_pair = spread.last(head), spread.last(tail)
         edges = spread.join(*head_pair)
+        head_rows = apply(edges[n], matrix[:window])
+        tail_rows = apply(edges[n + 1], matrix[local_rows - window :])
         if n:
             from_above = spread.join_above(
-                head_pair[0][:n, :, border:], head_pair[1][:n, :, border:]
+                head_pair[0][:n, :, border:], head_pair[1][:n, :, border:], head_rows, tail_rows
             )
             for k, q in enumerate(across):
                 crosses[q], above_crosses[q] = edges[k], from_above[k]
-            edges = edges[n:]
+        edges = edges[n:]
         prev, cross = above_crosses[r], crosses[r]
-        head_rows = apply(edges[0], matrix[:window])
-        tail_rows = apply(edges[1], matrix[local_rows - window :])
         begin, end = head_rows[:border], tail_rows[border:]
-        (above, below), swapped = swap_rows(begin, end)
+        above, below = swap_rows(begin, end)
         rest = spread.join(*tail_pair)
         if r == 0:
             ones, twos = rest[: wins - 2], rest[wins - 2 :]

time: 134 us -> 132 us (0.985)
  waiting for transfers between devices: 66.3 us -> 57.8 us
  other arithmetic: 9.45 us -> 15.8 us
    select_n x12 -> x11, other arithmetic: 5.78 us -> 12.1 us  [choose(): return jnp.where(mask, yes, no)]
    ppermute x23, waiting for transfers between devices: 40.7 us -> 36.1 us  [flip(): lax.ppermute(value, 'cols', [(d, d ^ 1 << bits[d & 1]) for d in range(cou...]
    ppermute x1, waiting for transfers between devices: 7.08 us -> 5.07 us  [shifted(): lax.ppermute(value, axis, [(source, source + steps) for source in range(i...]
    ppermute x4, waiting for transfers between devices: 18.6 us -> 16.7 us  [swap(): return lax.ppermute(value, 'rows', pairs + [(b, a) for a, b in pairs])]
    unnamed x16 -> x8, local copies, waits for them, and re-layouts: 4.64 us -> 3.09 us
  transfers between devices with their start and end apart: 28 -> 28, of which waited for: 15 -> 11; matrix products, arithmetic and copies ran while one was open for 12% -> 19% of each run, Pallas kernels for 3% -> 3%
where the time goes in v7:
time: 132 us; the launch traced here: 130 us
  waiting for transfers between devices  57.8 us (44%)
  starting transfers between devices  30.6 us (23%)
  other arithmetic  15.8 us (12%)
  matrix products  11.8 us (9%)
  local copies, waits for them, and re-layouts  5.24 us (4%)
  Pallas kernels  4.52 us (3%)
  between operations  4.24 us (3%)
    ppermute x23, waiting for transfers between devices, flip(): lax.ppermute(value, 'cols', [(d, d ^ 1 << bits[d & 1]) for d in range(cou...  36.1 us
    ppermute x23, starting transfers between devices, flip(): lax.ppermute(value, 'cols', [(d, d ^ 1 << bits[d & 1]) for d in range(cou...  20.1 us
    ppermute x4, waiting for transfers between devices, swap(): return lax.ppermute(value, 'rows', pairs + [(b, a) for a, b in pairs])  16.7 us
    select_n x11, other arithmetic, choose(): return jnp.where(mask, yes, no)  12.1 us
    ppermute x4, starting transfers between devices, swap(): return lax.ppermute(value, 'rows', pairs + [(b, a) for a, b in pairs])  7.17 us
    dot_general x4, matrix products, apply_many(): jnp.einsum('nab,nac->nbc', q, x, preferred_element_type=jnp.float32)  7.04 us
    ppermute x1, waiting for transfers between devices, shifted(): lax.ppermute(value, axis, [(source, source + steps) for source in range(i...  5.07 us
    dot_general x8, matrix products, apply(): lax.dot_general(q, x, (((0,), (0,)), ((), ())), preferred_element_type=jn...  4.78 us
  transfers between devices with their start and end apart: 28, of which 11 were waited for; matrix products, arithmetic and copies ran while one was open for 19% of the time, Pallas kernels for 3%

profile of v7, /device:TPU:8, one launch (start us, length us, event | category | flops | bytes accessed | tf_op | source)
XLA Modules:
  0.0 130.1 jit_solution(16825770229371452607)
XLA Ops:
  0.0 2.2 %copy-done.2 = bf16[1,4096,512]{2,1,0:T(8,128)(2,1)S(1)} copy-done((bf16[1,4096,512]{2,1,0:T(8,128)(2,1)S(1)}, bf16[1,4096,512]{2,1,0:T(8,128)(2,1)}, u32[]{:S(2)}) %copy-start.2) | copy-done | bytes 4194328
  3.1 1.9 %cut_slot.2 = (bf16[9,128,512]{2,1,0:T(8,128)(2,1)S(1)}, bf16[9,128,512]{2,1,0:T(8,128)(2,1)}, bf16[9,128,512]{2,1,0:T(8,128)(2,1)S(1)}) custom-call(bf16[8,2,2,128,512]{4,3,2,1,0:T(8,128)(2,1)S(1)} %bitcast.54), custom_call_target="tpu_custom_call" | custom-call | bytes 6291456 | tf_op jit(solution)/shard_map/cut_slot/pallas_call | solution.py:105
  7.5 2.2 %slice_select_fusion.4 = (bf16[4,128,512]{2,1,0:T(8,128)(2,1)S(1)}, bf16[4,128,512]{2,1,0:T(8,128)(2,1)}) fusion(bf16[9,128,512]{2,1,0:T(8,128)(2,1)} %collective-permute-done.1, bf16[9,128,512]{2,1,0:T(8,128)(2,1)S(1)} %get-tuple-element.10, pred[]{:T(512)S(6)} %eq.24, pred[4]{0:T(512)(128)(4,1)S(1)} %broadcast_select_fusion.13), kind=kLoop, calls=%fused_computation.50 | loop fusion | flops 524288 | bytes 3145733 | tf_op jit(solution)/shard_map/jit(_where)/select_n | solution.py:178
  11.2 2.0 %slice_select_fusion = bf16[5,128,512]{2,1,0:T(8,128)(2,1)} fusion(bf16[9,128,512]{2,1,0:T(8,128)(2,1)} %collective-permute-done.1, bf16[9,128,512]{2,1,0:T(8,128)(2,1)S(1)} %get-tuple-element.10, pred[]{:T(512)S(6)} %eq.26), kind=kLoop, calls=%fused_computation.37 | loop fusion | flops 327680 | bytes 1966081 | tf_op jit(solution)/shard_map/jit(_where)/select_n | solution.py:178
  15.0 4.1 %collective-permute-done.2 = bf16[4,128,512]{2,1,0:T(8,128)(2,1)S(1)} collective-permute-done((bf16[4,128,512]{2,1,0:T(8,128)(2,1)}, bf16[4,128,512]{2,1,0:T(8,128)(2,1)S(1)}, u32[]{:S(2)}, u32[]{:S(2)}) %collective-permute-start.2) | collective-permute-done | bytes 524320 | tf_op jit(solution)/shard_map/ppermute | solution.py:30
  19.1 2.0 %fusion.21 = bf16[4,128,512]{2,1,0:T(8,128)(2,1)} fusion(bf16[4,128,512]{2,1,0:T(8,128)(2,1)S(1)} %collective-permute-done.2, bf16[9,128,512]{2,1,0:T(8,128)(2,1)} %collective-permute-done, bf16[9,128,512]{2,1,0:T(8,128)(2,1)S(1)} %get-tuple-element.8, pred[4]{0:T(512)(128)(4,1)S(1)} %broadcast_select_fusion.13, pred[4]{0:T(512)(128)(4,1)S(1)} %broadcast_select_fusion.14), kind=kLoop, calls=%fused_computation.49 | loop fusion | flops 524288 | bytes 2097160 | tf_op jit(solution)/shard_map/jit(_where)/select_n | solution.py:178
  23.8 5.3 %collective-permute-done.16 = bf16[5,128,512]{2,1,0:T(8,128)(2,1)} collective-permute-done((bf16[5,128,512]{2,1,0:T(8,128)(2,1)}, bf16[5,128,512]{2,1,0:T(8,128)(2,1)}, u32[]{:S(2)}, u32[]{:S(2)}) %collective-permute-start.16) | collective-permute-done | bytes 655392 | tf_op jit(solution)/shard_map/ppermute | solution.py:30
  30.5 1.6 %collective-permute-start.17 = (bf16[5,128,512]{2,1,0:T(8,128)(2,1)S(1)}, bf16[5,128,512]{2,1,0:T(8,128)(2,1)S(1)}, u32[]{:S(2)}, u32[]{:S(2)}) collective-permute-start(bf16[5,128,512]{2,1,0:T(8,128)(2,1)S(1)} %fusion.20), channel_id=1, source_target_pairs={{0,4},{1,3},{2,6},{3,1},{4,0},{5,7},{6,2},{7,5},{8,12},{9,11},{10,... | collective-permute-start | bytes 1966088 | tf_op jit(solution)/shard_map/ppermute | solution.py:30
  36.7 10.1 %collective-permute-done.17.refs_0_ = bf16[5,128,512]{2,1,0:T(8,128)(2,1)S(1)} collective-permute-done((bf16[5,128,512]{2,1,0:T(8,128)(2,1)S(1)}, bf16[5,128,512]{2,1,0:T(8,128)(2,1)S(1)}, u32[]{:S(2)}, u32[]{:S(2)}) %collective-permute-start.17) | collective-permute-done | bytes 655392 | tf_op jit(solution)/shard_map/ppermute | solution.py:30
  50.0 2.5 %collective-permute-start.11 = (bf16[4,128,512]{2,1,0:T(8,128)(2,1)S(1)}, bf16[4,128,512]{2,1,0:T(8,128)(2,1)S(1)}, u32[]{:S(2)}, u32[]{:S(2)}) collective-permute-start(bf16[4,128,512]{2,1,0:T(8,128)(2,1)S(1)} %collective-permute-done.9.refs_1_), channel_id=1, source_target_pairs={{0,1},{1,0},{2,3},{3,2},{4,5},{5,4},{6,7},{7,6},{8,9},{9,8},{10,11... | collective-permute-start | bytes 1572872 | tf_op jit(solution)/shard_map/ppermute | solution.py:30
  53.6 8.3 %collective-permute-done.23 = bf16[3,128,512]{2,1,0:T(8,128)(2,1)S(1)} collective-permute-done((bf16[3,128,512]{2,1,0:T(8,128)(2,1)S(1)}, bf16[3,128,512]{2,1,0:T(8,128)(2,1)S(1)}, u32[]{:S(2)}, u32[]{:S(2)}) %collective-permute-start.23) | collective-permute-done | bytes 393248 | tf_op jit(solution)/shard_map/ppermute | solution.py:30
  68.1 3.0 %collective-permute-done.5 = bf16[4,128,512]{2,1,0:T(8,128)(2,1)S(1)} collective-permute-done((bf16[4,128,512]{2,1,0:T(8,128)(2,1)S(1)}, bf16[4,128,512]{2,1,0:T(8,128)(2,1)S(1)}, u32[]{:S(2)}, u32[]{:S(2)}) %collective-permute-start.5) | collective-permute-done | bytes 524320 | tf_op jit(solution)/shard_map/ppermute | solution.py:30
  71.8 3.3 %collective-permute-start.12 = (bf16[2,2,128,256]{3,2,1,0:T(8,128)(2,1)S(1)}, bf16[2,2,128,256]{3,2,1,0:T(8,128)(2,1)S(1)}, u32[]{:S(2)}, u32[]{:S(2)}) collective-permute-start(bf16[2,2,128,256]{3,2,1,0:T(8,128)(2,1)S(1)} %after.5), channel_id=1, source_target_pairs={{0,8},{8,16},{16,24},{1,9},{9,17},{17,25},{2,10},{10,18},{18,26},{... | collective-permute-start | bytes 786440 | tf_op jit(solution)/shard_map/ppermute | solution.py:12
  75.1 1.6 %collective-permute-start.24 = (bf16[3,128,512]{2,1,0:T(8,128)(2,1)S(1)}, bf16[3,128,512]{2,1,0:T(8,128)(2,1)S(1)}, u32[]{:S(2)}, u32[]{:S(2)}) collective-permute-start(bf16[3,128,512]{2,1,0:T(8,128)(2,1)S(1)} %after.7), channel_id=1, source_target_pairs={{0,4},{1,3},{2,6},{3,1},{4,0},{5,7},{6,2},{7,5},{8,12},{9,11},{10,... | collective-permute-start | bytes 1179656 | tf_op jit(solution)/shard_map/ppermute | solution.py:30
  77.0 5.1 %collective-permute-done.12 = bf16[2,2,128,256]{3,2,1,0:T(8,128)(2,1)S(1)} collective-permute-done((bf16[2,2,128,256]{3,2,1,0:T(8,128)(2,1)S(1)}, bf16[2,2,128,256]{3,2,1,0:T(8,128)(2,1)S(1)}, u32[]{:S(2)}, u32[]{:S(2)}) %collective-permute-start.12) | collective-permute-done | bytes 262176 | tf_op jit(solution)/shard_map/ppermute | solution.py:12
  83.3 4.0 %collective-permute-start.14 = (bf16[256,1024]{1,0:T(8,128)(2,1)S(1)}, bf16[256,1024]{1,0:T(8,128)(2,1)S(1)}, u32[]{:S(2)}, u32[]{:S(2)}) collective-permute-start(bf16[256,1024]{1,0:T(8,128)(2,1)S(1)} %get-tuple-element.17), channel_id=1, source_target_pairs={{8,16},{16,8},{9,17},{17,9},{10,18},{18,10},{11,19},{19,11},{12,20... | collective-permute-start | bytes 1572872 | tf_op jit(solution)/shard_map/ppermute | solution.py:21
  90.8 2.1 %convolution_convert_fusion = bf16[3,512,1024]{2,1,0:T(8,128)(2,1)S(1)} fusion(bf16[5,512,512]{2,1,0:T(8,128)(2,1)S(1)} %place.8, bf16[3,512,1024]{2,1,0:T(8,128)(2,1)S(1)} %bitcast.59), kind=kOutput, calls=%fused_computation.3 | convolution fusion | flops 1612185600 | bytes 8912896 | tf_op jit(solution)/shard_map/nab,nac->nbc/dot_general | solution.py:226
  93.0 5.3 %collective-permute-done.14 = bf16[256,1024]{1,0:T(8,128)(2,1)S(1)} collective-permute-done((bf16[256,1024]{1,0:T(8,128)(2,1)S(1)}, bf16[256,1024]{1,0:T(8,128)(2,1)S(1)}, u32[]{:S(2)}, u32[]{:S(2)}) %collective-permute-start.14) | collective-permute-done | bytes 524320 | tf_op jit(solution)/shard_map/ppermute | solution.py:21
  101.3 4.8 %collective-permute-done.25.refs_1_ = bf16[3,128,512]{2,1,0:T(8,128)(2,1)S(1)} collective-permute-done((bf16[3,128,512]{2,1,0:T(8,128)(2,1)S(1)}, bf16[3,128,512]{2,1,0:T(8,128)(2,1)S(1)}, u32[]{:S(2)}, u32[]{:S(2)}) %collective-permute-start.25) | collective-permute-done | bytes 393248 | tf_op jit(solution)/shard_map/ppermute | solution.py:30
  107.9 1.5 %convolution_convert_fusion.3 = bf16[2,512,1024]{2,1,0:T(8,128)(2,1)S(1)} fusion(bf16[4,512,512]{2,1,0:T(8,128)(2,1)S(1)} %place.5, bf16[2,512,1024]{2,1,0:T(8,128)(2,1)S(1)} %bitcast.64), kind=kOutput, calls=%fused_computation.6 | convolution fusion | flops 1074790400 | bytes 6291456 | tf_op jit(solution)/shard_map/nab,nac->nbc/dot_general | solution.py:226
  109.6 3.1 %collective-permute-start.21 = (bf16[256,1024]{1,0:T(8,128)(2,1)S(1)}, bf16[256,1024]{1,0:T(8,128)(2,1)S(1)}, u32[]{:S(2)}, u32[]{:S(2)}) collective-permute-start(bf16[256,1024]{1,0:T(8,128)(2,1)S(1)} %get-tuple-element.15), channel_id=1, source_target_pairs={{8,16},{16,8},{9,17},{17,9},{10,18},{18,10},{11,19},{19,11},{12,20... | collective-permute-start | bytes 1572872 | tf_op jit(solution)/shard_map/ppermute | solution.py:21
  113.5 1.9 %convolution_convert_fusion.1 = bf16[3,512,1024]{2,1,0:T(8,128)(2,1)S(1)} fusion(bf16[3,512,512]{2,1,0:T(8,128)(2,1)S(1)} %place.9, bf16[3,512,1024]{2,1,0:T(8,128)(2,1)S(1)} %bitcast.58), kind=kOutput, calls=%fused_computation.4 | convolution fusion | flops 1612185600 | bytes 7864320 | tf_op jit(solution)/shard_map/nab,nac->nbc/dot_general | solution.py:226
  115.4 10.4 %collective-permute-done.21 = bf16[256,1024]{1,0:T(8,128)(2,1)S(1)} collective-permute-done((bf16[256,1024]{1,0:T(8,128)(2,1)S(1)}, bf16[256,1024]{1,0:T(8,128)(2,1)S(1)}, u32[]{:S(2)}, u32[]{:S(2)}) %collective-permute-start.21) | collective-permute-done | bytes 524320 | tf_op jit(solution)/shard_map/ppermute | solution.py:21
  127.8 2.3 %pad_maximum_fusion = bf16[2048,1024]{1,0:T(8,128)(2,1)} fusion(bf16[256,1024]{1,0:T(8,128)(2,1)S(1)} %fusion.3, bf16[1536,1024]{1,0:T(8,128)(2,1)S(1)} %bitcast.60, bf16[256,1024]{1,0:T(8,128)(2,1)S(1)} %fusion.2), kind=kLoop, calls=%fused_computation | loop fusion | flops 12582912 | bytes 8388608 | tf_op jit(solution)/shard_map/concatenate | solution.py:288
  (95 shorter events, 35.3 us)
Async XLA Ops:
  5.0 9.9 %collective-permute-start = (bf16[9,128,512]{2,1,0:T(8,128)(2,1)}, bf16[9,128,512]{2,1,0:T(8,128)(2,1)}, u32[]{:S(2)}, u32[]{:S(2)}) collective-permute-start(bf16[9,128,512]{2,1,0:T(8,128)(2,1)} %get-tuple-element.9), channel_id=1, source_target_pairs={{0,1},{1,0},{2,3},{3,2},{4,5},{5,4},{6,7},{7,6},{8,9},{9,8},{10,11... | collective-permute-start | bytes 3538952 | tf_op jit(solution)/shard_map/ppermute | solution.py:30
  9.7 9.4 %collective-permute-start.2 = (bf16[4,128,512]{2,1,0:T(8,128)(2,1)}, bf16[4,128,512]{2,1,0:T(8,128)(2,1)S(1)}, u32[]{:S(2)}, u32[]{:S(2)}) collective-permute-start(bf16[4,128,512]{2,1,0:T(8,128)(2,1)} %get-tuple-element.12), channel_id=1, source_target_pairs={{0,2},{1,5},{2,0},{3,7},{4,6},{5,1},{6,4},{7,3},{8,10},{9,13},{10,... | collective-permute-start | bytes 1572872 | tf_op jit(solution)/shard_map/ppermute | solution.py:30
  13.2 16.0 %collective-permute-start.16 = (bf16[5,128,512]{2,1,0:T(8,128)(2,1)}, bf16[5,128,512]{2,1,0:T(8,128)(2,1)}, u32[]{:S(2)}, u32[]{:S(2)}) collective-permute-start(bf16[5,128,512]{2,1,0:T(8,128)(2,1)} %slice_select_fusion), channel_id=1, source_target_pairs={{0,2},{1,5},{2,0},{3,7},{4,6},{5,1},{6,4},{7,3},{8,10},{9,13},{10,... | collective-permute-start | bytes 1966088 | tf_op jit(solution)/shard_map/ppermute | solution.py:30
  21.1 11.0 %collective-permute-start.3 = (bf16[4,128,512]{2,1,0:T(8,128)(2,1)}, bf16[4,128,512]{2,1,0:T(8,128)(2,1)S(1)}, u32[]{:S(2)}, u32[]{:S(2)}) collective-permute-start(bf16[4,128,512]{2,1,0:T(8,128)(2,1)} %fusion.21), channel_id=1, source_target_pairs={{0,4},{1,3},{2,6},{3,1},{4,0},{5,7},{6,2},{7,5},{8,12},{9,11},{10,... | collective-permute-start | bytes 1572872 | tf_op jit(solution)/shard_map/ppermute | solution.py:30
  30.5 16.4 %collective-permute-start.17 = (bf16[5,128,512]{2,1,0:T(8,128)(2,1)S(1)}, bf16[5,128,512]{2,1,0:T(8,128)(2,1)S(1)}, u32[]{:S(2)}, u32[]{:S(2)}) collective-permute-start(bf16[5,128,512]{2,1,0:T(8,128)(2,1)S(1)} %fusion.20), channel_id=1, source_target_pairs={{0,4},{1,3},{2,6},{3,1},{4,0},{5,7},{6,2},{7,5},{8,12},{9,11},{10,... | collective-permute-start | bytes 1966088 | tf_op jit(solution)/shard_map/ppermute | solution.py:30
  33.3 15.1 %collective-permute-start.9 = (bf16[4,128,512]{2,1,0:T(8,128)(2,1)S(1)}, bf16[4,128,512]{2,1,0:T(8,128)(2,1)S(1)}, u32[]{:S(2)}, u32[]{:S(2)}) collective-permute-start(bf16[4,128,512]{2,1,0:T(8,128)(2,1)S(1)} %broadcast_select_fusion.1.refs_0_), channel_id=1, source_target_pairs={{0,2},{1,5},{2,0},{3,7},{4,6},{5,1},{6,4},{7,3},{8,10},{9,13},{10,... | collective-permute-start | bytes 1572872 | tf_op jit(solution)/shard_map/ppermute | solution.py:30
  35.7 29.9 %collective-permute-start.10 = (bf16[4,128,512]{2,1,0:T(8,128)(2,1)S(1)}, bf16[4,128,512]{2,1,0:T(8,128)(2,1)S(1)}, u32[]{:S(2)}, u32[]{:S(2)}) collective-permute-start(bf16[4,128,512]{2,1,0:T(8,128)(2,1)S(1)} %broadcast_select_fusion.1.refs_0_), channel_id=1, source_target_pairs={{0,1},{1,0},{2,3},{3,2},{4,5},{5,4},{6,7},{7,6},{8,9},{9,8},{10,11... | collective-permute-start | bytes 1572872 | tf_op jit(solution)/shard_map/ppermute | solution.py:30
  35.8 14.2 %collective-permute-start.4 = (bf16[4,128,512]{2,1,0:T(8,128)(2,1)S(1)}, bf16[4,128,512]{2,1,0:T(8,128)(2,1)S(1)}, u32[]{:S(2)}, u32[]{:S(2)}) collective-permute-start(bf16[4,128,512]{2,1,0:T(8,128)(2,1)S(1)} %after.4), channel_id=1, source_target_pairs={{0,2},{1,5},{2,0},{3,7},{4,6},{5,1},{6,4},{7,3},{8,10},{9,13},{10,... | collective-permute-start | bytes 1572872 | tf_op jit(solution)/shard_map/ppermute | solution.py:30
  47.0 40.4 %collective-permute-start.19 = (bf16[5,128,512]{2,1,0:T(8,128)(2,1)S(1)}, bf16[5,128,512]{2,1,0:T(8,128)(2,1)S(1)}, u32[]{:S(2)}, u32[]{:S(2)}) collective-permute-start(bf16[5,128,512]{2,1,0:T(8,128)(2,1)S(1)} %broadcast_select_fusion.refs_0_), channel_id=1, source_target_pairs={{0,1},{1,0},{2,3},{3,2},{4,5},{5,4},{6,7},{7,6},{8,9},{9,8},{10,11... | collective-permute-start | bytes 1966088 | tf_op jit(solution)/shard_map/ppermute | solution.py:30
  47.0 17.5 %collective-permute-start.18 = (bf16[5,128,512]{2,1,0:T(8,128)(2,1)S(1)}, bf16[5,128,512]{2,1,0:T(8,128)(2,1)S(1)}, u32[]{:S(2)}, u32[]{:S(2)}) collective-permute-start(bf16[5,128,512]{2,1,0:T(8,128)(2,1)S(1)} %broadcast_select_fusion.refs_0_), channel_id=1, source_target_pairs={{0,2},{1,5},{2,0},{3,7},{4,6},{5,1},{6,4},{7,3},{8,10},{9,13},{10,... | collective-permute-start | bytes 1966088 | tf_op jit(solution)/shard_map/ppermute | solution.py:30
  48.4 13.5 %collective-permute-start.23 = (bf16[3,128,512]{2,1,0:T(8,128)(2,1)S(1)}, bf16[3,128,512]{2,1,0:T(8,128)(2,1)S(1)}, u32[]{:S(2)}, u32[]{:S(2)}) collective-permute-start(bf16[3,128,512]{2,1,0:T(8,128)(2,1)S(1)} %after.6), channel_id=1, source_target_pairs={{0,2},{1,5},{2,0},{3,7},{4,6},{5,1},{6,4},{7,3},{8,10},{9,13},{10,... | collective-permute-start | bytes 1179656 | tf_op jit(solution)/shard_map/ppermute | solution.py:30
  50.0 15.6 %collective-permute-start.11 = (bf16[4,128,512]{2,1,0:T(8,128)(2,1)S(1)}, bf16[4,128,512]{2,1,0:T(8,128)(2,1)S(1)}, u32[]{:S(2)}, u32[]{:S(2)}) collective-permute-start(bf16[4,128,512]{2,1,0:T(8,128)(2,1)S(1)} %collective-permute-done.9.refs_1_), channel_id=1, source_target_pairs={{0,1},{1,0},{2,3},{3,2},{4,5},{5,4},{6,7},{7,6},{8,9},{9,8},{10,11... | collective-permute-start | bytes 1572872 | tf_op jit(solution)/shard_map/ppermute | solution.py:30
  61.9 9.2 %collective-permute-start.5 = (bf16[4,128,512]{2,1,0:T(8,128)(2,1)S(1)}, bf16[4,128,512]{2,1,0:T(8,128)(2,1)S(1)}, u32[]{:S(2)}, u32[]{:S(2)}) collective-permute-start(bf16[4,128,512]{2,1,0:T(8,128)(2,1)S(1)} %fusion.22), channel_id=1, source_target_pairs={{0,4},{1,3},{2,6},{3,1},{4,0},{5,7},{6,2},{7,5},{8,12},{9,11},{10,... | collective-permute-start | bytes 1572872 | tf_op jit(solution)/shard_map/ppermute | solution.py:30
  64.5 22.9 %collective-permute-start.20 = (bf16[5,128,512]{2,1,0:T(8,128)(2,1)S(1)}, bf16[5,128,512]{2,1,0:T(8,128)(2,1)S(1)}, u32[]{:S(2)}, u32[]{:S(2)}) collective-permute-start(bf16[5,128,512]{2,1,0:T(8,128)(2,1)S(1)} %collective-permute-done.18.refs_1_), channel_id=1, source_target_pairs={{0,1},{1,0},{2,3},{3,2},{4,5},{5,4},{6,7},{7,6},{8,9},{9,8},{10,11... | collective-permute-start | bytes 1966088 | tf_op jit(solution)/shard_map/ppermute | solution.py:30
  71.1 35.0 %collective-permute-start.7 = (bf16[4,128,512]{2,1,0:T(8,128)(2,1)S(1)}, bf16[4,128,512]{2,1,0:T(8,128)(2,1)S(1)}, u32[]{:S(2)}, u32[]{:S(2)}) collective-permute-start(bf16[4,128,512]{2,1,0:T(8,128)(2,1)S(1)} %broadcast_select_fusion.10.refs_0_), channel_id=1, source_target_pairs={{0,1},{1,0},{2,3},{3,2},{4,5},{5,4},{6,7},{7,6},{8,9},{9,8},{10,11... | collective-permute-start | bytes 1572872 | tf_op jit(solution)/shard_map/ppermute | solution.py:30
  71.8 10.2 %collective-permute-start.12 = (bf16[2,2,128,256]{3,2,1,0:T(8,128)(2,1)S(1)}, bf16[2,2,128,256]{3,2,1,0:T(8,128)(2,1)S(1)}, u32[]{:S(2)}, u32[]{:S(2)}) collective-permute-start(bf16[2,2,128,256]{3,2,1,0:T(8,128)(2,1)S(1)} %after.5), channel_id=1, source_target_pairs={{0,8},{8,16},{16,24},{1,9},{9,17},{17,25},{2,10},{10,18},{18,26},{... | collective-permute-start | bytes 786440 | tf_op jit(solution)/shard_map/ppermute | solution.py:12
  75.1 8.1 %collective-permute-start.24 = (bf16[3,128,512]{2,1,0:T(8,128)(2,1)S(1)}, bf16[3,128,512]{2,1,0:T(8,128)(2,1)S(1)}, u32[]{:S(2)}, u32[]{:S(2)}) collective-permute-start(bf16[3,128,512]{2,1,0:T(8,128)(2,1)S(1)} %after.7), channel_id=1, source_target_pairs={{0,4},{1,3},{2,6},{3,1},{4,0},{5,7},{6,2},{7,5},{8,12},{9,11},{10,... | collective-permute-start | bytes 1179656 | tf_op jit(solution)/shard_map/ppermute | solution.py:30
  82.1 10.9 %collective-permute-start.6 = (bf16[4,128,512]{2,1,0:T(8,128)(2,1)S(1)}, bf16[4,128,512]{2,1,0:T(8,128)(2,1)S(1)}, u32[]{:S(2)}, u32[]{:S(2)}) collective-permute-start(bf16[4,128,512]{2,1,0:T(8,128)(2,1)S(1)} %broadcast_select_fusion.10.refs_0_), channel_id=1, source_target_pairs={{0,2},{1,5},{2,0},{3,7},{4,6},{5,1},{6,4},{7,3},{8,10},{9,13},{10,... | collective-permute-start | bytes 1572872 | tf_op jit(solution)/shard_map/ppermute | solution.py:30
  83.3 15.1 %collective-permute-start.14 = (bf16[256,1024]{1,0:T(8,128)(2,1)S(1)}, bf16[256,1024]{1,0:T(8,128)(2,1)S(1)}, u32[]{:S(2)}, u32[]{:S(2)}) collective-permute-start(bf16[256,1024]{1,0:T(8,128)(2,1)S(1)} %get-tuple-element.17), channel_id=1, source_target_pairs={{8,16},{16,8},{9,17},{17,9},{10,18},{18,10},{11,19},{19,11},{12,20... | collective-permute-start | bytes 1572872 | tf_op jit(solution)/shard_map/ppermute | solution.py:21
  87.3 12.4 %collective-permute-start.15 = (bf16[256,1024]{1,0:T(8,128)(2,1)S(1)}, bf16[256,1024]{1,0:T(8,128)(2,1)S(1)}, u32[]{:S(2)}, u32[]{:S(2)}) collective-permute-start(bf16[256,1024]{1,0:T(8,128)(2,1)S(1)} %get-tuple-element.18), channel_id=1, source_target_pairs={{0,8},{16,24},{8,0},{24,16},{1,9},{17,25},{9,1},{25,17},{2,10},{18... | collective-permute-start | bytes 1572872 | tf_op jit(solution)/shard_map/ppermute | solution.py:21
  87.4 13.0 %collective-permute-start.13 = (bf16[2,2,128,256]{3,2,1,0:T(8,128)(2,1)S(1)}, bf16[2,2,128,256]{3,2,1,0:T(8,128)(2,1)S(1)}, u32[]{:S(2)}, u32[]{:S(2)}) collective-permute-start(bf16[2,2,128,256]{3,2,1,0:T(8,128)(2,1)S(1)} %collective-permute-done.12), channel_id=1, source_target_pairs={{0,1},{1,0},{2,3},{3,2},{4,5},{5,4},{6,7},{7,6},{8,9},{9,8},{10,11... | collective-permute-start | bytes 786440 | tf_op jit(solution)/shard_map/ppermute | solution.py:30
  93.0 20.2 %collective-permute-start.26 = (bf16[3,128,512]{2,1,0:T(8,128)(2,1)S(1)}, bf16[3,128,512]{2,1,0:T(8,128)(2,1)S(1)}, u32[]{:S(2)}, u32[]{:S(2)}) collective-permute-start(bf16[3,128,512]{2,1,0:T(8,128)(2,1)S(1)} %broadcast_select_fusion.11.refs_0_), channel_id=1, source_target_pairs={{0,1},{1,0},{2,3},{3,2},{4,5},{5,4},{6,7},{7,6},{8,9},{9,8},{10,11... | collective-permute-start | bytes 1179656 | tf_op jit(solution)/shard_map/ppermute | solution.py:30
  109.6 16.2 %collective-permute-start.21 = (bf16[256,1024]{1,0:T(8,128)(2,1)S(1)}, bf16[256,1024]{1,0:T(8,128)(2,1)S(1)}, u32[]{:S(2)}, u32[]{:S(2)}) collective-permute-start(bf16[256,1024]{1,0:T(8,128)(2,1)S(1)} %get-tuple-element.15), channel_id=1, source_target_pairs={{8,16},{16,8},{9,17},{17,9},{10,18},{18,10},{11,19},{19,11},{12,20... | collective-permute-start | bytes 1572872 | tf_op jit(solution)/shard_map/ppermute | solution.py:21
  112.7 14.1 %collective-permute-start.22 = (bf16[256,1024]{1,0:T(8,128)(2,1)S(1)}, bf16[256,1024]{1,0:T(8,128)(2,1)S(1)}, u32[]{:S(2)}, u32[]{:S(2)}) collective-permute-start(bf16[256,1024]{1,0:T(8,128)(2,1)S(1)} %get-tuple-element.16), channel_id=1, source_target_pairs={{0,8},{16,24},{8,0},{24,16},{1,9},{17,25},{9,1},{25,17},{2,10},{18... | collective-permute-start | bytes 1572872 | tf_op jit(solution)/shard_map/ppermute | solution.py:21
  (9 other events, 39.6 us)

commit v8 on v5

--- a/solution.py
+++ b/solution.py
@@ -227,6 +227,51 @@
     return product.astype(jnp.bfloat16)
 
 
+def write_inner(inner, border):
+    rows, cols = inner.shape
+
+    def kernel(source, out):
+        out[...] = source[...]
+
+    return pl.pallas_call(
+        kernel,
+        grid=(rows // border,),
+        out_shape=jax.ShapeDtypeStruct((rows + 2 * border, cols), inner.dtype),
+        in_specs=[pl.BlockSpec((border, cols), lambda i: (i, 0))],
+        out_specs=pl.BlockSpec((border, cols), lambda i: (i + 1, 0)),
+        compiler_params=pltpu.CompilerParams(vmem_limit_bytes=8 << 20),
+        cost_estimate=pl.CostEstimate(flops=0, bytes_accessed=4 * inner.size, transcendentals=0),
+        name="write_inner",
+    )(inner)
+
+
+def write_outer(whole, top, low):
+    border, cols = top.shape
+    last = whole.shape[0] // border - 1
+
+    def kernel(_, first, final, out):
+        @pl.when(pl.program_id(0) == 0)
+        def _():
+            out[...] = first[...]
+
+        @pl.when(pl.program_id(0) == 1)
+        def _():
+            out[...] = final[...]
+
+    block = pl.BlockSpec((border, cols), lambda i: (0, 0))
+    return pl.pallas_call(
+        kernel,
+        grid=(2,),
+        out_shape=jax.ShapeDtypeStruct(whole.shape, whole.dtype),
+        in_specs=[ANY, block, block],
+        out_specs=pl.BlockSpec((border, cols), lambda i: (i * last, 0)),
+        input_output_aliases={0: 0},
+        compiler_params=pltpu.CompilerParams(vmem_limit_bytes=8 << 20),
+        cost_estimate=pl.CostEstimate(flops=0, bytes_accessed=8 * top.size, transcendentals=0),
+        name="write_outer",
+    )(whole, top, low)
+
+
 def local(slab, transforms, owners):
     row_block = lax.axis_index("rows")
     last_block = lax.axis_size("rows") - 1
@@ -268,8 +313,10 @@
                 crosses[q], above_crosses[q] = edges[k], from_above[k]
             edges = edges[n:]
         prev, cross = above_crosses[r], crosses[r]
-        head_rows = apply(edges[0], matrix[:window])
-        tail_rows = apply(edges[1], matrix[local_rows - window :])
+        outer = apply_many(
+            edges[:2], jnp.stack([matrix[:window], matrix[local_rows - window :]])
+        )
+        head_rows, tail_rows = outer[0], outer[1]
         begin, end = head_rows[:border], tail_rows[border:]
         above, below = swap_rows(begin, end)
         rest = spread.join(*tail)
@@ -289,8 +336,9 @@
         low = jnp.where(row_block == last_block, end, low)
         top = apply(prev, jnp.concatenate([above, begin], 0))
         top = jnp.where(row_block == 0, begin, top)
-        matrix = jnp.concatenate([top, inner, low], 0)
-    return matrix
+        if r < rounds - 1:
+            matrix = jnp.concatenate([top, inner, low], 0)
+    return write_outer(write_inner(inner, border), top, low)
 
 
 def solution(mesh):

time: 118 us -> 117 us (level)
  Pallas kernels: 4.3 us -> 8.02 us
  other arithmetic: 13.2 us -> 10 us
  starting transfers between devices: 26 us -> 27.8 us
  waiting for transfers between devices: 51.1 us -> 49.6 us
    ppermute x4, waiting for transfers between devices: 12.7 us -> 8.91 us  [swap(): return lax.ppermute(value, 'rows', pairs + [(b, a) for a, b in pairs])]
    pallas_call x0 -> x2, Pallas kernels: none -> 3.72 us  [the longest x1 2.68 us: write_inner(): pl.pallas_call(kernel, grid=(rows // border,), out_shape=jax.ShapeDtypeSt...]
    dot_general x4 -> x6, matrix products: 7.04 us -> 10.1 us  [apply_many(): jnp.einsum('nab,nac->nbc', q, x, preferred_element_type=jnp.float32)]
    dot_general x8 -> x4, matrix products: 4.8 us -> 1.84 us  [apply(): lax.dot_general(q, x, (((0,), (0,)), ((), ())), preferred_element_type=jn...]
    concatenate x1 -> x0, other arithmetic: 2.29 us -> none  [local(): matrix = jnp.concatenate([top, inner, low], 0)]
    ppermute x23, waiting for transfers between devices: 36.8 us -> 39 us  [flip(): lax.ppermute(value, 'cols', [(d, d ^ 1 << bits[d & 1]) for d in range(cou...]
    ppermute x4, starting transfers between devices: 6.17 us -> 7.64 us  [swap(): return lax.ppermute(value, 'rows', pairs + [(b, a) for a, b in pairs])]
    unnamed x8, local copies, waits for them, and re-layouts: 3.52 us -> 2.22 us
  transfers between devices with their start and end apart: 28 -> 28, of which waited for: 12 -> 12; matrix products, arithmetic and copies ran while one was open for 17% -> 16% of each run, Pallas kernels for 3% -> 5%
where the time goes in v8:
time: 117 us; the launch traced here: 116 us
  waiting for transfers between devices  49.6 us (42%)
  starting transfers between devices  27.8 us (24%)
  matrix products  11.9 us (10%)
  other arithmetic  10 us (9%)
  Pallas kernels  8.02 us (7%)
  local copies, waits for them, and re-layouts  4.96 us (4%)
  between operations  4 us (3%)
    ppermute x23, waiting for transfers between devices, flip(): lax.ppermute(value, 'cols', [(d, d ^ 1 << bits[d & 1]) for d in range(cou...  39 us
    ppermute x23, starting transfers between devices, flip(): lax.ppermute(value, 'cols', [(d, d ^ 1 << bits[d & 1]) for d in range(cou...  16.7 us
    dot_general x6, matrix products, apply_many(): jnp.einsum('nab,nac->nbc', q, x, preferred_element_type=jnp.float32)  10.1 us
    ppermute x4, waiting for transfers between devices, swap(): return lax.ppermute(value, 'rows', pairs + [(b, a) for a, b in pairs])  8.91 us
    select_n x11, other arithmetic, choose(): return jnp.where(mask, yes, no)  8.75 us
    ppermute x4, starting transfers between devices, swap(): return lax.ppermute(value, 'rows', pairs + [(b, a) for a, b in pairs])  7.64 us
    ppermute x1, starting transfers between devices, shifted(): lax.ppermute(value, axis, [(source, source + steps) for source in range(i...  3.48 us
    pallas_call x2, Pallas kernels, cut_slot(): pl.pallas_call(kernel, out_shape=shapes, in_specs=[pl.BlockSpec(memory_sp...  2.73 us
  transfers between devices with their start and end apart: 28, of which 12 were waited for; matrix products, arithmetic and copies ran while one was open for 16% of the time, Pallas kernels for 5%

profile of v8, /device:TPU:8, one launch (start us, length us, event | category | flops | bytes accessed | tf_op | source)
XLA Modules:
  0.0 116.3 jit_solution(11269041588061812014)
XLA Ops:
  0.0 2.2 %copy-done.2 = bf16[1,4096,512]{2,1,0:T(8,128)(2,1)S(1)} copy-done((bf16[1,4096,512]{2,1,0:T(8,128)(2,1)S(1)}, bf16[1,4096,512]{2,1,0:T(8,128)(2,1)}, u32[]{:S(2)}) %copy-start.2) | copy-done | bytes 4194328
  3.1 1.9 %cut_slot.2 = (bf16[9,128,512]{2,1,0:T(8,128)(2,1)S(1)}, bf16[9,128,512]{2,1,0:T(8,128)(2,1)}, bf16[9,128,512]{2,1,0:T(8,128)(2,1)S(1)}) custom-call(bf16[8,2,2,128,512]{4,3,2,1,0:T(8,128)(2,1)S(1)} %bitcast.84), custom_call_target="tpu_custom_call" | custom-call | bytes 6291456 | tf_op jit(solution)/shard_map/cut_slot/pallas_call | solution.py:105
  11.3 1.6 %collective-permute-start.9 = (bf16[4,128,512]{2,1,0:T(8,128)(2,1)S(1)}, bf16[4,128,512]{2,1,0:T(8,128)(2,1)S(1)}, u32[]{:S(2)}, u32[]{:S(2)}) collective-permute-start(bf16[4,128,512]{2,1,0:T(8,128)(2,1)S(1)} %get-tuple-element.15), channel_id=1, source_target_pairs={{0,2},{1,5},{2,0},{3,7},{4,6},{5,1},{6,4},{7,3},{8,10},{9,13},{10,... | collective-permute-start | bytes 1572872 | tf_op jit(solution)/shard_map/ppermute | solution.py:30
  14.8 5.7 %collective-permute-done.9 = bf16[4,128,512]{2,1,0:T(8,128)(2,1)S(1)} collective-permute-done((bf16[4,128,512]{2,1,0:T(8,128)(2,1)S(1)}, bf16[4,128,512]{2,1,0:T(8,128)(2,1)S(1)}, u32[]{:S(2)}, u32[]{:S(2)}) %collective-permute-start.9) | collective-permute-done | bytes 524320 | tf_op jit(solution)/shard_map/ppermute | solution.py:30
  21.7 1.6 %collective-permute-start.10 = (bf16[4,128,512]{2,1,0:T(8,128)(2,1)S(1)}, bf16[4,128,512]{2,1,0:T(8,128)(2,1)S(1)}, u32[]{:S(2)}, u32[]{:S(2)}) collective-permute-start(bf16[4,128,512]{2,1,0:T(8,128)(2,1)S(1)} %fusion.33), channel_id=1, source_target_pairs={{0,4},{1,3},{2,6},{3,1},{4,0},{5,7},{6,2},{7,5},{8,12},{9,11},{10,... | collective-permute-start | bytes 1572872 | tf_op jit(solution)/shard_map/ppermute | solution.py:30
  23.3 8.1 %collective-permute-done.2 = bf16[5,128,512]{2,1,0:T(8,128)(2,1)S(1)} collective-permute-done((bf16[5,128,512]{2,1,0:T(8,128)(2,1)S(1)}, bf16[5,128,512]{2,1,0:T(8,128)(2,1)S(1)}, u32[]{:S(2)}, u32[]{:S(2)}) %collective-permute-start.2) | collective-permute-done | bytes 655392 | tf_op jit(solution)/shard_map/ppermute | solution.py:30
  32.6 1.6 %collective-permute-start.3 = (bf16[5,128,512]{2,1,0:T(8,128)(2,1)S(1)}, bf16[5,128,512]{2,1,0:T(8,128)(2,1)S(1)}, u32[]{:S(2)}, u32[]{:S(2)}) collective-permute-start(bf16[5,128,512]{2,1,0:T(8,128)(2,1)S(1)} %fusion.32), channel_id=1, source_target_pairs={{0,4},{1,3},{2,6},{3,1},{4,0},{5,7},{6,2},{7,5},{8,12},{9,11},{10,... | collective-permute-start | bytes 1966088 | tf_op jit(solution)/shard_map/ppermute | solution.py:30
  35.4 1.6 %collective-permute-start.11 = (bf16[4,128,512]{2,1,0:T(8,128)(2,1)S(1)}, bf16[4,128,512]{2,1,0:T(8,128)(2,1)S(1)}, u32[]{:S(2)}, u32[]{:S(2)}) collective-permute-start(bf16[4,128,512]{2,1,0:T(8,128)(2,1)S(1)} %after.3), channel_id=1, source_target_pairs={{0,2},{1,5},{2,0},{3,7},{4,6},{5,1},{6,4},{7,3},{8,10},{9,13},{10,... | collective-permute-start | bytes 1572872 | tf_op jit(solution)/shard_map/ppermute | solution.py:30
  37.7 12.5 %collective-permute-done.3.refs_0_ = bf16[5,128,512]{2,1,0:T(8,128)(2,1)S(1)} collective-permute-done((bf16[5,128,512]{2,1,0:T(8,128)(2,1)S(1)}, bf16[5,128,512]{2,1,0:T(8,128)(2,1)S(1)}, u32[]{:S(2)}, u32[]{:S(2)}) %collective-permute-start.3) | collective-permute-done | bytes 655392 | tf_op jit(solution)/shard_map/ppermute | solution.py:30
  50.5 1.6 %collective-permute-start.4 = (bf16[3,128,512]{2,1,0:T(8,128)(2,1)S(1)}, bf16[3,128,512]{2,1,0:T(8,128)(2,1)S(1)}, u32[]{:S(2)}, u32[]{:S(2)}) collective-permute-start(bf16[3,128,512]{2,1,0:T(8,128)(2,1)S(1)} %after.2), channel_id=1, source_target_pairs={{0,2},{1,5},{2,0},{3,7},{4,6},{5,1},{6,4},{7,3},{8,10},{9,13},{10,... | collective-permute-start | bytes 1179656 | tf_op jit(solution)/shard_map/ppermute | solution.py:30
  53.9 1.6 %collective-permute-start.12 = (bf16[4,128,512]{2,1,0:T(8,128)(2,1)S(1)}, bf16[4,128,512]{2,1,0:T(8,128)(2,1)S(1)}, u32[]{:S(2)}, u32[]{:S(2)}) collective-permute-start(bf16[4,128,512]{2,1,0:T(8,128)(2,1)S(1)} %fusion.34), channel_id=1, source_target_pairs={{0,4},{1,3},{2,6},{3,1},{4,0},{5,7},{6,2},{7,5},{8,12},{9,11},{10,... | collective-permute-start | bytes 1572872 | tf_op jit(solution)/shard_map/ppermute | solution.py:30
  55.5 3.5 %collective-permute-start.19 = (bf16[2,2,128,256]{3,2,1,0:T(8,128)(2,1)S(1)}, bf16[2,2,128,256]{3,2,1,0:T(8,128)(2,1)S(1)}, u32[]{:S(2)}, u32[]{:S(2)}) collective-permute-start(bf16[2,2,128,256]{3,2,1,0:T(8,128)(2,1)S(1)} %pad_maximum_fusion.4), channel_id=1, source_target_pairs={{0,8},{8,16},{16,24},{1,9},{9,17},{17,25},{2,10},{10,18},{18,26},{... | collective-permute-start | bytes 786440 | tf_op jit(solution)/shard_map/ppermute | solution.py:12
  59.0 2.2 %collective-permute-done.4 = bf16[3,128,512]{2,1,0:T(8,128)(2,1)S(1)} collective-permute-done((bf16[3,128,512]{2,1,0:T(8,128)(2,1)S(1)}, bf16[3,128,512]{2,1,0:T(8,128)(2,1)S(1)}, u32[]{:S(2)}, u32[]{:S(2)}) %collective-permute-start.4) | collective-permute-done | bytes 393248 | tf_op jit(solution)/shard_map/ppermute | solution.py:30
  62.3 1.6 %collective-permute-done.19 = bf16[2,2,128,256]{3,2,1,0:T(8,128)(2,1)S(1)} collective-permute-done((bf16[2,2,128,256]{3,2,1,0:T(8,128)(2,1)S(1)}, bf16[2,2,128,256]{3,2,1,0:T(8,128)(2,1)S(1)}, u32[]{:S(2)}, u32[]{:S(2)}) %collective-permute-start.19) | collective-permute-done | bytes 262176 | tf_op jit(solution)/shard_map/ppermute | solution.py:12
  63.9 4.9 %collective-permute-done.12 = bf16[4,128,512]{2,1,0:T(8,128)(2,1)S(1)} collective-permute-done((bf16[4,128,512]{2,1,0:T(8,128)(2,1)S(1)}, bf16[4,128,512]{2,1,0:T(8,128)(2,1)S(1)}, u32[]{:S(2)}, u32[]{:S(2)}) %collective-permute-start.12) | collective-permute-done | bytes 524320 | tf_op jit(solution)/shard_map/ppermute | solution.py:30
  72.8 4.4 %collective-permute-done.5 = bf16[3,128,512]{2,1,0:T(8,128)(2,1)S(1)} collective-permute-done((bf16[3,128,512]{2,1,0:T(8,128)(2,1)S(1)}, bf16[3,128,512]{2,1,0:T(8,128)(2,1)S(1)}, u32[]{:S(2)}, u32[]{:S(2)}) %collective-permute-start.5) | collective-permute-done | bytes 393248 | tf_op jit(solution)/shard_map/ppermute | solution.py:30
  80.2 3.7 %collective-permute-start.21 = (bf16[256,1024]{1,0:T(8,128)(2,1)S(1)}, bf16[256,1024]{1,0:T(8,128)(2,1)S(1)}, u32[]{:S(2)}, u32[]{:S(2)}) collective-permute-start(bf16[256,1024]{1,0:T(8,128)(2,1)S(1)} %get-tuple-element.29), channel_id=1, source_target_pairs={{8,16},{16,8},{9,17},{17,9},{10,18},{18,10},{11,19},{19,11},{12,20... | collective-permute-start | bytes 1572872 | tf_op jit(solution)/shard_map/ppermute | solution.py:21
  87.4 2.1 %convolution_convert_fusion = bf16[3,512,1024]{2,1,0:T(8,128)(2,1)S(1)} fusion(bf16[5,512,512]{2,1,0:T(8,128)(2,1)S(1)} %place.9, bf16[3,512,1024]{2,1,0:T(8,128)(2,1)S(1)} %bitcast.89), kind=kOutput, calls=%fused_computation.2 | convolution fusion | flops 1612185600 | bytes 8912896 | tf_op jit(solution)/shard_map/nab,nac->nbc/dot_general | solution.py:226
  91.4 1.7 %collective-permute-done.22 = bf16[256,1024]{1,0:T(8,128)(2,1)S(1)} collective-permute-done((bf16[256,1024]{1,0:T(8,128)(2,1)S(1)}, bf16[256,1024]{1,0:T(8,128)(2,1)S(1)}, u32[]{:S(2)}, u32[]{:S(2)}) %collective-permute-start.22) | collective-permute-done | bytes 524320 | tf_op jit(solution)/shard_map/ppermute | solution.py:21
  98.7 3.6 %collective-permute-start.26 = (bf16[256,1024]{1,0:T(8,128)(2,1)S(1)}, bf16[256,1024]{1,0:T(8,128)(2,1)S(1)}, u32[]{:S(2)}, u32[]{:S(2)}) collective-permute-start(bf16[256,1024]{1,0:T(8,128)(2,1)S(1)} %get-tuple-element.24), channel_id=1, source_target_pairs={{8,16},{16,8},{9,17},{17,9},{10,18},{18,10},{11,19},{19,11},{12,20... | collective-permute-start | bytes 1572872 | tf_op jit(solution)/shard_map/ppermute | solution.py:21
  102.7 1.9 %convolution_convert_fusion.1 = bf16[3,512,1024]{2,1,0:T(8,128)(2,1)S(1)} fusion(bf16[3,512,512]{2,1,0:T(8,128)(2,1)S(1)} %place.5, bf16[3,512,1024]{2,1,0:T(8,128)(2,1)S(1)} %bitcast.90), kind=kOutput, calls=%fused_computation.3 | convolution fusion | flops 1612185600 | bytes 7864320 | tf_op jit(solution)/shard_map/nab,nac->nbc/dot_general | solution.py:226
  104.6 2.7 %write_inner.1._ = bf16[2048,1024]{1,0:T(8,128)(2,1)} custom-call(bf16[1536,1024]{1,0:T(8,128)(2,1)S(1)} %bitcast.85), custom_call_target="tpu_custom_call" | custom-call | bytes 6291456 | tf_op jit(solution)/shard_map/write_inner/pallas_call | solution.py:236
  107.3 3.9 %collective-permute-done.27 = bf16[256,1024]{1,0:T(8,128)(2,1)S(1)} collective-permute-done((bf16[256,1024]{1,0:T(8,128)(2,1)S(1)}, bf16[256,1024]{1,0:T(8,128)(2,1)S(1)}, u32[]{:S(2)}, u32[]{:S(2)}) %collective-permute-start.27) | collective-permute-done | bytes 524320 | tf_op jit(solution)/shard_map/ppermute | solution.py:21
  111.2 3.0 %collective-permute-done.26 = bf16[256,1024]{1,0:T(8,128)(2,1)S(1)} collective-permute-done((bf16[256,1024]{1,0:T(8,128)(2,1)S(1)}, bf16[256,1024]{1,0:T(8,128)(2,1)S(1)}, u32[]{:S(2)}, u32[]{:S(2)}) %collective-permute-start.26) | collective-permute-done | bytes 524320 | tf_op jit(solution)/shard_map/ppermute | solution.py:21
  (96 shorter events, 33.1 us)
Async XLA Ops:
  5.0 9.7 %collective-permute-start = (bf16[9,128,512]{2,1,0:T(8,128)(2,1)}, bf16[9,128,512]{2,1,0:T(8,128)(2,1)}, u32[]{:S(2)}, u32[]{:S(2)}) collective-permute-start(bf16[9,128,512]{2,1,0:T(8,128)(2,1)} %get-tuple-element.9), channel_id=1, source_target_pairs={{0,1},{1,0},{2,3},{3,2},{4,5},{5,4},{6,7},{7,6},{8,9},{9,8},{10,11... | collective-permute-start | bytes 3538952 | tf_op jit(solution)/shard_map/ppermute | solution.py:30
  11.3 9.2 %collective-permute-start.9 = (bf16[4,128,512]{2,1,0:T(8,128)(2,1)S(1)}, bf16[4,128,512]{2,1,0:T(8,128)(2,1)S(1)}, u32[]{:S(2)}, u32[]{:S(2)}) collective-permute-start(bf16[4,128,512]{2,1,0:T(8,128)(2,1)S(1)} %get-tuple-element.15), channel_id=1, source_target_pairs={{0,2},{1,5},{2,0},{3,7},{4,6},{5,1},{6,4},{7,3},{8,10},{9,13},{10,... | collective-permute-start | bytes 1572872 | tf_op jit(solution)/shard_map/ppermute | solution.py:30
  14.0 17.4 %collective-permute-start.2 = (bf16[5,128,512]{2,1,0:T(8,128)(2,1)S(1)}, bf16[5,128,512]{2,1,0:T(8,128)(2,1)S(1)}, u32[]{:S(2)}, u32[]{:S(2)}) collective-permute-start(bf16[5,128,512]{2,1,0:T(8,128)(2,1)S(1)} %slice_select_fusion), channel_id=1, source_target_pairs={{0,2},{1,5},{2,0},{3,7},{4,6},{5,1},{6,4},{7,3},{8,10},{9,13},{10,... | collective-permute-start | bytes 1966088 | tf_op jit(solution)/shard_map/ppermute | solution.py:30
  21.7 13.6 %collective-permute-start.10 = (bf16[4,128,512]{2,1,0:T(8,128)(2,1)S(1)}, bf16[4,128,512]{2,1,0:T(8,128)(2,1)S(1)}, u32[]{:S(2)}, u32[]{:S(2)}) collective-permute-start(bf16[4,128,512]{2,1,0:T(8,128)(2,1)S(1)} %fusion.33), channel_id=1, source_target_pairs={{0,4},{1,3},{2,6},{3,1},{4,0},{5,7},{6,2},{7,5},{8,12},{9,11},{10,... | collective-permute-start | bytes 1572872 | tf_op jit(solution)/shard_map/ppermute | solution.py:30
  32.6 17.6 %collective-permute-start.3 = (bf16[5,128,512]{2,1,0:T(8,128)(2,1)S(1)}, bf16[5,128,512]{2,1,0:T(8,128)(2,1)S(1)}, u32[]{:S(2)}, u32[]{:S(2)}) collective-permute-start(bf16[5,128,512]{2,1,0:T(8,128)(2,1)S(1)} %fusion.32), channel_id=1, source_target_pairs={{0,4},{1,3},{2,6},{3,1},{4,0},{5,7},{6,2},{7,5},{8,12},{9,11},{10,... | collective-permute-start | bytes 1966088 | tf_op jit(solution)/shard_map/ppermute | solution.py:30
  35.4 17.4 %collective-permute-start.11 = (bf16[4,128,512]{2,1,0:T(8,128)(2,1)S(1)}, bf16[4,128,512]{2,1,0:T(8,128)(2,1)S(1)}, u32[]{:S(2)}, u32[]{:S(2)}) collective-permute-start(bf16[4,128,512]{2,1,0:T(8,128)(2,1)S(1)} %after.3), channel_id=1, source_target_pairs={{0,2},{1,5},{2,0},{3,7},{4,6},{5,1},{6,4},{7,3},{8,10},{9,13},{10,... | collective-permute-start | bytes 1572872 | tf_op jit(solution)/shard_map/ppermute | solution.py:30
  37.0 33.4 %collective-permute-start.17 = (bf16[4,128,512]{2,1,0:T(8,128)(2,1)S(1)}, bf16[4,128,512]{2,1,0:T(8,128)(2,1)S(1)}, u32[]{:S(2)}, u32[]{:S(2)}) collective-permute-start(bf16[4,128,512]{2,1,0:T(8,128)(2,1)S(1)} %broadcast_select_fusion.1.refs_0_), channel_id=1, source_target_pairs={{0,1},{1,0},{2,3},{3,2},{4,5},{5,4},{6,7},{7,6},{8,9},{9,8},{10,11... | collective-permute-start | bytes 1572872 | tf_op jit(solution)/shard_map/ppermute | solution.py:30
  37.1 18.4 %collective-permute-start.16 = (bf16[4,128,512]{2,1,0:T(8,128)(2,1)S(1)}, bf16[4,128,512]{2,1,0:T(8,128)(2,1)S(1)}, u32[]{:S(2)}, u32[]{:S(2)}) collective-permute-start(bf16[4,128,512]{2,1,0:T(8,128)(2,1)S(1)} %broadcast_select_fusion.1.refs_0_), channel_id=1, source_target_pairs={{0,2},{1,5},{2,0},{3,7},{4,6},{5,1},{6,4},{7,3},{8,10},{9,13},{10,... | collective-permute-start | bytes 1572872 | tf_op jit(solution)/shard_map/ppermute | solution.py:30
  50.5 10.8 %collective-permute-start.4 = (bf16[3,128,512]{2,1,0:T(8,128)(2,1)S(1)}, bf16[3,128,512]{2,1,0:T(8,128)(2,1)S(1)}, u32[]{:S(2)}, u32[]{:S(2)}) collective-permute-start(bf16[3,128,512]{2,1,0:T(8,128)(2,1)S(1)} %after.2), channel_id=1, source_target_pairs={{0,2},{1,5},{2,0},{3,7},{4,6},{5,1},{6,4},{7,3},{8,10},{9,13},{10,... | collective-permute-start | bytes 1179656 | tf_op jit(solution)/shard_map/ppermute | solution.py:30
  52.1 18.4 %collective-permute-start.23 = (bf16[5,128,512]{2,1,0:T(8,128)(2,1)S(1)}, bf16[5,128,512]{2,1,0:T(8,128)(2,1)S(1)}, u32[]{:S(2)}, u32[]{:S(2)}) collective-permute-start(bf16[5,128,512]{2,1,0:T(8,128)(2,1)S(1)} %broadcast_select_fusion.refs_0_), channel_id=1, source_target_pairs={{0,2},{1,5},{2,0},{3,7},{4,6},{5,1},{6,4},{7,3},{8,10},{9,13},{10,... | collective-permute-start | bytes 1966088 | tf_op jit(solution)/shard_map/ppermute | solution.py:30
  53.9 14.9 %collective-permute-start.12 = (bf16[4,128,512]{2,1,0:T(8,128)(2,1)S(1)}, bf16[4,128,512]{2,1,0:T(8,128)(2,1)S(1)}, u32[]{:S(2)}, u32[]{:S(2)}) collective-permute-start(bf16[4,128,512]{2,1,0:T(8,128)(2,1)S(1)} %fusion.34), channel_id=1, source_target_pairs={{0,4},{1,3},{2,6},{3,1},{4,0},{5,7},{6,2},{7,5},{8,12},{9,11},{10,... | collective-permute-start | bytes 1572872 | tf_op jit(solution)/shard_map/ppermute | solution.py:30
  55.5 8.4 %collective-permute-start.19 = (bf16[2,2,128,256]{3,2,1,0:T(8,128)(2,1)S(1)}, bf16[2,2,128,256]{3,2,1,0:T(8,128)(2,1)S(1)}, u32[]{:S(2)}, u32[]{:S(2)}) collective-permute-start(bf16[2,2,128,256]{3,2,1,0:T(8,128)(2,1)S(1)} %pad_maximum_fusion.4), channel_id=1, source_target_pairs={{0,8},{8,16},{16,24},{1,9},{9,17},{17,25},{2,10},{10,18},{18,26},{... | collective-permute-start | bytes 786440 | tf_op jit(solution)/shard_map/ppermute | solution.py:12
  61.2 9.8 %collective-permute-start.18 = (bf16[4,128,512]{2,1,0:T(8,128)(2,1)S(1)}, bf16[4,128,512]{2,1,0:T(8,128)(2,1)S(1)}, u32[]{:S(2)}, u32[]{:S(2)}) collective-permute-start(bf16[4,128,512]{2,1,0:T(8,128)(2,1)S(1)} %collective-permute-done.16.refs_1_), channel_id=1, source_target_pairs={{0,1},{1,0},{2,3},{3,2},{4,5},{5,4},{6,7},{7,6},{8,9},{9,8},{10,11... | collective-permute-start | bytes 1572872 | tf_op jit(solution)/shard_map/ppermute | solution.py:30
  63.9 16.2 %collective-permute-start.24 = (bf16[5,128,512]{2,1,0:T(8,128)(2,1)S(1)}, bf16[5,128,512]{2,1,0:T(8,128)(2,1)S(1)}, u32[]{:S(2)}, u32[]{:S(2)}) collective-permute-start(bf16[5,128,512]{2,1,0:T(8,128)(2,1)S(1)} %broadcast_select_fusion.refs_0_), channel_id=1, source_target_pairs={{0,1},{1,0},{2,3},{3,2},{4,5},{5,4},{6,7},{7,6},{8,9},{9,8},{10,11... | collective-permute-start | bytes 1966088 | tf_op jit(solution)/shard_map/ppermute | solution.py:30
  68.8 8.4 %collective-permute-start.5 = (bf16[3,128,512]{2,1,0:T(8,128)(2,1)S(1)}, bf16[3,128,512]{2,1,0:T(8,128)(2,1)S(1)}, u32[]{:S(2)}, u32[]{:S(2)}) collective-permute-start(bf16[3,128,512]{2,1,0:T(8,128)(2,1)S(1)} %fusion.35), channel_id=1, source_target_pairs={{0,4},{1,3},{2,6},{3,1},{4,0},{5,7},{6,2},{7,5},{8,12},{9,11},{10,... | collective-permute-start | bytes 1179656 | tf_op jit(solution)/shard_map/ppermute | solution.py:30
  70.4 8.4 %collective-permute-start.20 = (bf16[2,2,128,256]{3,2,1,0:T(8,128)(2,1)S(1)}, bf16[2,2,128,256]{3,2,1,0:T(8,128)(2,1)S(1)}, u32[]{:S(2)}, u32[]{:S(2)}) collective-permute-start(bf16[2,2,128,256]{3,2,1,0:T(8,128)(2,1)S(1)} %collective-permute-done.19), channel_id=1, source_target_pairs={{0,1},{1,0},{2,3},{3,2},{4,5},{5,4},{6,7},{7,6},{8,9},{9,8},{10,11... | collective-permute-start | bytes 786440 | tf_op jit(solution)/shard_map/ppermute | solution.py:30
  70.5 13.3 %collective-permute-start.25 = (bf16[5,128,512]{2,1,0:T(8,128)(2,1)S(1)}, bf16[5,128,512]{2,1,0:T(8,128)(2,1)S(1)}, u32[]{:S(2)}, u32[]{:S(2)}) collective-permute-start(bf16[5,128,512]{2,1,0:T(8,128)(2,1)S(1)} %collective-permute-done.23.refs_1_), channel_id=1, source_target_pairs={{0,1},{1,0},{2,3},{3,2},{4,5},{5,4},{6,7},{7,6},{8,9},{9,8},{10,11... | collective-permute-start | bytes 1966088 | tf_op jit(solution)/shard_map/ppermute | solution.py:30
  71.0 23.8 %collective-permute-start.14 = (bf16[4,128,512]{2,1,0:T(8,128)(2,1)S(1)}, bf16[4,128,512]{2,1,0:T(8,128)(2,1)S(1)}, u32[]{:S(2)}, u32[]{:S(2)}) collective-permute-start(bf16[4,128,512]{2,1,0:T(8,128)(2,1)S(1)} %broadcast_select_fusion.10.refs_0_), channel_id=1, source_target_pairs={{0,1},{1,0},{2,3},{3,2},{4,5},{5,4},{6,7},{7,6},{8,9},{9,8},{10,11... | collective-permute-start | bytes 1572872 | tf_op jit(solution)/shard_map/ppermute | solution.py:30
  77.2 13.4 %collective-permute-start.13 = (bf16[4,128,512]{2,1,0:T(8,128)(2,1)S(1)}, bf16[4,128,512]{2,1,0:T(8,128)(2,1)S(1)}, u32[]{:S(2)}, u32[]{:S(2)}) collective-permute-start(bf16[4,128,512]{2,1,0:T(8,128)(2,1)S(1)} %broadcast_select_fusion.10.refs_0_), channel_id=1, source_target_pairs={{0,2},{1,5},{2,0},{3,7},{4,6},{5,1},{6,4},{7,3},{8,10},{9,13},{10,... | collective-permute-start | bytes 1572872 | tf_op jit(solution)/shard_map/ppermute | solution.py:30
  78.8 11.8 %collective-permute-start.6 = (bf16[3,128,512]{2,1,0:T(8,128)(2,1)S(1)}, bf16[3,128,512]{2,1,0:T(8,128)(2,1)S(1)}, u32[]{:S(2)}, u32[]{:S(2)}) collective-permute-start(bf16[3,128,512]{2,1,0:T(8,128)(2,1)S(1)} %broadcast_select_fusion.11.refs_0_), channel_id=1, source_target_pairs={{0,2},{1,5},{2,0},{3,7},{4,6},{5,1},{6,4},{7,3},{8,10},{9,13},{10,... | collective-permute-start | bytes 1179656 | tf_op jit(solution)/shard_map/ppermute | solution.py:30
  80.2 11.3 %collective-permute-start.21 = (bf16[256,1024]{1,0:T(8,128)(2,1)S(1)}, bf16[256,1024]{1,0:T(8,128)(2,1)S(1)}, u32[]{:S(2)}, u32[]{:S(2)}) collective-permute-start(bf16[256,1024]{1,0:T(8,128)(2,1)S(1)} %get-tuple-element.29), channel_id=1, source_target_pairs={{8,16},{16,8},{9,17},{17,9},{10,18},{18,10},{11,19},{19,11},{12,20... | collective-permute-start | bytes 1572872 | tf_op jit(solution)/shard_map/ppermute | solution.py:21
  83.9 9.2 %collective-permute-start.22 = (bf16[256,1024]{1,0:T(8,128)(2,1)S(1)}, bf16[256,1024]{1,0:T(8,128)(2,1)S(1)}, u32[]{:S(2)}, u32[]{:S(2)}) collective-permute-start(bf16[256,1024]{1,0:T(8,128)(2,1)S(1)} %get-tuple-element.30), channel_id=1, source_target_pairs={{0,8},{16,24},{8,0},{24,16},{1,9},{17,25},{9,1},{25,17},{2,10},{18... | collective-permute-start | bytes 1572872 | tf_op jit(solution)/shard_map/ppermute | solution.py:21
  98.4 12.8 %collective-permute-start.27 = (bf16[256,1024]{1,0:T(8,128)(2,1)S(1)}, bf16[256,1024]{1,0:T(8,128)(2,1)S(1)}, u32[]{:S(2)}, u32[]{:S(2)}) collective-permute-start(bf16[256,1024]{1,0:T(8,128)(2,1)S(1)} %get-tuple-element.23), channel_id=1, source_target_pairs={{0,8},{16,24},{8,0},{24,16},{1,9},{17,25},{9,1},{25,17},{2,10},{18... | collective-permute-start | bytes 1572872 | tf_op jit(solution)/shard_map/ppermute | solution.py:21
  98.7 15.6 %collective-permute-start.26 = (bf16[256,1024]{1,0:T(8,128)(2,1)S(1)}, bf16[256,1024]{1,0:T(8,128)(2,1)S(1)}, u32[]{:S(2)}, u32[]{:S(2)}) collective-permute-start(bf16[256,1024]{1,0:T(8,128)(2,1)S(1)} %get-tuple-element.24), channel_id=1, source_target_pairs={{8,16},{16,8},{9,17},{17,9},{10,18},{18,10},{11,19},{19,11},{12,20... | collective-permute-start | bytes 1572872 | tf_op jit(solution)/shard_map/ppermute | solution.py:21
  (9 other events, 33.1 us)

commit v9 on v8

--- a/solution.py
+++ b/solution.py
@@ -208,8 +208,11 @@
             hold = after(hold, *first)
         return hold, flip(hold, self.cut)
 
-    def join(self, hold, got):
-        return place(self.cut, hold, got, flip(hold, (0, 0)), flip(got, (0, 0)))
+    def swap(self, pair):
+        return (*pair, *[flip(piece, (0, 0)) for piece in pair])
+
+    def join(self, pieces):
+        return place(self.cut, *pieces)
 
     def join_above(self, hold, got):
         both = shifted(jnp.stack([hold, got]), "rows", 1)
@@ -296,15 +299,16 @@
         else:
             head = spread.begin(across + [r] * wins, slice(2 - len(across), cut_one), head[2])
             tail = spread.begin([r] * (cut_two - cut_one), slice(cut_one, cut_two), tail[2])
-        head, tail = spread.middle(head), spread.middle(tail)
-        heads.append(spread.last(head))
-        tails.append(spread.last(tail))
+        head = spread.middle(head, *([] if r == 0 else [heads[r - 1][3]]))
+        tail = spread.middle(tail)
+        heads.append(spread.swap(spread.last(head)))
+        tails.append(spread.swap(spread.last(tail)))
 
     matrix = slab
     crosses, above_crosses = {}, {}
     for r in range(rounds):
         head, tail = heads[r], tails[r]
-        edges = spread.join(*head)
+        edges = spread.join(head)
         across = ([r + 1] if r + 1 < rounds else []) + ([r] if r == 0 else [])
         if across:
             n = len(across)
@@ -319,7 +323,7 @@
         head_rows, tail_rows = outer[0], outer[1]
         begin, end = head_rows[:border], tail_rows[border:]
         above, below = swap_rows(begin, end)
-        rest = spread.join(*tail)
+        rest = spread.join(tail)
         if r == 0:
             ones, twos = rest[: wins - 2], rest[wins - 2 :]
         else:

time: 117 us -> 129 us (1.10)
  waiting for transfers between devices: 49.6 us -> 64.4 us
  starting transfers between devices: 27.8 us -> 26.3 us
    ppermute x23, waiting for transfers between devices: 39 us -> 44.7 us  [flip(): lax.ppermute(value, 'cols', [(d, d ^ 1 << bits[d & 1]) for d in range(cou...]
    ppermute x4, waiting for transfers between devices: 8.91 us -> 14.1 us  [swap(): return lax.ppermute(value, 'rows', pairs + [(b, a) for a, b in pairs])]
    ppermute x1, waiting for transfers between devices: 1.62 us -> 5.5 us  [shifted(): lax.ppermute(value, axis, [(source, source + steps) for source in range(i...]
  transfers between devices with their start and end apart: 28 -> 28, of which waited for: 12 -> 12; matrix products, arithmetic and copies ran while one was open for 16% -> 15% of each run, Pallas kernels for 5% -> 5%
where the time goes in v9:
time: 129 us; the launch traced here: 128 us
  waiting for transfers between devices  64.4 us (50%)
  starting transfers between devices  26.3 us (20%)
  matrix products  11.9 us (9%)
  other arithmetic  10 us (8%)
  Pallas kernels  8.02 us (6%)
  between operations  4.08 us (3%)
  local copies, waits for them, and re-layouts  3.71 us (3%)
    ppermute x23, waiting for transfers between devices, flip(): lax.ppermute(value, 'cols', [(d, d ^ 1 << bits[d & 1]) for d in range(cou...  44.7 us
    ppermute x23, starting transfers between devices, flip(): lax.ppermute(value, 'cols', [(d, d ^ 1 << bits[d & 1]) for d in range(cou...  16.4 us
    ppermute x4, waiting for transfers between devices, swap(): return lax.ppermute(value, 'rows', pairs + [(b, a) for a, b in pairs])  14.1 us
    dot_general x6, matrix products, apply_many(): jnp.einsum('nab,nac->nbc', q, x, preferred_element_type=jnp.float32)  10.1 us
    select_n x11, other arithmetic, choose(): return jnp.where(mask, yes, no)  8.75 us
    ppermute x4, starting transfers between devices, swap(): return lax.ppermute(value, 'rows', pairs + [(b, a) for a, b in pairs])  6.42 us
    ppermute x1, waiting for transfers between devices, shifted(): lax.ppermute(value, axis, [(source, source + steps) for source in range(i...  5.5 us
    ppermute x1, starting transfers between devices, shifted(): lax.ppermute(value, axis, [(source, source + steps) for source in range(i...  3.47 us
  transfers between devices with their start and end apart: 28, of which 12 were waited for; matrix products, arithmetic and copies ran while one was open for 15% of the time, Pallas kernels for 5%

profile of v9, /device:TPU:8, one launch (start us, length us, event | category | flops | bytes accessed | tf_op | source)
XLA Modules:
  0.0 128.5 jit_solution(6279394912570334249)
XLA Ops:
  0.0 2.2 %copy-done.2 = bf16[1,4096,512]{2,1,0:T(8,128)(2,1)S(1)} copy-done((bf16[1,4096,512]{2,1,0:T(8,128)(2,1)S(1)}, bf16[1,4096,512]{2,1,0:T(8,128)(2,1)}, u32[]{:S(2)}) %copy-start.2) | copy-done | bytes 4194328
  3.1 1.9 %cut_slot.2 = (bf16[9,128,512]{2,1,0:T(8,128)(2,1)S(1)}, bf16[9,128,512]{2,1,0:T(8,128)(2,1)}, bf16[9,128,512]{2,1,0:T(8,128)(2,1)S(1)}) custom-call(bf16[8,2,2,128,512]{4,3,2,1,0:T(8,128)(2,1)S(1)} %bitcast.84), custom_call_target="tpu_custom_call" | custom-call | bytes 6291456 | tf_op jit(solution)/shard_map/cut_slot/pallas_call | solution.py:105
  14.8 5.7 %collective-permute-done.9 = bf16[4,128,512]{2,1,0:T(8,128)(2,1)S(1)} collective-permute-done((bf16[4,128,512]{2,1,0:T(8,128)(2,1)S(1)}, bf16[4,128,512]{2,1,0:T(8,128)(2,1)S(1)}, u32[]{:S(2)}, u32[]{:S(2)}) %collective-permute-start.9) | collective-permute-done | bytes 524320 | tf_op jit(solution)/shard_map/ppermute | solution.py:30
  21.7 1.6 %collective-permute-start.10 = (bf16[4,128,512]{2,1,0:T(8,128)(2,1)S(1)}, bf16[4,128,512]{2,1,0:T(8,128)(2,1)S(1)}, u32[]{:S(2)}, u32[]{:S(2)}) collective-permute-start(bf16[4,128,512]{2,1,0:T(8,128)(2,1)S(1)} %fusion.33), channel_id=1, source_target_pairs={{0,4},{1,3},{2,6},{3,1},{4,0},{5,7},{6,2},{7,5},{8,12},{9,11},{10,... | collective-permute-start | bytes 1572872 | tf_op jit(solution)/shard_map/ppermute | solution.py:30
  23.3 8.1 %collective-permute-done.2 = bf16[5,128,512]{2,1,0:T(8,128)(2,1)S(1)} collective-permute-done((bf16[5,128,512]{2,1,0:T(8,128)(2,1)S(1)}, bf16[5,128,512]{2,1,0:T(8,128)(2,1)S(1)}, u32[]{:S(2)}, u32[]{:S(2)}) %collective-permute-start.2) | collective-permute-done | bytes 655392 | tf_op jit(solution)/shard_map/ppermute | solution.py:30
  32.7 1.6 %collective-permute-start.3 = (bf16[5,128,512]{2,1,0:T(8,128)(2,1)S(1)}, bf16[5,128,512]{2,1,0:T(8,128)(2,1)S(1)}, u32[]{:S(2)}, u32[]{:S(2)}) collective-permute-start(bf16[5,128,512]{2,1,0:T(8,128)(2,1)S(1)} %fusion.32), channel_id=1, source_target_pairs={{0,4},{1,3},{2,6},{3,1},{4,0},{5,7},{6,2},{7,5},{8,12},{9,11},{10,... | collective-permute-start | bytes 1966088 | tf_op jit(solution)/shard_map/ppermute | solution.py:30
  35.4 1.6 %collective-permute-start.11 = (bf16[4,128,512]{2,1,0:T(8,128)(2,1)S(1)}, bf16[4,128,512]{2,1,0:T(8,128)(2,1)S(1)}, u32[]{:S(2)}, u32[]{:S(2)}) collective-permute-start(bf16[4,128,512]{2,1,0:T(8,128)(2,1)S(1)} %after.4), channel_id=1, source_target_pairs={{0,2},{1,5},{2,0},{3,7},{4,6},{5,1},{6,4},{7,3},{8,10},{9,13},{10,... | collective-permute-start | bytes 1572872 | tf_op jit(solution)/shard_map/ppermute | solution.py:30
  37.7 12.5 %collective-permute-done.3.refs_0_ = bf16[5,128,512]{2,1,0:T(8,128)(2,1)S(1)} collective-permute-done((bf16[5,128,512]{2,1,0:T(8,128)(2,1)S(1)}, bf16[5,128,512]{2,1,0:T(8,128)(2,1)S(1)}, u32[]{:S(2)}, u32[]{:S(2)}) %collective-permute-start.3) | collective-permute-done | bytes 655392 | tf_op jit(solution)/shard_map/ppermute | solution.py:30
  54.1 11.2 %collective-permute-done.4 = bf16[3,128,512]{2,1,0:T(8,128)(2,1)S(1)} collective-permute-done((bf16[3,128,512]{2,1,0:T(8,128)(2,1)S(1)}, bf16[3,128,512]{2,1,0:T(8,128)(2,1)S(1)}, u32[]{:S(2)}, u32[]{:S(2)}) %collective-permute-start.4) | collective-permute-done | bytes 393248 | tf_op jit(solution)/shard_map/ppermute | solution.py:30
  65.3 3.5 %collective-permute-start.19 = (bf16[2,2,128,256]{3,2,1,0:T(8,128)(2,1)S(1)}, bf16[2,2,128,256]{3,2,1,0:T(8,128)(2,1)S(1)}, u32[]{:S(2)}, u32[]{:S(2)}) collective-permute-start(bf16[2,2,128,256]{3,2,1,0:T(8,128)(2,1)S(1)} %pad_maximum_fusion.4), channel_id=1, source_target_pairs={{0,8},{8,16},{16,24},{1,9},{9,17},{17,25},{2,10},{10,18},{18,26},{... | collective-permute-start | bytes 786440 | tf_op jit(solution)/shard_map/ppermute | solution.py:12
  69.9 5.5 %collective-permute-done.19 = bf16[2,2,128,256]{3,2,1,0:T(8,128)(2,1)S(1)} collective-permute-done((bf16[2,2,128,256]{3,2,1,0:T(8,128)(2,1)S(1)}, bf16[2,2,128,256]{3,2,1,0:T(8,128)(2,1)S(1)}, u32[]{:S(2)}, u32[]{:S(2)}) %collective-permute-start.19) | collective-permute-done | bytes 262176 | tf_op jit(solution)/shard_map/ppermute | solution.py:12
  78.4 4.7 %collective-permute-done.5 = bf16[3,128,512]{2,1,0:T(8,128)(2,1)S(1)} collective-permute-done((bf16[3,128,512]{2,1,0:T(8,128)(2,1)S(1)}, bf16[3,128,512]{2,1,0:T(8,128)(2,1)S(1)}, u32[]{:S(2)}, u32[]{:S(2)}) %collective-permute-start.5) | collective-permute-done | bytes 393248 | tf_op jit(solution)/shard_map/ppermute | solution.py:30
  85.1 1.6 %collective-permute-start.6 = (bf16[3,128,512]{2,1,0:T(8,128)(2,1)S(1)}, bf16[3,128,512]{2,1,0:T(8,128)(2,1)S(1)}, u32[]{:S(2)}, u32[]{:S(2)}) collective-permute-start(bf16[3,128,512]{2,1,0:T(8,128)(2,1)S(1)} %broadcast_select_fusion.11.refs_0_), channel_id=1, source_target_pairs={{0,2},{1,5},{2,0},{3,7},{4,6},{5,1},{6,4},{7,3},{8,10},{9,13},{10,... | collective-permute-start | bytes 1179656 | tf_op jit(solution)/shard_map/ppermute | solution.py:30
  87.1 2.1 %collective-permute-done.14 = bf16[4,128,512]{2,1,0:T(8,128)(2,1)S(1)} collective-permute-done((bf16[4,128,512]{2,1,0:T(8,128)(2,1)S(1)}, bf16[4,128,512]{2,1,0:T(8,128)(2,1)S(1)}, u32[]{:S(2)}, u32[]{:S(2)}) %collective-permute-start.14) | collective-permute-done | bytes 524320 | tf_op jit(solution)/shard_map/ppermute | solution.py:30
  89.2 3.7 %collective-permute-start.21 = (bf16[256,1024]{1,0:T(8,128)(2,1)S(1)}, bf16[256,1024]{1,0:T(8,128)(2,1)S(1)}, u32[]{:S(2)}, u32[]{:S(2)}) collective-permute-start(bf16[256,1024]{1,0:T(8,128)(2,1)S(1)} %get-tuple-element.29), channel_id=1, source_target_pairs={{8,16},{16,8},{9,17},{17,9},{10,18},{18,10},{11,19},{19,11},{12,20... | collective-permute-start | bytes 1572872 | tf_op jit(solution)/shard_map/ppermute | solution.py:21
  93.1 1.6 %collective-permute-start.15 = (bf16[4,128,512]{2,1,0:T(8,128)(2,1)S(1)}, bf16[4,128,512]{2,1,0:T(8,128)(2,1)S(1)}, u32[]{:S(2)}, u32[]{:S(2)}) collective-permute-start(bf16[4,128,512]{2,1,0:T(8,128)(2,1)S(1)} %broadcast_select_fusion.10.refs_0_), channel_id=1, source_target_pairs={{0,2},{1,5},{2,0},{3,7},{4,6},{5,1},{6,4},{7,3},{8,10},{9,13},{10,... | collective-permute-start | bytes 1572872 | tf_op jit(solution)/shard_map/ppermute | solution.py:30
  96.9 2.1 %convolution_convert_fusion = bf16[3,512,1024]{2,1,0:T(8,128)(2,1)S(1)} fusion(bf16[5,512,512]{2,1,0:T(8,128)(2,1)S(1)} %place.9, bf16[3,512,1024]{2,1,0:T(8,128)(2,1)S(1)} %bitcast.89), kind=kOutput, calls=%fused_computation.2 | convolution fusion | flops 1612185600 | bytes 8912896 | tf_op jit(solution)/shard_map/nab,nac->nbc/dot_general | solution.py:229
  99.0 4.1 %collective-permute-done.21 = bf16[256,1024]{1,0:T(8,128)(2,1)S(1)} collective-permute-done((bf16[256,1024]{1,0:T(8,128)(2,1)S(1)}, bf16[256,1024]{1,0:T(8,128)(2,1)S(1)}, u32[]{:S(2)}, u32[]{:S(2)}) %collective-permute-start.21) | collective-permute-done | bytes 524320 | tf_op jit(solution)/shard_map/ppermute | solution.py:21
  103.1 1.7 %collective-permute-done.22 = bf16[256,1024]{1,0:T(8,128)(2,1)S(1)} collective-permute-done((bf16[256,1024]{1,0:T(8,128)(2,1)S(1)}, bf16[256,1024]{1,0:T(8,128)(2,1)S(1)}, u32[]{:S(2)}, u32[]{:S(2)}) %collective-permute-start.22) | collective-permute-done | bytes 524320 | tf_op jit(solution)/shard_map/ppermute | solution.py:21
  110.7 2.3 %collective-permute-start.26 = (bf16[256,1024]{1,0:T(8,128)(2,1)S(1)}, bf16[256,1024]{1,0:T(8,128)(2,1)S(1)}, u32[]{:S(2)}, u32[]{:S(2)}) collective-permute-start(bf16[256,1024]{1,0:T(8,128)(2,1)S(1)} %get-tuple-element.24), channel_id=1, source_target_pairs={{8,16},{16,8},{9,17},{17,9},{10,18},{18,10},{11,19},{19,11},{12,20... | collective-permute-start | bytes 1572872 | tf_op jit(solution)/shard_map/ppermute | solution.py:21
  113.4 1.9 %convolution_convert_fusion.1 = bf16[3,512,1024]{2,1,0:T(8,128)(2,1)S(1)} fusion(bf16[3,512,512]{2,1,0:T(8,128)(2,1)S(1)} %place.5, bf16[3,512,1024]{2,1,0:T(8,128)(2,1)S(1)} %bitcast.90), kind=kOutput, calls=%fused_computation.3 | convolution fusion | flops 1612185600 | bytes 7864320 | tf_op jit(solution)/shard_map/nab,nac->nbc/dot_general | solution.py:229
  115.3 2.7 %write_inner.1._ = bf16[2048,1024]{1,0:T(8,128)(2,1)} custom-call(bf16[1536,1024]{1,0:T(8,128)(2,1)S(1)} %bitcast.85), custom_call_target="tpu_custom_call" | custom-call | bytes 6291456 | tf_op jit(solution)/shard_map/write_inner/pallas_call | solution.py:239
  118.0 6.5 %collective-permute-done.27 = bf16[256,1024]{1,0:T(8,128)(2,1)S(1)} collective-permute-done((bf16[256,1024]{1,0:T(8,128)(2,1)S(1)}, bf16[256,1024]{1,0:T(8,128)(2,1)S(1)}, u32[]{:S(2)}, u32[]{:S(2)}) %collective-permute-start.27) | collective-permute-done | bytes 524320 | tf_op jit(solution)/shard_map/ppermute | solution.py:21
  124.5 1.9 %collective-permute-done.26 = bf16[256,1024]{1,0:T(8,128)(2,1)S(1)} collective-permute-done((bf16[256,1024]{1,0:T(8,128)(2,1)S(1)}, bf16[256,1024]{1,0:T(8,128)(2,1)S(1)}, u32[]{:S(2)}, u32[]{:S(2)}) %collective-permute-start.26) | collective-permute-done | bytes 524320 | tf_op jit(solution)/shard_map/ppermute | solution.py:21
  (97 shorter events, 32.2 us)
Async XLA Ops:
  5.0 9.7 %collective-permute-start = (bf16[9,128,512]{2,1,0:T(8,128)(2,1)}, bf16[9,128,512]{2,1,0:T(8,128)(2,1)}, u32[]{:S(2)}, u32[]{:S(2)}) collective-permute-start(bf16[9,128,512]{2,1,0:T(8,128)(2,1)} %get-tuple-element.9), channel_id=1, source_target_pairs={{0,1},{1,0},{2,3},{3,2},{4,5},{5,4},{6,7},{7,6},{8,9},{9,8},{10,11... | collective-permute-start | bytes 3538952 | tf_op jit(solution)/shard_map/ppermute | solution.py:30
  11.3 9.2 %collective-permute-start.9 = (bf16[4,128,512]{2,1,0:T(8,128)(2,1)S(1)}, bf16[4,128,512]{2,1,0:T(8,128)(2,1)S(1)}, u32[]{:S(2)}, u32[]{:S(2)}) collective-permute-start(bf16[4,128,512]{2,1,0:T(8,128)(2,1)S(1)} %get-tuple-element.15), channel_id=1, source_target_pairs={{0,2},{1,5},{2,0},{3,7},{4,6},{5,1},{6,4},{7,3},{8,10},{9,13},{10,... | collective-permute-start | bytes 1572872 | tf_op jit(solution)/shard_map/ppermute | solution.py:30
  14.0 17.4 %collective-permute-start.2 = (bf16[5,128,512]{2,1,0:T(8,128)(2,1)S(1)}, bf16[5,128,512]{2,1,0:T(8,128)(2,1)S(1)}, u32[]{:S(2)}, u32[]{:S(2)}) collective-permute-start(bf16[5,128,512]{2,1,0:T(8,128)(2,1)S(1)} %slice_select_fusion), channel_id=1, source_target_pairs={{0,2},{1,5},{2,0},{3,7},{4,6},{5,1},{6,4},{7,3},{8,10},{9,13},{10,... | collective-permute-start | bytes 1966088 | tf_op jit(solution)/shard_map/ppermute | solution.py:30
  21.7 13.6 %collective-permute-start.10 = (bf16[4,128,512]{2,1,0:T(8,128)(2,1)S(1)}, bf16[4,128,512]{2,1,0:T(8,128)(2,1)S(1)}, u32[]{:S(2)}, u32[]{:S(2)}) collective-permute-start(bf16[4,128,512]{2,1,0:T(8,128)(2,1)S(1)} %fusion.33), channel_id=1, source_target_pairs={{0,4},{1,3},{2,6},{3,1},{4,0},{5,7},{6,2},{7,5},{8,12},{9,11},{10,... | collective-permute-start | bytes 1572872 | tf_op jit(solution)/shard_map/ppermute | solution.py:30
  32.7 17.6 %collective-permute-start.3 = (bf16[5,128,512]{2,1,0:T(8,128)(2,1)S(1)}, bf16[5,128,512]{2,1,0:T(8,128)(2,1)S(1)}, u32[]{:S(2)}, u32[]{:S(2)}) collective-permute-start(bf16[5,128,512]{2,1,0:T(8,128)(2,1)S(1)} %fusion.32), channel_id=1, source_target_pairs={{0,4},{1,3},{2,6},{3,1},{4,0},{5,7},{6,2},{7,5},{8,12},{9,11},{10,... | collective-permute-start | bytes 1966088 | tf_op jit(solution)/shard_map/ppermute | solution.py:30
  35.4 16.8 %collective-permute-start.11 = (bf16[4,128,512]{2,1,0:T(8,128)(2,1)S(1)}, bf16[4,128,512]{2,1,0:T(8,128)(2,1)S(1)}, u32[]{:S(2)}, u32[]{:S(2)}) collective-permute-start(bf16[4,128,512]{2,1,0:T(8,128)(2,1)S(1)} %after.4), channel_id=1, source_target_pairs={{0,2},{1,5},{2,0},{3,7},{4,6},{5,1},{6,4},{7,3},{8,10},{9,13},{10,... | collective-permute-start | bytes 1572872 | tf_op jit(solution)/shard_map/ppermute | solution.py:30
  37.0 40.5 %collective-permute-start.18 = (bf16[4,128,512]{2,1,0:T(8,128)(2,1)S(1)}, bf16[4,128,512]{2,1,0:T(8,128)(2,1)S(1)}, u32[]{:S(2)}, u32[]{:S(2)}) collective-permute-start(bf16[4,128,512]{2,1,0:T(8,128)(2,1)S(1)} %broadcast_select_fusion.1.refs_0_), channel_id=1, source_target_pairs={{0,1},{1,0},{2,3},{3,2},{4,5},{5,4},{6,7},{7,6},{8,9},{9,8},{10,11... | collective-permute-start | bytes 1572872 | tf_op jit(solution)/shard_map/ppermute | solution.py:30
  37.1 16.9 %collective-permute-start.12 = (bf16[4,128,512]{2,1,0:T(8,128)(2,1)S(1)}, bf16[4,128,512]{2,1,0:T(8,128)(2,1)S(1)}, u32[]{:S(2)}, u32[]{:S(2)}) collective-permute-start(bf16[4,128,512]{2,1,0:T(8,128)(2,1)S(1)} %broadcast_select_fusion.1.refs_0_), channel_id=1, source_target_pairs={{0,2},{1,5},{2,0},{3,7},{4,6},{5,1},{6,4},{7,3},{8,10},{9,13},{10,... | collective-permute-start | bytes 1572872 | tf_op jit(solution)/shard_map/ppermute | solution.py:30
  50.4 42.6 %collective-permute-start.24 = (bf16[5,128,512]{2,1,0:T(8,128)(2,1)S(1)}, bf16[5,128,512]{2,1,0:T(8,128)(2,1)S(1)}, u32[]{:S(2)}, u32[]{:S(2)}) collective-permute-start(bf16[5,128,512]{2,1,0:T(8,128)(2,1)S(1)} %broadcast_select_fusion.refs_0_), channel_id=1, source_target_pairs={{0,1},{1,0},{2,3},{3,2},{4,5},{5,4},{6,7},{7,6},{8,9},{9,8},{10,11... | collective-permute-start | bytes 1966088 | tf_op jit(solution)/shard_map/ppermute | solution.py:30
  50.4 26.5 %collective-permute-start.23 = (bf16[5,128,512]{2,1,0:T(8,128)(2,1)S(1)}, bf16[5,128,512]{2,1,0:T(8,128)(2,1)S(1)}, u32[]{:S(2)}, u32[]{:S(2)}) collective-permute-start(bf16[5,128,512]{2,1,0:T(8,128)(2,1)S(1)} %broadcast_select_fusion.refs_0_), channel_id=1, source_target_pairs={{0,2},{1,5},{2,0},{3,7},{4,6},{5,1},{6,4},{7,3},{8,10},{9,13},{10,... | collective-permute-start | bytes 1966088 | tf_op jit(solution)/shard_map/ppermute | solution.py:30
  52.2 13.1 %collective-permute-start.4 = (bf16[3,128,512]{2,1,0:T(8,128)(2,1)S(1)}, bf16[3,128,512]{2,1,0:T(8,128)(2,1)S(1)}, u32[]{:S(2)}, u32[]{:S(2)}) collective-permute-start(bf16[3,128,512]{2,1,0:T(8,128)(2,1)S(1)} %after.3), channel_id=1, source_target_pairs={{0,2},{1,5},{2,0},{3,7},{4,6},{5,1},{6,4},{7,3},{8,10},{9,13},{10,... | collective-permute-start | bytes 1179656 | tf_op jit(solution)/shard_map/ppermute | solution.py:30
  54.0 23.0 %collective-permute-start.13 = (bf16[4,128,512]{2,1,0:T(8,128)(2,1)S(1)}, bf16[4,128,512]{2,1,0:T(8,128)(2,1)S(1)}, u32[]{:S(2)}, u32[]{:S(2)}) collective-permute-start(bf16[4,128,512]{2,1,0:T(8,128)(2,1)S(1)} %collective-permute-done.12.refs_1_), channel_id=1, source_target_pairs={{0,1},{1,0},{2,3},{3,2},{4,5},{5,4},{6,7},{7,6},{8,9},{9,8},{10,11... | collective-permute-start | bytes 1572872 | tf_op jit(solution)/shard_map/ppermute | solution.py:30
  65.3 10.1 %collective-permute-start.19 = (bf16[2,2,128,256]{3,2,1,0:T(8,128)(2,1)S(1)}, bf16[2,2,128,256]{3,2,1,0:T(8,128)(2,1)S(1)}, u32[]{:S(2)}, u32[]{:S(2)}) collective-permute-start(bf16[2,2,128,256]{3,2,1,0:T(8,128)(2,1)S(1)} %pad_maximum_fusion.4), channel_id=1, source_target_pairs={{0,8},{8,16},{16,24},{1,9},{9,17},{17,25},{2,10},{10,18},{18,26},{... | collective-permute-start | bytes 786440 | tf_op jit(solution)/shard_map/ppermute | solution.py:12
  76.9 8.2 %collective-permute-start.20 = (bf16[2,2,128,256]{3,2,1,0:T(8,128)(2,1)S(1)}, bf16[2,2,128,256]{3,2,1,0:T(8,128)(2,1)S(1)}, u32[]{:S(2)}, u32[]{:S(2)}) collective-permute-start(bf16[2,2,128,256]{3,2,1,0:T(8,128)(2,1)S(1)} %collective-permute-done.19), channel_id=1, source_target_pairs={{0,1},{1,0},{2,3},{3,2},{4,5},{5,4},{6,7},{7,6},{8,9},{9,8},{10,11... | collective-permute-start | bytes 786440 | tf_op jit(solution)/shard_map/ppermute | solution.py:30
  77.0 16.1 %collective-permute-start.25 = (bf16[5,128,512]{2,1,0:T(8,128)(2,1)S(1)}, bf16[5,128,512]{2,1,0:T(8,128)(2,1)S(1)}, u32[]{:S(2)}, u32[]{:S(2)}) collective-permute-start(bf16[5,128,512]{2,1,0:T(8,128)(2,1)S(1)} %collective-permute-done.23.refs_1_), channel_id=1, source_target_pairs={{0,1},{1,0},{2,3},{3,2},{4,5},{5,4},{6,7},{7,6},{8,9},{9,8},{10,11... | collective-permute-start | bytes 1966088 | tf_op jit(solution)/shard_map/ppermute | solution.py:30
  77.6 11.6 %collective-permute-start.14 = (bf16[4,128,512]{2,1,0:T(8,128)(2,1)S(1)}, bf16[4,128,512]{2,1,0:T(8,128)(2,1)S(1)}, u32[]{:S(2)}, u32[]{:S(2)}) collective-permute-start(bf16[4,128,512]{2,1,0:T(8,128)(2,1)S(1)} %after.5), channel_id=1, source_target_pairs={{0,4},{1,3},{2,6},{3,1},{4,0},{5,7},{6,2},{7,5},{8,12},{9,11},{10,... | collective-permute-start | bytes 1572872 | tf_op jit(solution)/shard_map/ppermute | solution.py:30
  83.2 23.0 %collective-permute-start.7 = (bf16[3,128,512]{2,1,0:T(8,128)(2,1)S(1)}, bf16[3,128,512]{2,1,0:T(8,128)(2,1)S(1)}, u32[]{:S(2)}, u32[]{:S(2)}) collective-permute-start(bf16[3,128,512]{2,1,0:T(8,128)(2,1)S(1)} %broadcast_select_fusion.11.refs_0_), channel_id=1, source_target_pairs={{0,1},{1,0},{2,3},{3,2},{4,5},{5,4},{6,7},{7,6},{8,9},{9,8},{10,11... | collective-permute-start | bytes 1179656 | tf_op jit(solution)/shard_map/ppermute | solution.py:30
  85.1 7.9 %collective-permute-start.6 = (bf16[3,128,512]{2,1,0:T(8,128)(2,1)S(1)}, bf16[3,128,512]{2,1,0:T(8,128)(2,1)S(1)}, u32[]{:S(2)}, u32[]{:S(2)}) collective-permute-start(bf16[3,128,512]{2,1,0:T(8,128)(2,1)S(1)} %broadcast_select_fusion.11.refs_0_), channel_id=1, source_target_pairs={{0,2},{1,5},{2,0},{3,7},{4,6},{5,1},{6,4},{7,3},{8,10},{9,13},{10,... | collective-permute-start | bytes 1179656 | tf_op jit(solution)/shard_map/ppermute | solution.py:30
  89.2 13.9 %collective-permute-start.21 = (bf16[256,1024]{1,0:T(8,128)(2,1)S(1)}, bf16[256,1024]{1,0:T(8,128)(2,1)S(1)}, u32[]{:S(2)}, u32[]{:S(2)}) collective-permute-start(bf16[256,1024]{1,0:T(8,128)(2,1)S(1)} %get-tuple-element.29), channel_id=1, source_target_pairs={{8,16},{16,8},{9,17},{17,9},{10,18},{18,10},{11,19},{19,11},{12,20... | collective-permute-start | bytes 1572872 | tf_op jit(solution)/shard_map/ppermute | solution.py:21
  93.0 11.8 %collective-permute-start.22 = (bf16[256,1024]{1,0:T(8,128)(2,1)S(1)}, bf16[256,1024]{1,0:T(8,128)(2,1)S(1)}, u32[]{:S(2)}, u32[]{:S(2)}) collective-permute-start(bf16[256,1024]{1,0:T(8,128)(2,1)S(1)} %get-tuple-element.30), channel_id=1, source_target_pairs={{0,8},{16,24},{8,0},{24,16},{1,9},{17,25},{9,1},{25,17},{2,10},{18... | collective-permute-start | bytes 1572872 | tf_op jit(solution)/shard_map/ppermute | solution.py:21
  93.0 13.2 %collective-permute-start.8 = (bf16[3,128,512]{2,1,0:T(8,128)(2,1)S(1)}, bf16[3,128,512]{2,1,0:T(8,128)(2,1)S(1)}, u32[]{:S(2)}, u32[]{:S(2)}) collective-permute-start(bf16[3,128,512]{2,1,0:T(8,128)(2,1)S(1)} %collective-permute-done.6.refs_1_), channel_id=1, source_target_pairs={{0,1},{1,0},{2,3},{3,2},{4,5},{5,4},{6,7},{7,6},{8,9},{9,8},{10,11... | collective-permute-start | bytes 1179656 | tf_op jit(solution)/shard_map/ppermute | solution.py:30
  93.1 11.7 %collective-permute-start.15 = (bf16[4,128,512]{2,1,0:T(8,128)(2,1)S(1)}, bf16[4,128,512]{2,1,0:T(8,128)(2,1)S(1)}, u32[]{:S(2)}, u32[]{:S(2)}) collective-permute-start(bf16[4,128,512]{2,1,0:T(8,128)(2,1)S(1)} %broadcast_select_fusion.10.refs_0_), channel_id=1, source_target_pairs={{0,2},{1,5},{2,0},{3,7},{4,6},{5,1},{6,4},{7,3},{8,10},{9,13},{10,... | collective-permute-start | bytes 1572872 | tf_op jit(solution)/shard_map/ppermute | solution.py:30
  110.3 14.2 %collective-permute-start.27 = (bf16[256,1024]{1,0:T(8,128)(2,1)S(1)}, bf16[256,1024]{1,0:T(8,128)(2,1)S(1)}, u32[]{:S(2)}, u32[]{:S(2)}) collective-permute-start(bf16[256,1024]{1,0:T(8,128)(2,1)S(1)} %get-tuple-element.23), channel_id=1, source_target_pairs={{0,8},{16,24},{8,0},{24,16},{1,9},{17,25},{9,1},{25,17},{2,10},{18... | collective-permute-start | bytes 1572872 | tf_op jit(solution)/shard_map/ppermute | solution.py:21
  110.7 15.7 %collective-permute-start.26 = (bf16[256,1024]{1,0:T(8,128)(2,1)S(1)}, bf16[256,1024]{1,0:T(8,128)(2,1)S(1)}, u32[]{:S(2)}, u32[]{:S(2)}) collective-permute-start(bf16[256,1024]{1,0:T(8,128)(2,1)S(1)} %get-tuple-element.24), channel_id=1, source_target_pairs={{8,16},{16,8},{9,17},{17,9},{10,18},{18,10},{11,19},{19,11},{12,20... | collective-permute-start | bytes 1572872 | tf_op jit(solution)/shard_map/ppermute | solution.py:21
  (9 other events, 35.6 us)

commit v10 on v8

--- a/solution.py
+++ b/solution.py
@@ -285,25 +285,22 @@
     middle_one, middle_two = list(range(1, wins - 1)), list(range(wins, crossing))
     order = [crossing, crossing, 0, wins - 1] + middle_one + middle_two
     spread = Spread(slot, owners[:, row_block], order)
-    cut_one, cut_two = 4 + len(middle_one), len(order)
-
-    heads, tails = [], []
+    streams = []
     for r in range(rounds):
         across = ([r + 1] if r + 1 < rounds else []) + ([r] if r == 0 else [])
+        first = 2 - len(across)
         if r == 0:
-            head = spread.begin(across + [r, r], slice(2 - len(across), 4))
-            tail = spread.begin([r] * (cut_two - 4), slice(4, cut_two))
+            streams.append(spread.middle(spread.begin(across + [r, r], slice(first, 4))))
+            streams.append(spread.middle(spread.begin([r] * (len(order) - 4), slice(4, len(order)))))
         else:
-            head = spread.begin(across + [r] * wins, slice(2 - len(across), cut_one), head[2])
-            tail = spread.begin([r] * (cut_two - cut_one), slice(cut_one, cut_two), tail[2])
-        head, tail = spread.middle(head), spread.middle(tail)
-        heads.append(spread.last(head))
-        tails.append(spread.last(tail))
+            begun = spread.begin(across + [r] * crossing, slice(first, len(order)), streams[r - 1][2])
+            streams.append(spread.middle(begun))
+    pairs = [spread.last(stream) for stream in streams]
 
     matrix = slab
     crosses, above_crosses = {}, {}
     for r in range(rounds):
-        head, tail = heads[r], tails[r]
+        head = pairs[0] if r == 0 else pairs[r + 1]
         edges = spread.join(*head)
         across = ([r + 1] if r + 1 < rounds else []) + ([r] if r == 0 else [])
         if across:
@@ -319,11 +316,8 @@
         head_rows, tail_rows = outer[0], outer[1]
         begin, end = head_rows[:border], tail_rows[border:]
         above, below = swap_rows(begin, end)
-        rest = spread.join(*tail)
-        if r == 0:
-            ones, twos = rest[: wins - 2], rest[wins - 2 :]
-        else:
-            ones, twos = edges[2:], rest
+        rest = spread.join(*pairs[1]) if r == 0 else edges[2:]
+        ones, twos = rest[: wins - 2], rest[wins - 2 :]
         mid = apply_many(
             ones,
             matrix[window : local_rows - window].reshape(wins - 2, window, local_cols),

time: 117 us -> 117 us (level)
  waiting for transfers between devices: 49.6 us -> 48 us
    ppermute x4, waiting for transfers between devices: 8.91 us -> 6.52 us  [swap(): return lax.ppermute(value, 'rows', pairs + [(b, a) for a, b in pairs])]
    ppermute x1, waiting for transfers between devices: 1.62 us -> 3.71 us  [shifted(): lax.ppermute(value, axis, [(source, source + steps) for source in range(i...]
    ppermute x23 -> x18, starting transfers between devices: 16.7 us -> 15.1 us  [flip(): lax.ppermute(value, 'cols', [(d, d ^ 1 << bits[d & 1]) for d in range(cou...]
    ppermute x4, starting transfers between devices: 7.64 us -> 8.9 us  [swap(): return lax.ppermute(value, 'rows', pairs + [(b, a) for a, b in pairs])]
    ppermute x23 -> x18, waiting for transfers between devices: 39 us -> 37.8 us  [flip(): lax.ppermute(value, 'cols', [(d, d ^ 1 << bits[d & 1]) for d in range(cou...]
    unnamed x8 -> x10, local copies, waits for them, and re-layouts: 2.22 us -> 3.01 us
    select_n x11 -> x9, other arithmetic: 8.75 us -> 8.83 us  [choose(): return jnp.where(mask, yes, no)]
  transfers between devices with their start and end apart: 28 -> 23, of which waited for: 12 -> 10; matrix products, arithmetic and copies ran while one was open for 16% -> 17% of each run, Pallas kernels for 5% -> 5%
where the time goes in v10:
time: 117 us; the launch traced here: 116 us
  waiting for transfers between devices  48 us (41%)
  starting transfers between devices  27.8 us (24%)
  matrix products  12.2 us (10%)
  other arithmetic  10.1 us (9%)
  Pallas kernels  7.89 us (7%)
  local copies, waits for them, and re-layouts  5.82 us (5%)
  between operations  4.23 us (4%)
    ppermute x18, waiting for transfers between devices, flip(): lax.ppermute(value, 'cols', [(d, d ^ 1 << bits[d & 1]) for d in range(cou...  37.8 us
    ppermute x18, starting transfers between devices, flip(): lax.ppermute(value, 'cols', [(d, d ^ 1 << bits[d & 1]) for d in range(cou...  15.1 us
    dot_general x6, matrix products, apply_many(): jnp.einsum('nab,nac->nbc', q, x, preferred_element_type=jnp.float32)  10.3 us
    ppermute x4, starting transfers between devices, swap(): return lax.ppermute(value, 'rows', pairs + [(b, a) for a, b in pairs])  8.9 us
    select_n x9, other arithmetic, choose(): return jnp.where(mask, yes, no)  8.83 us
    ppermute x4, waiting for transfers between devices, swap(): return lax.ppermute(value, 'rows', pairs + [(b, a) for a, b in pairs])  6.52 us
    ppermute x1, starting transfers between devices, shifted(): lax.ppermute(value, axis, [(source, source + steps) for source in range(i...  3.79 us
    ppermute x1, waiting for transfers between devices, shifted(): lax.ppermute(value, axis, [(source, source + steps) for source in range(i...  3.71 us
  transfers between devices with their start and end apart: 23, of which 10 were waited for; matrix products, arithmetic and copies ran while one was open for 17% of the time, Pallas kernels for 5%

profile of v10, /device:TPU:8, one launch (start us, length us, event | category | flops | bytes accessed | tf_op | source)
XLA Modules:
  0.0 116.1 jit_solution(11820425453702030680)
XLA Ops:
  0.0 2.2 %copy-done.2 = bf16[1,4096,512]{2,1,0:T(8,128)(2,1)S(1)} copy-done((bf16[1,4096,512]{2,1,0:T(8,128)(2,1)S(1)}, bf16[1,4096,512]{2,1,0:T(8,128)(2,1)}, u32[]{:S(2)}) %copy-start.2) | copy-done | bytes 4194328
  3.1 1.9 %cut_slot.2 = (bf16[9,128,512]{2,1,0:T(8,128)(2,1)S(1)}, bf16[9,128,512]{2,1,0:T(8,128)(2,1)}, bf16[9,128,512]{2,1,0:T(8,128)(2,1)S(1)}) custom-call(bf16[8,2,2,128,512]{4,3,2,1,0:T(8,128)(2,1)S(1)} %bitcast.84), custom_call_target="tpu_custom_call" | custom-call | bytes 6291456 | tf_op jit(solution)/shard_map/cut_slot/pallas_call | solution.py:105
  8.7 1.6 %collective-permute-start.2 = (bf16[4,128,512]{2,1,0:T(8,128)(2,1)S(1)}, bf16[4,128,512]{2,1,0:T(8,128)(2,1)S(1)}, u32[]{:S(2)}, u32[]{:S(2)}) collective-permute-start(bf16[4,128,512]{2,1,0:T(8,128)(2,1)S(1)} %slice_select_fusion.4), channel_id=1, source_target_pairs={{0,2},{1,5},{2,0},{3,7},{4,6},{5,1},{6,4},{7,3},{8,10},{9,13},{10,... | collective-permute-start | bytes 1572872 | tf_op jit(solution)/shard_map/ppermute | solution.py:30
  10.2 2.0 %slice_select_fusion.2 = bf16[5,128,512]{2,1,0:T(8,128)(2,1)} fusion(bf16[9,128,512]{2,1,0:T(8,128)(2,1)} %collective-permute-done.1, bf16[9,128,512]{2,1,0:T(8,128)(2,1)S(1)} %get-tuple-element.10, pred[]{:T(512)S(6)} %eq.25), kind=kLoop, calls=%fused_computation.46 | loop fusion | flops 327680 | bytes 1966081 | tf_op jit(solution)/shard_map/jit(_where)/select_n | solution.py:178
  14.0 3.9 %collective-permute-done.2 = bf16[4,128,512]{2,1,0:T(8,128)(2,1)S(1)} collective-permute-done((bf16[4,128,512]{2,1,0:T(8,128)(2,1)S(1)}, bf16[4,128,512]{2,1,0:T(8,128)(2,1)S(1)}, u32[]{:S(2)}, u32[]{:S(2)}) %collective-permute-start.2) | collective-permute-done | bytes 524320 | tf_op jit(solution)/shard_map/ppermute | solution.py:30
  20.0 1.6 %collective-permute-start.3 = (bf16[4,128,512]{2,1,0:T(8,128)(2,1)S(1)}, bf16[4,128,512]{2,1,0:T(8,128)(2,1)S(1)}, u32[]{:S(2)}, u32[]{:S(2)}) collective-permute-start(bf16[4,128,512]{2,1,0:T(8,128)(2,1)S(1)} %fusion.34), channel_id=1, source_target_pairs={{0,4},{1,3},{2,6},{3,1},{4,0},{5,7},{6,2},{7,5},{8,12},{9,11},{10,... | collective-permute-start | bytes 1572872 | tf_op jit(solution)/shard_map/ppermute | solution.py:30
  22.9 5.1 %collective-permute-done.16 = bf16[5,128,512]{2,1,0:T(8,128)(2,1)} collective-permute-done((bf16[5,128,512]{2,1,0:T(8,128)(2,1)}, bf16[5,128,512]{2,1,0:T(8,128)(2,1)}, u32[]{:S(2)}, u32[]{:S(2)}) %collective-permute-start.16) | collective-permute-done | bytes 655392 | tf_op jit(solution)/shard_map/ppermute | solution.py:30
  29.4 1.6 %collective-permute-start.17 = (bf16[5,128,512]{2,1,0:T(8,128)(2,1)S(1)}, bf16[5,128,512]{2,1,0:T(8,128)(2,1)S(1)}, u32[]{:S(2)}, u32[]{:S(2)}) collective-permute-start(bf16[5,128,512]{2,1,0:T(8,128)(2,1)S(1)} %fusion.33), channel_id=1, source_target_pairs={{0,4},{1,3},{2,6},{3,1},{4,0},{5,7},{6,2},{7,5},{8,12},{9,11},{10,... | collective-permute-start | bytes 1966088 | tf_op jit(solution)/shard_map/ppermute | solution.py:30
  34.8 12.1 %collective-permute-done.17 = bf16[5,128,512]{2,1,0:T(8,128)(2,1)S(1)} collective-permute-done((bf16[5,128,512]{2,1,0:T(8,128)(2,1)S(1)}, bf16[5,128,512]{2,1,0:T(8,128)(2,1)S(1)}, u32[]{:S(2)}, u32[]{:S(2)}) %collective-permute-start.17) | collective-permute-done | bytes 655392 | tf_op jit(solution)/shard_map/ppermute | solution.py:30
  48.2 3.8 %collective-permute-start.12 = (bf16[2,2,128,256]{3,2,1,0:T(8,128)(2,1)S(1)}, bf16[2,2,128,256]{3,2,1,0:T(8,128)(2,1)S(1)}, u32[]{:S(2)}, u32[]{:S(2)}) collective-permute-start(bf16[2,2,128,256]{3,2,1,0:T(8,128)(2,1)S(1)} %pad_maximum_fusion.4), channel_id=1, source_target_pairs={{0,8},{8,16},{16,24},{1,9},{9,17},{17,25},{2,10},{10,18},{18,26},{... | collective-permute-start | bytes 786440 | tf_op jit(solution)/shard_map/ppermute | solution.py:12
  52.8 3.7 %collective-permute-done.12 = bf16[2,2,128,256]{3,2,1,0:T(8,128)(2,1)S(1)} collective-permute-done((bf16[2,2,128,256]{3,2,1,0:T(8,128)(2,1)S(1)}, bf16[2,2,128,256]{3,2,1,0:T(8,128)(2,1)S(1)}, u32[]{:S(2)}, u32[]{:S(2)}) %collective-permute-start.12) | collective-permute-done | bytes 262176 | tf_op jit(solution)/shard_map/ppermute | solution.py:12
  56.5 3.5 %collective-permute-done.18.refs_1_ = bf16[5,128,512]{2,1,0:T(8,128)(2,1)S(1)} collective-permute-done((bf16[5,128,512]{2,1,0:T(8,128)(2,1)S(1)}, bf16[5,128,512]{2,1,0:T(8,128)(2,1)S(1)}, u32[]{:S(2)}, u32[]{:S(2)}) %collective-permute-start.18) | collective-permute-done | bytes 655392 | tf_op jit(solution)/shard_map/ppermute | solution.py:30
  60.0 2.3 %collective-permute-start.13 = (bf16[2,2,128,256]{3,2,1,0:T(8,128)(2,1)S(1)}, bf16[2,2,128,256]{3,2,1,0:T(8,128)(2,1)S(1)}, u32[]{:S(2)}, u32[]{:S(2)}) collective-permute-start(bf16[2,2,128,256]{3,2,1,0:T(8,128)(2,1)S(1)} %collective-permute-done.12), channel_id=1, source_target_pairs={{0,1},{1,0},{2,3},{3,2},{4,5},{5,4},{6,7},{7,6},{8,9},{9,8},{10,11... | collective-permute-start | bytes 786440 | tf_op jit(solution)/shard_map/ppermute | solution.py:30
  63.7 1.6 %collective-permute-start.5 = (bf16[7,128,512]{2,1,0:T(8,128)(2,1)S(1)}, bf16[7,128,512]{2,1,0:T(8,128)(2,1)S(1)}, u32[]{:S(2)}, u32[]{:S(2)}) collective-permute-start(bf16[7,128,512]{2,1,0:T(8,128)(2,1)S(1)} %fusion.32), channel_id=1, source_target_pairs={{0,4},{1,3},{2,6},{3,1},{4,0},{5,7},{6,2},{7,5},{8,12},{9,11},{10,... | collective-permute-start | bytes 2752520 | tf_op jit(solution)/shard_map/ppermute | solution.py:30
  67.1 3.5 %collective-permute-start.14 = (bf16[256,1024]{1,0:T(8,128)(2,1)S(1)}, bf16[256,1024]{1,0:T(8,128)(2,1)S(1)}, u32[]{:S(2)}, u32[]{:S(2)}) collective-permute-start(bf16[256,1024]{1,0:T(8,128)(2,1)S(1)} %get-tuple-element.27), channel_id=1, source_target_pairs={{8,16},{16,8},{9,17},{17,9},{10,18},{18,10},{11,19},{19,11},{12,20... | collective-permute-start | bytes 1572872 | tf_op jit(solution)/shard_map/ppermute | solution.py:21
  74.9 2.2 %collective-permute-done.5 = bf16[7,128,512]{2,1,0:T(8,128)(2,1)S(1)} collective-permute-done((bf16[7,128,512]{2,1,0:T(8,128)(2,1)S(1)}, bf16[7,128,512]{2,1,0:T(8,128)(2,1)S(1)}, u32[]{:S(2)}, u32[]{:S(2)}) %collective-permute-start.5) | collective-permute-done | bytes 917536 | tf_op jit(solution)/shard_map/ppermute | solution.py:30
  78.6 2.1 %convolution_convert_fusion = bf16[3,512,1024]{2,1,0:T(8,128)(2,1)S(1)} fusion(bf16[5,512,512]{2,1,0:T(8,128)(2,1)S(1)} %place.7, bf16[3,512,1024]{2,1,0:T(8,128)(2,1)S(1)} %bitcast.89), kind=kOutput, calls=%fused_computation.2 | convolution fusion | flops 1612185600 | bytes 8912896 | tf_op jit(solution)/shard_map/nab,nac->nbc/dot_general | solution.py:226
  81.0 9.7 %collective-permute-done.6.refs_1_ = bf16[7,128,512]{2,1,0:T(8,128)(2,1)S(1)} collective-permute-done((bf16[7,128,512]{2,1,0:T(8,128)(2,1)S(1)}, bf16[7,128,512]{2,1,0:T(8,128)(2,1)S(1)}, u32[]{:S(2)}, u32[]{:S(2)}) %collective-permute-start.6) | collective-permute-done | bytes 917536 | tf_op jit(solution)/shard_map/ppermute | solution.py:30
  95.4 1.5 %convolution_convert_fusion.2 = bf16[2,512,1024]{2,1,0:T(8,128)(2,1)S(1)} fusion(bf16[7,512,512]{2,1,0:T(8,128)(2,1)S(1)} %place.4, bf16[2,512,1024]{2,1,0:T(8,128)(2,1)S(1)} %bitcast.93), kind=kOutput, calls=%fused_computation.12 | convolution fusion | flops 1074790400 | bytes 7864320 | tf_op jit(solution)/shard_map/nab,nac->nbc/dot_general | solution.py:226
  97.0 5.3 %collective-permute-start.21 = (bf16[256,1024]{1,0:T(8,128)(2,1)S(1)}, bf16[256,1024]{1,0:T(8,128)(2,1)S(1)}, u32[]{:S(2)}, u32[]{:S(2)}) collective-permute-start(bf16[256,1024]{1,0:T(8,128)(2,1)S(1)} %get-tuple-element.22), channel_id=1, source_target_pairs={{8,16},{16,8},{9,17},{17,9},{10,18},{18,10},{11,19},{19,11},{12,20... | collective-permute-start | bytes 1572872 | tf_op jit(solution)/shard_map/ppermute | solution.py:21
  102.7 2.1 %convolution_convert_fusion.1 = bf16[3,512,1024]{2,1,0:T(8,128)(2,1)S(1)} fusion(bf16[7,512,512]{2,1,0:T(8,128)(2,1)S(1)} %place.4, bf16[3,512,1024]{2,1,0:T(8,128)(2,1)S(1)} %bitcast.90), kind=kOutput, calls=%fused_computation.3 | convolution fusion | flops 1612185600 | bytes 9961472 | tf_op jit(solution)/shard_map/nab,nac->nbc/dot_general | solution.py:226
  104.8 2.7 %write_inner.1._ = bf16[2048,1024]{1,0:T(8,128)(2,1)} custom-call(bf16[1536,1024]{1,0:T(8,128)(2,1)S(1)} %bitcast.85), custom_call_target="tpu_custom_call" | custom-call | bytes 6291456 | tf_op jit(solution)/shard_map/write_inner/pallas_call | solution.py:236
  107.5 3.5 %collective-permute-done.22 = bf16[256,1024]{1,0:T(8,128)(2,1)S(1)} collective-permute-done((bf16[256,1024]{1,0:T(8,128)(2,1)S(1)}, bf16[256,1024]{1,0:T(8,128)(2,1)S(1)}, u32[]{:S(2)}, u32[]{:S(2)}) %collective-permute-start.22) | collective-permute-done | bytes 524320 | tf_op jit(solution)/shard_map/ppermute | solution.py:21
  111.0 3.0 %collective-permute-done.21 = bf16[256,1024]{1,0:T(8,128)(2,1)S(1)} collective-permute-done((bf16[256,1024]{1,0:T(8,128)(2,1)S(1)}, bf16[256,1024]{1,0:T(8,128)(2,1)S(1)}, u32[]{:S(2)}, u32[]{:S(2)}) %collective-permute-start.21) | collective-permute-done | bytes 524320 | tf_op jit(solution)/shard_map/ppermute | solution.py:21
  (84 shorter events, 29.4 us)
Async XLA Ops:
  3.0 4.5 %collective-permute-start.1 = (bf16[9,128,512]{2,1,0:T(8,128)(2,1)S(1)}, bf16[9,128,512]{2,1,0:T(8,128)(2,1)}, u32[]{:S(2)}, u32[]{:S(2)}) collective-permute-start(bf16[9,128,512]{2,1,0:T(8,128)(2,1)S(1)} %cut_slot.3), channel_id=1, source_target_pairs={{0,1},{1,0},{2,3},{3,2},{4,5},{5,4},{6,7},{7,6},{8,9},{9,8},{10,11... | collective-permute-start | bytes 3538952 | tf_op jit(solution)/shard_map/ppermute | solution.py:30
  5.0 9.0 %collective-permute-start = (bf16[9,128,512]{2,1,0:T(8,128)(2,1)}, bf16[9,128,512]{2,1,0:T(8,128)(2,1)}, u32[]{:S(2)}, u32[]{:S(2)}) collective-permute-start(bf16[9,128,512]{2,1,0:T(8,128)(2,1)} %get-tuple-element.9), channel_id=1, source_target_pairs={{0,1},{1,0},{2,3},{3,2},{4,5},{5,4},{6,7},{7,6},{8,9},{9,8},{10,11... | collective-permute-start | bytes 3538952 | tf_op jit(solution)/shard_map/ppermute | solution.py:30
  8.7 9.2 %collective-permute-start.2 = (bf16[4,128,512]{2,1,0:T(8,128)(2,1)S(1)}, bf16[4,128,512]{2,1,0:T(8,128)(2,1)S(1)}, u32[]{:S(2)}, u32[]{:S(2)}) collective-permute-start(bf16[4,128,512]{2,1,0:T(8,128)(2,1)S(1)} %slice_select_fusion.4), channel_id=1, source_target_pairs={{0,2},{1,5},{2,0},{3,7},{4,6},{5,1},{6,4},{7,3},{8,10},{9,13},{10,... | collective-permute-start | bytes 1572872 | tf_op jit(solution)/shard_map/ppermute | solution.py:30
  12.2 15.8 %collective-permute-start.16 = (bf16[5,128,512]{2,1,0:T(8,128)(2,1)}, bf16[5,128,512]{2,1,0:T(8,128)(2,1)}, u32[]{:S(2)}, u32[]{:S(2)}) collective-permute-start(bf16[5,128,512]{2,1,0:T(8,128)(2,1)} %slice_select_fusion.2), channel_id=1, source_target_pairs={{0,2},{1,5},{2,0},{3,7},{4,6},{5,1},{6,4},{7,3},{8,10},{9,13},{10,... | collective-permute-start | bytes 1966088 | tf_op jit(solution)/shard_map/ppermute | solution.py:30
  20.0 10.9 %collective-permute-start.3 = (bf16[4,128,512]{2,1,0:T(8,128)(2,1)S(1)}, bf16[4,128,512]{2,1,0:T(8,128)(2,1)S(1)}, u32[]{:S(2)}, u32[]{:S(2)}) collective-permute-start(bf16[4,128,512]{2,1,0:T(8,128)(2,1)S(1)} %fusion.34), channel_id=1, source_target_pairs={{0,4},{1,3},{2,6},{3,1},{4,0},{5,7},{6,2},{7,5},{8,12},{9,11},{10,... | collective-permute-start | bytes 1572872 | tf_op jit(solution)/shard_map/ppermute | solution.py:30
  29.4 17.5 %collective-permute-start.17 = (bf16[5,128,512]{2,1,0:T(8,128)(2,1)S(1)}, bf16[5,128,512]{2,1,0:T(8,128)(2,1)S(1)}, u32[]{:S(2)}, u32[]{:S(2)}) collective-permute-start(bf16[5,128,512]{2,1,0:T(8,128)(2,1)S(1)} %fusion.33), channel_id=1, source_target_pairs={{0,4},{1,3},{2,6},{3,1},{4,0},{5,7},{6,2},{7,5},{8,12},{9,11},{10,... | collective-permute-start | bytes 1966088 | tf_op jit(solution)/shard_map/ppermute | solution.py:30
  31.1 17.1 %collective-permute-start.9 = (bf16[4,128,512]{2,1,0:T(8,128)(2,1)S(1)}, bf16[4,128,512]{2,1,0:T(8,128)(2,1)S(1)}, u32[]{:S(2)}, u32[]{:S(2)}) collective-permute-start(bf16[4,128,512]{2,1,0:T(8,128)(2,1)S(1)} %broadcast_select_fusion.2.refs_0_), channel_id=1, source_target_pairs={{0,2},{1,5},{2,0},{3,7},{4,6},{5,1},{6,4},{7,3},{8,10},{9,13},{10,... | collective-permute-start | bytes 1572872 | tf_op jit(solution)/shard_map/ppermute | solution.py:30
  33.7 18.3 %copy-start.3 = (bf16[2048,1024]{1,0:T(8,128)(2,1)S(1)}, bf16[2048,1024]{1,0:T(8,128)(2,1)}, u32[]{:S(2)}) copy-start(bf16[2048,1024]{1,0:T(8,128)(2,1)} %param.3) | copy-start | bytes 12582916
  34.0 28.3 %collective-permute-start.4 = (bf16[7,128,512]{2,1,0:T(8,128)(2,1)S(1)}, bf16[7,128,512]{2,1,0:T(8,128)(2,1)S(1)}, u32[]{:S(2)}, u32[]{:S(2)}) collective-permute-start(bf16[7,128,512]{2,1,0:T(8,128)(2,1)S(1)} %after.1), channel_id=1, source_target_pairs={{0,2},{1,5},{2,0},{3,7},{4,6},{5,1},{6,4},{7,3},{8,10},{9,13},{10,... | collective-permute-start | bytes 2752520 | tf_op jit(solution)/shard_map/ppermute | solution.py:30
  46.9 13.1 %collective-permute-start.18 = (bf16[5,128,512]{2,1,0:T(8,128)(2,1)S(1)}, bf16[5,128,512]{2,1,0:T(8,128)(2,1)S(1)}, u32[]{:S(2)}, u32[]{:S(2)}) collective-permute-start(bf16[5,128,512]{2,1,0:T(8,128)(2,1)S(1)} %broadcast_select_fusion.1.refs_0_), channel_id=1, source_target_pairs={{0,2},{1,5},{2,0},{3,7},{4,6},{5,1},{6,4},{7,3},{8,10},{9,13},{10,... | collective-permute-start | bytes 1966088 | tf_op jit(solution)/shard_map/ppermute | solution.py:30
  48.2 8.3 %collective-permute-start.12 = (bf16[2,2,128,256]{3,2,1,0:T(8,128)(2,1)S(1)}, bf16[2,2,128,256]{3,2,1,0:T(8,128)(2,1)S(1)}, u32[]{:S(2)}, u32[]{:S(2)}) collective-permute-start(bf16[2,2,128,256]{3,2,1,0:T(8,128)(2,1)S(1)} %pad_maximum_fusion.4), channel_id=1, source_target_pairs={{0,8},{8,16},{16,24},{1,9},{9,17},{17,25},{2,10},{10,18},{18,26},{... | collective-permute-start | bytes 786440 | tf_op jit(solution)/shard_map/ppermute | solution.py:12
  52.2 11.5 %collective-permute-start.10 = (bf16[4,128,512]{2,1,0:T(8,128)(2,1)S(1)}, bf16[4,128,512]{2,1,0:T(8,128)(2,1)S(1)}, u32[]{:S(2)}, u32[]{:S(2)}) collective-permute-start(bf16[4,128,512]{2,1,0:T(8,128)(2,1)S(1)} %broadcast_select_fusion.2.refs_0_), channel_id=1, source_target_pairs={{0,1},{1,0},{2,3},{3,2},{4,5},{5,4},{6,7},{7,6},{8,9},{9,8},{10,11... | collective-permute-start | bytes 1572872 | tf_op jit(solution)/shard_map/ppermute | solution.py:30
  52.3 19.1 %collective-permute-start.19 = (bf16[5,128,512]{2,1,0:T(8,128)(2,1)S(1)}, bf16[5,128,512]{2,1,0:T(8,128)(2,1)S(1)}, u32[]{:S(2)}, u32[]{:S(2)}) collective-permute-start(bf16[5,128,512]{2,1,0:T(8,128)(2,1)S(1)} %broadcast_select_fusion.1.refs_0_), channel_id=1, source_target_pairs={{0,1},{1,0},{2,3},{3,2},{4,5},{5,4},{6,7},{7,6},{8,9},{9,8},{10,11... | collective-permute-start | bytes 1966088 | tf_op jit(solution)/shard_map/ppermute | solution.py:30
  56.5 8.8 %collective-permute-start.11 = (bf16[4,128,512]{2,1,0:T(8,128)(2,1)S(1)}, bf16[4,128,512]{2,1,0:T(8,128)(2,1)S(1)}, u32[]{:S(2)}, u32[]{:S(2)}) collective-permute-start(bf16[4,128,512]{2,1,0:T(8,128)(2,1)S(1)} %collective-permute-done.9.refs_1_), channel_id=1, source_target_pairs={{0,1},{1,0},{2,3},{3,2},{4,5},{5,4},{6,7},{7,6},{8,9},{9,8},{10,11... | collective-permute-start | bytes 1572872 | tf_op jit(solution)/shard_map/ppermute | solution.py:30
  60.0 10.9 %collective-permute-start.13 = (bf16[2,2,128,256]{3,2,1,0:T(8,128)(2,1)S(1)}, bf16[2,2,128,256]{3,2,1,0:T(8,128)(2,1)S(1)}, u32[]{:S(2)}, u32[]{:S(2)}) collective-permute-start(bf16[2,2,128,256]{3,2,1,0:T(8,128)(2,1)S(1)} %collective-permute-done.12), channel_id=1, source_target_pairs={{0,1},{1,0},{2,3},{3,2},{4,5},{5,4},{6,7},{7,6},{8,9},{9,8},{10,11... | collective-permute-start | bytes 786440 | tf_op jit(solution)/shard_map/ppermute | solution.py:30
  62.3 9.1 %collective-permute-start.20 = (bf16[5,128,512]{2,1,0:T(8,128)(2,1)S(1)}, bf16[5,128,512]{2,1,0:T(8,128)(2,1)S(1)}, u32[]{:S(2)}, u32[]{:S(2)}) collective-permute-start(bf16[5,128,512]{2,1,0:T(8,128)(2,1)S(1)} %collective-permute-done.18.refs_1_), channel_id=1, source_target_pairs={{0,1},{1,0},{2,3},{3,2},{4,5},{5,4},{6,7},{7,6},{8,9},{9,8},{10,11... | collective-permute-start | bytes 1966088 | tf_op jit(solution)/shard_map/ppermute | solution.py:30
  63.7 13.5 %collective-permute-start.5 = (bf16[7,128,512]{2,1,0:T(8,128)(2,1)S(1)}, bf16[7,128,512]{2,1,0:T(8,128)(2,1)S(1)}, u32[]{:S(2)}, u32[]{:S(2)}) collective-permute-start(bf16[7,128,512]{2,1,0:T(8,128)(2,1)S(1)} %fusion.32), channel_id=1, source_target_pairs={{0,4},{1,3},{2,6},{3,1},{4,0},{5,7},{6,2},{7,5},{8,12},{9,11},{10,... | collective-permute-start | bytes 2752520 | tf_op jit(solution)/shard_map/ppermute | solution.py:30
  67.1 23.6 %collective-permute-start.14 = (bf16[256,1024]{1,0:T(8,128)(2,1)S(1)}, bf16[256,1024]{1,0:T(8,128)(2,1)S(1)}, u32[]{:S(2)}, u32[]{:S(2)}) collective-permute-start(bf16[256,1024]{1,0:T(8,128)(2,1)S(1)} %get-tuple-element.27), channel_id=1, source_target_pairs={{8,16},{16,8},{9,17},{17,9},{10,18},{18,10},{11,19},{19,11},{12,20... | collective-permute-start | bytes 1572872 | tf_op jit(solution)/shard_map/ppermute | solution.py:21
  70.9 19.8 %collective-permute-start.15 = (bf16[256,1024]{1,0:T(8,128)(2,1)S(1)}, bf16[256,1024]{1,0:T(8,128)(2,1)S(1)}, u32[]{:S(2)}, u32[]{:S(2)}) collective-permute-start(bf16[256,1024]{1,0:T(8,128)(2,1)S(1)} %get-tuple-element.28), channel_id=1, source_target_pairs={{0,8},{16,24},{8,0},{24,16},{1,9},{17,25},{9,1},{25,17},{2,10},{18... | collective-permute-start | bytes 1572872 | tf_op jit(solution)/shard_map/ppermute | solution.py:21
  77.3 13.5 %collective-permute-start.6 = (bf16[7,128,512]{2,1,0:T(8,128)(2,1)S(1)}, bf16[7,128,512]{2,1,0:T(8,128)(2,1)S(1)}, u32[]{:S(2)}, u32[]{:S(2)}) collective-permute-start(bf16[7,128,512]{2,1,0:T(8,128)(2,1)S(1)} %broadcast_select_fusion.refs_0_), channel_id=1, source_target_pairs={{0,2},{1,5},{2,0},{3,7},{4,6},{5,1},{6,4},{7,3},{8,10},{9,13},{10,... | collective-permute-start | bytes 2752520 | tf_op jit(solution)/shard_map/ppermute | solution.py:30
  80.9 11.0 %collective-permute-start.7 = (bf16[7,128,512]{2,1,0:T(8,128)(2,1)S(1)}, bf16[7,128,512]{2,1,0:T(8,128)(2,1)S(1)}, u32[]{:S(2)}, u32[]{:S(2)}) collective-permute-start(bf16[7,128,512]{2,1,0:T(8,128)(2,1)S(1)} %broadcast_select_fusion.refs_0_), channel_id=1, source_target_pairs={{0,1},{1,0},{2,3},{3,2},{4,5},{5,4},{6,7},{7,6},{8,9},{9,8},{10,11... | collective-permute-start | bytes 2752520 | tf_op jit(solution)/shard_map/ppermute | solution.py:30
  90.7 2.5 %collective-permute-start.8 = (bf16[7,128,512]{2,1,0:T(8,128)(2,1)S(1)}, bf16[7,128,512]{2,1,0:T(8,128)(2,1)S(1)}, u32[]{:S(2)}, u32[]{:S(2)}) collective-permute-start(bf16[7,128,512]{2,1,0:T(8,128)(2,1)S(1)} %collective-permute-done.6.refs_1_), channel_id=1, source_target_pairs={{0,1},{1,0},{2,3},{3,2},{4,5},{5,4},{6,7},{7,6},{8,9},{9,8},{10,11... | collective-permute-start | bytes 2752520 | tf_op jit(solution)/shard_map/ppermute | solution.py:30
  96.9 14.0 %collective-permute-start.22 = (bf16[256,1024]{1,0:T(8,128)(2,1)S(1)}, bf16[256,1024]{1,0:T(8,128)(2,1)S(1)}, u32[]{:S(2)}, u32[]{:S(2)}) collective-permute-start(bf16[256,1024]{1,0:T(8,128)(2,1)S(1)} %get-tuple-element.21), channel_id=1, source_target_pairs={{0,8},{16,24},{8,0},{24,16},{1,9},{17,25},{9,1},{25,17},{2,10},{18... | collective-permute-start | bytes 1572872 | tf_op jit(solution)/shard_map/ppermute | solution.py:21
  97.0 17.0 %collective-permute-start.21 = (bf16[256,1024]{1,0:T(8,128)(2,1)S(1)}, bf16[256,1024]{1,0:T(8,128)(2,1)S(1)}, u32[]{:S(2)}, u32[]{:S(2)}) collective-permute-start(bf16[256,1024]{1,0:T(8,128)(2,1)S(1)} %get-tuple-element.22), channel_id=1, source_target_pairs={{8,16},{16,8},{9,17},{17,9},{10,18},{18,10},{11,19},{19,11},{12,20... | collective-permute-start | bytes 1572872 | tf_op jit(solution)/shard_map/ppermute | solution.py:21
  (5 other events, 11.2 us)

commit v11 on v10

--- a/solution.py
+++ b/solution.py
@@ -211,8 +211,9 @@
     def join(self, hold, got):
         return place(self.cut, hold, got, flip(hold, (0, 0)), flip(got, (0, 0)))
 
-    def join_above(self, hold, got):
-        both = shifted(jnp.stack([hold, got]), "rows", 1)
+    def join_above(self, hold, got, *later):
+        both = jnp.stack([hold, got])
+        both = shifted(after(both, *later) if later else both, "rows", 1)
         other = flip(both, (0, 0))
         return place(self.cut, both[0], both[1], other[0], other[1])
 
@@ -285,16 +286,18 @@
     middle_one, middle_two = list(range(1, wins - 1)), list(range(wins, crossing))
     order = [crossing, crossing, 0, wins - 1] + middle_one + middle_two
     spread = Spread(slot, owners[:, row_block], order)
-    streams = []
+    streams, opening = [], None
     for r in range(rounds):
         across = ([r + 1] if r + 1 < rounds else []) + ([r] if r == 0 else [])
         first = 2 - len(across)
         if r == 0:
             streams.append(spread.middle(spread.begin(across + [r, r], slice(first, 4))))
-            streams.append(spread.middle(spread.begin([r] * (len(order) - 4), slice(4, len(order)))))
+            opening = spread.begin([r] * (len(order) - 4), slice(4, len(order)))
+            streams.append(spread.middle(opening))
         else:
-            begun = spread.begin(across + [r] * crossing, slice(first, len(order)), streams[r - 1][2])
+            begun = spread.begin(across + [r] * crossing, slice(first, len(order)), opening[2])
             streams.append(spread.middle(begun))
+            opening = begun
     pairs = [spread.last(stream) for stream in streams]
 
     matrix = slab
@@ -305,7 +308,10 @@
         across = ([r + 1] if r + 1 < rounds else []) + ([r] if r == 0 else [])
         if across:
             n = len(across)
-            from_above = spread.join_above(head[0][:n, :, border:], head[1][:n, :, border:])
+            later = [streams[r + 2][1]] if r + 2 < len(streams) else []
+            from_above = spread.join_above(
+                head[0][:n, :, border:], head[1][:n, :, border:], *later
+            )
             for k, q in enumerate(across):
                 crosses[q], above_crosses[q] = edges[k], from_above[k]
             edges = edges[n:]

time: 117 us -> 119 us (1.017)
  local copies, waits for them, and re-layouts: 5.82 us -> 3.73 us
  other arithmetic: 10.1 us -> 12 us
  starting transfers between devices: 27.8 us -> 29 us
    ppermute x18, starting transfers between devices: 15.1 us -> 18 us  [flip(): lax.ppermute(value, 'cols', [(d, d ^ 1 << bits[d & 1]) for d in range(cou...]
    select_n x9, other arithmetic: 8.83 us -> 10.7 us  [choose(): return jnp.where(mask, yes, no)]
    ppermute x4, starting transfers between devices: 8.9 us -> 7.51 us  [swap(): return lax.ppermute(value, 'rows', pairs + [(b, a) for a, b in pairs])]
    slice x3, local copies, waits for them, and re-layouts: 1.49 us -> 0.18 us  [local(): matrix[window:local_rows - window].reshape(wins - 2, window, local_cols)]
    unnamed x10 -> x8, local copies, waits for them, and re-layouts: 3.01 us -> 2.22 us
  transfers between devices with their start and end apart: 23 -> 23, of which waited for: 10 -> 10; matrix products, arithmetic and copies ran while one was open for 17% -> 20% of each run, Pallas kernels for 5% -> 5%
where the time goes in v11:
time: 119 us; the launch traced here: 117 us
  waiting for transfers between devices  47.3 us (40%)
  starting transfers between devices  29 us (24%)
  matrix products  12.2 us (10%)
  other arithmetic  12 us (10%)
  Pallas kernels  8.62 us (7%)
  between operations  4.24 us (4%)
  local copies, waits for them, and re-layouts  3.73 us (3%)
    ppermute x18, waiting for transfers between devices, flip(): lax.ppermute(value, 'cols', [(d, d ^ 1 << bits[d & 1]) for d in range(cou...  36.7 us
    ppermute x18, starting transfers between devices, flip(): lax.ppermute(value, 'cols', [(d, d ^ 1 << bits[d & 1]) for d in range(cou...  18 us
    select_n x9, other arithmetic, choose(): return jnp.where(mask, yes, no)  10.7 us
    dot_general x6, matrix products, apply_many(): jnp.einsum('nab,nac->nbc', q, x, preferred_element_type=jnp.float32)  10.3 us
    ppermute x4, starting transfers between devices, swap(): return lax.ppermute(value, 'rows', pairs + [(b, a) for a, b in pairs])  7.51 us
    ppermute x4, waiting for transfers between devices, swap(): return lax.ppermute(value, 'rows', pairs + [(b, a) for a, b in pairs])  6.95 us
    ppermute x1, waiting for transfers between devices, shifted(): lax.ppermute(value, axis, [(source, source + steps) for source in range(i...  3.65 us
    ppermute x1, starting transfers between devices, shifted(): lax.ppermute(value, axis, [(source, source + steps) for source in range(i...  3.48 us
  transfers between devices with their start and end apart: 23, of which 10 were waited for; matrix products, arithmetic and copies ran while one was open for 20% of the time, Pallas kernels for 5%

profile of v11, /device:TPU:8, one launch (start us, length us, event | category | flops | bytes accessed | tf_op | source)
XLA Modules:
  0.0 117.1 jit_solution(12690682611127463316)
XLA Ops:
  0.0 2.2 %copy-done.2 = bf16[1,4096,512]{2,1,0:T(8,128)(2,1)S(1)} copy-done((bf16[1,4096,512]{2,1,0:T(8,128)(2,1)S(1)}, bf16[1,4096,512]{2,1,0:T(8,128)(2,1)}, u32[]{:S(2)}) %copy-start.2) | copy-done | bytes 4194328
  3.1 1.9 %cut_slot.2 = (bf16[9,128,512]{2,1,0:T(8,128)(2,1)S(1)}, bf16[9,128,512]{2,1,0:T(8,128)(2,1)}, bf16[9,128,512]{2,1,0:T(8,128)(2,1)S(1)}) custom-call(bf16[8,2,2,128,512]{4,3,2,1,0:T(8,128)(2,1)S(1)} %bitcast.84), custom_call_target="tpu_custom_call" | custom-call | bytes 6291456 | tf_op jit(solution)/shard_map/cut_slot/pallas_call | solution.py:105
  10.2 2.0 %slice_select_fusion.3 = bf16[5,128,512]{2,1,0:T(8,128)(2,1)} fusion(bf16[9,128,512]{2,1,0:T(8,128)(2,1)} %collective-permute-done.1, bf16[9,128,512]{2,1,0:T(8,128)(2,1)S(1)} %get-tuple-element.10, pred[]{:T(512)S(6)} %eq.24), kind=kLoop, calls=%fused_computation.48 | loop fusion | flops 327680 | bytes 1966081 | tf_op jit(solution)/shard_map/jit(_where)/select_n | solution.py:178
  15.3 2.7 %collective-permute-done.8 = bf16[4,128,512]{2,1,0:T(8,128)(2,1)} collective-permute-done((bf16[4,128,512]{2,1,0:T(8,128)(2,1)S(1)}, bf16[4,128,512]{2,1,0:T(8,128)(2,1)}, u32[]{:S(2)}, u32[]{:S(2)}) %collective-permute-start.8) | collective-permute-done | bytes 524320 | tf_op jit(solution)/shard_map/ppermute | solution.py:30
  19.4 1.6 %collective-permute-start.9 = (bf16[4,128,512]{2,1,0:T(8,128)(2,1)S(1)}, bf16[4,128,512]{2,1,0:T(8,128)(2,1)S(1)}, u32[]{:S(2)}, u32[]{:S(2)}) collective-permute-start(bf16[4,128,512]{2,1,0:T(8,128)(2,1)S(1)} %fusion.34), channel_id=1, source_target_pairs={{0,4},{1,3},{2,6},{3,1},{4,0},{5,7},{6,2},{7,5},{8,12},{9,11},{10,... | collective-permute-start | bytes 1572872 | tf_op jit(solution)/shard_map/ppermute | solution.py:30
  21.0 7.6 %collective-permute-done.2.refs_0_ = bf16[5,128,512]{2,1,0:T(8,128)(2,1)S(1)} collective-permute-done((bf16[5,128,512]{2,1,0:T(8,128)(2,1)}, bf16[5,128,512]{2,1,0:T(8,128)(2,1)S(1)}, u32[]{:S(2)}, u32[]{:S(2)}) %collective-permute-start.2) | collective-permute-done | bytes 655392 | tf_op jit(solution)/shard_map/ppermute | solution.py:30
  28.6 2.1 %fusion.33 = bf16[5,128,512]{2,1,0:T(8,128)(2,1)} fusion(bf16[5,128,512]{2,1,0:T(8,128)(2,1)S(1)} %collective-permute-done.2.refs_0_, bf16[9,128,512]{2,1,0:T(8,128)(2,1)} %collective-permute-done, bf16[9,128,512]{2,1,0:T(8,128)(2,1)S(1)} %get-tuple-element.8, pred[]{:T(512)S(6)} %eq.27, pred[]{:T(512)S(6)} %eq.24), kind=kLoop, calls=%fused_computation.47 | loop fusion | flops 655360 | bytes 2621442 | tf_op jit(solution)/shard_map/jit(_where)/select_n | solution.py:178
  36.7 11.9 %collective-permute-done.17 = bf16[5,128,512]{2,1,0:T(8,128)(2,1)} collective-permute-done((bf16[5,128,512]{2,1,0:T(8,128)(2,1)}, bf16[5,128,512]{2,1,0:T(8,128)(2,1)}, u32[]{:S(2)}, u32[]{:S(2)}) %collective-permute-start.17) | collective-permute-done | bytes 655392 | tf_op jit(solution)/shard_map/ppermute | solution.py:30
  49.7 1.6 %collective-permute-start.18 = (bf16[5,128,512]{2,1,0:T(8,128)(2,1)S(1)}, bf16[5,128,512]{2,1,0:T(8,128)(2,1)S(1)}, u32[]{:S(2)}, u32[]{:S(2)}) collective-permute-start(bf16[5,128,512]{2,1,0:T(8,128)(2,1)S(1)} %broadcast_select_fusion.1.refs_0_), channel_id=1, source_target_pairs={{0,2},{1,5},{2,0},{3,7},{4,6},{5,1},{6,4},{7,3},{8,10},{9,13},{10,... | collective-permute-start | bytes 1966088 | tf_op jit(solution)/shard_map/ppermute | solution.py:30
  51.4 2.3 %collective-permute-done.10.refs_1_ = bf16[4,128,512]{2,1,0:T(8,128)(2,1)S(1)} collective-permute-done((bf16[4,128,512]{2,1,0:T(8,128)(2,1)S(1)}, bf16[4,128,512]{2,1,0:T(8,128)(2,1)S(1)}, u32[]{:S(2)}, u32[]{:S(2)}) %collective-permute-start.10) | collective-permute-done | bytes 524320 | tf_op jit(solution)/shard_map/ppermute | solution.py:30
  55.3 3.5 %collective-permute-start.13 = (bf16[2,2,128,256]{3,2,1,0:T(8,128)(2,1)S(1)}, bf16[2,2,128,256]{3,2,1,0:T(8,128)(2,1)S(1)}, u32[]{:S(2)}, u32[]{:S(2)}) collective-permute-start(bf16[2,2,128,256]{3,2,1,0:T(8,128)(2,1)S(1)} %after.3), channel_id=1, source_target_pairs={{0,8},{8,16},{16,24},{1,9},{9,17},{17,25},{2,10},{10,18},{18,26},{... | collective-permute-start | bytes 786440 | tf_op jit(solution)/shard_map/ppermute | solution.py:12
  58.8 2.2 %collective-permute-start.12 = (bf16[4,128,512]{2,1,0:T(8,128)(2,1)S(1)}, bf16[4,128,512]{2,1,0:T(8,128)(2,1)S(1)}, u32[]{:S(2)}, u32[]{:S(2)}) collective-permute-start(bf16[4,128,512]{2,1,0:T(8,128)(2,1)S(1)} %collective-permute-done.10.refs_1_), channel_id=1, source_target_pairs={{0,1},{1,0},{2,3},{3,2},{4,5},{5,4},{6,7},{7,6},{8,9},{9,8},{10,11... | collective-permute-start | bytes 1572872 | tf_op jit(solution)/shard_map/ppermute | solution.py:30
  61.2 3.6 %collective-permute-done.13 = bf16[2,2,128,256]{3,2,1,0:T(8,128)(2,1)S(1)} collective-permute-done((bf16[2,2,128,256]{3,2,1,0:T(8,128)(2,1)S(1)}, bf16[2,2,128,256]{3,2,1,0:T(8,128)(2,1)S(1)}, u32[]{:S(2)}, u32[]{:S(2)}) %collective-permute-start.13) | collective-permute-done | bytes 262176 | tf_op jit(solution)/shard_map/ppermute | solution.py:12
  64.9 2.9 %collective-permute-start.14 = (bf16[2,2,128,256]{3,2,1,0:T(8,128)(2,1)S(1)}, bf16[2,2,128,256]{3,2,1,0:T(8,128)(2,1)S(1)}, u32[]{:S(2)}, u32[]{:S(2)}) collective-permute-start(bf16[2,2,128,256]{3,2,1,0:T(8,128)(2,1)S(1)} %collective-permute-done.13), channel_id=1, source_target_pairs={{0,1},{1,0},{2,3},{3,2},{4,5},{5,4},{6,7},{7,6},{8,9},{9,8},{10,11... | collective-permute-start | bytes 786440 | tf_op jit(solution)/shard_map/ppermute | solution.py:30
  69.8 3.7 %collective-permute-start.15 = (bf16[256,1024]{1,0:T(8,128)(2,1)S(1)}, bf16[256,1024]{1,0:T(8,128)(2,1)S(1)}, u32[]{:S(2)}, u32[]{:S(2)}) collective-permute-start(bf16[256,1024]{1,0:T(8,128)(2,1)S(1)} %get-tuple-element.27), channel_id=1, source_target_pairs={{8,16},{16,8},{9,17},{17,9},{10,18},{18,10},{11,19},{19,11},{12,20... | collective-permute-start | bytes 1572872 | tf_op jit(solution)/shard_map/ppermute | solution.py:21
  74.2 4.0 %collective-permute-done.4 = bf16[7,128,512]{2,1,0:T(8,128)(2,1)S(1)} collective-permute-done((bf16[7,128,512]{2,1,0:T(8,128)(2,1)S(1)}, bf16[7,128,512]{2,1,0:T(8,128)(2,1)S(1)}, u32[]{:S(2)}, u32[]{:S(2)}) %collective-permute-start.4) | collective-permute-done | bytes 917536 | tf_op jit(solution)/shard_map/ppermute | solution.py:30
  78.4 3.1 %collective-permute-start.5 = (bf16[7,128,512]{2,1,0:T(8,128)(2,1)S(1)}, bf16[7,128,512]{2,1,0:T(8,128)(2,1)S(1)}, u32[]{:S(2)}, u32[]{:S(2)}) collective-permute-start(bf16[7,128,512]{2,1,0:T(8,128)(2,1)S(1)} %broadcast_select_fusion.refs_0_), channel_id=1, source_target_pairs={{0,2},{1,5},{2,0},{3,7},{4,6},{5,1},{6,4},{7,3},{8,10},{9,13},{10,... | collective-permute-start | bytes 2752520 | tf_op jit(solution)/shard_map/ppermute | solution.py:30
  83.7 2.1 %convolution_convert_fusion = bf16[3,512,1024]{2,1,0:T(8,128)(2,1)S(1)} fusion(bf16[5,512,512]{2,1,0:T(8,128)(2,1)S(1)} %place.7, bf16[3,512,1024]{2,1,0:T(8,128)(2,1)S(1)} %bitcast.89), kind=kOutput, calls=%fused_computation.2 | convolution fusion | flops 1612185600 | bytes 8912896 | tf_op jit(solution)/shard_map/nab,nac->nbc/dot_general | solution.py:227
  86.0 6.9 %collective-permute-done.5.refs_1_ = bf16[7,128,512]{2,1,0:T(8,128)(2,1)S(1)} collective-permute-done((bf16[7,128,512]{2,1,0:T(8,128)(2,1)S(1)}, bf16[7,128,512]{2,1,0:T(8,128)(2,1)S(1)}, u32[]{:S(2)}, u32[]{:S(2)}) %collective-permute-start.5) | collective-permute-done | bytes 917536 | tf_op jit(solution)/shard_map/ppermute | solution.py:30
  97.6 3.7 %collective-permute-start.21 = (bf16[256,1024]{1,0:T(8,128)(2,1)S(1)}, bf16[256,1024]{1,0:T(8,128)(2,1)S(1)}, u32[]{:S(2)}, u32[]{:S(2)}) collective-permute-start(bf16[256,1024]{1,0:T(8,128)(2,1)S(1)} %get-tuple-element.22), channel_id=1, source_target_pairs={{8,16},{16,8},{9,17},{17,9},{10,18},{18,10},{11,19},{19,11},{12,20... | collective-permute-start | bytes 1572872 | tf_op jit(solution)/shard_map/ppermute | solution.py:21
  103.3 2.1 %convolution_convert_fusion.1 = bf16[3,512,1024]{2,1,0:T(8,128)(2,1)S(1)} fusion(bf16[7,512,512]{2,1,0:T(8,128)(2,1)S(1)} %place.4, bf16[3,512,1024]{2,1,0:T(8,128)(2,1)S(1)} %bitcast.90), kind=kOutput, calls=%fused_computation.3 | convolution fusion | flops 1612185600 | bytes 9961472 | tf_op jit(solution)/shard_map/nab,nac->nbc/dot_general | solution.py:227
  105.4 2.7 %write_inner.1._ = bf16[2048,1024]{1,0:T(8,128)(2,1)} custom-call(bf16[1536,1024]{1,0:T(8,128)(2,1)S(1)} %bitcast.85), custom_call_target="tpu_custom_call" | custom-call | bytes 6291456 | tf_op jit(solution)/shard_map/write_inner/pallas_call | solution.py:237
  108.1 5.3 %collective-permute-done.21 = bf16[256,1024]{1,0:T(8,128)(2,1)S(1)} collective-permute-done((bf16[256,1024]{1,0:T(8,128)(2,1)S(1)}, bf16[256,1024]{1,0:T(8,128)(2,1)S(1)}, u32[]{:S(2)}, u32[]{:S(2)}) %collective-permute-start.21) | collective-permute-done | bytes 524320 | tf_op jit(solution)/shard_map/ppermute | solution.py:21
  113.4 1.6 %collective-permute-done.22 = bf16[256,1024]{1,0:T(8,128)(2,1)S(1)} collective-permute-done((bf16[256,1024]{1,0:T(8,128)(2,1)S(1)}, bf16[256,1024]{1,0:T(8,128)(2,1)S(1)}, u32[]{:S(2)}, u32[]{:S(2)}) %collective-permute-start.22) | collective-permute-done | bytes 524320 | tf_op jit(solution)/shard_map/ppermute | solution.py:21
  (83 shorter events, 29.4 us)
Async XLA Ops:
  3.0 4.5 %collective-permute-start.1 = (bf16[9,128,512]{2,1,0:T(8,128)(2,1)S(1)}, bf16[9,128,512]{2,1,0:T(8,128)(2,1)}, u32[]{:S(2)}, u32[]{:S(2)}) collective-permute-start(bf16[9,128,512]{2,1,0:T(8,128)(2,1)S(1)} %cut_slot.3), channel_id=1, source_target_pairs={{0,1},{1,0},{2,3},{3,2},{4,5},{5,4},{6,7},{7,6},{8,9},{9,8},{10,11... | collective-permute-start | bytes 3538952 | tf_op jit(solution)/shard_map/ppermute | solution.py:30
  5.0 10.3 %collective-permute-start = (bf16[9,128,512]{2,1,0:T(8,128)(2,1)}, bf16[9,128,512]{2,1,0:T(8,128)(2,1)}, u32[]{:S(2)}, u32[]{:S(2)}) collective-permute-start(bf16[9,128,512]{2,1,0:T(8,128)(2,1)} %get-tuple-element.9), channel_id=1, source_target_pairs={{0,1},{1,0},{2,3},{3,2},{4,5},{5,4},{6,7},{7,6},{8,9},{9,8},{10,11... | collective-permute-start | bytes 3538952 | tf_op jit(solution)/shard_map/ppermute | solution.py:30
  8.7 9.4 %collective-permute-start.8 = (bf16[4,128,512]{2,1,0:T(8,128)(2,1)S(1)}, bf16[4,128,512]{2,1,0:T(8,128)(2,1)}, u32[]{:S(2)}, u32[]{:S(2)}) collective-permute-start(bf16[4,128,512]{2,1,0:T(8,128)(2,1)S(1)} %slice_select_fusion.4), channel_id=1, source_target_pairs={{0,2},{1,5},{2,0},{3,7},{4,6},{5,1},{6,4},{7,3},{8,10},{9,13},{10,... | collective-permute-start | bytes 1572872 | tf_op jit(solution)/shard_map/ppermute | solution.py:30
  12.2 16.4 %collective-permute-start.2 = (bf16[5,128,512]{2,1,0:T(8,128)(2,1)}, bf16[5,128,512]{2,1,0:T(8,128)(2,1)S(1)}, u32[]{:S(2)}, u32[]{:S(2)}) collective-permute-start(bf16[5,128,512]{2,1,0:T(8,128)(2,1)} %slice_select_fusion.3), channel_id=1, source_target_pairs={{0,2},{1,5},{2,0},{3,7},{4,6},{5,1},{6,4},{7,3},{8,10},{9,13},{10,... | collective-permute-start | bytes 1966088 | tf_op jit(solution)/shard_map/ppermute | solution.py:30
  19.4 16.6 %collective-permute-start.9 = (bf16[4,128,512]{2,1,0:T(8,128)(2,1)S(1)}, bf16[4,128,512]{2,1,0:T(8,128)(2,1)S(1)}, u32[]{:S(2)}, u32[]{:S(2)}) collective-permute-start(bf16[4,128,512]{2,1,0:T(8,128)(2,1)S(1)} %fusion.34), channel_id=1, source_target_pairs={{0,4},{1,3},{2,6},{3,1},{4,0},{5,7},{6,2},{7,5},{8,12},{9,11},{10,... | collective-permute-start | bytes 1572872 | tf_op jit(solution)/shard_map/ppermute | solution.py:30
  30.7 17.9 %collective-permute-start.17 = (bf16[5,128,512]{2,1,0:T(8,128)(2,1)}, bf16[5,128,512]{2,1,0:T(8,128)(2,1)}, u32[]{:S(2)}, u32[]{:S(2)}) collective-permute-start(bf16[5,128,512]{2,1,0:T(8,128)(2,1)} %fusion.33), channel_id=1, source_target_pairs={{0,4},{1,3},{2,6},{3,1},{4,0},{5,7},{6,2},{7,5},{8,12},{9,11},{10,... | collective-permute-start | bytes 1966088 | tf_op jit(solution)/shard_map/ppermute | solution.py:30
  34.4 19.3 %collective-permute-start.3 = (bf16[7,128,512]{2,1,0:T(8,128)(2,1)}, bf16[7,128,512]{2,1,0:T(8,128)(2,1)}, u32[]{:S(2)}, u32[]{:S(2)}) collective-permute-start(bf16[7,128,512]{2,1,0:T(8,128)(2,1)} %after.2), channel_id=1, source_target_pairs={{0,2},{1,5},{2,0},{3,7},{4,6},{5,1},{6,4},{7,3},{8,10},{9,13},{10,... | collective-permute-start | bytes 2752520 | tf_op jit(solution)/shard_map/ppermute | solution.py:30
  36.1 17.6 %collective-permute-start.10 = (bf16[4,128,512]{2,1,0:T(8,128)(2,1)S(1)}, bf16[4,128,512]{2,1,0:T(8,128)(2,1)S(1)}, u32[]{:S(2)}, u32[]{:S(2)}) collective-permute-start(bf16[4,128,512]{2,1,0:T(8,128)(2,1)S(1)} %broadcast_select_fusion.2.refs_0_), channel_id=1, source_target_pairs={{0,2},{1,5},{2,0},{3,7},{4,6},{5,1},{6,4},{7,3},{8,10},{9,13},{10,... | collective-permute-start | bytes 1572872 | tf_op jit(solution)/shard_map/ppermute | solution.py:30
  36.7 28.2 %collective-permute-start.11 = (bf16[4,128,512]{2,1,0:T(8,128)(2,1)S(1)}, bf16[4,128,512]{2,1,0:T(8,128)(2,1)S(1)}, u32[]{:S(2)}, u32[]{:S(2)}) collective-permute-start(bf16[4,128,512]{2,1,0:T(8,128)(2,1)S(1)} %broadcast_select_fusion.2.refs_0_), channel_id=1, source_target_pairs={{0,1},{1,0},{2,3},{3,2},{4,5},{5,4},{6,7},{7,6},{8,9},{9,8},{10,11... | collective-permute-start | bytes 1572872 | tf_op jit(solution)/shard_map/ppermute | solution.py:30
  49.7 18.1 %collective-permute-start.18 = (bf16[5,128,512]{2,1,0:T(8,128)(2,1)S(1)}, bf16[5,128,512]{2,1,0:T(8,128)(2,1)S(1)}, u32[]{:S(2)}, u32[]{:S(2)}) collective-permute-start(bf16[5,128,512]{2,1,0:T(8,128)(2,1)S(1)} %broadcast_select_fusion.1.refs_0_), channel_id=1, source_target_pairs={{0,2},{1,5},{2,0},{3,7},{4,6},{5,1},{6,4},{7,3},{8,10},{9,13},{10,... | collective-permute-start | bytes 1966088 | tf_op jit(solution)/shard_map/ppermute | solution.py:30
  53.7 7.2 %copy-start.3 = (bf16[2048,1024]{1,0:T(8,128)(2,1)S(1)}, bf16[2048,1024]{1,0:T(8,128)(2,1)}, u32[]{:S(2)}) copy-start(bf16[2048,1024]{1,0:T(8,128)(2,1)} %param.3) | copy-start | bytes 12582916
  55.3 9.6 %collective-permute-start.13 = (bf16[2,2,128,256]{3,2,1,0:T(8,128)(2,1)S(1)}, bf16[2,2,128,256]{3,2,1,0:T(8,128)(2,1)S(1)}, u32[]{:S(2)}, u32[]{:S(2)}) collective-permute-start(bf16[2,2,128,256]{3,2,1,0:T(8,128)(2,1)S(1)} %after.3), channel_id=1, source_target_pairs={{0,8},{8,16},{16,24},{1,9},{9,17},{17,25},{2,10},{10,18},{18,26},{... | collective-permute-start | bytes 786440 | tf_op jit(solution)/shard_map/ppermute | solution.py:12
  58.8 9.2 %collective-permute-start.12 = (bf16[4,128,512]{2,1,0:T(8,128)(2,1)S(1)}, bf16[4,128,512]{2,1,0:T(8,128)(2,1)S(1)}, u32[]{:S(2)}, u32[]{:S(2)}) collective-permute-start(bf16[4,128,512]{2,1,0:T(8,128)(2,1)S(1)} %collective-permute-done.10.refs_1_), channel_id=1, source_target_pairs={{0,1},{1,0},{2,3},{3,2},{4,5},{5,4},{6,7},{7,6},{8,9},{9,8},{10,11... | collective-permute-start | bytes 1572872 | tf_op jit(solution)/shard_map/ppermute | solution.py:30
  61.1 20.4 %collective-permute-start.19 = (bf16[5,128,512]{2,1,0:T(8,128)(2,1)S(1)}, bf16[5,128,512]{2,1,0:T(8,128)(2,1)S(1)}, u32[]{:S(2)}, u32[]{:S(2)}) collective-permute-start(bf16[5,128,512]{2,1,0:T(8,128)(2,1)S(1)} %broadcast_select_fusion.1.refs_0_), channel_id=1, source_target_pairs={{0,1},{1,0},{2,3},{3,2},{4,5},{5,4},{6,7},{7,6},{8,9},{9,8},{10,11... | collective-permute-start | bytes 1966088 | tf_op jit(solution)/shard_map/ppermute | solution.py:30
  64.9 13.4 %collective-permute-start.4 = (bf16[7,128,512]{2,1,0:T(8,128)(2,1)S(1)}, bf16[7,128,512]{2,1,0:T(8,128)(2,1)S(1)}, u32[]{:S(2)}, u32[]{:S(2)}) collective-permute-start(bf16[7,128,512]{2,1,0:T(8,128)(2,1)S(1)} %fusion.32.refs_0_), channel_id=1, source_target_pairs={{0,4},{1,3},{2,6},{3,1},{4,0},{5,7},{6,2},{7,5},{8,12},{9,11},{10,... | collective-permute-start | bytes 2752520 | tf_op jit(solution)/shard_map/ppermute | solution.py:30
  64.9 8.6 %collective-permute-start.14 = (bf16[2,2,128,256]{3,2,1,0:T(8,128)(2,1)S(1)}, bf16[2,2,128,256]{3,2,1,0:T(8,128)(2,1)S(1)}, u32[]{:S(2)}, u32[]{:S(2)}) collective-permute-start(bf16[2,2,128,256]{3,2,1,0:T(8,128)(2,1)S(1)} %collective-permute-done.13), channel_id=1, source_target_pairs={{0,1},{1,0},{2,3},{3,2},{4,5},{5,4},{6,7},{7,6},{8,9},{9,8},{10,11... | collective-permute-start | bytes 786440 | tf_op jit(solution)/shard_map/ppermute | solution.py:30
  67.9 13.7 %collective-permute-start.20 = (bf16[5,128,512]{2,1,0:T(8,128)(2,1)S(1)}, bf16[5,128,512]{2,1,0:T(8,128)(2,1)S(1)}, u32[]{:S(2)}, u32[]{:S(2)}) collective-permute-start(bf16[5,128,512]{2,1,0:T(8,128)(2,1)S(1)} %collective-permute-done.18.refs_1_), channel_id=1, source_target_pairs={{0,1},{1,0},{2,3},{3,2},{4,5},{5,4},{6,7},{7,6},{8,9},{9,8},{10,11... | collective-permute-start | bytes 1966088 | tf_op jit(solution)/shard_map/ppermute | solution.py:30
  69.8 23.1 %collective-permute-start.15 = (bf16[256,1024]{1,0:T(8,128)(2,1)S(1)}, bf16[256,1024]{1,0:T(8,128)(2,1)S(1)}, u32[]{:S(2)}, u32[]{:S(2)}) collective-permute-start(bf16[256,1024]{1,0:T(8,128)(2,1)S(1)} %get-tuple-element.27), channel_id=1, source_target_pairs={{8,16},{16,8},{9,17},{17,9},{10,18},{18,10},{11,19},{19,11},{12,20... | collective-permute-start | bytes 1572872 | tf_op jit(solution)/shard_map/ppermute | solution.py:21
  73.5 19.4 %collective-permute-start.16 = (bf16[256,1024]{1,0:T(8,128)(2,1)S(1)}, bf16[256,1024]{1,0:T(8,128)(2,1)S(1)}, u32[]{:S(2)}, u32[]{:S(2)}) collective-permute-start(bf16[256,1024]{1,0:T(8,128)(2,1)S(1)} %get-tuple-element.28), channel_id=1, source_target_pairs={{0,8},{16,24},{8,0},{24,16},{1,9},{17,25},{9,1},{25,17},{2,10},{18... | collective-permute-start | bytes 1572872 | tf_op jit(solution)/shard_map/ppermute | solution.py:21
  78.4 14.5 %collective-permute-start.5 = (bf16[7,128,512]{2,1,0:T(8,128)(2,1)S(1)}, bf16[7,128,512]{2,1,0:T(8,128)(2,1)S(1)}, u32[]{:S(2)}, u32[]{:S(2)}) collective-permute-start(bf16[7,128,512]{2,1,0:T(8,128)(2,1)S(1)} %broadcast_select_fusion.refs_0_), channel_id=1, source_target_pairs={{0,2},{1,5},{2,0},{3,7},{4,6},{5,1},{6,4},{7,3},{8,10},{9,13},{10,... | collective-permute-start | bytes 2752520 | tf_op jit(solution)/shard_map/ppermute | solution.py:30
  81.5 12.6 %collective-permute-start.6 = (bf16[7,128,512]{2,1,0:T(8,128)(2,1)S(1)}, bf16[7,128,512]{2,1,0:T(8,128)(2,1)S(1)}, u32[]{:S(2)}, u32[]{:S(2)}) collective-permute-start(bf16[7,128,512]{2,1,0:T(8,128)(2,1)S(1)} %broadcast_select_fusion.refs_0_), channel_id=1, source_target_pairs={{0,1},{1,0},{2,3},{3,2},{4,5},{5,4},{6,7},{7,6},{8,9},{9,8},{10,11... | collective-permute-start | bytes 2752520 | tf_op jit(solution)/shard_map/ppermute | solution.py:30
  92.9 2.5 %collective-permute-start.7 = (bf16[7,128,512]{2,1,0:T(8,128)(2,1)S(1)}, bf16[7,128,512]{2,1,0:T(8,128)(2,1)S(1)}, u32[]{:S(2)}, u32[]{:S(2)}) collective-permute-start(bf16[7,128,512]{2,1,0:T(8,128)(2,1)S(1)} %collective-permute-done.5.refs_1_), channel_id=1, source_target_pairs={{0,1},{1,0},{2,3},{3,2},{4,5},{5,4},{6,7},{7,6},{8,9},{9,8},{10,11... | collective-permute-start | bytes 2752520 | tf_op jit(solution)/shard_map/ppermute | solution.py:30
  97.6 15.9 %collective-permute-start.21 = (bf16[256,1024]{1,0:T(8,128)(2,1)S(1)}, bf16[256,1024]{1,0:T(8,128)(2,1)S(1)}, u32[]{:S(2)}, u32[]{:S(2)}) collective-permute-start(bf16[256,1024]{1,0:T(8,128)(2,1)S(1)} %get-tuple-element.22), channel_id=1, source_target_pairs={{8,16},{16,8},{9,17},{17,9},{10,18},{18,10},{11,19},{19,11},{12,20... | collective-permute-start | bytes 1572872 | tf_op jit(solution)/shard_map/ppermute | solution.py:21
  101.3 13.8 %collective-permute-start.22 = (bf16[256,1024]{1,0:T(8,128)(2,1)S(1)}, bf16[256,1024]{1,0:T(8,128)(2,1)S(1)}, u32[]{:S(2)}, u32[]{:S(2)}) collective-permute-start(bf16[256,1024]{1,0:T(8,128)(2,1)S(1)} %get-tuple-element.21), channel_id=1, source_target_pairs={{0,8},{16,24},{8,0},{24,16},{1,9},{17,25},{9,1},{25,17},{2,10},{18... | collective-permute-start | bytes 1572872 | tf_op jit(solution)/shard_map/ppermute | solution.py:21
  (4 other events, 12.2 us)

commit v12 on v10

--- a/solution.py
+++ b/solution.py
@@ -211,8 +211,8 @@
     def join(self, hold, got):
         return place(self.cut, hold, got, flip(hold, (0, 0)), flip(got, (0, 0)))
 
-    def join_above(self, hold, got):
-        both = shifted(jnp.stack([hold, got]), "rows", 1)
+    def join_above(self, hold, got, done):
+        both = shifted(after(jnp.stack([hold, got]), done), "rows", 1)
         other = flip(both, (0, 0))
         return place(self.cut, both[0], both[1], other[0], other[1])
 
@@ -303,13 +303,10 @@
         head = pairs[0] if r == 0 else pairs[r + 1]
         edges = spread.join(*head)
         across = ([r + 1] if r + 1 < rounds else []) + ([r] if r == 0 else [])
-        if across:
-            n = len(across)
-            from_above = spread.join_above(head[0][:n, :, border:], head[1][:n, :, border:])
-            for k, q in enumerate(across):
-                crosses[q], above_crosses[q] = edges[k], from_above[k]
-            edges = edges[n:]
-        prev, cross = above_crosses[r], crosses[r]
+        n = len(across)
+        for k, q in enumerate(across):
+            crosses[q] = edges[k]
+        edges = edges[n:]
         outer = apply_many(
             edges[:2], jnp.stack([matrix[:window], matrix[local_rows - window :]])
         )
@@ -326,6 +323,13 @@
         inner = apply_many(twos, centre.reshape(wins - 1, window, local_cols)).reshape(
             local_rows - window, local_cols
         )
+        if n:
+            from_above = spread.join_above(
+                head[0][:n, :, border:], head[1][:n, :, border:], inner
+            )
+            for k, q in enumerate(across):
+                above_crosses[q] = from_above[k]
+        prev, cross = above_crosses[r], crosses[r]
         low = apply(cross[:, :border], jnp.concatenate([end, below], 0))
         low = jnp.where(row_block == last_block, end, low)
         top = apply(prev, jnp.concatenate([above, begin], 0))

time: 117 us -> 118 us (level)
  Pallas kernels: 7.89 us -> 9.91 us
    ppermute x18, waiting for transfers between devices: 37.8 us -> 34.7 us  [flip(): lax.ppermute(value, 'cols', [(d, d ^ 1 << bits[d & 1]) for d in range(cou...]
    pallas_call x4, Pallas kernels: 1.21 us -> 3.21 us  [place(): pl.pallas_call(lambda *refs: place_kernel(cut, *refs), out_shape=jax.Shap...]
    ppermute x18, starting transfers between devices: 15.1 us -> 16.5 us  [flip(): lax.ppermute(value, 'cols', [(d, d ^ 1 << bits[d & 1]) for d in range(cou...]
    ppermute x1, waiting for transfers between devices: 3.71 us -> 5.07 us  [shifted(): lax.ppermute(value, axis, [(source, source + steps) for source in range(i...]
    another operation x1, local copies, waits for them, and re-layouts: 0.17 us -> 1.5 us  [local(): jnp.stack([matrix[:window], matrix[local_rows - window:]])]
    unnamed x10 -> x12, local copies, waits for them, and re-layouts: 3.01 us -> 2.23 us
  transfers between devices with their start and end apart: 23 -> 23, of which waited for: 10 -> 12; matrix products, arithmetic and copies ran while one was open for 17% -> 18% of each run, Pallas kernels for 5% -> 7%
where the time goes in v12:
time: 118 us; the launch traced here: 117 us
  waiting for transfers between devices  47.2 us (40%)
  starting transfers between devices  28 us (24%)
  matrix products  12.2 us (10%)
  Pallas kernels  9.91 us (8%)
  other arithmetic  9.33 us (8%)
  local copies, waits for them, and re-layouts  6.37 us (5%)
  between operations  4.18 us (4%)
    ppermute x18, waiting for transfers between devices, flip(): lax.ppermute(value, 'cols', [(d, d ^ 1 << bits[d & 1]) for d in range(cou...  34.7 us
    ppermute x18, starting transfers between devices, flip(): lax.ppermute(value, 'cols', [(d, d ^ 1 << bits[d & 1]) for d in range(cou...  16.5 us
    dot_general x6, matrix products, apply_many(): jnp.einsum('nab,nac->nbc', q, x, preferred_element_type=jnp.float32)  10.3 us
    select_n x9, other arithmetic, choose(): return jnp.where(mask, yes, no)  8.01 us
    ppermute x4, starting transfers between devices, swap(): return lax.ppermute(value, 'rows', pairs + [(b, a) for a, b in pairs])  7.86 us
    ppermute x4, waiting for transfers between devices, swap(): return lax.ppermute(value, 'rows', pairs + [(b, a) for a, b in pairs])  7.43 us
    ppermute x1, waiting for transfers between devices, shifted(): lax.ppermute(value, axis, [(source, source + steps) for source in range(i...  5.07 us
    ppermute x1, starting transfers between devices, shifted(): lax.ppermute(value, axis, [(source, source + steps) for source in range(i...  3.66 us
  transfers between devices with their start and end apart: 23, of which 12 were waited for; matrix products, arithmetic and copies ran while one was open for 18% of the time, Pallas kernels for 7%

profile of v12, /device:TPU:8, one launch (start us, length us, event | category | flops | bytes accessed | tf_op | source)
XLA Modules:
  0.0 117.2 jit_solution(16392655227849000566)
XLA Ops:
  0.0 2.2 %copy-done.2 = bf16[1,4096,512]{2,1,0:T(8,128)(2,1)S(1)} copy-done((bf16[1,4096,512]{2,1,0:T(8,128)(2,1)S(1)}, bf16[1,4096,512]{2,1,0:T(8,128)(2,1)}, u32[]{:S(2)}) %copy-start.2) | copy-done | bytes 4194328
  3.1 1.9 %cut_slot.2 = (bf16[9,128,512]{2,1,0:T(8,128)(2,1)S(1)}, bf16[9,128,512]{2,1,0:T(8,128)(2,1)}, bf16[9,128,512]{2,1,0:T(8,128)(2,1)S(1)}) custom-call(bf16[8,2,2,128,512]{4,3,2,1,0:T(8,128)(2,1)S(1)} %bitcast.87), custom_call_target="tpu_custom_call" | custom-call | bytes 6291456 | tf_op jit(solution)/shard_map/cut_slot/pallas_call | solution.py:105
  8.7 1.6 %collective-permute-start.2 = (bf16[4,128,512]{2,1,0:T(8,128)(2,1)S(1)}, bf16[4,128,512]{2,1,0:T(8,128)(2,1)}, u32[]{:S(2)}, u32[]{:S(2)}) collective-permute-start(bf16[4,128,512]{2,1,0:T(8,128)(2,1)S(1)} %slice_select_fusion.4), channel_id=1, source_target_pairs={{0,2},{1,5},{2,0},{3,7},{4,6},{5,1},{6,4},{7,3},{8,10},{9,13},{10,... | collective-permute-start | bytes 1572872 | tf_op jit(solution)/shard_map/ppermute | solution.py:30
  14.5 3.5 %collective-permute-done.2 = bf16[4,128,512]{2,1,0:T(8,128)(2,1)} collective-permute-done((bf16[4,128,512]{2,1,0:T(8,128)(2,1)S(1)}, bf16[4,128,512]{2,1,0:T(8,128)(2,1)}, u32[]{:S(2)}, u32[]{:S(2)}) %collective-permute-start.2) | collective-permute-done | bytes 524320 | tf_op jit(solution)/shard_map/ppermute | solution.py:30
  19.4 1.6 %collective-permute-start.3 = (bf16[4,128,512]{2,1,0:T(8,128)(2,1)S(1)}, bf16[4,128,512]{2,1,0:T(8,128)(2,1)S(1)}, u32[]{:S(2)}, u32[]{:S(2)}) collective-permute-start(bf16[4,128,512]{2,1,0:T(8,128)(2,1)S(1)} %fusion.34), channel_id=1, source_target_pairs={{0,4},{1,3},{2,6},{3,1},{4,0},{5,7},{6,2},{7,5},{8,12},{9,11},{10,... | collective-permute-start | bytes 1572872 | tf_op jit(solution)/shard_map/ppermute | solution.py:30
  20.9 7.7 %collective-permute-done.12 = bf16[5,128,512]{2,1,0:T(8,128)(2,1)} collective-permute-done((bf16[5,128,512]{2,1,0:T(8,128)(2,1)S(1)}, bf16[5,128,512]{2,1,0:T(8,128)(2,1)}, u32[]{:S(2)}, u32[]{:S(2)}) %collective-permute-start.12) | collective-permute-done | bytes 655392 | tf_op jit(solution)/shard_map/ppermute | solution.py:30
  30.0 1.6 %collective-permute-start.13 = (bf16[5,128,512]{2,1,0:T(8,128)(2,1)S(1)}, bf16[5,128,512]{2,1,0:T(8,128)(2,1)S(1)}, u32[]{:S(2)}, u32[]{:S(2)}) collective-permute-start(bf16[5,128,512]{2,1,0:T(8,128)(2,1)S(1)} %fusion.33), channel_id=1, source_target_pairs={{0,4},{1,3},{2,6},{3,1},{4,0},{5,7},{6,2},{7,5},{8,12},{9,11},{10,... | collective-permute-start | bytes 1966088 | tf_op jit(solution)/shard_map/ppermute | solution.py:30
  35.5 12.2 %collective-permute-done.13 = bf16[5,128,512]{2,1,0:T(8,128)(2,1)S(1)} collective-permute-done((bf16[5,128,512]{2,1,0:T(8,128)(2,1)S(1)}, bf16[5,128,512]{2,1,0:T(8,128)(2,1)S(1)}, u32[]{:S(2)}, u32[]{:S(2)}) %collective-permute-start.13) | collective-permute-done | bytes 655392 | tf_op jit(solution)/shard_map/ppermute | solution.py:30
  52.3 7.8 %collective-permute-done.14.refs_1_ = bf16[5,128,512]{2,1,0:T(8,128)(2,1)} collective-permute-done((bf16[5,128,512]{2,1,0:T(8,128)(2,1)S(1)}, bf16[5,128,512]{2,1,0:T(8,128)(2,1)}, u32[]{:S(2)}, u32[]{:S(2)}) %collective-permute-start.14) | collective-permute-done | bytes 655392 | tf_op jit(solution)/shard_map/ppermute | solution.py:30
  60.1 2.4 %collective-permute-start.16 = (bf16[5,128,512]{2,1,0:T(8,128)(2,1)}, bf16[5,128,512]{2,1,0:T(8,128)(2,1)S(1)}, u32[]{:S(2)}, u32[]{:S(2)}) collective-permute-start(bf16[5,128,512]{2,1,0:T(8,128)(2,1)} %collective-permute-done.14.refs_1_), channel_id=1, source_target_pairs={{0,1},{1,0},{2,3},{3,2},{4,5},{5,4},{6,7},{7,6},{8,9},{9,8},{10,11... | collective-permute-start | bytes 1966088 | tf_op jit(solution)/shard_map/ppermute | solution.py:30
  63.9 1.6 %collective-permute-start.5 = (bf16[7,128,512]{2,1,0:T(8,128)(2,1)S(1)}, bf16[7,128,512]{2,1,0:T(8,128)(2,1)S(1)}, u32[]{:S(2)}, u32[]{:S(2)}) collective-permute-start(bf16[7,128,512]{2,1,0:T(8,128)(2,1)S(1)} %fusion.32), channel_id=1, source_target_pairs={{0,4},{1,3},{2,6},{3,1},{4,0},{5,7},{6,2},{7,5},{8,12},{9,11},{10,... | collective-permute-start | bytes 2752520 | tf_op jit(solution)/shard_map/ppermute | solution.py:30
  66.7 1.5 %fusion.11 = bf16[2,512,1024]{2,1,0:T(8,128)(2,1)S(1)} fusion(bf16[4,512,512]{2,1,0:T(8,128)(2,1)S(1)} %place.5, bf16[1,512,1024]{2,1,0:T(8,128)(2,1)S(1)} %copy-done.5, bf16[1,512,1024]{2,1,0:T(8,128)(2,1)S(1)} %copy-done.4), kind=kOutput, calls=%fused_computation.15 | convolution fusion | flops 1078984704 | bytes 6291456 | tf_op jit(solution)/shard_map/nab,nac->nbc/dot_general | solution.py:226
  68.6 3.5 %collective-permute-start.19 = (bf16[256,1024]{1,0:T(8,128)(2,1)S(1)}, bf16[256,1024]{1,0:T(8,128)(2,1)S(1)}, u32[]{:S(2)}, u32[]{:S(2)}) collective-permute-start(bf16[256,1024]{1,0:T(8,128)(2,1)S(1)} %get-tuple-element.27), channel_id=1, source_target_pairs={{8,16},{16,8},{9,17},{17,9},{10,18},{18,10},{11,19},{19,11},{12,20... | collective-permute-start | bytes 1572872 | tf_op jit(solution)/shard_map/ppermute | solution.py:21
  75.8 1.6 %collective-permute-done.5 = bf16[7,128,512]{2,1,0:T(8,128)(2,1)S(1)} collective-permute-done((bf16[7,128,512]{2,1,0:T(8,128)(2,1)S(1)}, bf16[7,128,512]{2,1,0:T(8,128)(2,1)S(1)}, u32[]{:S(2)}, u32[]{:S(2)}) %collective-permute-start.5) | collective-permute-done | bytes 917536 | tf_op jit(solution)/shard_map/ppermute | solution.py:30
  77.5 1.8 %collective-permute-start.6 = (bf16[7,128,512]{2,1,0:T(8,128)(2,1)S(1)}, bf16[7,128,512]{2,1,0:T(8,128)(2,1)S(1)}, u32[]{:S(2)}, u32[]{:S(2)}) collective-permute-start(bf16[7,128,512]{2,1,0:T(8,128)(2,1)S(1)} %broadcast_select_fusion.refs_0_), channel_id=1, source_target_pairs={{0,2},{1,5},{2,0},{3,7},{4,6},{5,1},{6,4},{7,3},{8,10},{9,13},{10,... | collective-permute-start | bytes 2752520 | tf_op jit(solution)/shard_map/ppermute | solution.py:30
  79.3 2.1 %convolution_convert_fusion = bf16[3,512,1024]{2,1,0:T(8,128)(2,1)S(1)} fusion(bf16[5,512,512]{2,1,0:T(8,128)(2,1)S(1)} %place.6, bf16[3,512,1024]{2,1,0:T(8,128)(2,1)S(1)} %bitcast.90), kind=kOutput, calls=%fused_computation.2 | convolution fusion | flops 1612185600 | bytes 8912896 | tf_op jit(solution)/shard_map/nab,nac->nbc/dot_general | solution.py:226
  81.5 3.7 %collective-permute-start.17 = (bf16[2,2,128,256]{3,2,1,0:T(8,128)(2,1)S(1)}, bf16[2,2,128,256]{3,2,1,0:T(8,128)(2,1)S(1)}, u32[]{:S(2)}, u32[]{:S(2)}) collective-permute-start(bf16[2,2,128,256]{3,2,1,0:T(8,128)(2,1)S(1)} %after.3), channel_id=1, source_target_pairs={{0,8},{8,16},{16,24},{1,9},{9,17},{17,25},{2,10},{10,18},{18,26},{... | collective-permute-start | bytes 786440 | tf_op jit(solution)/shard_map/ppermute | solution.py:12
  85.9 5.1 %collective-permute-done.17 = bf16[2,2,128,256]{3,2,1,0:T(8,128)(2,1)S(1)} collective-permute-done((bf16[2,2,128,256]{3,2,1,0:T(8,128)(2,1)S(1)}, bf16[2,2,128,256]{3,2,1,0:T(8,128)(2,1)S(1)}, u32[]{:S(2)}, u32[]{:S(2)}) %collective-permute-start.17) | collective-permute-done | bytes 262176 | tf_op jit(solution)/shard_map/ppermute | solution.py:12
  97.4 1.5 %convolution_convert_fusion.2 = bf16[2,512,1024]{2,1,0:T(8,128)(2,1)S(1)} fusion(bf16[7,512,512]{2,1,0:T(8,128)(2,1)S(1)} %place.4, bf16[2,512,1024]{2,1,0:T(8,128)(2,1)S(1)} %bitcast.94), kind=kOutput, calls=%fused_computation.12 | convolution fusion | flops 1074790400 | bytes 7864320 | tf_op jit(solution)/shard_map/nab,nac->nbc/dot_general | solution.py:226
  99.0 4.2 %collective-permute-start.21 = (bf16[256,1024]{1,0:T(8,128)(2,1)S(1)}, bf16[256,1024]{1,0:T(8,128)(2,1)S(1)}, u32[]{:S(2)}, u32[]{:S(2)}) collective-permute-start(bf16[256,1024]{1,0:T(8,128)(2,1)S(1)} %get-tuple-element.22), channel_id=1, source_target_pairs={{8,16},{16,8},{9,17},{17,9},{10,18},{18,10},{11,19},{19,11},{12,20... | collective-permute-start | bytes 1572872 | tf_op jit(solution)/shard_map/ppermute | solution.py:21
  103.6 2.1 %convolution_convert_fusion.1 = bf16[3,512,1024]{2,1,0:T(8,128)(2,1)S(1)} fusion(bf16[7,512,512]{2,1,0:T(8,128)(2,1)S(1)} %place.4, bf16[3,512,1024]{2,1,0:T(8,128)(2,1)S(1)} %bitcast.91), kind=kOutput, calls=%fused_computation.3 | convolution fusion | flops 1612185600 | bytes 9961472 | tf_op jit(solution)/shard_map/nab,nac->nbc/dot_general | solution.py:226
  105.8 2.7 %write_inner.1._ = bf16[2048,1024]{1,0:T(8,128)(2,1)} custom-call(bf16[1536,1024]{1,0:T(8,128)(2,1)S(1)} %bitcast.88), custom_call_target="tpu_custom_call" | custom-call | bytes 6291456 | tf_op jit(solution)/shard_map/write_inner/pallas_call | solution.py:236
  108.4 4.5 %collective-permute-done.22 = bf16[256,1024]{1,0:T(8,128)(2,1)S(1)} collective-permute-done((bf16[256,1024]{1,0:T(8,128)(2,1)S(1)}, bf16[256,1024]{1,0:T(8,128)(2,1)S(1)}, u32[]{:S(2)}, u32[]{:S(2)}) %collective-permute-start.22) | collective-permute-done | bytes 524320 | tf_op jit(solution)/shard_map/ppermute | solution.py:21
  113.0 2.2 %collective-permute-done.21 = bf16[256,1024]{1,0:T(8,128)(2,1)S(1)} collective-permute-done((bf16[256,1024]{1,0:T(8,128)(2,1)S(1)}, bf16[256,1024]{1,0:T(8,128)(2,1)S(1)}, u32[]{:S(2)}, u32[]{:S(2)}) %collective-permute-start.21) | collective-permute-done | bytes 524320 | tf_op jit(solution)/shard_map/ppermute | solution.py:21
  (87 shorter events, 32.4 us)
Async XLA Ops:
  3.0 4.5 %collective-permute-start.1 = (bf16[9,128,512]{2,1,0:T(8,128)(2,1)S(1)}, bf16[9,128,512]{2,1,0:T(8,128)(2,1)}, u32[]{:S(2)}, u32[]{:S(2)}) collective-permute-start(bf16[9,128,512]{2,1,0:T(8,128)(2,1)S(1)} %cut_slot.3), channel_id=1, source_target_pairs={{0,1},{1,0},{2,3},{3,2},{4,5},{5,4},{6,7},{7,6},{8,9},{9,8},{10,11... | collective-permute-start | bytes 3538952 | tf_op jit(solution)/shard_map/ppermute | solution.py:30
  5.0 9.4 %collective-permute-start = (bf16[9,128,512]{2,1,0:T(8,128)(2,1)}, bf16[9,128,512]{2,1,0:T(8,128)(2,1)}, u32[]{:S(2)}, u32[]{:S(2)}) collective-permute-start(bf16[9,128,512]{2,1,0:T(8,128)(2,1)} %get-tuple-element.9), channel_id=1, source_target_pairs={{0,1},{1,0},{2,3},{3,2},{4,5},{5,4},{6,7},{7,6},{8,9},{9,8},{10,11... | collective-permute-start | bytes 3538952 | tf_op jit(solution)/shard_map/ppermute | solution.py:30
  8.7 9.4 %collective-permute-start.2 = (bf16[4,128,512]{2,1,0:T(8,128)(2,1)S(1)}, bf16[4,128,512]{2,1,0:T(8,128)(2,1)}, u32[]{:S(2)}, u32[]{:S(2)}) collective-permute-start(bf16[4,128,512]{2,1,0:T(8,128)(2,1)S(1)} %slice_select_fusion.4), channel_id=1, source_target_pairs={{0,2},{1,5},{2,0},{3,7},{4,6},{5,1},{6,4},{7,3},{8,10},{9,13},{10,... | collective-permute-start | bytes 1572872 | tf_op jit(solution)/shard_map/ppermute | solution.py:30
  11.4 17.3 %collective-permute-start.12 = (bf16[5,128,512]{2,1,0:T(8,128)(2,1)S(1)}, bf16[5,128,512]{2,1,0:T(8,128)(2,1)}, u32[]{:S(2)}, u32[]{:S(2)}) collective-permute-start(bf16[5,128,512]{2,1,0:T(8,128)(2,1)S(1)} %slice_select_fusion.2), channel_id=1, source_target_pairs={{0,2},{1,5},{2,0},{3,7},{4,6},{5,1},{6,4},{7,3},{8,10},{9,13},{10,... | collective-permute-start | bytes 1966088 | tf_op jit(solution)/shard_map/ppermute | solution.py:30
  19.4 13.6 %collective-permute-start.3 = (bf16[4,128,512]{2,1,0:T(8,128)(2,1)S(1)}, bf16[4,128,512]{2,1,0:T(8,128)(2,1)S(1)}, u32[]{:S(2)}, u32[]{:S(2)}) collective-permute-start(bf16[4,128,512]{2,1,0:T(8,128)(2,1)S(1)} %fusion.34), channel_id=1, source_target_pairs={{0,4},{1,3},{2,6},{3,1},{4,0},{5,7},{6,2},{7,5},{8,12},{9,11},{10,... | collective-permute-start | bytes 1572872 | tf_op jit(solution)/shard_map/ppermute | solution.py:30
  30.0 17.6 %collective-permute-start.13 = (bf16[5,128,512]{2,1,0:T(8,128)(2,1)S(1)}, bf16[5,128,512]{2,1,0:T(8,128)(2,1)S(1)}, u32[]{:S(2)}, u32[]{:S(2)}) collective-permute-start(bf16[5,128,512]{2,1,0:T(8,128)(2,1)S(1)} %fusion.33), channel_id=1, source_target_pairs={{0,4},{1,3},{2,6},{3,1},{4,0},{5,7},{6,2},{7,5},{8,12},{9,11},{10,... | collective-permute-start | bytes 1966088 | tf_op jit(solution)/shard_map/ppermute | solution.py:30
  33.1 16.1 %copy-start.3 = (bf16[2048,1024]{1,0:T(8,128)(2,1)S(1)}, bf16[2048,1024]{1,0:T(8,128)(2,1)}, u32[]{:S(2)}) copy-start(bf16[2048,1024]{1,0:T(8,128)(2,1)} %param.3) | copy-start | bytes 12582916
  33.1 18.2 %collective-permute-start.9 = (bf16[4,128,512]{2,1,0:T(8,128)(2,1)S(1)}, bf16[4,128,512]{2,1,0:T(8,128)(2,1)}, u32[]{:S(2)}, u32[]{:S(2)}) collective-permute-start(bf16[4,128,512]{2,1,0:T(8,128)(2,1)S(1)} %broadcast_select_fusion.2.refs_0_), channel_id=1, source_target_pairs={{0,2},{1,5},{2,0},{3,7},{4,6},{5,1},{6,4},{7,3},{8,10},{9,13},{10,... | collective-permute-start | bytes 1572872 | tf_op jit(solution)/shard_map/ppermute | solution.py:30
  34.7 27.9 %collective-permute-start.4 = (bf16[7,128,512]{2,1,0:T(8,128)(2,1)S(1)}, bf16[7,128,512]{2,1,0:T(8,128)(2,1)}, u32[]{:S(2)}, u32[]{:S(2)}) collective-permute-start(bf16[7,128,512]{2,1,0:T(8,128)(2,1)S(1)} %after.2), channel_id=1, source_target_pairs={{0,2},{1,5},{2,0},{3,7},{4,6},{5,1},{6,4},{7,3},{8,10},{9,13},{10,... | collective-permute-start | bytes 2752520 | tf_op jit(solution)/shard_map/ppermute | solution.py:30
  47.7 12.4 %collective-permute-start.14 = (bf16[5,128,512]{2,1,0:T(8,128)(2,1)S(1)}, bf16[5,128,512]{2,1,0:T(8,128)(2,1)}, u32[]{:S(2)}, u32[]{:S(2)}) collective-permute-start(bf16[5,128,512]{2,1,0:T(8,128)(2,1)S(1)} %broadcast_select_fusion.1.refs_0_), channel_id=1, source_target_pairs={{0,2},{1,5},{2,0},{3,7},{4,6},{5,1},{6,4},{7,3},{8,10},{9,13},{10,... | collective-permute-start | bytes 1966088 | tf_op jit(solution)/shard_map/ppermute | solution.py:30
  50.7 14.9 %collective-permute-start.10 = (bf16[4,128,512]{2,1,0:T(8,128)(2,1)S(1)}, bf16[4,128,512]{2,1,0:T(8,128)(2,1)S(1)}, u32[]{:S(2)}, u32[]{:S(2)}) collective-permute-start(bf16[4,128,512]{2,1,0:T(8,128)(2,1)S(1)} %broadcast_select_fusion.2.refs_0_), channel_id=1, source_target_pairs={{0,1},{1,0},{2,3},{3,2},{4,5},{5,4},{6,7},{7,6},{8,9},{9,8},{10,11... | collective-permute-start | bytes 1572872 | tf_op jit(solution)/shard_map/ppermute | solution.py:30
  50.7 21.5 %collective-permute-start.15 = (bf16[5,128,512]{2,1,0:T(8,128)(2,1)S(1)}, bf16[5,128,512]{2,1,0:T(8,128)(2,1)S(1)}, u32[]{:S(2)}, u32[]{:S(2)}) collective-permute-start(bf16[5,128,512]{2,1,0:T(8,128)(2,1)S(1)} %broadcast_select_fusion.1.refs_0_), channel_id=1, source_target_pairs={{0,1},{1,0},{2,3},{3,2},{4,5},{5,4},{6,7},{7,6},{8,9},{9,8},{10,11... | collective-permute-start | bytes 1966088 | tf_op jit(solution)/shard_map/ppermute | solution.py:30
  51.2 14.3 %collective-permute-start.11 = (bf16[4,128,512]{2,1,0:T(8,128)(2,1)}, bf16[4,128,512]{2,1,0:T(8,128)(2,1)S(1)}, u32[]{:S(2)}, u32[]{:S(2)}) collective-permute-start(bf16[4,128,512]{2,1,0:T(8,128)(2,1)} %collective-permute-done.9.refs_1_), channel_id=1, source_target_pairs={{0,1},{1,0},{2,3},{3,2},{4,5},{5,4},{6,7},{7,6},{8,9},{9,8},{10,11... | collective-permute-start | bytes 1572872 | tf_op jit(solution)/shard_map/ppermute | solution.py:30
  60.1 12.0 %collective-permute-start.16 = (bf16[5,128,512]{2,1,0:T(8,128)(2,1)}, bf16[5,128,512]{2,1,0:T(8,128)(2,1)S(1)}, u32[]{:S(2)}, u32[]{:S(2)}) collective-permute-start(bf16[5,128,512]{2,1,0:T(8,128)(2,1)} %collective-permute-done.14.refs_1_), channel_id=1, source_target_pairs={{0,1},{1,0},{2,3},{3,2},{4,5},{5,4},{6,7},{7,6},{8,9},{9,8},{10,11... | collective-permute-start | bytes 1966088 | tf_op jit(solution)/shard_map/ppermute | solution.py:30
  63.9 13.5 %collective-permute-start.5 = (bf16[7,128,512]{2,1,0:T(8,128)(2,1)S(1)}, bf16[7,128,512]{2,1,0:T(8,128)(2,1)S(1)}, u32[]{:S(2)}, u32[]{:S(2)}) collective-permute-start(bf16[7,128,512]{2,1,0:T(8,128)(2,1)S(1)} %fusion.32), channel_id=1, source_target_pairs={{0,4},{1,3},{2,6},{3,1},{4,0},{5,7},{6,2},{7,5},{8,12},{9,11},{10,... | collective-permute-start | bytes 2752520 | tf_op jit(solution)/shard_map/ppermute | solution.py:30
  68.6 16.6 %collective-permute-start.19 = (bf16[256,1024]{1,0:T(8,128)(2,1)S(1)}, bf16[256,1024]{1,0:T(8,128)(2,1)S(1)}, u32[]{:S(2)}, u32[]{:S(2)}) collective-permute-start(bf16[256,1024]{1,0:T(8,128)(2,1)S(1)} %get-tuple-element.27), channel_id=1, source_target_pairs={{8,16},{16,8},{9,17},{17,9},{10,18},{18,10},{11,19},{19,11},{12,20... | collective-permute-start | bytes 1572872 | tf_op jit(solution)/shard_map/ppermute | solution.py:21
  72.1 13.8 %collective-permute-start.20 = (bf16[256,1024]{1,0:T(8,128)(2,1)S(1)}, bf16[256,1024]{1,0:T(8,128)(2,1)S(1)}, u32[]{:S(2)}, u32[]{:S(2)}) collective-permute-start(bf16[256,1024]{1,0:T(8,128)(2,1)S(1)} %get-tuple-element.28), channel_id=1, source_target_pairs={{0,8},{16,24},{8,0},{24,16},{1,9},{17,25},{9,1},{25,17},{2,10},{18... | collective-permute-start | bytes 1572872 | tf_op jit(solution)/shard_map/ppermute | solution.py:21
  77.5 14.0 %collective-permute-start.6 = (bf16[7,128,512]{2,1,0:T(8,128)(2,1)S(1)}, bf16[7,128,512]{2,1,0:T(8,128)(2,1)S(1)}, u32[]{:S(2)}, u32[]{:S(2)}) collective-permute-start(bf16[7,128,512]{2,1,0:T(8,128)(2,1)S(1)} %broadcast_select_fusion.refs_0_), channel_id=1, source_target_pairs={{0,2},{1,5},{2,0},{3,7},{4,6},{5,1},{6,4},{7,3},{8,10},{9,13},{10,... | collective-permute-start | bytes 2752520 | tf_op jit(solution)/shard_map/ppermute | solution.py:30
  81.5 9.5 %collective-permute-start.17 = (bf16[2,2,128,256]{3,2,1,0:T(8,128)(2,1)S(1)}, bf16[2,2,128,256]{3,2,1,0:T(8,128)(2,1)S(1)}, u32[]{:S(2)}, u32[]{:S(2)}) collective-permute-start(bf16[2,2,128,256]{3,2,1,0:T(8,128)(2,1)S(1)} %after.3), channel_id=1, source_target_pairs={{0,8},{8,16},{16,24},{1,9},{9,17},{17,25},{2,10},{10,18},{18,26},{... | collective-permute-start | bytes 786440 | tf_op jit(solution)/shard_map/ppermute | solution.py:12
  91.0 1.5 %collective-permute-start.18 = (bf16[2,2,128,256]{3,2,1,0:T(8,128)(2,1)S(1)}, bf16[2,2,128,256]{3,2,1,0:T(8,128)(2,1)S(1)}, u32[]{:S(2)}, u32[]{:S(2)}) collective-permute-start(bf16[2,2,128,256]{3,2,1,0:T(8,128)(2,1)S(1)} %collective-permute-done.17), channel_id=1, source_target_pairs={{0,1},{1,0},{2,3},{3,2},{4,5},{5,4},{6,7},{7,6},{8,9},{9,8},{10,11... | collective-permute-start | bytes 786440 | tf_op jit(solution)/shard_map/ppermute | solution.py:30
  91.0 2.8 %collective-permute-start.7 = (bf16[7,128,512]{2,1,0:T(8,128)(2,1)S(1)}, bf16[7,128,512]{2,1,0:T(8,128)(2,1)S(1)}, u32[]{:S(2)}, u32[]{:S(2)}) collective-permute-start(bf16[7,128,512]{2,1,0:T(8,128)(2,1)S(1)} %broadcast_select_fusion.refs_0_), channel_id=1, source_target_pairs={{0,1},{1,0},{2,3},{3,2},{4,5},{5,4},{6,7},{7,6},{8,9},{9,8},{10,11... | collective-permute-start | bytes 2752520 | tf_op jit(solution)/shard_map/ppermute | solution.py:30
  91.5 3.6 %collective-permute-start.8 = (bf16[7,128,512]{2,1,0:T(8,128)(2,1)S(1)}, bf16[7,128,512]{2,1,0:T(8,128)(2,1)S(1)}, u32[]{:S(2)}, u32[]{:S(2)}) collective-permute-start(bf16[7,128,512]{2,1,0:T(8,128)(2,1)S(1)} %collective-permute-done.6.refs_1_), channel_id=1, source_target_pairs={{0,1},{1,0},{2,3},{3,2},{4,5},{5,4},{6,7},{7,6},{8,9},{9,8},{10,11... | collective-permute-start | bytes 2752520 | tf_op jit(solution)/shard_map/ppermute | solution.py:30
  98.9 14.0 %collective-permute-start.22 = (bf16[256,1024]{1,0:T(8,128)(2,1)S(1)}, bf16[256,1024]{1,0:T(8,128)(2,1)S(1)}, u32[]{:S(2)}, u32[]{:S(2)}) collective-permute-start(bf16[256,1024]{1,0:T(8,128)(2,1)S(1)} %get-tuple-element.21), channel_id=1, source_target_pairs={{0,8},{16,24},{8,0},{24,16},{1,9},{17,25},{9,1},{25,17},{2,10},{18... | collective-permute-start | bytes 1572872 | tf_op jit(solution)/shard_map/ppermute | solution.py:21
  99.0 16.2 %collective-permute-start.21 = (bf16[256,1024]{1,0:T(8,128)(2,1)S(1)}, bf16[256,1024]{1,0:T(8,128)(2,1)S(1)}, u32[]{:S(2)}, u32[]{:S(2)}) collective-permute-start(bf16[256,1024]{1,0:T(8,128)(2,1)S(1)} %get-tuple-element.22), channel_id=1, source_target_pairs={{8,16},{16,8},{9,17},{17,9},{10,18},{18,10},{11,19},{19,11},{12,20... | collective-permute-start | bytes 1572872 | tf_op jit(solution)/shard_map/ppermute | solution.py:21
  (6 other events, 16.1 us)

commit v13 on v10

--- a/solution.py
+++ b/solution.py
@@ -207,6 +207,10 @@
         if first:
             hold = after(hold, *first)
         return hold, flip(hold, self.cut)
+
+    def last_two(self, state, count):
+        hold = self.keep(state, self.others[-1])
+        return [(part, flip(part, self.cut)) for part in (hold[:count], hold[count:])]
 
     def join(self, hold, got):
         return place(self.cut, hold, got, flip(hold, (0, 0)), flip(got, (0, 0)))
@@ -295,12 +299,14 @@
         else:
             begun = spread.begin(across + [r] * crossing, slice(first, len(order)), streams[r - 1][2])
             streams.append(spread.middle(begun))
-    pairs = [spread.last(stream) for stream in streams]
+    pairs = [spread.last(stream) for stream in streams[:2]]
+    for r in range(1, rounds):
+        pairs += spread.last_two(streams[r + 1], 3 if r + 1 < rounds else 2)
 
     matrix = slab
     crosses, above_crosses = {}, {}
     for r in range(rounds):
-        head = pairs[0] if r == 0 else pairs[r + 1]
+        head, tail = pairs[2 * r], pairs[2 * r + 1]
         edges = spread.join(*head)
         across = ([r + 1] if r + 1 < rounds else []) + ([r] if r == 0 else [])
         if across:
@@ -316,7 +322,7 @@
         head_rows, tail_rows = outer[0], outer[1]
         begin, end = head_rows[:border], tail_rows[border:]
         above, below = swap_rows(begin, end)
-        rest = spread.join(*pairs[1]) if r == 0 else edges[2:]
+        rest = spread.join(*tail)
         ones, twos = rest[: wins - 2], rest[wins - 2 :]
         mid = apply_many(
             ones,

time: 117 us -> 114 us (0.974)
  waiting for transfers between devices: 48 us -> 45.7 us
    ppermute x18 -> x21, waiting for transfers between devices: 37.8 us -> 28.3 us  [flip(): lax.ppermute(value, 'cols', [(d, d ^ 1 << bits[d & 1]) for d in range(cou...]
    ppermute x4, waiting for transfers between devices: 6.52 us -> 13.4 us  [swap(): return lax.ppermute(value, 'rows', pairs + [(b, a) for a, b in pairs])]
    ppermute x18 -> x21, starting transfers between devices: 15.1 us -> 16.9 us  [flip(): lax.ppermute(value, 'cols', [(d, d ^ 1 << bits[d & 1]) for d in range(cou...]
  transfers between devices with their start and end apart: 23 -> 26, of which waited for: 10 -> 11; matrix products, arithmetic and copies ran while one was open for 17% -> 17% of each run, Pallas kernels for 5% -> 3%
where the time goes in v13:
time: 114 us
  waiting for transfers between devices  45.7 us (40%)
  starting transfers between devices  28.1 us (25%)
  matrix products  12 us (11%)
  other arithmetic  9.98 us (9%)
  Pallas kernels  7.82 us (7%)
  local copies, waits for them, and re-layouts  5.93 us (5%)
  between operations  4.19 us (4%)
    ppermute x21, waiting for transfers between devices, flip(): lax.ppermute(value, 'cols', [(d, d ^ 1 << bits[d & 1]) for d in range(cou...  28.3 us
    ppermute x21, starting transfers between devices, flip(): lax.ppermute(value, 'cols', [(d, d ^ 1 << bits[d & 1]) for d in range(cou...  16.9 us
    ppermute x4, waiting for transfers between devices, swap(): return lax.ppermute(value, 'rows', pairs + [(b, a) for a, b in pairs])  13.4 us
    dot_general x6, matrix products, apply_many(): jnp.einsum('nab,nac->nbc', q, x, preferred_element_type=jnp.float32)  10.1 us
    select_n x9, other arithmetic, choose(): return jnp.where(mask, yes, no)  8.65 us
    ppermute x4, starting transfers between devices, swap(): return lax.ppermute(value, 'rows', pairs + [(b, a) for a, b in pairs])  7.76 us
    ppermute x1, waiting for transfers between devices, shifted(): lax.ppermute(value, axis, [(source, source + steps) for source in range(i...  4.01 us
    ppermute x1, starting transfers between devices, shifted(): lax.ppermute(value, axis, [(source, source + steps) for source in range(i...  3.48 us
  transfers between devices with their start and end apart: 26, of which 11 were waited for; matrix products, arithmetic and copies ran while one was open for 17% of the time, Pallas kernels for 3%

profile of v13, /device:TPU:8, one launch (start us, length us, event | category | flops | bytes accessed | tf_op | source)
XLA Modules:
  0.0 113.7 jit_solution(13000776008545431226)
XLA Ops:
  0.0 2.2 %copy-done.2 = bf16[1,4096,512]{2,1,0:T(8,128)(2,1)S(1)} copy-done((bf16[1,4096,512]{2,1,0:T(8,128)(2,1)S(1)}, bf16[1,4096,512]{2,1,0:T(8,128)(2,1)}, u32[]{:S(2)}) %copy-start.2) | copy-done | bytes 4194328
  3.1 1.9 %cut_slot.2 = (bf16[9,128,512]{2,1,0:T(8,128)(2,1)S(1)}, bf16[9,128,512]{2,1,0:T(8,128)(2,1)}, bf16[9,128,512]{2,1,0:T(8,128)(2,1)S(1)}) custom-call(bf16[8,2,2,128,512]{4,3,2,1,0:T(8,128)(2,1)S(1)} %bitcast.84), custom_call_target="tpu_custom_call" | custom-call | bytes 6291456 | tf_op jit(solution)/shard_map/cut_slot/pallas_call | solution.py:105
  10.2 2.0 %slice_select_fusion.2 = bf16[5,128,512]{2,1,0:T(8,128)(2,1)} fusion(bf16[9,128,512]{2,1,0:T(8,128)(2,1)} %collective-permute-done.1, bf16[9,128,512]{2,1,0:T(8,128)(2,1)S(1)} %get-tuple-element.10, pred[]{:T(512)S(6)} %eq.25), kind=kLoop, calls=%fused_computation.46 | loop fusion | flops 327680 | bytes 1966081 | tf_op jit(solution)/shard_map/jit(_where)/select_n | solution.py:178
  14.0 3.9 %collective-permute-done.2 = bf16[4,128,512]{2,1,0:T(8,128)(2,1)S(1)} collective-permute-done((bf16[4,128,512]{2,1,0:T(8,128)(2,1)S(1)}, bf16[4,128,512]{2,1,0:T(8,128)(2,1)S(1)}, u32[]{:S(2)}, u32[]{:S(2)}) %collective-permute-start.2) | collective-permute-done | bytes 524320 | tf_op jit(solution)/shard_map/ppermute | solution.py:30
  20.0 1.6 %collective-permute-start.3 = (bf16[4,128,512]{2,1,0:T(8,128)(2,1)S(1)}, bf16[4,128,512]{2,1,0:T(8,128)(2,1)S(1)}, u32[]{:S(2)}, u32[]{:S(2)}) collective-permute-start(bf16[4,128,512]{2,1,0:T(8,128)(2,1)S(1)} %fusion.34), channel_id=1, source_target_pairs={{0,4},{1,3},{2,6},{3,1},{4,0},{5,7},{6,2},{7,5},{8,12},{9,11},{10,... | collective-permute-start | bytes 1572872 | tf_op jit(solution)/shard_map/ppermute | solution.py:30
  22.8 5.1 %collective-permute-done.19 = bf16[5,128,512]{2,1,0:T(8,128)(2,1)} collective-permute-done((bf16[5,128,512]{2,1,0:T(8,128)(2,1)}, bf16[5,128,512]{2,1,0:T(8,128)(2,1)}, u32[]{:S(2)}, u32[]{:S(2)}) %collective-permute-start.19) | collective-permute-done | bytes 655392 | tf_op jit(solution)/shard_map/ppermute | solution.py:30
  29.1 1.6 %collective-permute-start.20 = (bf16[5,128,512]{2,1,0:T(8,128)(2,1)S(1)}, bf16[5,128,512]{2,1,0:T(8,128)(2,1)S(1)}, u32[]{:S(2)}, u32[]{:S(2)}) collective-permute-start(bf16[5,128,512]{2,1,0:T(8,128)(2,1)S(1)} %fusion.33), channel_id=1, source_target_pairs={{0,4},{1,3},{2,6},{3,1},{4,0},{5,7},{6,2},{7,5},{8,12},{9,11},{10,... | collective-permute-start | bytes 1966088 | tf_op jit(solution)/shard_map/ppermute | solution.py:30
  30.8 1.8 %collective-permute-start.12 = (bf16[4,128,512]{2,1,0:T(8,128)(2,1)S(1)}, bf16[4,128,512]{2,1,0:T(8,128)(2,1)S(1)}, u32[]{:S(2)}, u32[]{:S(2)}) collective-permute-start(bf16[4,128,512]{2,1,0:T(8,128)(2,1)S(1)} %broadcast_select_fusion.2.refs_0_), channel_id=1, source_target_pairs={{0,2},{1,5},{2,0},{3,7},{4,6},{5,1},{6,4},{7,3},{8,10},{9,13},{10,... | collective-permute-start | bytes 1572872 | tf_op jit(solution)/shard_map/ppermute | solution.py:30
  34.5 12.0 %collective-permute-done.20 = bf16[5,128,512]{2,1,0:T(8,128)(2,1)S(1)} collective-permute-done((bf16[5,128,512]{2,1,0:T(8,128)(2,1)S(1)}, bf16[5,128,512]{2,1,0:T(8,128)(2,1)S(1)}, u32[]{:S(2)}, u32[]{:S(2)}) %collective-permute-start.20) | collective-permute-done | bytes 655392 | tf_op jit(solution)/shard_map/ppermute | solution.py:30
  46.6 1.9 %collective-permute-start.21 = (bf16[5,128,512]{2,1,0:T(8,128)(2,1)S(1)}, bf16[5,128,512]{2,1,0:T(8,128)(2,1)S(1)}, u32[]{:S(2)}, u32[]{:S(2)}) collective-permute-start(bf16[5,128,512]{2,1,0:T(8,128)(2,1)S(1)} %broadcast_select_fusion.1.refs_0_), channel_id=1, source_target_pairs={{0,2},{1,5},{2,0},{3,7},{4,6},{5,1},{6,4},{7,3},{8,10},{9,13},{10,... | collective-permute-start | bytes 1966088 | tf_op jit(solution)/shard_map/ppermute | solution.py:30
  48.5 3.5 %collective-permute-start.15 = (bf16[2,2,128,256]{3,2,1,0:T(8,128)(2,1)S(1)}, bf16[2,2,128,256]{3,2,1,0:T(8,128)(2,1)S(1)}, u32[]{:S(2)}, u32[]{:S(2)}) collective-permute-start(bf16[2,2,128,256]{3,2,1,0:T(8,128)(2,1)S(1)} %pad_maximum_fusion.4), channel_id=1, source_target_pairs={{0,8},{8,16},{16,24},{1,9},{9,17},{17,25},{2,10},{10,18},{18,26},{... | collective-permute-start | bytes 786440 | tf_op jit(solution)/shard_map/ppermute | solution.py:12
  52.8 4.0 %collective-permute-done.15 = bf16[2,2,128,256]{3,2,1,0:T(8,128)(2,1)S(1)} collective-permute-done((bf16[2,2,128,256]{3,2,1,0:T(8,128)(2,1)S(1)}, bf16[2,2,128,256]{3,2,1,0:T(8,128)(2,1)S(1)}, u32[]{:S(2)}, u32[]{:S(2)}) %collective-permute-start.15) | collective-permute-done | bytes 262176 | tf_op jit(solution)/shard_map/ppermute | solution.py:12
  56.8 3.2 %collective-permute-done.21.refs_1_ = bf16[5,128,512]{2,1,0:T(8,128)(2,1)S(1)} collective-permute-done((bf16[5,128,512]{2,1,0:T(8,128)(2,1)S(1)}, bf16[5,128,512]{2,1,0:T(8,128)(2,1)S(1)}, u32[]{:S(2)}, u32[]{:S(2)}) %collective-permute-start.21) | collective-permute-done | bytes 655392 | tf_op jit(solution)/shard_map/ppermute | solution.py:30
  60.0 2.1 %collective-permute-start.16 = (bf16[2,2,128,256]{3,2,1,0:T(8,128)(2,1)S(1)}, bf16[2,2,128,256]{3,2,1,0:T(8,128)(2,1)S(1)}, u32[]{:S(2)}, u32[]{:S(2)}) collective-permute-start(bf16[2,2,128,256]{3,2,1,0:T(8,128)(2,1)S(1)} %collective-permute-done.15), channel_id=1, source_target_pairs={{0,1},{1,0},{2,3},{3,2},{4,5},{5,4},{6,7},{7,6},{8,9},{9,8},{10,11... | collective-permute-start | bytes 786440 | tf_op jit(solution)/shard_map/ppermute | solution.py:30
  66.9 3.5 %collective-permute-start.17 = (bf16[256,1024]{1,0:T(8,128)(2,1)S(1)}, bf16[256,1024]{1,0:T(8,128)(2,1)S(1)}, u32[]{:S(2)}, u32[]{:S(2)}) collective-permute-start(bf16[256,1024]{1,0:T(8,128)(2,1)S(1)} %get-tuple-element.27), channel_id=1, source_target_pairs={{8,16},{16,8},{9,17},{17,9},{10,18},{18,10},{11,19},{19,11},{12,20... | collective-permute-start | bytes 1572872 | tf_op jit(solution)/shard_map/ppermute | solution.py:21
  74.8 2.1 %convolution_convert_fusion.1 = bf16[3,512,1024]{2,1,0:T(8,128)(2,1)S(1)} fusion(bf16[5,512,512]{2,1,0:T(8,128)(2,1)S(1)} %place.9, bf16[3,512,1024]{2,1,0:T(8,128)(2,1)S(1)} %bitcast.89), kind=kOutput, calls=%fused_computation.3 | convolution fusion | flops 1612185600 | bytes 8912896 | tf_op jit(solution)/shard_map/nab,nac->nbc/dot_general | solution.py:230
  77.1 1.8 %collective-permute-start.9 = (bf16[2,128,512]{2,1,0:T(8,128)(2,1)S(1)}, bf16[2,128,512]{2,1,0:T(8,128)(2,1)S(1)}, u32[]{:S(2)}, u32[]{:S(2)}) collective-permute-start(bf16[2,128,512]{2,1,0:T(8,128)(2,1)S(1)} %slice.255.refs_0_), channel_id=1, source_target_pairs={{0,2},{1,5},{2,0},{3,7},{4,6},{5,1},{6,4},{7,3},{8,10},{9,13},{10,... | collective-permute-start | bytes 786440 | tf_op jit(solution)/shard_map/ppermute | solution.py:30
  78.8 4.2 %collective-permute-done.17 = bf16[256,1024]{1,0:T(8,128)(2,1)S(1)} collective-permute-done((bf16[256,1024]{1,0:T(8,128)(2,1)S(1)}, bf16[256,1024]{1,0:T(8,128)(2,1)S(1)}, u32[]{:S(2)}, u32[]{:S(2)}) %collective-permute-start.17) | collective-permute-done | bytes 524320 | tf_op jit(solution)/shard_map/ppermute | solution.py:21
  89.5 3.1 %collective-permute-start.24 = (bf16[256,1024]{1,0:T(8,128)(2,1)S(1)}, bf16[256,1024]{1,0:T(8,128)(2,1)S(1)}, u32[]{:S(2)}, u32[]{:S(2)}) collective-permute-start(bf16[256,1024]{1,0:T(8,128)(2,1)S(1)} %get-tuple-element.22), channel_id=1, source_target_pairs={{8,16},{16,8},{9,17},{17,9},{10,18},{18,10},{11,19},{19,11},{12,20... | collective-permute-start | bytes 1572872 | tf_op jit(solution)/shard_map/ppermute | solution.py:21
  93.1 3.8 %collective-permute-done.6.refs_1_ = bf16[5,128,512]{2,1,0:T(8,128)(2,1)S(1)} collective-permute-done((bf16[5,128,512]{2,1,0:T(8,128)(2,1)S(1)}, bf16[5,128,512]{2,1,0:T(8,128)(2,1)S(1)}, u32[]{:S(2)}, u32[]{:S(2)}) %collective-permute-start.6) | collective-permute-done | bytes 655392 | tf_op jit(solution)/shard_map/ppermute | solution.py:30
  96.9 5.9 %collective-permute-done.25 = bf16[256,1024]{1,0:T(8,128)(2,1)S(1)} collective-permute-done((bf16[256,1024]{1,0:T(8,128)(2,1)S(1)}, bf16[256,1024]{1,0:T(8,128)(2,1)S(1)}, u32[]{:S(2)}, u32[]{:S(2)}) %collective-permute-start.25) | collective-permute-done | bytes 524320 | tf_op jit(solution)/shard_map/ppermute | solution.py:21
  102.8 1.9 %collective-permute-done.24 = bf16[256,1024]{1,0:T(8,128)(2,1)S(1)} collective-permute-done((bf16[256,1024]{1,0:T(8,128)(2,1)S(1)}, bf16[256,1024]{1,0:T(8,128)(2,1)S(1)}, u32[]{:S(2)}, u32[]{:S(2)}) %collective-permute-start.24) | collective-permute-done | bytes 524320 | tf_op jit(solution)/shard_map/ppermute | solution.py:21
  107.9 2.1 %convolution_convert_fusion = bf16[3,512,1024]{2,1,0:T(8,128)(2,1)S(1)} fusion(bf16[5,512,512]{2,1,0:T(8,128)(2,1)S(1)} %place.5, bf16[3,512,1024]{2,1,0:T(8,128)(2,1)S(1)} %bitcast.90), kind=kOutput, calls=%fused_computation.2 | convolution fusion | flops 1612185600 | bytes 8912896 | tf_op jit(solution)/shard_map/nab,nac->nbc/dot_general | solution.py:230
  110.0 2.7 %write_inner.1._ = bf16[2048,1024]{1,0:T(8,128)(2,1)} custom-call(bf16[1536,1024]{1,0:T(8,128)(2,1)S(1)} %bitcast.85), custom_call_target="tpu_custom_call" | custom-call | bytes 6291456 | tf_op jit(solution)/shard_map/write_inner/pallas_call | solution.py:240
  (93 shorter events, 31.8 us)
Async XLA Ops:
  3.0 4.5 %collective-permute-start.1 = (bf16[9,128,512]{2,1,0:T(8,128)(2,1)S(1)}, bf16[9,128,512]{2,1,0:T(8,128)(2,1)}, u32[]{:S(2)}, u32[]{:S(2)}) collective-permute-start(bf16[9,128,512]{2,1,0:T(8,128)(2,1)S(1)} %cut_slot.3), channel_id=1, source_target_pairs={{0,1},{1,0},{2,3},{3,2},{4,5},{5,4},{6,7},{7,6},{8,9},{9,8},{10,11... | collective-permute-start | bytes 3538952 | tf_op jit(solution)/shard_map/ppermute | solution.py:30
  5.0 8.9 %collective-permute-start = (bf16[9,128,512]{2,1,0:T(8,128)(2,1)}, bf16[9,128,512]{2,1,0:T(8,128)(2,1)}, u32[]{:S(2)}, u32[]{:S(2)}) collective-permute-start(bf16[9,128,512]{2,1,0:T(8,128)(2,1)} %get-tuple-element.9), channel_id=1, source_target_pairs={{0,1},{1,0},{2,3},{3,2},{4,5},{5,4},{6,7},{7,6},{8,9},{9,8},{10,11... | collective-permute-start | bytes 3538952 | tf_op jit(solution)/shard_map/ppermute | solution.py:30
  8.6 9.2 %collective-permute-start.2 = (bf16[4,128,512]{2,1,0:T(8,128)(2,1)S(1)}, bf16[4,128,512]{2,1,0:T(8,128)(2,1)S(1)}, u32[]{:S(2)}, u32[]{:S(2)}) collective-permute-start(bf16[4,128,512]{2,1,0:T(8,128)(2,1)S(1)} %slice_select_fusion.4), channel_id=1, source_target_pairs={{0,2},{1,5},{2,0},{3,7},{4,6},{5,1},{6,4},{7,3},{8,10},{9,13},{10,... | collective-permute-start | bytes 1572872 | tf_op jit(solution)/shard_map/ppermute | solution.py:30
  12.2 15.8 %collective-permute-start.19 = (bf16[5,128,512]{2,1,0:T(8,128)(2,1)}, bf16[5,128,512]{2,1,0:T(8,128)(2,1)}, u32[]{:S(2)}, u32[]{:S(2)}) collective-permute-start(bf16[5,128,512]{2,1,0:T(8,128)(2,1)} %slice_select_fusion.2), channel_id=1, source_target_pairs={{0,2},{1,5},{2,0},{3,7},{4,6},{5,1},{6,4},{7,3},{8,10},{9,13},{10,... | collective-permute-start | bytes 1966088 | tf_op jit(solution)/shard_map/ppermute | solution.py:30
  20.0 10.7 %collective-permute-start.3 = (bf16[4,128,512]{2,1,0:T(8,128)(2,1)S(1)}, bf16[4,128,512]{2,1,0:T(8,128)(2,1)S(1)}, u32[]{:S(2)}, u32[]{:S(2)}) collective-permute-start(bf16[4,128,512]{2,1,0:T(8,128)(2,1)S(1)} %fusion.34), channel_id=1, source_target_pairs={{0,4},{1,3},{2,6},{3,1},{4,0},{5,7},{6,2},{7,5},{8,12},{9,11},{10,... | collective-permute-start | bytes 1572872 | tf_op jit(solution)/shard_map/ppermute | solution.py:30
  29.1 17.4 %collective-permute-start.20 = (bf16[5,128,512]{2,1,0:T(8,128)(2,1)S(1)}, bf16[5,128,512]{2,1,0:T(8,128)(2,1)S(1)}, u32[]{:S(2)}, u32[]{:S(2)}) collective-permute-start(bf16[5,128,512]{2,1,0:T(8,128)(2,1)S(1)} %fusion.33), channel_id=1, source_target_pairs={{0,4},{1,3},{2,6},{3,1},{4,0},{5,7},{6,2},{7,5},{8,12},{9,11},{10,... | collective-permute-start | bytes 1966088 | tf_op jit(solution)/shard_map/ppermute | solution.py:30
  30.8 17.6 %collective-permute-start.12 = (bf16[4,128,512]{2,1,0:T(8,128)(2,1)S(1)}, bf16[4,128,512]{2,1,0:T(8,128)(2,1)S(1)}, u32[]{:S(2)}, u32[]{:S(2)}) collective-permute-start(bf16[4,128,512]{2,1,0:T(8,128)(2,1)S(1)} %broadcast_select_fusion.2.refs_0_), channel_id=1, source_target_pairs={{0,2},{1,5},{2,0},{3,7},{4,6},{5,1},{6,4},{7,3},{8,10},{9,13},{10,... | collective-permute-start | bytes 1572872 | tf_op jit(solution)/shard_map/ppermute | solution.py:30
  34.1 27.9 %collective-permute-start.4 = (bf16[7,128,512]{2,1,0:T(8,128)(2,1)S(1)}, bf16[7,128,512]{2,1,0:T(8,128)(2,1)S(1)}, u32[]{:S(2)}, u32[]{:S(2)}) collective-permute-start(bf16[7,128,512]{2,1,0:T(8,128)(2,1)S(1)} %after.1), channel_id=1, source_target_pairs={{0,2},{1,5},{2,0},{3,7},{4,6},{5,1},{6,4},{7,3},{8,10},{9,13},{10,... | collective-permute-start | bytes 2752520 | tf_op jit(solution)/shard_map/ppermute | solution.py:30
  46.6 13.4 %collective-permute-start.21 = (bf16[5,128,512]{2,1,0:T(8,128)(2,1)S(1)}, bf16[5,128,512]{2,1,0:T(8,128)(2,1)S(1)}, u32[]{:S(2)}, u32[]{:S(2)}) collective-permute-start(bf16[5,128,512]{2,1,0:T(8,128)(2,1)S(1)} %broadcast_select_fusion.1.refs_0_), channel_id=1, source_target_pairs={{0,2},{1,5},{2,0},{3,7},{4,6},{5,1},{6,4},{7,3},{8,10},{9,13},{10,... | collective-permute-start | bytes 1966088 | tf_op jit(solution)/shard_map/ppermute | solution.py:30
  48.5 8.3 %collective-permute-start.15 = (bf16[2,2,128,256]{3,2,1,0:T(8,128)(2,1)S(1)}, bf16[2,2,128,256]{3,2,1,0:T(8,128)(2,1)S(1)}, u32[]{:S(2)}, u32[]{:S(2)}) collective-permute-start(bf16[2,2,128,256]{3,2,1,0:T(8,128)(2,1)S(1)} %pad_maximum_fusion.4), channel_id=1, source_target_pairs={{0,8},{8,16},{16,24},{1,9},{9,17},{17,25},{2,10},{10,18},{18,26},{... | collective-permute-start | bytes 786440 | tf_op jit(solution)/shard_map/ppermute | solution.py:12
  52.2 11.3 %collective-permute-start.13 = (bf16[4,128,512]{2,1,0:T(8,128)(2,1)S(1)}, bf16[4,128,512]{2,1,0:T(8,128)(2,1)S(1)}, u32[]{:S(2)}, u32[]{:S(2)}) collective-permute-start(bf16[4,128,512]{2,1,0:T(8,128)(2,1)S(1)} %broadcast_select_fusion.2.refs_0_), channel_id=1, source_target_pairs={{0,1},{1,0},{2,3},{3,2},{4,5},{5,4},{6,7},{7,6},{8,9},{9,8},{10,11... | collective-permute-start | bytes 1572872 | tf_op jit(solution)/shard_map/ppermute | solution.py:30
  52.3 19.0 %collective-permute-start.22 = (bf16[5,128,512]{2,1,0:T(8,128)(2,1)S(1)}, bf16[5,128,512]{2,1,0:T(8,128)(2,1)S(1)}, u32[]{:S(2)}, u32[]{:S(2)}) collective-permute-start(bf16[5,128,512]{2,1,0:T(8,128)(2,1)S(1)} %broadcast_select_fusion.1.refs_0_), channel_id=1, source_target_pairs={{0,1},{1,0},{2,3},{3,2},{4,5},{5,4},{6,7},{7,6},{8,9},{9,8},{10,11... | collective-permute-start | bytes 1966088 | tf_op jit(solution)/shard_map/ppermute | solution.py:30
  56.8 8.3 %collective-permute-start.14 = (bf16[4,128,512]{2,1,0:T(8,128)(2,1)S(1)}, bf16[4,128,512]{2,1,0:T(8,128)(2,1)S(1)}, u32[]{:S(2)}, u32[]{:S(2)}) collective-permute-start(bf16[4,128,512]{2,1,0:T(8,128)(2,1)S(1)} %collective-permute-done.12.refs_1_), channel_id=1, source_target_pairs={{0,1},{1,0},{2,3},{3,2},{4,5},{5,4},{6,7},{7,6},{8,9},{9,8},{10,11... | collective-permute-start | bytes 1572872 | tf_op jit(solution)/shard_map/ppermute | solution.py:30
  60.0 10.4 %collective-permute-start.16 = (bf16[2,2,128,256]{3,2,1,0:T(8,128)(2,1)S(1)}, bf16[2,2,128,256]{3,2,1,0:T(8,128)(2,1)S(1)}, u32[]{:S(2)}, u32[]{:S(2)}) collective-permute-start(bf16[2,2,128,256]{3,2,1,0:T(8,128)(2,1)S(1)} %collective-permute-done.15), channel_id=1, source_target_pairs={{0,1},{1,0},{2,3},{3,2},{4,5},{5,4},{6,7},{7,6},{8,9},{9,8},{10,11... | collective-permute-start | bytes 786440 | tf_op jit(solution)/shard_map/ppermute | solution.py:30
  62.1 9.2 %collective-permute-start.23 = (bf16[5,128,512]{2,1,0:T(8,128)(2,1)S(1)}, bf16[5,128,512]{2,1,0:T(8,128)(2,1)S(1)}, u32[]{:S(2)}, u32[]{:S(2)}) collective-permute-start(bf16[5,128,512]{2,1,0:T(8,128)(2,1)S(1)} %collective-permute-done.21.refs_1_), channel_id=1, source_target_pairs={{0,1},{1,0},{2,3},{3,2},{4,5},{5,4},{6,7},{7,6},{8,9},{9,8},{10,11... | collective-permute-start | bytes 1966088 | tf_op jit(solution)/shard_map/ppermute | solution.py:30
  63.5 13.5 %collective-permute-start.5 = (bf16[7,128,512]{2,1,0:T(8,128)(2,1)S(1)}, bf16[7,128,512]{2,1,0:T(8,128)(2,1)S(1)}, u32[]{:S(2)}, u32[]{:S(2)}) collective-permute-start(bf16[7,128,512]{2,1,0:T(8,128)(2,1)S(1)} %fusion.32), channel_id=1, source_target_pairs={{0,4},{1,3},{2,6},{3,1},{4,0},{5,7},{6,2},{7,5},{8,12},{9,11},{10,... | collective-permute-start | bytes 2752520 | tf_op jit(solution)/shard_map/ppermute | solution.py:30
  66.9 16.2 %collective-permute-start.17 = (bf16[256,1024]{1,0:T(8,128)(2,1)S(1)}, bf16[256,1024]{1,0:T(8,128)(2,1)S(1)}, u32[]{:S(2)}, u32[]{:S(2)}) collective-permute-start(bf16[256,1024]{1,0:T(8,128)(2,1)S(1)} %get-tuple-element.27), channel_id=1, source_target_pairs={{8,16},{16,8},{9,17},{17,9},{10,18},{18,10},{11,19},{19,11},{12,20... | collective-permute-start | bytes 1572872 | tf_op jit(solution)/shard_map/ppermute | solution.py:21
  70.4 14.0 %collective-permute-start.18 = (bf16[256,1024]{1,0:T(8,128)(2,1)S(1)}, bf16[256,1024]{1,0:T(8,128)(2,1)S(1)}, u32[]{:S(2)}, u32[]{:S(2)}) collective-permute-start(bf16[256,1024]{1,0:T(8,128)(2,1)S(1)} %get-tuple-element.28), channel_id=1, source_target_pairs={{0,8},{16,24},{8,0},{24,16},{1,9},{17,25},{9,1},{25,17},{2,10},{18... | collective-permute-start | bytes 1572872 | tf_op jit(solution)/shard_map/ppermute | solution.py:21
  77.1 7.9 %collective-permute-start.9 = (bf16[2,128,512]{2,1,0:T(8,128)(2,1)S(1)}, bf16[2,128,512]{2,1,0:T(8,128)(2,1)S(1)}, u32[]{:S(2)}, u32[]{:S(2)}) collective-permute-start(bf16[2,128,512]{2,1,0:T(8,128)(2,1)S(1)} %slice.255.refs_0_), channel_id=1, source_target_pairs={{0,2},{1,5},{2,0},{3,7},{4,6},{5,1},{6,4},{7,3},{8,10},{9,13},{10,... | collective-permute-start | bytes 786440 | tf_op jit(solution)/shard_map/ppermute | solution.py:30
  86.2 10.7 %collective-permute-start.6 = (bf16[5,128,512]{2,1,0:T(8,128)(2,1)S(1)}, bf16[5,128,512]{2,1,0:T(8,128)(2,1)S(1)}, u32[]{:S(2)}, u32[]{:S(2)}) collective-permute-start(bf16[5,128,512]{2,1,0:T(8,128)(2,1)S(1)} %slice.254.refs_0_), channel_id=1, source_target_pairs={{0,2},{1,5},{2,0},{3,7},{4,6},{5,1},{6,4},{7,3},{8,10},{9,13},{10,... | collective-permute-start | bytes 1966088 | tf_op jit(solution)/shard_map/ppermute | solution.py:30
  88.5 14.3 %collective-permute-start.25 = (bf16[256,1024]{1,0:T(8,128)(2,1)S(1)}, bf16[256,1024]{1,0:T(8,128)(2,1)S(1)}, u32[]{:S(2)}, u32[]{:S(2)}) collective-permute-start(bf16[256,1024]{1,0:T(8,128)(2,1)S(1)} %get-tuple-element.21), channel_id=1, source_target_pairs={{0,8},{16,24},{8,0},{24,16},{1,9},{17,25},{9,1},{25,17},{2,10},{18... | collective-permute-start | bytes 1572872 | tf_op jit(solution)/shard_map/ppermute | solution.py:21
  89.5 15.2 %collective-permute-start.24 = (bf16[256,1024]{1,0:T(8,128)(2,1)S(1)}, bf16[256,1024]{1,0:T(8,128)(2,1)S(1)}, u32[]{:S(2)}, u32[]{:S(2)}) collective-permute-start(bf16[256,1024]{1,0:T(8,128)(2,1)S(1)} %get-tuple-element.22), channel_id=1, source_target_pairs={{8,16},{16,8},{9,17},{17,9},{10,18},{18,10},{11,19},{19,11},{12,20... | collective-permute-start | bytes 1572872 | tf_op jit(solution)/shard_map/ppermute | solution.py:21
  92.8 12.9 %collective-permute-start.7 = (bf16[5,128,512]{2,1,0:T(8,128)(2,1)S(1)}, bf16[5,128,512]{2,1,0:T(8,128)(2,1)S(1)}, u32[]{:S(2)}, u32[]{:S(2)}) collective-permute-start(bf16[5,128,512]{2,1,0:T(8,128)(2,1)S(1)} %slice.254.refs_0_), channel_id=1, source_target_pairs={{0,1},{1,0},{2,3},{3,2},{4,5},{5,4},{6,7},{7,6},{8,9},{9,8},{10,11... | collective-permute-start | bytes 1966088 | tf_op jit(solution)/shard_map/ppermute | solution.py:30
  96.9 8.8 %collective-permute-start.8 = (bf16[5,128,512]{2,1,0:T(8,128)(2,1)S(1)}, bf16[5,128,512]{2,1,0:T(8,128)(2,1)S(1)}, u32[]{:S(2)}, u32[]{:S(2)}) collective-permute-start(bf16[5,128,512]{2,1,0:T(8,128)(2,1)S(1)} %collective-permute-done.6.refs_1_), channel_id=1, source_target_pairs={{0,1},{1,0},{2,3},{3,2},{4,5},{5,4},{6,7},{7,6},{8,9},{9,8},{10,11... | collective-permute-start | bytes 1966088 | tf_op jit(solution)/shard_map/ppermute | solution.py:30
  (8 other events, 32.9 us)

commit v14 on v13

--- a/solution.py
+++ b/solution.py
@@ -332,13 +332,16 @@
         inner = apply_many(twos, centre.reshape(wins - 1, window, local_cols)).reshape(
             local_rows - window, local_cols
         )
+        if r == rounds - 1:
+            whole = write_inner(inner, border)
+            prev, cross = after(prev, whole), after(cross, whole)
         low = apply(cross[:, :border], jnp.concatenate([end, below], 0))
         low = jnp.where(row_block == last_block, end, low)
         top = apply(prev, jnp.concatenate([above, begin], 0))
         top = jnp.where(row_block == 0, begin, top)
         if r < rounds - 1:
             matrix = jnp.concatenate([top, inner, low], 0)
-    return write_outer(write_inner(inner, border), top, low)
+    return write_outer(whole, top, low)
 
 
 def solution(mesh):

time: 114 us -> 117 us (1.026)
  local copies, waits for them, and re-layouts: 5.93 us -> 8.08 us
    unnamed x10 -> x12, local copies, waits for them, and re-layouts: 3.01 us -> 5.2 us
  transfers between devices with their start and end apart: 26 -> 26, of which waited for: 11 -> 11; matrix products, arithmetic and copies ran while one was open for 17% -> 16% of each run, Pallas kernels for 3% -> 3%
where the time goes in v14:
time: 117 us
  waiting for transfers between devices  46.6 us (40%)
  starting transfers between devices  28.3 us (24%)
  matrix products  12 us (10%)
  other arithmetic  10.2 us (9%)
  local copies, waits for them, and re-layouts  8.08 us (7%)
  Pallas kernels  7.93 us (7%)
  between operations  3.89 us (3%)
    ppermute x21, waiting for transfers between devices, flip(): lax.ppermute(value, 'cols', [(d, d ^ 1 << bits[d & 1]) for d in range(cou...  28.8 us
    ppermute x21, starting transfers between devices, flip(): lax.ppermute(value, 'cols', [(d, d ^ 1 << bits[d & 1]) for d in range(cou...  17 us
    ppermute x4, waiting for transfers between devices, swap(): return lax.ppermute(value, 'rows', pairs + [(b, a) for a, b in pairs])  14.1 us
    dot_general x6, matrix products, apply_many(): jnp.einsum('nab,nac->nbc', q, x, preferred_element_type=jnp.float32)  10.1 us
    select_n x9, other arithmetic, choose(): return jnp.where(mask, yes, no)  8.85 us
    ppermute x4, starting transfers between devices, swap(): return lax.ppermute(value, 'rows', pairs + [(b, a) for a, b in pairs])  7.43 us
    unnamed x12, local copies, waits for them, and re-layouts  5.2 us
    ppermute x1, starting transfers between devices, shifted(): lax.ppermute(value, axis, [(source, source + steps) for source in range(i...  3.79 us
  transfers between devices with their start and end apart: 26, of which 11 were waited for; matrix products, arithmetic and copies ran while one was open for 16% of the time, Pallas kernels for 3%

profile of v14, /device:TPU:8, one launch (start us, length us, event | category | flops | bytes accessed | tf_op | source)
XLA Modules:
  0.0 116.9 jit_solution(641200895660383088)
XLA Ops:
  0.0 2.2 %copy-done.3 = bf16[1,4096,512]{2,1,0:T(8,128)(2,1)S(1)} copy-done((bf16[1,4096,512]{2,1,0:T(8,128)(2,1)S(1)}, bf16[1,4096,512]{2,1,0:T(8,128)(2,1)}, u32[]{:S(2)}) %copy-start.3) | copy-done | bytes 4194328
  3.1 1.9 %cut_slot.2 = (bf16[9,128,512]{2,1,0:T(8,128)(2,1)S(1)}, bf16[9,128,512]{2,1,0:T(8,128)(2,1)}, bf16[9,128,512]{2,1,0:T(8,128)(2,1)S(1)}) custom-call(bf16[8,2,2,128,512]{4,3,2,1,0:T(8,128)(2,1)S(1)} %bitcast.84), custom_call_target="tpu_custom_call" | custom-call | bytes 6291456 | tf_op jit(solution)/shard_map/cut_slot/pallas_call | solution.py:105
  10.0 2.0 %slice_select_fusion.2 = bf16[5,128,512]{2,1,0:T(8,128)(2,1)} fusion(bf16[9,128,512]{2,1,0:T(8,128)(2,1)} %collective-permute-done.1, bf16[9,128,512]{2,1,0:T(8,128)(2,1)S(1)} %get-tuple-element.10, pred[]{:T(512)S(6)} %eq.25), kind=kLoop, calls=%fused_computation.46 | loop fusion | flops 327680 | bytes 1966081 | tf_op jit(solution)/shard_map/jit(_where)/select_n | solution.py:178
  13.7 4.0 %collective-permute-done.2 = bf16[4,128,512]{2,1,0:T(8,128)(2,1)S(1)} collective-permute-done((bf16[4,128,512]{2,1,0:T(8,128)(2,1)S(1)}, bf16[4,128,512]{2,1,0:T(8,128)(2,1)S(1)}, u32[]{:S(2)}, u32[]{:S(2)}) %collective-permute-start.2) | collective-permute-done | bytes 524320 | tf_op jit(solution)/shard_map/ppermute | solution.py:30
  19.8 1.6 %collective-permute-start.3 = (bf16[4,128,512]{2,1,0:T(8,128)(2,1)S(1)}, bf16[4,128,512]{2,1,0:T(8,128)(2,1)S(1)}, u32[]{:S(2)}, u32[]{:S(2)}) collective-permute-start(bf16[4,128,512]{2,1,0:T(8,128)(2,1)S(1)} %fusion.34), channel_id=1, source_target_pairs={{0,4},{1,3},{2,6},{3,1},{4,0},{5,7},{6,2},{7,5},{8,12},{9,11},{10,... | collective-permute-start | bytes 1572872 | tf_op jit(solution)/shard_map/ppermute | solution.py:30
  22.6 5.2 %collective-permute-done.19 = bf16[5,128,512]{2,1,0:T(8,128)(2,1)} collective-permute-done((bf16[5,128,512]{2,1,0:T(8,128)(2,1)}, bf16[5,128,512]{2,1,0:T(8,128)(2,1)}, u32[]{:S(2)}, u32[]{:S(2)}) %collective-permute-start.19) | collective-permute-done | bytes 655392 | tf_op jit(solution)/shard_map/ppermute | solution.py:30
  29.2 1.6 %collective-permute-start.20 = (bf16[5,128,512]{2,1,0:T(8,128)(2,1)S(1)}, bf16[5,128,512]{2,1,0:T(8,128)(2,1)S(1)}, u32[]{:S(2)}, u32[]{:S(2)}) collective-permute-start(bf16[5,128,512]{2,1,0:T(8,128)(2,1)S(1)} %fusion.33), channel_id=1, source_target_pairs={{0,4},{1,3},{2,6},{3,1},{4,0},{5,7},{6,2},{7,5},{8,12},{9,11},{10,... | collective-permute-start | bytes 1966088 | tf_op jit(solution)/shard_map/ppermute | solution.py:30
  34.6 12.1 %collective-permute-done.20 = bf16[5,128,512]{2,1,0:T(8,128)(2,1)S(1)} collective-permute-done((bf16[5,128,512]{2,1,0:T(8,128)(2,1)S(1)}, bf16[5,128,512]{2,1,0:T(8,128)(2,1)S(1)}, u32[]{:S(2)}, u32[]{:S(2)}) %collective-permute-start.20) | collective-permute-done | bytes 655392 | tf_op jit(solution)/shard_map/ppermute | solution.py:30
  48.1 3.8 %collective-permute-start.15 = (bf16[2,2,128,256]{3,2,1,0:T(8,128)(2,1)S(1)}, bf16[2,2,128,256]{3,2,1,0:T(8,128)(2,1)S(1)}, u32[]{:S(2)}, u32[]{:S(2)}) collective-permute-start(bf16[2,2,128,256]{3,2,1,0:T(8,128)(2,1)S(1)} %pad_maximum_fusion.4), channel_id=1, source_target_pairs={{0,8},{8,16},{16,24},{1,9},{9,17},{17,25},{2,10},{10,18},{18,26},{... | collective-permute-start | bytes 786440 | tf_op jit(solution)/shard_map/ppermute | solution.py:12
  52.6 3.7 %collective-permute-done.15 = bf16[2,2,128,256]{3,2,1,0:T(8,128)(2,1)S(1)} collective-permute-done((bf16[2,2,128,256]{3,2,1,0:T(8,128)(2,1)S(1)}, bf16[2,2,128,256]{3,2,1,0:T(8,128)(2,1)S(1)}, u32[]{:S(2)}, u32[]{:S(2)}) %collective-permute-start.15) | collective-permute-done | bytes 262176 | tf_op jit(solution)/shard_map/ppermute | solution.py:12
  56.4 3.5 %collective-permute-done.21.refs_1_ = bf16[5,128,512]{2,1,0:T(8,128)(2,1)S(1)} collective-permute-done((bf16[5,128,512]{2,1,0:T(8,128)(2,1)S(1)}, bf16[5,128,512]{2,1,0:T(8,128)(2,1)S(1)}, u32[]{:S(2)}, u32[]{:S(2)}) %collective-permute-start.21) | collective-permute-done | bytes 655392 | tf_op jit(solution)/shard_map/ppermute | solution.py:30
  59.8 2.3 %collective-permute-start.16 = (bf16[2,2,128,256]{3,2,1,0:T(8,128)(2,1)S(1)}, bf16[2,2,128,256]{3,2,1,0:T(8,128)(2,1)S(1)}, u32[]{:S(2)}, u32[]{:S(2)}) collective-permute-start(bf16[2,2,128,256]{3,2,1,0:T(8,128)(2,1)S(1)} %collective-permute-done.15), channel_id=1, source_target_pairs={{0,1},{1,0},{2,3},{3,2},{4,5},{5,4},{6,7},{7,6},{8,9},{9,8},{10,11... | collective-permute-start | bytes 786440 | tf_op jit(solution)/shard_map/ppermute | solution.py:30
  66.9 3.5 %collective-permute-start.17 = (bf16[256,1024]{1,0:T(8,128)(2,1)S(1)}, bf16[256,1024]{1,0:T(8,128)(2,1)S(1)}, u32[]{:S(2)}, u32[]{:S(2)}) collective-permute-start(bf16[256,1024]{1,0:T(8,128)(2,1)S(1)} %get-tuple-element.27), channel_id=1, source_target_pairs={{8,16},{16,8},{9,17},{17,9},{10,18},{18,10},{11,19},{19,11},{12,20... | collective-permute-start | bytes 1572872 | tf_op jit(solution)/shard_map/ppermute | solution.py:21
  74.8 2.1 %convolution_convert_fusion.1 = bf16[3,512,1024]{2,1,0:T(8,128)(2,1)S(1)} fusion(bf16[5,512,512]{2,1,0:T(8,128)(2,1)S(1)} %place.9, bf16[3,512,1024]{2,1,0:T(8,128)(2,1)S(1)} %bitcast.89), kind=kOutput, calls=%fused_computation.3 | convolution fusion | flops 1612185600 | bytes 8912896 | tf_op jit(solution)/shard_map/nab,nac->nbc/dot_general | solution.py:230
  77.1 1.6 %collective-permute-start.9 = (bf16[2,128,512]{2,1,0:T(8,128)(2,1)S(1)}, bf16[2,128,512]{2,1,0:T(8,128)(2,1)S(1)}, u32[]{:S(2)}, u32[]{:S(2)}) collective-permute-start(bf16[2,128,512]{2,1,0:T(8,128)(2,1)S(1)} %slice.255.refs_0_), channel_id=1, source_target_pairs={{0,2},{1,5},{2,0},{3,7},{4,6},{5,1},{6,4},{7,3},{8,10},{9,13},{10,... | collective-permute-start | bytes 786440 | tf_op jit(solution)/shard_map/ppermute | solution.py:30
  78.8 3.9 %collective-permute-done.17 = bf16[256,1024]{1,0:T(8,128)(2,1)S(1)} collective-permute-done((bf16[256,1024]{1,0:T(8,128)(2,1)S(1)}, bf16[256,1024]{1,0:T(8,128)(2,1)S(1)}, u32[]{:S(2)}, u32[]{:S(2)}) %collective-permute-start.17) | collective-permute-done | bytes 524320 | tf_op jit(solution)/shard_map/ppermute | solution.py:21
  82.7 1.7 %collective-permute-done.18 = bf16[256,1024]{1,0:T(8,128)(2,1)S(1)} collective-permute-done((bf16[256,1024]{1,0:T(8,128)(2,1)S(1)}, bf16[256,1024]{1,0:T(8,128)(2,1)S(1)}, u32[]{:S(2)}, u32[]{:S(2)}) %collective-permute-start.18) | collective-permute-done | bytes 524320 | tf_op jit(solution)/shard_map/ppermute | solution.py:21
  89.7 3.2 %collective-permute-start.24 = (bf16[256,1024]{1,0:T(8,128)(2,1)S(1)}, bf16[256,1024]{1,0:T(8,128)(2,1)S(1)}, u32[]{:S(2)}, u32[]{:S(2)}) collective-permute-start(bf16[256,1024]{1,0:T(8,128)(2,1)S(1)} %get-tuple-element.22), channel_id=1, source_target_pairs={{8,16},{16,8},{9,17},{17,9},{10,18},{18,10},{11,19},{19,11},{12,20... | collective-permute-start | bytes 1572872 | tf_op jit(solution)/shard_map/ppermute | solution.py:21
  92.9 3.9 %collective-permute-done.6.refs_1_ = bf16[5,128,512]{2,1,0:T(8,128)(2,1)S(1)} collective-permute-done((bf16[5,128,512]{2,1,0:T(8,128)(2,1)S(1)}, bf16[5,128,512]{2,1,0:T(8,128)(2,1)S(1)}, u32[]{:S(2)}, u32[]{:S(2)}) %collective-permute-start.6) | collective-permute-done | bytes 655392 | tf_op jit(solution)/shard_map/ppermute | solution.py:30
  97.2 5.8 %collective-permute-done.25 = bf16[256,1024]{1,0:T(8,128)(2,1)S(1)} collective-permute-done((bf16[256,1024]{1,0:T(8,128)(2,1)S(1)}, bf16[256,1024]{1,0:T(8,128)(2,1)S(1)}, u32[]{:S(2)}, u32[]{:S(2)}) %collective-permute-start.25) | collective-permute-done | bytes 524320 | tf_op jit(solution)/shard_map/ppermute | solution.py:21
  102.9 2.6 %collective-permute-done.24 = bf16[256,1024]{1,0:T(8,128)(2,1)S(1)} collective-permute-done((bf16[256,1024]{1,0:T(8,128)(2,1)S(1)}, bf16[256,1024]{1,0:T(8,128)(2,1)S(1)}, u32[]{:S(2)}, u32[]{:S(2)}) %collective-permute-start.24) | collective-permute-done | bytes 524320 | tf_op jit(solution)/shard_map/ppermute | solution.py:21
  107.8 2.1 %convolution_convert_fusion = bf16[3,512,1024]{2,1,0:T(8,128)(2,1)S(1)} fusion(bf16[5,512,512]{2,1,0:T(8,128)(2,1)S(1)} %place.5, bf16[3,512,1024]{2,1,0:T(8,128)(2,1)S(1)} %bitcast.90), kind=kOutput, calls=%fused_computation.2 | convolution fusion | flops 1612185600 | bytes 8912896 | tf_op jit(solution)/shard_map/nab,nac->nbc/dot_general | solution.py:230
  109.9 2.7 %write_inner.1.refs_0_._ = bf16[2048,1024]{1,0:T(8,128)(2,1)} custom-call(bf16[1536,1024]{1,0:T(8,128)(2,1)S(1)} %bitcast.85), custom_call_target="tpu_custom_call" | custom-call | bytes 6291456 | tf_op jit(solution)/shard_map/write_inner/pallas_call | solution.py:240
  112.6 2.2 %copy-done.2 = bf16[2048,1024]{1,0:T(8,128)(2,1)S(1)} copy-done((bf16[2048,1024]{1,0:T(8,128)(2,1)S(1)}, bf16[2048,1024]{1,0:T(8,128)(2,1)}, u32[]{:S(2)}) %copy-start.2) | copy-done | bytes 4194328
  (98 shorter events, 33.8 us)
Async XLA Ops:
  3.0 4.3 %collective-permute-start.1 = (bf16[9,128,512]{2,1,0:T(8,128)(2,1)S(1)}, bf16[9,128,512]{2,1,0:T(8,128)(2,1)}, u32[]{:S(2)}, u32[]{:S(2)}) collective-permute-start(bf16[9,128,512]{2,1,0:T(8,128)(2,1)S(1)} %cut_slot.3), channel_id=1, source_target_pairs={{0,1},{1,0},{2,3},{3,2},{4,5},{5,4},{6,7},{7,6},{8,9},{9,8},{10,11... | collective-permute-start | bytes 3538952 | tf_op jit(solution)/shard_map/ppermute | solution.py:30
  5.0 8.7 %collective-permute-start = (bf16[9,128,512]{2,1,0:T(8,128)(2,1)}, bf16[9,128,512]{2,1,0:T(8,128)(2,1)}, u32[]{:S(2)}, u32[]{:S(2)}) collective-permute-start(bf16[9,128,512]{2,1,0:T(8,128)(2,1)} %get-tuple-element.9), channel_id=1, source_target_pairs={{0,1},{1,0},{2,3},{3,2},{4,5},{5,4},{6,7},{7,6},{8,9},{9,8},{10,11... | collective-permute-start | bytes 3538952 | tf_op jit(solution)/shard_map/ppermute | solution.py:30
  8.5 9.2 %collective-permute-start.2 = (bf16[4,128,512]{2,1,0:T(8,128)(2,1)S(1)}, bf16[4,128,512]{2,1,0:T(8,128)(2,1)S(1)}, u32[]{:S(2)}, u32[]{:S(2)}) collective-permute-start(bf16[4,128,512]{2,1,0:T(8,128)(2,1)S(1)} %slice_select_fusion.4), channel_id=1, source_target_pairs={{0,2},{1,5},{2,0},{3,7},{4,6},{5,1},{6,4},{7,3},{8,10},{9,13},{10,... | collective-permute-start | bytes 1572872 | tf_op jit(solution)/shard_map/ppermute | solution.py:30
  12.0 15.8 %collective-permute-start.19 = (bf16[5,128,512]{2,1,0:T(8,128)(2,1)}, bf16[5,128,512]{2,1,0:T(8,128)(2,1)}, u32[]{:S(2)}, u32[]{:S(2)}) collective-permute-start(bf16[5,128,512]{2,1,0:T(8,128)(2,1)} %slice_select_fusion.2), channel_id=1, source_target_pairs={{0,2},{1,5},{2,0},{3,7},{4,6},{5,1},{6,4},{7,3},{8,10},{9,13},{10,... | collective-permute-start | bytes 1966088 | tf_op jit(solution)/shard_map/ppermute | solution.py:30
  19.8 10.9 %collective-permute-start.3 = (bf16[4,128,512]{2,1,0:T(8,128)(2,1)S(1)}, bf16[4,128,512]{2,1,0:T(8,128)(2,1)S(1)}, u32[]{:S(2)}, u32[]{:S(2)}) collective-permute-start(bf16[4,128,512]{2,1,0:T(8,128)(2,1)S(1)} %fusion.34), channel_id=1, source_target_pairs={{0,4},{1,3},{2,6},{3,1},{4,0},{5,7},{6,2},{7,5},{8,12},{9,11},{10,... | collective-permute-start | bytes 1572872 | tf_op jit(solution)/shard_map/ppermute | solution.py:30
  29.2 17.5 %collective-permute-start.20 = (bf16[5,128,512]{2,1,0:T(8,128)(2,1)S(1)}, bf16[5,128,512]{2,1,0:T(8,128)(2,1)S(1)}, u32[]{:S(2)}, u32[]{:S(2)}) collective-permute-start(bf16[5,128,512]{2,1,0:T(8,128)(2,1)S(1)} %fusion.33), channel_id=1, source_target_pairs={{0,4},{1,3},{2,6},{3,1},{4,0},{5,7},{6,2},{7,5},{8,12},{9,11},{10,... | collective-permute-start | bytes 1966088 | tf_op jit(solution)/shard_map/ppermute | solution.py:30
  30.9 17.1 %collective-permute-start.12 = (bf16[4,128,512]{2,1,0:T(8,128)(2,1)S(1)}, bf16[4,128,512]{2,1,0:T(8,128)(2,1)S(1)}, u32[]{:S(2)}, u32[]{:S(2)}) collective-permute-start(bf16[4,128,512]{2,1,0:T(8,128)(2,1)S(1)} %broadcast_select_fusion.2.refs_0_), channel_id=1, source_target_pairs={{0,2},{1,5},{2,0},{3,7},{4,6},{5,1},{6,4},{7,3},{8,10},{9,13},{10,... | collective-permute-start | bytes 1572872 | tf_op jit(solution)/shard_map/ppermute | solution.py:30
  33.8 28.3 %collective-permute-start.4 = (bf16[7,128,512]{2,1,0:T(8,128)(2,1)S(1)}, bf16[7,128,512]{2,1,0:T(8,128)(2,1)S(1)}, u32[]{:S(2)}, u32[]{:S(2)}) collective-permute-start(bf16[7,128,512]{2,1,0:T(8,128)(2,1)S(1)} %after.3), channel_id=1, source_target_pairs={{0,2},{1,5},{2,0},{3,7},{4,6},{5,1},{6,4},{7,3},{8,10},{9,13},{10,... | collective-permute-start | bytes 2752520 | tf_op jit(solution)/shard_map/ppermute | solution.py:30
  46.8 13.1 %collective-permute-start.21 = (bf16[5,128,512]{2,1,0:T(8,128)(2,1)S(1)}, bf16[5,128,512]{2,1,0:T(8,128)(2,1)S(1)}, u32[]{:S(2)}, u32[]{:S(2)}) collective-permute-start(bf16[5,128,512]{2,1,0:T(8,128)(2,1)S(1)} %broadcast_select_fusion.1.refs_0_), channel_id=1, source_target_pairs={{0,2},{1,5},{2,0},{3,7},{4,6},{5,1},{6,4},{7,3},{8,10},{9,13},{10,... | collective-permute-start | bytes 1966088 | tf_op jit(solution)/shard_map/ppermute | solution.py:30
  48.1 8.3 %collective-permute-start.15 = (bf16[2,2,128,256]{3,2,1,0:T(8,128)(2,1)S(1)}, bf16[2,2,128,256]{3,2,1,0:T(8,128)(2,1)S(1)}, u32[]{:S(2)}, u32[]{:S(2)}) collective-permute-start(bf16[2,2,128,256]{3,2,1,0:T(8,128)(2,1)S(1)} %pad_maximum_fusion.4), channel_id=1, source_target_pairs={{0,8},{8,16},{16,24},{1,9},{9,17},{17,25},{2,10},{10,18},{18,26},{... | collective-permute-start | bytes 786440 | tf_op jit(solution)/shard_map/ppermute | solution.py:12
  52.0 11.5 %collective-permute-start.13 = (bf16[4,128,512]{2,1,0:T(8,128)(2,1)S(1)}, bf16[4,128,512]{2,1,0:T(8,128)(2,1)S(1)}, u32[]{:S(2)}, u32[]{:S(2)}) collective-permute-start(bf16[4,128,512]{2,1,0:T(8,128)(2,1)S(1)} %broadcast_select_fusion.2.refs_0_), channel_id=1, source_target_pairs={{0,1},{1,0},{2,3},{3,2},{4,5},{5,4},{6,7},{7,6},{8,9},{9,8},{10,11... | collective-permute-start | bytes 1572872 | tf_op jit(solution)/shard_map/ppermute | solution.py:30
  52.1 19.1 %collective-permute-start.22 = (bf16[5,128,512]{2,1,0:T(8,128)(2,1)S(1)}, bf16[5,128,512]{2,1,0:T(8,128)(2,1)S(1)}, u32[]{:S(2)}, u32[]{:S(2)}) collective-permute-start(bf16[5,128,512]{2,1,0:T(8,128)(2,1)S(1)} %broadcast_select_fusion.1.refs_0_), channel_id=1, source_target_pairs={{0,1},{1,0},{2,3},{3,2},{4,5},{5,4},{6,7},{7,6},{8,9},{9,8},{10,11... | collective-permute-start | bytes 1966088 | tf_op jit(solution)/shard_map/ppermute | solution.py:30
  56.3 8.8 %collective-permute-start.14 = (bf16[4,128,512]{2,1,0:T(8,128)(2,1)S(1)}, bf16[4,128,512]{2,1,0:T(8,128)(2,1)S(1)}, u32[]{:S(2)}, u32[]{:S(2)}) collective-permute-start(bf16[4,128,512]{2,1,0:T(8,128)(2,1)S(1)} %collective-permute-done.12.refs_1_), channel_id=1, source_target_pairs={{0,1},{1,0},{2,3},{3,2},{4,5},{5,4},{6,7},{7,6},{8,9},{9,8},{10,11... | collective-permute-start | bytes 1572872 | tf_op jit(solution)/shard_map/ppermute | solution.py:30
  59.8 10.6 %collective-permute-start.16 = (bf16[2,2,128,256]{3,2,1,0:T(8,128)(2,1)S(1)}, bf16[2,2,128,256]{3,2,1,0:T(8,128)(2,1)S(1)}, u32[]{:S(2)}, u32[]{:S(2)}) collective-permute-start(bf16[2,2,128,256]{3,2,1,0:T(8,128)(2,1)S(1)} %collective-permute-done.15), channel_id=1, source_target_pairs={{0,1},{1,0},{2,3},{3,2},{4,5},{5,4},{6,7},{7,6},{8,9},{9,8},{10,11... | collective-permute-start | bytes 786440 | tf_op jit(solution)/shard_map/ppermute | solution.py:30
  62.1 9.2 %collective-permute-start.23 = (bf16[5,128,512]{2,1,0:T(8,128)(2,1)S(1)}, bf16[5,128,512]{2,1,0:T(8,128)(2,1)S(1)}, u32[]{:S(2)}, u32[]{:S(2)}) collective-permute-start(bf16[5,128,512]{2,1,0:T(8,128)(2,1)S(1)} %collective-permute-done.21.refs_1_), channel_id=1, source_target_pairs={{0,1},{1,0},{2,3},{3,2},{4,5},{5,4},{6,7},{7,6},{8,9},{9,8},{10,11... | collective-permute-start | bytes 1966088 | tf_op jit(solution)/shard_map/ppermute | solution.py:30
  63.5 13.5 %collective-permute-start.5 = (bf16[7,128,512]{2,1,0:T(8,128)(2,1)S(1)}, bf16[7,128,512]{2,1,0:T(8,128)(2,1)S(1)}, u32[]{:S(2)}, u32[]{:S(2)}) collective-permute-start(bf16[7,128,512]{2,1,0:T(8,128)(2,1)S(1)} %fusion.32), channel_id=1, source_target_pairs={{0,4},{1,3},{2,6},{3,1},{4,0},{5,7},{6,2},{7,5},{8,12},{9,11},{10,... | collective-permute-start | bytes 2752520 | tf_op jit(solution)/shard_map/ppermute | solution.py:30
  66.9 15.8 %collective-permute-start.17 = (bf16[256,1024]{1,0:T(8,128)(2,1)S(1)}, bf16[256,1024]{1,0:T(8,128)(2,1)S(1)}, u32[]{:S(2)}, u32[]{:S(2)}) collective-permute-start(bf16[256,1024]{1,0:T(8,128)(2,1)S(1)} %get-tuple-element.27), channel_id=1, source_target_pairs={{8,16},{16,8},{9,17},{17,9},{10,18},{18,10},{11,19},{19,11},{12,20... | collective-permute-start | bytes 1572872 | tf_op jit(solution)/shard_map/ppermute | solution.py:21
  70.5 14.0 %collective-permute-start.18 = (bf16[256,1024]{1,0:T(8,128)(2,1)S(1)}, bf16[256,1024]{1,0:T(8,128)(2,1)S(1)}, u32[]{:S(2)}, u32[]{:S(2)}) collective-permute-start(bf16[256,1024]{1,0:T(8,128)(2,1)S(1)} %get-tuple-element.28), channel_id=1, source_target_pairs={{0,8},{16,24},{8,0},{24,16},{1,9},{17,25},{9,1},{25,17},{2,10},{18... | collective-permute-start | bytes 1572872 | tf_op jit(solution)/shard_map/ppermute | solution.py:21
  77.1 7.9 %collective-permute-start.9 = (bf16[2,128,512]{2,1,0:T(8,128)(2,1)S(1)}, bf16[2,128,512]{2,1,0:T(8,128)(2,1)S(1)}, u32[]{:S(2)}, u32[]{:S(2)}) collective-permute-start(bf16[2,128,512]{2,1,0:T(8,128)(2,1)S(1)} %slice.255.refs_0_), channel_id=1, source_target_pairs={{0,2},{1,5},{2,0},{3,7},{4,6},{5,1},{6,4},{7,3},{8,10},{9,13},{10,... | collective-permute-start | bytes 786440 | tf_op jit(solution)/shard_map/ppermute | solution.py:30
  86.1 10.7 %collective-permute-start.6 = (bf16[5,128,512]{2,1,0:T(8,128)(2,1)S(1)}, bf16[5,128,512]{2,1,0:T(8,128)(2,1)S(1)}, u32[]{:S(2)}, u32[]{:S(2)}) collective-permute-start(bf16[5,128,512]{2,1,0:T(8,128)(2,1)S(1)} %slice.254.refs_0_), channel_id=1, source_target_pairs={{0,2},{1,5},{2,0},{3,7},{4,6},{5,1},{6,4},{7,3},{8,10},{9,13},{10,... | collective-permute-start | bytes 1966088 | tf_op jit(solution)/shard_map/ppermute | solution.py:30
  86.7 18.9 %collective-permute-start.7 = (bf16[5,128,512]{2,1,0:T(8,128)(2,1)S(1)}, bf16[5,128,512]{2,1,0:T(8,128)(2,1)S(1)}, u32[]{:S(2)}, u32[]{:S(2)}) collective-permute-start(bf16[5,128,512]{2,1,0:T(8,128)(2,1)S(1)} %slice.254.refs_0_), channel_id=1, source_target_pairs={{0,1},{1,0},{2,3},{3,2},{4,5},{5,4},{6,7},{7,6},{8,9},{9,8},{10,11... | collective-permute-start | bytes 1966088 | tf_op jit(solution)/shard_map/ppermute | solution.py:30
  89.0 13.9 %collective-permute-start.25 = (bf16[256,1024]{1,0:T(8,128)(2,1)S(1)}, bf16[256,1024]{1,0:T(8,128)(2,1)S(1)}, u32[]{:S(2)}, u32[]{:S(2)}) collective-permute-start(bf16[256,1024]{1,0:T(8,128)(2,1)S(1)} %get-tuple-element.21), channel_id=1, source_target_pairs={{0,8},{16,24},{8,0},{24,16},{1,9},{17,25},{9,1},{25,17},{2,10},{18... | collective-permute-start | bytes 1572872 | tf_op jit(solution)/shard_map/ppermute | solution.py:21
  89.7 15.9 %collective-permute-start.24 = (bf16[256,1024]{1,0:T(8,128)(2,1)S(1)}, bf16[256,1024]{1,0:T(8,128)(2,1)S(1)}, u32[]{:S(2)}, u32[]{:S(2)}) collective-permute-start(bf16[256,1024]{1,0:T(8,128)(2,1)S(1)} %get-tuple-element.22), channel_id=1, source_target_pairs={{8,16},{16,8},{9,17},{17,9},{10,18},{18,10},{11,19},{19,11},{12,20... | collective-permute-start | bytes 1572872 | tf_op jit(solution)/shard_map/ppermute | solution.py:21
  96.7 8.9 %collective-permute-start.8 = (bf16[5,128,512]{2,1,0:T(8,128)(2,1)S(1)}, bf16[5,128,512]{2,1,0:T(8,128)(2,1)S(1)}, u32[]{:S(2)}, u32[]{:S(2)}) collective-permute-start(bf16[5,128,512]{2,1,0:T(8,128)(2,1)S(1)} %collective-permute-done.6.refs_1_), channel_id=1, source_target_pairs={{0,1},{1,0},{2,3},{3,2},{4,5},{5,4},{6,7},{7,6},{8,9},{9,8},{10,11... | collective-permute-start | bytes 1966088 | tf_op jit(solution)/shard_map/ppermute | solution.py:30
  (9 other events, 36.6 us)

commit v15 on v5

--- a/solution.py
+++ b/solution.py
@@ -208,6 +208,10 @@
             hold = after(hold, *first)
         return hold, flip(hold, self.cut)
 
+    def last_two(self, state, count):
+        hold = self.keep(state, self.others[-1])
+        return [(part, flip(part, self.cut)) for part in (hold[:count], hold[count:])]
+
     def join(self, hold, got):
         return place(self.cut, hold, got, flip(hold, (0, 0)), flip(got, (0, 0)))
 
@@ -240,25 +244,24 @@
     middle_one, middle_two = list(range(1, wins - 1)), list(range(wins, crossing))
     order = [crossing, crossing, 0, wins - 1] + middle_one + middle_two
     spread = Spread(slot, owners[:, row_block], order)
-    cut_one, cut_two = 4 + len(middle_one), len(order)
-
-    heads, tails = [], []
+    streams = []
     for r in range(rounds):
         across = ([r + 1] if r + 1 < rounds else []) + ([r] if r == 0 else [])
+        first = 2 - len(across)
         if r == 0:
-            head = spread.begin(across + [r, r], slice(2 - len(across), 4))
-            tail = spread.begin([r] * (cut_two - 4), slice(4, cut_two))
+            streams.append(spread.middle(spread.begin(across + [r, r], slice(first, 4))))
+            streams.append(spread.middle(spread.begin([r] * (len(order) - 4), slice(4, len(order)))))
         else:
-            head = spread.begin(across + [r] * wins, slice(2 - len(across), cut_one), head[2])
-            tail = spread.begin([r] * (cut_two - cut_one), slice(cut_one, cut_two), tail[2])
-        head, tail = spread.middle(head), spread.middle(tail)
-        heads.append(spread.last(head))
-        tails.append(spread.last(tail))
+            begun = spread.begin(across + [r] * crossing, slice(first, len(order)), streams[r - 1][2])
+            streams.append(spread.middle(begun))
+    pairs = [spread.last(stream) for stream in streams[:2]]
+    for r in range(1, rounds):
+        pairs += spread.last_two(streams[r + 1], 3 if r + 1 < rounds else 2)
 
     matrix = slab
     crosses, above_crosses = {}, {}
     for r in range(rounds):
-        head, tail = heads[r], tails[r]
+        head, tail = pairs[2 * r], pairs[2 * r + 1]
         edges = spread.join(*head)
         across = ([r + 1] if r + 1 < rounds else []) + ([r] if r == 0 else [])
         if across:
@@ -268,15 +271,14 @@
                 crosses[q], above_crosses[q] = edges[k], from_above[k]
             edges = edges[n:]
         prev, cross = above_crosses[r], crosses[r]
-        head_rows = apply(edges[0], matrix[:window])
-        tail_rows = apply(edges[1], matrix[local_rows - window :])
+        outer = apply_many(
+            edges[:2], jnp.stack([matrix[:window], matrix[local_rows - window :]])
+        )
+        head_rows, tail_rows = outer[0], outer[1]
         begin, end = head_rows[:border], tail_rows[border:]
         above, below = swap_rows(begin, end)
         rest = spread.join(*tail)
-        if r == 0:
-            ones, twos = rest[: wins - 2], rest[wins - 2 :]
-        else:
-            ones, twos = edges[2:], rest
+        ones, twos = rest[: wins - 2], rest[wins - 2 :]
         mid = apply_many(
             ones,
             matrix[window : local_rows - window].reshape(wins - 2, window, local_cols),

time: 118 us -> 115 us (0.975)
  waiting for transfers between devices: 51.1 us -> 47.6 us
    ppermute x23 -> x21, waiting for transfers between devices: 36.8 us -> 29.6 us  [flip(): lax.ppermute(value, 'cols', [(d, d ^ 1 << bits[d & 1]) for d in range(cou...]
    dot_general x4 -> x6, matrix products: 7.04 us -> 10.1 us  [apply_many(): jnp.einsum('nab,nac->nbc', q, x, preferred_element_type=jnp.float32)]
    dot_general x8 -> x4, matrix products: 4.8 us -> 1.84 us  [apply(): lax.dot_general(q, x, (((0,), (0,)), ((), ())), preferred_element_type=jn...]
    ppermute x1, waiting for transfers between devices: 1.62 us -> 4.01 us  [shifted(): lax.ppermute(value, axis, [(source, source + steps) for source in range(i...]
    ppermute x4, waiting for transfers between devices: 12.7 us -> 14 us  [swap(): return lax.ppermute(value, 'rows', pairs + [(b, a) for a, b in pairs])]
    select_n x11 -> x9, other arithmetic: 9.52 us -> 8.85 us  [choose(): return jnp.where(mask, yes, no)]
    unnamed x8 -> x10, local copies, waits for them, and re-layouts: 3.52 us -> 3.01 us
    ppermute x23 -> x21, starting transfers between devices: 16.6 us -> 16.7 us  [flip(): lax.ppermute(value, 'cols', [(d, d ^ 1 << bits[d & 1]) for d in range(cou...]
  transfers between devices with their start and end apart: 28 -> 26, of which waited for: 12 -> 11; matrix products, arithmetic and copies ran while one was open for 17% -> 17% of each run, Pallas kernels for 3% -> 3%
where the time goes in v15:
time: 115 us; the launch traced here: 113 us
  waiting for transfers between devices  47.6 us (41%)
  starting transfers between devices  26.4 us (23%)
  other arithmetic  12.4 us (11%)
  matrix products  12 us (10%)
  local copies, waits for them, and re-layouts  5.96 us (5%)
  between operations  4.2 us (4%)
  Pallas kernels  4.14 us (4%)
    ppermute x21, waiting for transfers between devices, flip(): lax.ppermute(value, 'cols', [(d, d ^ 1 << bits[d & 1]) for d in range(cou...  29.6 us
    ppermute x21, starting transfers between devices, flip(): lax.ppermute(value, 'cols', [(d, d ^ 1 << bits[d & 1]) for d in range(cou...  16.7 us
    ppermute x4, waiting for transfers between devices, swap(): return lax.ppermute(value, 'rows', pairs + [(b, a) for a, b in pairs])  14 us
    dot_general x6, matrix products, apply_many(): jnp.einsum('nab,nac->nbc', q, x, preferred_element_type=jnp.float32)  10.1 us
    select_n x9, other arithmetic, choose(): return jnp.where(mask, yes, no)  8.85 us
    ppermute x4, starting transfers between devices, swap(): return lax.ppermute(value, 'rows', pairs + [(b, a) for a, b in pairs])  6.24 us
    ppermute x1, waiting for transfers between devices, shifted(): lax.ppermute(value, axis, [(source, source + steps) for source in range(i...  4.01 us
    ppermute x1, starting transfers between devices, shifted(): lax.ppermute(value, axis, [(source, source + steps) for source in range(i...  3.48 us
  transfers between devices with their start and end apart: 26, of which 11 were waited for; matrix products, arithmetic and copies ran while one was open for 17% of the time, Pallas kernels for 3%

profile of v15, /device:TPU:8, one launch (start us, length us, event | category | flops | bytes accessed | tf_op | source)
XLA Modules:
  0.0 112.8 jit_solution(6764784264737977713)
XLA Ops:
  0.0 2.2 %copy-done.2 = bf16[1,4096,512]{2,1,0:T(8,128)(2,1)S(1)} copy-done((bf16[1,4096,512]{2,1,0:T(8,128)(2,1)S(1)}, bf16[1,4096,512]{2,1,0:T(8,128)(2,1)}, u32[]{:S(2)}) %copy-start.2) | copy-done | bytes 4194328
  3.1 1.9 %cut_slot.2 = (bf16[9,128,512]{2,1,0:T(8,128)(2,1)S(1)}, bf16[9,128,512]{2,1,0:T(8,128)(2,1)}, bf16[9,128,512]{2,1,0:T(8,128)(2,1)S(1)}) custom-call(bf16[8,2,2,128,512]{4,3,2,1,0:T(8,128)(2,1)S(1)} %bitcast.84), custom_call_target="tpu_custom_call" | custom-call | bytes 6291456 | tf_op jit(solution)/shard_map/cut_slot/pallas_call | solution.py:105
  8.6 1.6 %collective-permute-start.2 = (bf16[4,128,512]{2,1,0:T(8,128)(2,1)S(1)}, bf16[4,128,512]{2,1,0:T(8,128)(2,1)S(1)}, u32[]{:S(2)}, u32[]{:S(2)}) collective-permute-start(bf16[4,128,512]{2,1,0:T(8,128)(2,1)S(1)} %slice_select_fusion.4), channel_id=1, source_target_pairs={{0,2},{1,5},{2,0},{3,7},{4,6},{5,1},{6,4},{7,3},{8,10},{9,13},{10,... | collective-permute-start | bytes 1572872 | tf_op jit(solution)/shard_map/ppermute | solution.py:30
  10.2 2.0 %slice_select_fusion.2 = bf16[5,128,512]{2,1,0:T(8,128)(2,1)} fusion(bf16[9,128,512]{2,1,0:T(8,128)(2,1)} %collective-permute-done.1, bf16[9,128,512]{2,1,0:T(8,128)(2,1)S(1)} %get-tuple-element.10, pred[]{:T(512)S(6)} %eq.26), kind=kLoop, calls=%fused_computation.47 | loop fusion | flops 327680 | bytes 1966081 | tf_op jit(solution)/shard_map/jit(_where)/select_n | solution.py:178
  14.0 3.9 %collective-permute-done.2 = bf16[4,128,512]{2,1,0:T(8,128)(2,1)S(1)} collective-permute-done((bf16[4,128,512]{2,1,0:T(8,128)(2,1)S(1)}, bf16[4,128,512]{2,1,0:T(8,128)(2,1)S(1)}, u32[]{:S(2)}, u32[]{:S(2)}) %collective-permute-start.2) | collective-permute-done | bytes 524320 | tf_op jit(solution)/shard_map/ppermute | solution.py:30
  20.0 1.6 %collective-permute-start.3 = (bf16[4,128,512]{2,1,0:T(8,128)(2,1)S(1)}, bf16[4,128,512]{2,1,0:T(8,128)(2,1)S(1)}, u32[]{:S(2)}, u32[]{:S(2)}) collective-permute-start(bf16[4,128,512]{2,1,0:T(8,128)(2,1)S(1)} %fusion.34), channel_id=1, source_target_pairs={{0,4},{1,3},{2,6},{3,1},{4,0},{5,7},{6,2},{7,5},{8,12},{9,11},{10,... | collective-permute-start | bytes 1572872 | tf_op jit(solution)/shard_map/ppermute | solution.py:30
  22.8 5.1 %collective-permute-done.16 = bf16[5,128,512]{2,1,0:T(8,128)(2,1)} collective-permute-done((bf16[5,128,512]{2,1,0:T(8,128)(2,1)}, bf16[5,128,512]{2,1,0:T(8,128)(2,1)}, u32[]{:S(2)}, u32[]{:S(2)}) %collective-permute-start.16) | collective-permute-done | bytes 655392 | tf_op jit(solution)/shard_map/ppermute | solution.py:30
  29.3 1.6 %collective-permute-start.17 = (bf16[5,128,512]{2,1,0:T(8,128)(2,1)S(1)}, bf16[5,128,512]{2,1,0:T(8,128)(2,1)S(1)}, u32[]{:S(2)}, u32[]{:S(2)}) collective-permute-start(bf16[5,128,512]{2,1,0:T(8,128)(2,1)S(1)} %fusion.33), channel_id=1, source_target_pairs={{0,4},{1,3},{2,6},{3,1},{4,0},{5,7},{6,2},{7,5},{8,12},{9,11},{10,... | collective-permute-start | bytes 1966088 | tf_op jit(solution)/shard_map/ppermute | solution.py:30
  34.7 12.1 %collective-permute-done.17 = bf16[5,128,512]{2,1,0:T(8,128)(2,1)S(1)} collective-permute-done((bf16[5,128,512]{2,1,0:T(8,128)(2,1)S(1)}, bf16[5,128,512]{2,1,0:T(8,128)(2,1)S(1)}, u32[]{:S(2)}, u32[]{:S(2)}) %collective-permute-start.17) | collective-permute-done | bytes 655392 | tf_op jit(solution)/shard_map/ppermute | solution.py:30
  48.2 3.5 %collective-permute-start.12 = (bf16[2,2,128,256]{3,2,1,0:T(8,128)(2,1)S(1)}, bf16[2,2,128,256]{3,2,1,0:T(8,128)(2,1)S(1)}, u32[]{:S(2)}, u32[]{:S(2)}) collective-permute-start(bf16[2,2,128,256]{3,2,1,0:T(8,128)(2,1)S(1)} %pad_maximum_fusion.5), channel_id=1, source_target_pairs={{0,8},{8,16},{16,24},{1,9},{9,17},{17,25},{2,10},{10,18},{18,26},{... | collective-permute-start | bytes 786440 | tf_op jit(solution)/shard_map/ppermute | solution.py:12
  52.5 4.0 %collective-permute-done.12 = bf16[2,2,128,256]{3,2,1,0:T(8,128)(2,1)S(1)} collective-permute-done((bf16[2,2,128,256]{3,2,1,0:T(8,128)(2,1)S(1)}, bf16[2,2,128,256]{3,2,1,0:T(8,128)(2,1)S(1)}, u32[]{:S(2)}, u32[]{:S(2)}) %collective-permute-start.12) | collective-permute-done | bytes 262176 | tf_op jit(solution)/shard_map/ppermute | solution.py:12
  56.5 3.5 %collective-permute-done.18.refs_1_ = bf16[5,128,512]{2,1,0:T(8,128)(2,1)S(1)} collective-permute-done((bf16[5,128,512]{2,1,0:T(8,128)(2,1)S(1)}, bf16[5,128,512]{2,1,0:T(8,128)(2,1)S(1)}, u32[]{:S(2)}, u32[]{:S(2)}) %collective-permute-start.18) | collective-permute-done | bytes 655392 | tf_op jit(solution)/shard_map/ppermute | solution.py:30
  60.0 2.3 %collective-permute-start.13 = (bf16[2,2,128,256]{3,2,1,0:T(8,128)(2,1)S(1)}, bf16[2,2,128,256]{3,2,1,0:T(8,128)(2,1)S(1)}, u32[]{:S(2)}, u32[]{:S(2)}) collective-permute-start(bf16[2,2,128,256]{3,2,1,0:T(8,128)(2,1)S(1)} %collective-permute-done.12), channel_id=1, source_target_pairs={{0,1},{1,0},{2,3},{3,2},{4,5},{5,4},{6,7},{7,6},{8,9},{9,8},{10,11... | collective-permute-start | bytes 786440 | tf_op jit(solution)/shard_map/ppermute | solution.py:30
  63.7 1.6 %collective-permute-start.5 = (bf16[7,128,512]{2,1,0:T(8,128)(2,1)S(1)}, bf16[7,128,512]{2,1,0:T(8,128)(2,1)S(1)}, u32[]{:S(2)}, u32[]{:S(2)}) collective-permute-start(bf16[7,128,512]{2,1,0:T(8,128)(2,1)S(1)} %fusion.32), channel_id=1, source_target_pairs={{0,4},{1,3},{2,6},{3,1},{4,0},{5,7},{6,2},{7,5},{8,12},{9,11},{10,... | collective-permute-start | bytes 2752520 | tf_op jit(solution)/shard_map/ppermute | solution.py:30
  67.1 3.5 %collective-permute-start.14 = (bf16[256,1024]{1,0:T(8,128)(2,1)S(1)}, bf16[256,1024]{1,0:T(8,128)(2,1)S(1)}, u32[]{:S(2)}, u32[]{:S(2)}) collective-permute-start(bf16[256,1024]{1,0:T(8,128)(2,1)S(1)} %get-tuple-element.27), channel_id=1, source_target_pairs={{8,16},{16,8},{9,17},{17,9},{10,18},{18,10},{11,19},{19,11},{12,20... | collective-permute-start | bytes 1572872 | tf_op jit(solution)/shard_map/ppermute | solution.py:21
  73.0 1.5 %convolution_convert_fusion.3 = bf16[2,512,1024]{2,1,0:T(8,128)(2,1)S(1)} fusion(bf16[5,512,512]{2,1,0:T(8,128)(2,1)S(1)} %place.8, bf16[2,512,1024]{2,1,0:T(8,128)(2,1)S(1)} %bitcast.87), kind=kOutput, calls=%fused_computation.14 | convolution fusion | flops 1074790400 | bytes 6815744 | tf_op jit(solution)/shard_map/nab,nac->nbc/dot_general | solution.py:230
  75.0 2.1 %convolution_convert_fusion.1 = bf16[3,512,1024]{2,1,0:T(8,128)(2,1)S(1)} fusion(bf16[5,512,512]{2,1,0:T(8,128)(2,1)S(1)} %place.8, bf16[3,512,1024]{2,1,0:T(8,128)(2,1)S(1)} %bitcast.88), kind=kOutput, calls=%fused_computation.4 | convolution fusion | flops 1612185600 | bytes 8912896 | tf_op jit(solution)/shard_map/nab,nac->nbc/dot_general | solution.py:230
  78.6 4.2 %collective-permute-done.14 = bf16[256,1024]{1,0:T(8,128)(2,1)S(1)} collective-permute-done((bf16[256,1024]{1,0:T(8,128)(2,1)S(1)}, bf16[256,1024]{1,0:T(8,128)(2,1)S(1)}, u32[]{:S(2)}, u32[]{:S(2)}) %collective-permute-start.14) | collective-permute-done | bytes 524320 | tf_op jit(solution)/shard_map/ppermute | solution.py:21
  88.4 2.6 %collective-permute-start.21 = (bf16[256,1024]{1,0:T(8,128)(2,1)S(1)}, bf16[256,1024]{1,0:T(8,128)(2,1)S(1)}, u32[]{:S(2)}, u32[]{:S(2)}) collective-permute-start(bf16[256,1024]{1,0:T(8,128)(2,1)S(1)} %get-tuple-element.21), channel_id=1, source_target_pairs={{8,16},{16,8},{9,17},{17,9},{10,18},{18,10},{11,19},{19,11},{12,20... | collective-permute-start | bytes 1572872 | tf_op jit(solution)/shard_map/ppermute | solution.py:21
  91.8 4.9 %collective-permute-done.23.refs_1_ = bf16[5,128,512]{2,1,0:T(8,128)(2,1)S(1)} collective-permute-done((bf16[5,128,512]{2,1,0:T(8,128)(2,1)S(1)}, bf16[5,128,512]{2,1,0:T(8,128)(2,1)S(1)}, u32[]{:S(2)}, u32[]{:S(2)}) %collective-permute-start.23) | collective-permute-done | bytes 655392 | tf_op jit(solution)/shard_map/ppermute | solution.py:30
  96.7 8.0 %collective-permute-done.21 = bf16[256,1024]{1,0:T(8,128)(2,1)S(1)} collective-permute-done((bf16[256,1024]{1,0:T(8,128)(2,1)S(1)}, bf16[256,1024]{1,0:T(8,128)(2,1)S(1)}, u32[]{:S(2)}, u32[]{:S(2)}) %collective-permute-start.21) | collective-permute-done | bytes 524320 | tf_op jit(solution)/shard_map/ppermute | solution.py:21
  106.4 1.5 %convolution_convert_fusion.2 = bf16[2,512,1024]{2,1,0:T(8,128)(2,1)S(1)} fusion(bf16[5,512,512]{2,1,0:T(8,128)(2,1)S(1)} %place.9, bf16[2,512,1024]{2,1,0:T(8,128)(2,1)S(1)} %bitcast.93), kind=kOutput, calls=%fused_computation.13 | convolution fusion | flops 1074790400 | bytes 6815744 | tf_op jit(solution)/shard_map/nab,nac->nbc/dot_general | solution.py:230
  108.3 2.1 %convolution_convert_fusion = bf16[3,512,1024]{2,1,0:T(8,128)(2,1)S(1)} fusion(bf16[5,512,512]{2,1,0:T(8,128)(2,1)S(1)} %place.9, bf16[3,512,1024]{2,1,0:T(8,128)(2,1)S(1)} %bitcast.89), kind=kOutput, calls=%fused_computation.3 | convolution fusion | flops 1612185600 | bytes 8912896 | tf_op jit(solution)/shard_map/nab,nac->nbc/dot_general | solution.py:230
  110.5 2.3 %pad_maximum_fusion = bf16[2048,1024]{1,0:T(8,128)(2,1)} fusion(bf16[256,1024]{1,0:T(8,128)(2,1)S(1)} %fusion.17, bf16[1536,1024]{1,0:T(8,128)(2,1)S(1)} %bitcast.90, bf16[256,1024]{1,0:T(8,128)(2,1)S(1)} %fusion.16), kind=kLoop, calls=%fused_computation | loop fusion | flops 12582912 | bytes 8388608 | tf_op jit(solution)/shard_map/concatenate | solution.py:294
  (92 shorter events, 29.1 us)
Async XLA Ops:
  3.0 4.5 %collective-permute-start.1 = (bf16[9,128,512]{2,1,0:T(8,128)(2,1)S(1)}, bf16[9,128,512]{2,1,0:T(8,128)(2,1)}, u32[]{:S(2)}, u32[]{:S(2)}) collective-permute-start(bf16[9,128,512]{2,1,0:T(8,128)(2,1)S(1)} %cut_slot.3), channel_id=1, source_target_pairs={{0,1},{1,0},{2,3},{3,2},{4,5},{5,4},{6,7},{7,6},{8,9},{9,8},{10,11... | collective-permute-start | bytes 3538952 | tf_op jit(solution)/shard_map/ppermute | solution.py:30
  5.0 8.9 %collective-permute-start = (bf16[9,128,512]{2,1,0:T(8,128)(2,1)}, bf16[9,128,512]{2,1,0:T(8,128)(2,1)}, u32[]{:S(2)}, u32[]{:S(2)}) collective-permute-start(bf16[9,128,512]{2,1,0:T(8,128)(2,1)} %get-tuple-element.9), channel_id=1, source_target_pairs={{0,1},{1,0},{2,3},{3,2},{4,5},{5,4},{6,7},{7,6},{8,9},{9,8},{10,11... | collective-permute-start | bytes 3538952 | tf_op jit(solution)/shard_map/ppermute | solution.py:30
  8.6 9.2 %collective-permute-start.2 = (bf16[4,128,512]{2,1,0:T(8,128)(2,1)S(1)}, bf16[4,128,512]{2,1,0:T(8,128)(2,1)S(1)}, u32[]{:S(2)}, u32[]{:S(2)}) collective-permute-start(bf16[4,128,512]{2,1,0:T(8,128)(2,1)S(1)} %slice_select_fusion.4), channel_id=1, source_target_pairs={{0,2},{1,5},{2,0},{3,7},{4,6},{5,1},{6,4},{7,3},{8,10},{9,13},{10,... | collective-permute-start | bytes 1572872 | tf_op jit(solution)/shard_map/ppermute | solution.py:30
  12.2 15.8 %collective-permute-start.16 = (bf16[5,128,512]{2,1,0:T(8,128)(2,1)}, bf16[5,128,512]{2,1,0:T(8,128)(2,1)}, u32[]{:S(2)}, u32[]{:S(2)}) collective-permute-start(bf16[5,128,512]{2,1,0:T(8,128)(2,1)} %slice_select_fusion.2), channel_id=1, source_target_pairs={{0,2},{1,5},{2,0},{3,7},{4,6},{5,1},{6,4},{7,3},{8,10},{9,13},{10,... | collective-permute-start | bytes 1966088 | tf_op jit(solution)/shard_map/ppermute | solution.py:30
  20.0 10.9 %collective-permute-start.3 = (bf16[4,128,512]{2,1,0:T(8,128)(2,1)S(1)}, bf16[4,128,512]{2,1,0:T(8,128)(2,1)S(1)}, u32[]{:S(2)}, u32[]{:S(2)}) collective-permute-start(bf16[4,128,512]{2,1,0:T(8,128)(2,1)S(1)} %fusion.34), channel_id=1, source_target_pairs={{0,4},{1,3},{2,6},{3,1},{4,0},{5,7},{6,2},{7,5},{8,12},{9,11},{10,... | collective-permute-start | bytes 1572872 | tf_op jit(solution)/shard_map/ppermute | solution.py:30
  29.3 17.5 %collective-permute-start.17 = (bf16[5,128,512]{2,1,0:T(8,128)(2,1)S(1)}, bf16[5,128,512]{2,1,0:T(8,128)(2,1)S(1)}, u32[]{:S(2)}, u32[]{:S(2)}) collective-permute-start(bf16[5,128,512]{2,1,0:T(8,128)(2,1)S(1)} %fusion.33), channel_id=1, source_target_pairs={{0,4},{1,3},{2,6},{3,1},{4,0},{5,7},{6,2},{7,5},{8,12},{9,11},{10,... | collective-permute-start | bytes 1966088 | tf_op jit(solution)/shard_map/ppermute | solution.py:30
  31.0 17.1 %collective-permute-start.9 = (bf16[4,128,512]{2,1,0:T(8,128)(2,1)S(1)}, bf16[4,128,512]{2,1,0:T(8,128)(2,1)S(1)}, u32[]{:S(2)}, u32[]{:S(2)}) collective-permute-start(bf16[4,128,512]{2,1,0:T(8,128)(2,1)S(1)} %broadcast_select_fusion.2.refs_0_), channel_id=1, source_target_pairs={{0,2},{1,5},{2,0},{3,7},{4,6},{5,1},{6,4},{7,3},{8,10},{9,13},{10,... | collective-permute-start | bytes 1572872 | tf_op jit(solution)/shard_map/ppermute | solution.py:30
  33.9 28.3 %collective-permute-start.4 = (bf16[7,128,512]{2,1,0:T(8,128)(2,1)S(1)}, bf16[7,128,512]{2,1,0:T(8,128)(2,1)S(1)}, u32[]{:S(2)}, u32[]{:S(2)}) collective-permute-start(bf16[7,128,512]{2,1,0:T(8,128)(2,1)S(1)} %after.1), channel_id=1, source_target_pairs={{0,2},{1,5},{2,0},{3,7},{4,6},{5,1},{6,4},{7,3},{8,10},{9,13},{10,... | collective-permute-start | bytes 2752520 | tf_op jit(solution)/shard_map/ppermute | solution.py:30
  46.9 13.1 %collective-permute-start.18 = (bf16[5,128,512]{2,1,0:T(8,128)(2,1)S(1)}, bf16[5,128,512]{2,1,0:T(8,128)(2,1)S(1)}, u32[]{:S(2)}, u32[]{:S(2)}) collective-permute-start(bf16[5,128,512]{2,1,0:T(8,128)(2,1)S(1)} %broadcast_select_fusion.1.refs_0_), channel_id=1, source_target_pairs={{0,2},{1,5},{2,0},{3,7},{4,6},{5,1},{6,4},{7,3},{8,10},{9,13},{10,... | collective-permute-start | bytes 1966088 | tf_op jit(solution)/shard_map/ppermute | solution.py:30
  48.2 8.3 %collective-permute-start.12 = (bf16[2,2,128,256]{3,2,1,0:T(8,128)(2,1)S(1)}, bf16[2,2,128,256]{3,2,1,0:T(8,128)(2,1)S(1)}, u32[]{:S(2)}, u32[]{:S(2)}) collective-permute-start(bf16[2,2,128,256]{3,2,1,0:T(8,128)(2,1)S(1)} %pad_maximum_fusion.5), channel_id=1, source_target_pairs={{0,8},{8,16},{16,24},{1,9},{9,17},{17,25},{2,10},{10,18},{18,26},{... | collective-permute-start | bytes 786440 | tf_op jit(solution)/shard_map/ppermute | solution.py:12
  51.9 11.8 %collective-permute-start.10 = (bf16[4,128,512]{2,1,0:T(8,128)(2,1)S(1)}, bf16[4,128,512]{2,1,0:T(8,128)(2,1)S(1)}, u32[]{:S(2)}, u32[]{:S(2)}) collective-permute-start(bf16[4,128,512]{2,1,0:T(8,128)(2,1)S(1)} %broadcast_select_fusion.2.refs_0_), channel_id=1, source_target_pairs={{0,1},{1,0},{2,3},{3,2},{4,5},{5,4},{6,7},{7,6},{8,9},{9,8},{10,11... | collective-permute-start | bytes 1572872 | tf_op jit(solution)/shard_map/ppermute | solution.py:30
  52.0 19.4 %collective-permute-start.19 = (bf16[5,128,512]{2,1,0:T(8,128)(2,1)S(1)}, bf16[5,128,512]{2,1,0:T(8,128)(2,1)S(1)}, u32[]{:S(2)}, u32[]{:S(2)}) collective-permute-start(bf16[5,128,512]{2,1,0:T(8,128)(2,1)S(1)} %broadcast_select_fusion.1.refs_0_), channel_id=1, source_target_pairs={{0,1},{1,0},{2,3},{3,2},{4,5},{5,4},{6,7},{7,6},{8,9},{9,8},{10,11... | collective-permute-start | bytes 1966088 | tf_op jit(solution)/shard_map/ppermute | solution.py:30
  56.5 8.8 %collective-permute-start.11 = (bf16[4,128,512]{2,1,0:T(8,128)(2,1)S(1)}, bf16[4,128,512]{2,1,0:T(8,128)(2,1)S(1)}, u32[]{:S(2)}, u32[]{:S(2)}) collective-permute-start(bf16[4,128,512]{2,1,0:T(8,128)(2,1)S(1)} %collective-permute-done.9.refs_1_), channel_id=1, source_target_pairs={{0,1},{1,0},{2,3},{3,2},{4,5},{5,4},{6,7},{7,6},{8,9},{9,8},{10,11... | collective-permute-start | bytes 1572872 | tf_op jit(solution)/shard_map/ppermute | solution.py:30
  60.0 10.6 %collective-permute-start.13 = (bf16[2,2,128,256]{3,2,1,0:T(8,128)(2,1)S(1)}, bf16[2,2,128,256]{3,2,1,0:T(8,128)(2,1)S(1)}, u32[]{:S(2)}, u32[]{:S(2)}) collective-permute-start(bf16[2,2,128,256]{3,2,1,0:T(8,128)(2,1)S(1)} %collective-permute-done.12), channel_id=1, source_target_pairs={{0,1},{1,0},{2,3},{3,2},{4,5},{5,4},{6,7},{7,6},{8,9},{9,8},{10,11... | collective-permute-start | bytes 786440 | tf_op jit(solution)/shard_map/ppermute | solution.py:30
  62.3 9.2 %collective-permute-start.20 = (bf16[5,128,512]{2,1,0:T(8,128)(2,1)S(1)}, bf16[5,128,512]{2,1,0:T(8,128)(2,1)S(1)}, u32[]{:S(2)}, u32[]{:S(2)}) collective-permute-start(bf16[5,128,512]{2,1,0:T(8,128)(2,1)S(1)} %collective-permute-done.18.refs_1_), channel_id=1, source_target_pairs={{0,1},{1,0},{2,3},{3,2},{4,5},{5,4},{6,7},{7,6},{8,9},{9,8},{10,11... | collective-permute-start | bytes 1966088 | tf_op jit(solution)/shard_map/ppermute | solution.py:30
  63.7 13.5 %collective-permute-start.5 = (bf16[7,128,512]{2,1,0:T(8,128)(2,1)S(1)}, bf16[7,128,512]{2,1,0:T(8,128)(2,1)S(1)}, u32[]{:S(2)}, u32[]{:S(2)}) collective-permute-start(bf16[7,128,512]{2,1,0:T(8,128)(2,1)S(1)} %fusion.32), channel_id=1, source_target_pairs={{0,4},{1,3},{2,6},{3,1},{4,0},{5,7},{6,2},{7,5},{8,12},{9,11},{10,... | collective-permute-start | bytes 2752520 | tf_op jit(solution)/shard_map/ppermute | solution.py:30
  67.1 15.7 %collective-permute-start.14 = (bf16[256,1024]{1,0:T(8,128)(2,1)S(1)}, bf16[256,1024]{1,0:T(8,128)(2,1)S(1)}, u32[]{:S(2)}, u32[]{:S(2)}) collective-permute-start(bf16[256,1024]{1,0:T(8,128)(2,1)S(1)} %get-tuple-element.27), channel_id=1, source_target_pairs={{8,16},{16,8},{9,17},{17,9},{10,18},{18,10},{11,19},{19,11},{12,20... | collective-permute-start | bytes 1572872 | tf_op jit(solution)/shard_map/ppermute | solution.py:21
  70.6 13.6 %collective-permute-start.15 = (bf16[256,1024]{1,0:T(8,128)(2,1)S(1)}, bf16[256,1024]{1,0:T(8,128)(2,1)S(1)}, u32[]{:S(2)}, u32[]{:S(2)}) collective-permute-start(bf16[256,1024]{1,0:T(8,128)(2,1)S(1)} %get-tuple-element.28), channel_id=1, source_target_pairs={{0,8},{16,24},{8,0},{24,16},{1,9},{17,25},{9,1},{25,17},{2,10},{18... | collective-permute-start | bytes 1572872 | tf_op jit(solution)/shard_map/ppermute | solution.py:21
  77.3 7.5 %collective-permute-start.6 = (bf16[2,128,512]{2,1,0:T(8,128)(2,1)S(1)}, bf16[2,128,512]{2,1,0:T(8,128)(2,1)S(1)}, u32[]{:S(2)}, u32[]{:S(2)}) collective-permute-start(bf16[2,128,512]{2,1,0:T(8,128)(2,1)S(1)} %slice.254.refs_0_), channel_id=1, source_target_pairs={{0,2},{1,5},{2,0},{3,7},{4,6},{5,1},{6,4},{7,3},{8,10},{9,13},{10,... | collective-permute-start | bytes 786440 | tf_op jit(solution)/shard_map/ppermute | solution.py:30
  86.0 10.7 %collective-permute-start.23 = (bf16[5,128,512]{2,1,0:T(8,128)(2,1)S(1)}, bf16[5,128,512]{2,1,0:T(8,128)(2,1)S(1)}, u32[]{:S(2)}, u32[]{:S(2)}) collective-permute-start(bf16[5,128,512]{2,1,0:T(8,128)(2,1)S(1)} %slice.273.refs_0_), channel_id=1, source_target_pairs={{0,2},{1,5},{2,0},{3,7},{4,6},{5,1},{6,4},{7,3},{8,10},{9,13},{10,... | collective-permute-start | bytes 1966088 | tf_op jit(solution)/shard_map/ppermute | solution.py:30
  88.4 16.3 %collective-permute-start.21 = (bf16[256,1024]{1,0:T(8,128)(2,1)S(1)}, bf16[256,1024]{1,0:T(8,128)(2,1)S(1)}, u32[]{:S(2)}, u32[]{:S(2)}) collective-permute-start(bf16[256,1024]{1,0:T(8,128)(2,1)S(1)} %get-tuple-element.21), channel_id=1, source_target_pairs={{8,16},{16,8},{9,17},{17,9},{10,18},{18,10},{11,19},{19,11},{12,20... | collective-permute-start | bytes 1572872 | tf_op jit(solution)/shard_map/ppermute | solution.py:21
  91.0 14.1 %collective-permute-start.22 = (bf16[256,1024]{1,0:T(8,128)(2,1)S(1)}, bf16[256,1024]{1,0:T(8,128)(2,1)S(1)}, u32[]{:S(2)}, u32[]{:S(2)}) collective-permute-start(bf16[256,1024]{1,0:T(8,128)(2,1)S(1)} %get-tuple-element.22), channel_id=1, source_target_pairs={{0,8},{16,24},{8,0},{24,16},{1,9},{17,25},{9,1},{25,17},{2,10},{18... | collective-permute-start | bytes 1572872 | tf_op jit(solution)/shard_map/ppermute | solution.py:21
  91.3 14.9 %collective-permute-start.24 = (bf16[5,128,512]{2,1,0:T(8,128)(2,1)S(1)}, bf16[5,128,512]{2,1,0:T(8,128)(2,1)S(1)}, u32[]{:S(2)}, u32[]{:S(2)}) collective-permute-start(bf16[5,128,512]{2,1,0:T(8,128)(2,1)S(1)} %slice.273.refs_0_), channel_id=1, source_target_pairs={{0,1},{1,0},{2,3},{3,2},{4,5},{5,4},{6,7},{7,6},{8,9},{9,8},{10,11... | collective-permute-start | bytes 1966088 | tf_op jit(solution)/shard_map/ppermute | solution.py:30
  96.7 9.5 %collective-permute-start.25 = (bf16[5,128,512]{2,1,0:T(8,128)(2,1)S(1)}, bf16[5,128,512]{2,1,0:T(8,128)(2,1)S(1)}, u32[]{:S(2)}, u32[]{:S(2)}) collective-permute-start(bf16[5,128,512]{2,1,0:T(8,128)(2,1)S(1)} %collective-permute-done.23.refs_1_), channel_id=1, source_target_pairs={{0,1},{1,0},{2,3},{3,2},{4,5},{5,4},{6,7},{7,6},{8,9},{9,8},{10,11... | collective-permute-start | bytes 1966088 | tf_op jit(solution)/shard_map/ppermute | solution.py:30
  (8 other events, 34.6 us)

commit v16 on v13

--- a/solution.py
+++ b/solution.py
@@ -301,7 +301,7 @@
             streams.append(spread.middle(begun))
     pairs = [spread.last(stream) for stream in streams[:2]]
     for r in range(1, rounds):
-        pairs += spread.last_two(streams[r + 1], 3 if r + 1 < rounds else 2)
+        pairs += spread.last_two(streams[r + 1], wins + (1 if r + 1 < rounds else 0))
 
     matrix = slab
     crosses, above_crosses = {}, {}
@@ -323,7 +323,10 @@
         begin, end = head_rows[:border], tail_rows[border:]
         above, below = swap_rows(begin, end)
         rest = spread.join(*tail)
-        ones, twos = rest[: wins - 2], rest[wins - 2 :]
+        if r == 0:
+            ones, twos = rest[: wins - 2], rest[wins - 2 :]
+        else:
+            ones, twos = edges[2:], rest
         mid = apply_many(
             ones,
             matrix[window : local_rows - window].reshape(wins - 2, window, local_cols),

time: 114 us -> 116 us (1.018)
    ppermute x21, waiting for transfers between devices: 28.3 us -> 32.4 us  [flip(): lax.ppermute(value, 'cols', [(d, d ^ 1 << bits[d & 1]) for d in range(cou...]
    ppermute x4, waiting for transfers between devices: 13.4 us -> 9.77 us  [swap(): return lax.ppermute(value, 'rows', pairs + [(b, a) for a, b in pairs])]
    ppermute x4, starting transfers between devices: 7.76 us -> 9.06 us  [swap(): return lax.ppermute(value, 'rows', pairs + [(b, a) for a, b in pairs])]
  transfers between devices with their start and end apart: 26 -> 26, of which waited for: 11 -> 13; matrix products, arithmetic and copies ran while one was open for 17% -> 17% of each run, Pallas kernels for 3% -> 5%
where the time goes in v16:
time: 116 us; the launch traced here: 115 us
  waiting for transfers between devices  46.2 us (40%)
  starting transfers between devices  29 us (25%)
  matrix products  12 us (10%)
  other arithmetic  10.2 us (9%)
  Pallas kernels  7.99 us (7%)
  local copies, waits for them, and re-layouts  5.91 us (5%)
  between operations  4.2 us (4%)
    ppermute x21, waiting for transfers between devices, flip(): lax.ppermute(value, 'cols', [(d, d ^ 1 << bits[d & 1]) for d in range(cou...  32.4 us
    ppermute x21, starting transfers between devices, flip(): lax.ppermute(value, 'cols', [(d, d ^ 1 << bits[d & 1]) for d in range(cou...  16.5 us
    dot_general x6, matrix products, apply_many(): jnp.einsum('nab,nac->nbc', q, x, preferred_element_type=jnp.float32)  10.1 us
    ppermute x4, waiting for transfers between devices, swap(): return lax.ppermute(value, 'rows', pairs + [(b, a) for a, b in pairs])  9.77 us
    ppermute x4, starting transfers between devices, swap(): return lax.ppermute(value, 'rows', pairs + [(b, a) for a, b in pairs])  9.06 us
    select_n x9, other arithmetic, choose(): return jnp.where(mask, yes, no)  8.83 us
    ppermute x1, waiting for transfers between devices, shifted(): lax.ppermute(value, axis, [(source, source + steps) for source in range(i...  4.01 us
    ppermute x1, starting transfers between devices, shifted(): lax.ppermute(value, axis, [(source, source + steps) for source in range(i...  3.48 us
  transfers between devices with their start and end apart: 26, of which 13 were waited for; matrix products, arithmetic and copies ran while one was open for 17% of the time, Pallas kernels for 5%

profile of v16, /device:TPU:8, one launch (start us, length us, event | category | flops | bytes accessed | tf_op | source)
XLA Modules:
  0.0 115.5 jit_solution(9087152976505196312)
XLA Ops:
  0.0 2.2 %copy-done.2 = bf16[1,4096,512]{2,1,0:T(8,128)(2,1)S(1)} copy-done((bf16[1,4096,512]{2,1,0:T(8,128)(2,1)S(1)}, bf16[1,4096,512]{2,1,0:T(8,128)(2,1)}, u32[]{:S(2)}) %copy-start.2) | copy-done | bytes 4194328
  3.1 1.9 %cut_slot.2 = (bf16[9,128,512]{2,1,0:T(8,128)(2,1)S(1)}, bf16[9,128,512]{2,1,0:T(8,128)(2,1)}, bf16[9,128,512]{2,1,0:T(8,128)(2,1)S(1)}) custom-call(bf16[8,2,2,128,512]{4,3,2,1,0:T(8,128)(2,1)S(1)} %bitcast.84), custom_call_target="tpu_custom_call" | custom-call | bytes 6291456 | tf_op jit(solution)/shard_map/cut_slot/pallas_call | solution.py:105
  10.2 2.0 %slice_select_fusion.2 = bf16[5,128,512]{2,1,0:T(8,128)(2,1)} fusion(bf16[9,128,512]{2,1,0:T(8,128)(2,1)} %collective-permute-done.1, bf16[9,128,512]{2,1,0:T(8,128)(2,1)S(1)} %get-tuple-element.10, pred[]{:T(512)S(6)} %eq.25), kind=kLoop, calls=%fused_computation.46 | loop fusion | flops 327680 | bytes 1966081 | tf_op jit(solution)/shard_map/jit(_where)/select_n | solution.py:178
  14.0 3.9 %collective-permute-done.2 = bf16[4,128,512]{2,1,0:T(8,128)(2,1)S(1)} collective-permute-done((bf16[4,128,512]{2,1,0:T(8,128)(2,1)S(1)}, bf16[4,128,512]{2,1,0:T(8,128)(2,1)S(1)}, u32[]{:S(2)}, u32[]{:S(2)}) %collective-permute-start.2) | collective-permute-done | bytes 524320 | tf_op jit(solution)/shard_map/ppermute | solution.py:30
  20.0 1.6 %collective-permute-start.3 = (bf16[4,128,512]{2,1,0:T(8,128)(2,1)S(1)}, bf16[4,128,512]{2,1,0:T(8,128)(2,1)S(1)}, u32[]{:S(2)}, u32[]{:S(2)}) collective-permute-start(bf16[4,128,512]{2,1,0:T(8,128)(2,1)S(1)} %fusion.34), channel_id=1, source_target_pairs={{0,4},{1,3},{2,6},{3,1},{4,0},{5,7},{6,2},{7,5},{8,12},{9,11},{10,... | collective-permute-start | bytes 1572872 | tf_op jit(solution)/shard_map/ppermute | solution.py:30
  22.8 5.1 %collective-permute-done.19 = bf16[5,128,512]{2,1,0:T(8,128)(2,1)} collective-permute-done((bf16[5,128,512]{2,1,0:T(8,128)(2,1)}, bf16[5,128,512]{2,1,0:T(8,128)(2,1)}, u32[]{:S(2)}, u32[]{:S(2)}) %collective-permute-start.19) | collective-permute-done | bytes 655392 | tf_op jit(solution)/shard_map/ppermute | solution.py:30
  29.3 1.6 %collective-permute-start.20 = (bf16[5,128,512]{2,1,0:T(8,128)(2,1)S(1)}, bf16[5,128,512]{2,1,0:T(8,128)(2,1)S(1)}, u32[]{:S(2)}, u32[]{:S(2)}) collective-permute-start(bf16[5,128,512]{2,1,0:T(8,128)(2,1)S(1)} %fusion.33), channel_id=1, source_target_pairs={{0,4},{1,3},{2,6},{3,1},{4,0},{5,7},{6,2},{7,5},{8,12},{9,11},{10,... | collective-permute-start | bytes 1966088 | tf_op jit(solution)/shard_map/ppermute | solution.py:30
  34.7 12.1 %collective-permute-done.20 = bf16[5,128,512]{2,1,0:T(8,128)(2,1)S(1)} collective-permute-done((bf16[5,128,512]{2,1,0:T(8,128)(2,1)S(1)}, bf16[5,128,512]{2,1,0:T(8,128)(2,1)S(1)}, u32[]{:S(2)}, u32[]{:S(2)}) %collective-permute-start.20) | collective-permute-done | bytes 655392 | tf_op jit(solution)/shard_map/ppermute | solution.py:30
  48.2 3.5 %collective-permute-start.15 = (bf16[2,2,128,256]{3,2,1,0:T(8,128)(2,1)S(1)}, bf16[2,2,128,256]{3,2,1,0:T(8,128)(2,1)S(1)}, u32[]{:S(2)}, u32[]{:S(2)}) collective-permute-start(bf16[2,2,128,256]{3,2,1,0:T(8,128)(2,1)S(1)} %pad_maximum_fusion.4), channel_id=1, source_target_pairs={{0,8},{8,16},{16,24},{1,9},{9,17},{17,25},{2,10},{10,18},{18,26},{... | collective-permute-start | bytes 786440 | tf_op jit(solution)/shard_map/ppermute | solution.py:12
  52.5 4.0 %collective-permute-done.15 = bf16[2,2,128,256]{3,2,1,0:T(8,128)(2,1)S(1)} collective-permute-done((bf16[2,2,128,256]{3,2,1,0:T(8,128)(2,1)S(1)}, bf16[2,2,128,256]{3,2,1,0:T(8,128)(2,1)S(1)}, u32[]{:S(2)}, u32[]{:S(2)}) %collective-permute-start.15) | collective-permute-done | bytes 262176 | tf_op jit(solution)/shard_map/ppermute | solution.py:12
  56.5 3.5 %collective-permute-done.21.refs_1_ = bf16[5,128,512]{2,1,0:T(8,128)(2,1)S(1)} collective-permute-done((bf16[5,128,512]{2,1,0:T(8,128)(2,1)S(1)}, bf16[5,128,512]{2,1,0:T(8,128)(2,1)S(1)}, u32[]{:S(2)}, u32[]{:S(2)}) %collective-permute-start.21) | collective-permute-done | bytes 655392 | tf_op jit(solution)/shard_map/ppermute | solution.py:30
  60.0 2.3 %collective-permute-start.16 = (bf16[2,2,128,256]{3,2,1,0:T(8,128)(2,1)S(1)}, bf16[2,2,128,256]{3,2,1,0:T(8,128)(2,1)S(1)}, u32[]{:S(2)}, u32[]{:S(2)}) collective-permute-start(bf16[2,2,128,256]{3,2,1,0:T(8,128)(2,1)S(1)} %collective-permute-done.15), channel_id=1, source_target_pairs={{0,1},{1,0},{2,3},{3,2},{4,5},{5,4},{6,7},{7,6},{8,9},{9,8},{10,11... | collective-permute-start | bytes 786440 | tf_op jit(solution)/shard_map/ppermute | solution.py:30
  63.7 1.6 %collective-permute-start.5 = (bf16[7,128,512]{2,1,0:T(8,128)(2,1)S(1)}, bf16[7,128,512]{2,1,0:T(8,128)(2,1)S(1)}, u32[]{:S(2)}, u32[]{:S(2)}) collective-permute-start(bf16[7,128,512]{2,1,0:T(8,128)(2,1)S(1)} %fusion.32), channel_id=1, source_target_pairs={{0,4},{1,3},{2,6},{3,1},{4,0},{5,7},{6,2},{7,5},{8,12},{9,11},{10,... | collective-permute-start | bytes 2752520 | tf_op jit(solution)/shard_map/ppermute | solution.py:30
  67.1 3.7 %collective-permute-start.17 = (bf16[256,1024]{1,0:T(8,128)(2,1)S(1)}, bf16[256,1024]{1,0:T(8,128)(2,1)S(1)}, u32[]{:S(2)}, u32[]{:S(2)}) collective-permute-start(bf16[256,1024]{1,0:T(8,128)(2,1)S(1)} %get-tuple-element.27), channel_id=1, source_target_pairs={{8,16},{16,8},{9,17},{17,9},{10,18},{18,10},{11,19},{19,11},{12,20... | collective-permute-start | bytes 1572872 | tf_op jit(solution)/shard_map/ppermute | solution.py:21
  75.1 2.0 %collective-permute-done.5 = bf16[7,128,512]{2,1,0:T(8,128)(2,1)S(1)} collective-permute-done((bf16[7,128,512]{2,1,0:T(8,128)(2,1)S(1)}, bf16[7,128,512]{2,1,0:T(8,128)(2,1)S(1)}, u32[]{:S(2)}, u32[]{:S(2)}) %collective-permute-start.5) | collective-permute-done | bytes 917536 | tf_op jit(solution)/shard_map/ppermute | solution.py:30
  78.7 2.1 %convolution_convert_fusion = bf16[3,512,1024]{2,1,0:T(8,128)(2,1)S(1)} fusion(bf16[5,512,512]{2,1,0:T(8,128)(2,1)S(1)} %place.9, bf16[3,512,1024]{2,1,0:T(8,128)(2,1)S(1)} %bitcast.89), kind=kOutput, calls=%fused_computation.2 | convolution fusion | flops 1612185600 | bytes 8912896 | tf_op jit(solution)/shard_map/nab,nac->nbc/dot_general | solution.py:230
  82.8 1.9 %collective-permute-done.18 = bf16[256,1024]{1,0:T(8,128)(2,1)S(1)} collective-permute-done((bf16[256,1024]{1,0:T(8,128)(2,1)S(1)}, bf16[256,1024]{1,0:T(8,128)(2,1)S(1)}, u32[]{:S(2)}, u32[]{:S(2)}) %collective-permute-start.18) | collective-permute-done | bytes 524320 | tf_op jit(solution)/shard_map/ppermute | solution.py:21
  84.8 1.7 %collective-permute-done.9.refs_1_ = bf16[4,128,512]{2,1,0:T(8,128)(2,1)S(1)} collective-permute-done((bf16[4,128,512]{2,1,0:T(8,128)(2,1)S(1)}, bf16[4,128,512]{2,1,0:T(8,128)(2,1)S(1)}, u32[]{:S(2)}, u32[]{:S(2)}) %collective-permute-start.9) | collective-permute-done | bytes 524320 | tf_op jit(solution)/shard_map/ppermute | solution.py:30
  87.8 3.0 %collective-permute-done.6.refs_1_ = bf16[3,128,512]{2,1,0:T(8,128)(2,1)S(1)} collective-permute-done((bf16[3,128,512]{2,1,0:T(8,128)(2,1)S(1)}, bf16[3,128,512]{2,1,0:T(8,128)(2,1)S(1)}, u32[]{:S(2)}, u32[]{:S(2)}) %collective-permute-start.6) | collective-permute-done | bytes 393248 | tf_op jit(solution)/shard_map/ppermute | solution.py:30
  96.4 5.3 %collective-permute-start.24 = (bf16[256,1024]{1,0:T(8,128)(2,1)S(1)}, bf16[256,1024]{1,0:T(8,128)(2,1)S(1)}, u32[]{:S(2)}, u32[]{:S(2)}) collective-permute-start(bf16[256,1024]{1,0:T(8,128)(2,1)S(1)} %get-tuple-element.22), channel_id=1, source_target_pairs={{8,16},{16,8},{9,17},{17,9},{10,18},{18,10},{11,19},{19,11},{12,20... | collective-permute-start | bytes 1572872 | tf_op jit(solution)/shard_map/ppermute | solution.py:21
  102.1 1.9 %convolution_convert_fusion.1 = bf16[3,512,1024]{2,1,0:T(8,128)(2,1)S(1)} fusion(bf16[3,512,512]{2,1,0:T(8,128)(2,1)S(1)} %place.5, bf16[3,512,1024]{2,1,0:T(8,128)(2,1)S(1)} %bitcast.90), kind=kOutput, calls=%fused_computation.3 | convolution fusion | flops 1612185600 | bytes 7864320 | tf_op jit(solution)/shard_map/nab,nac->nbc/dot_general | solution.py:230
  104.0 2.7 %write_inner.1._ = bf16[2048,1024]{1,0:T(8,128)(2,1)} custom-call(bf16[1536,1024]{1,0:T(8,128)(2,1)S(1)} %bitcast.85), custom_call_target="tpu_custom_call" | custom-call | bytes 6291456 | tf_op jit(solution)/shard_map/write_inner/pallas_call | solution.py:240
  106.7 3.7 %collective-permute-done.25 = bf16[256,1024]{1,0:T(8,128)(2,1)S(1)} collective-permute-done((bf16[256,1024]{1,0:T(8,128)(2,1)S(1)}, bf16[256,1024]{1,0:T(8,128)(2,1)S(1)}, u32[]{:S(2)}, u32[]{:S(2)}) %collective-permute-start.25) | collective-permute-done | bytes 524320 | tf_op jit(solution)/shard_map/ppermute | solution.py:21
  110.4 3.0 %collective-permute-done.24 = bf16[256,1024]{1,0:T(8,128)(2,1)S(1)} collective-permute-done((bf16[256,1024]{1,0:T(8,128)(2,1)S(1)}, bf16[256,1024]{1,0:T(8,128)(2,1)S(1)}, u32[]{:S(2)}, u32[]{:S(2)}) %collective-permute-start.24) | collective-permute-done | bytes 524320 | tf_op jit(solution)/shard_map/ppermute | solution.py:21
  (93 shorter events, 35.1 us)
Async XLA Ops:
  3.0 4.5 %collective-permute-start.1 = (bf16[9,128,512]{2,1,0:T(8,128)(2,1)S(1)}, bf16[9,128,512]{2,1,0:T(8,128)(2,1)}, u32[]{:S(2)}, u32[]{:S(2)}) collective-permute-start(bf16[9,128,512]{2,1,0:T(8,128)(2,1)S(1)} %cut_slot.3), channel_id=1, source_target_pairs={{0,1},{1,0},{2,3},{3,2},{4,5},{5,4},{6,7},{7,6},{8,9},{9,8},{10,11... | collective-permute-start | bytes 3538952 | tf_op jit(solution)/shard_map/ppermute | solution.py:30
  5.0 8.9 %collective-permute-start = (bf16[9,128,512]{2,1,0:T(8,128)(2,1)}, bf16[9,128,512]{2,1,0:T(8,128)(2,1)}, u32[]{:S(2)}, u32[]{:S(2)}) collective-permute-start(bf16[9,128,512]{2,1,0:T(8,128)(2,1)} %get-tuple-element.9), channel_id=1, source_target_pairs={{0,1},{1,0},{2,3},{3,2},{4,5},{5,4},{6,7},{7,6},{8,9},{9,8},{10,11... | collective-permute-start | bytes 3538952 | tf_op jit(solution)/shard_map/ppermute | solution.py:30
  8.6 9.2 %collective-permute-start.2 = (bf16[4,128,512]{2,1,0:T(8,128)(2,1)S(1)}, bf16[4,128,512]{2,1,0:T(8,128)(2,1)S(1)}, u32[]{:S(2)}, u32[]{:S(2)}) collective-permute-start(bf16[4,128,512]{2,1,0:T(8,128)(2,1)S(1)} %slice_select_fusion.4), channel_id=1, source_target_pairs={{0,2},{1,5},{2,0},{3,7},{4,6},{5,1},{6,4},{7,3},{8,10},{9,13},{10,... | collective-permute-start | bytes 1572872 | tf_op jit(solution)/shard_map/ppermute | solution.py:30
  12.2 15.8 %collective-permute-start.19 = (bf16[5,128,512]{2,1,0:T(8,128)(2,1)}, bf16[5,128,512]{2,1,0:T(8,128)(2,1)}, u32[]{:S(2)}, u32[]{:S(2)}) collective-permute-start(bf16[5,128,512]{2,1,0:T(8,128)(2,1)} %slice_select_fusion.2), channel_id=1, source_target_pairs={{0,2},{1,5},{2,0},{3,7},{4,6},{5,1},{6,4},{7,3},{8,10},{9,13},{10,... | collective-permute-start | bytes 1966088 | tf_op jit(solution)/shard_map/ppermute | solution.py:30
  20.0 10.9 %collective-permute-start.3 = (bf16[4,128,512]{2,1,0:T(8,128)(2,1)S(1)}, bf16[4,128,512]{2,1,0:T(8,128)(2,1)S(1)}, u32[]{:S(2)}, u32[]{:S(2)}) collective-permute-start(bf16[4,128,512]{2,1,0:T(8,128)(2,1)S(1)} %fusion.34), channel_id=1, source_target_pairs={{0,4},{1,3},{2,6},{3,1},{4,0},{5,7},{6,2},{7,5},{8,12},{9,11},{10,... | collective-permute-start | bytes 1572872 | tf_op jit(solution)/shard_map/ppermute | solution.py:30
  29.3 17.5 %collective-permute-start.20 = (bf16[5,128,512]{2,1,0:T(8,128)(2,1)S(1)}, bf16[5,128,512]{2,1,0:T(8,128)(2,1)S(1)}, u32[]{:S(2)}, u32[]{:S(2)}) collective-permute-start(bf16[5,128,512]{2,1,0:T(8,128)(2,1)S(1)} %fusion.33), channel_id=1, source_target_pairs={{0,4},{1,3},{2,6},{3,1},{4,0},{5,7},{6,2},{7,5},{8,12},{9,11},{10,... | collective-permute-start | bytes 1966088 | tf_op jit(solution)/shard_map/ppermute | solution.py:30
  31.0 17.1 %collective-permute-start.12 = (bf16[4,128,512]{2,1,0:T(8,128)(2,1)S(1)}, bf16[4,128,512]{2,1,0:T(8,128)(2,1)S(1)}, u32[]{:S(2)}, u32[]{:S(2)}) collective-permute-start(bf16[4,128,512]{2,1,0:T(8,128)(2,1)S(1)} %broadcast_select_fusion.2.refs_0_), channel_id=1, source_target_pairs={{0,2},{1,5},{2,0},{3,7},{4,6},{5,1},{6,4},{7,3},{8,10},{9,13},{10,... | collective-permute-start | bytes 1572872 | tf_op jit(solution)/shard_map/ppermute | solution.py:30
  33.9 28.3 %collective-permute-start.4 = (bf16[7,128,512]{2,1,0:T(8,128)(2,1)S(1)}, bf16[7,128,512]{2,1,0:T(8,128)(2,1)S(1)}, u32[]{:S(2)}, u32[]{:S(2)}) collective-permute-start(bf16[7,128,512]{2,1,0:T(8,128)(2,1)S(1)} %after.1), channel_id=1, source_target_pairs={{0,2},{1,5},{2,0},{3,7},{4,6},{5,1},{6,4},{7,3},{8,10},{9,13},{10,... | collective-permute-start | bytes 2752520 | tf_op jit(solution)/shard_map/ppermute | solution.py:30
  46.9 13.1 %collective-permute-start.21 = (bf16[5,128,512]{2,1,0:T(8,128)(2,1)S(1)}, bf16[5,128,512]{2,1,0:T(8,128)(2,1)S(1)}, u32[]{:S(2)}, u32[]{:S(2)}) collective-permute-start(bf16[5,128,512]{2,1,0:T(8,128)(2,1)S(1)} %broadcast_select_fusion.1.refs_0_), channel_id=1, source_target_pairs={{0,2},{1,5},{2,0},{3,7},{4,6},{5,1},{6,4},{7,3},{8,10},{9,13},{10,... | collective-permute-start | bytes 1966088 | tf_op jit(solution)/shard_map/ppermute | solution.py:30
  48.2 8.3 %collective-permute-start.15 = (bf16[2,2,128,256]{3,2,1,0:T(8,128)(2,1)S(1)}, bf16[2,2,128,256]{3,2,1,0:T(8,128)(2,1)S(1)}, u32[]{:S(2)}, u32[]{:S(2)}) collective-permute-start(bf16[2,2,128,256]{3,2,1,0:T(8,128)(2,1)S(1)} %pad_maximum_fusion.4), channel_id=1, source_target_pairs={{0,8},{8,16},{16,24},{1,9},{9,17},{17,25},{2,10},{10,18},{18,26},{... | collective-permute-start | bytes 786440 | tf_op jit(solution)/shard_map/ppermute | solution.py:12
  51.9 11.8 %collective-permute-start.13 = (bf16[4,128,512]{2,1,0:T(8,128)(2,1)S(1)}, bf16[4,128,512]{2,1,0:T(8,128)(2,1)S(1)}, u32[]{:S(2)}, u32[]{:S(2)}) collective-permute-start(bf16[4,128,512]{2,1,0:T(8,128)(2,1)S(1)} %broadcast_select_fusion.2.refs_0_), channel_id=1, source_target_pairs={{0,1},{1,0},{2,3},{3,2},{4,5},{5,4},{6,7},{7,6},{8,9},{9,8},{10,11... | collective-permute-start | bytes 1572872 | tf_op jit(solution)/shard_map/ppermute | solution.py:30
  52.0 19.6 %collective-permute-start.22 = (bf16[5,128,512]{2,1,0:T(8,128)(2,1)S(1)}, bf16[5,128,512]{2,1,0:T(8,128)(2,1)S(1)}, u32[]{:S(2)}, u32[]{:S(2)}) collective-permute-start(bf16[5,128,512]{2,1,0:T(8,128)(2,1)S(1)} %broadcast_select_fusion.1.refs_0_), channel_id=1, source_target_pairs={{0,1},{1,0},{2,3},{3,2},{4,5},{5,4},{6,7},{7,6},{8,9},{9,8},{10,11... | collective-permute-start | bytes 1966088 | tf_op jit(solution)/shard_map/ppermute | solution.py:30
  56.5 8.8 %collective-permute-start.14 = (bf16[4,128,512]{2,1,0:T(8,128)(2,1)S(1)}, bf16[4,128,512]{2,1,0:T(8,128)(2,1)S(1)}, u32[]{:S(2)}, u32[]{:S(2)}) collective-permute-start(bf16[4,128,512]{2,1,0:T(8,128)(2,1)S(1)} %collective-permute-done.12.refs_1_), channel_id=1, source_target_pairs={{0,1},{1,0},{2,3},{3,2},{4,5},{5,4},{6,7},{7,6},{8,9},{9,8},{10,11... | collective-permute-start | bytes 1572872 | tf_op jit(solution)/shard_map/ppermute | solution.py:30
  60.0 11.0 %collective-permute-start.16 = (bf16[2,2,128,256]{3,2,1,0:T(8,128)(2,1)S(1)}, bf16[2,2,128,256]{3,2,1,0:T(8,128)(2,1)S(1)}, u32[]{:S(2)}, u32[]{:S(2)}) collective-permute-start(bf16[2,2,128,256]{3,2,1,0:T(8,128)(2,1)S(1)} %collective-permute-done.15), channel_id=1, source_target_pairs={{0,1},{1,0},{2,3},{3,2},{4,5},{5,4},{6,7},{7,6},{8,9},{9,8},{10,11... | collective-permute-start | bytes 786440 | tf_op jit(solution)/shard_map/ppermute | solution.py:30
  62.3 9.3 %collective-permute-start.23 = (bf16[5,128,512]{2,1,0:T(8,128)(2,1)S(1)}, bf16[5,128,512]{2,1,0:T(8,128)(2,1)S(1)}, u32[]{:S(2)}, u32[]{:S(2)}) collective-permute-start(bf16[5,128,512]{2,1,0:T(8,128)(2,1)S(1)} %collective-permute-done.21.refs_1_), channel_id=1, source_target_pairs={{0,1},{1,0},{2,3},{3,2},{4,5},{5,4},{6,7},{7,6},{8,9},{9,8},{10,11... | collective-permute-start | bytes 1966088 | tf_op jit(solution)/shard_map/ppermute | solution.py:30
  63.7 13.5 %collective-permute-start.5 = (bf16[7,128,512]{2,1,0:T(8,128)(2,1)S(1)}, bf16[7,128,512]{2,1,0:T(8,128)(2,1)S(1)}, u32[]{:S(2)}, u32[]{:S(2)}) collective-permute-start(bf16[7,128,512]{2,1,0:T(8,128)(2,1)S(1)} %fusion.32), channel_id=1, source_target_pairs={{0,4},{1,3},{2,6},{3,1},{4,0},{5,7},{6,2},{7,5},{8,12},{9,11},{10,... | collective-permute-start | bytes 2752520 | tf_op jit(solution)/shard_map/ppermute | solution.py:30
  67.1 15.7 %collective-permute-start.17 = (bf16[256,1024]{1,0:T(8,128)(2,1)S(1)}, bf16[256,1024]{1,0:T(8,128)(2,1)S(1)}, u32[]{:S(2)}, u32[]{:S(2)}) collective-permute-start(bf16[256,1024]{1,0:T(8,128)(2,1)S(1)} %get-tuple-element.27), channel_id=1, source_target_pairs={{8,16},{16,8},{9,17},{17,9},{10,18},{18,10},{11,19},{19,11},{12,20... | collective-permute-start | bytes 1572872 | tf_op jit(solution)/shard_map/ppermute | solution.py:21
  71.1 13.6 %collective-permute-start.18 = (bf16[256,1024]{1,0:T(8,128)(2,1)S(1)}, bf16[256,1024]{1,0:T(8,128)(2,1)S(1)}, u32[]{:S(2)}, u32[]{:S(2)}) collective-permute-start(bf16[256,1024]{1,0:T(8,128)(2,1)S(1)} %get-tuple-element.28), channel_id=1, source_target_pairs={{0,8},{16,24},{8,0},{24,16},{1,9},{17,25},{9,1},{25,17},{2,10},{18... | collective-permute-start | bytes 1572872 | tf_op jit(solution)/shard_map/ppermute | solution.py:21
  77.3 9.2 %collective-permute-start.9 = (bf16[4,128,512]{2,1,0:T(8,128)(2,1)S(1)}, bf16[4,128,512]{2,1,0:T(8,128)(2,1)S(1)}, u32[]{:S(2)}, u32[]{:S(2)}) collective-permute-start(bf16[4,128,512]{2,1,0:T(8,128)(2,1)S(1)} %slice.255.refs_0_), channel_id=1, source_target_pairs={{0,2},{1,5},{2,0},{3,7},{4,6},{5,1},{6,4},{7,3},{8,10},{9,13},{10,... | collective-permute-start | bytes 1572872 | tf_op jit(solution)/shard_map/ppermute | solution.py:30
  80.8 9.9 %collective-permute-start.6 = (bf16[3,128,512]{2,1,0:T(8,128)(2,1)S(1)}, bf16[3,128,512]{2,1,0:T(8,128)(2,1)S(1)}, u32[]{:S(2)}, u32[]{:S(2)}) collective-permute-start(bf16[3,128,512]{2,1,0:T(8,128)(2,1)S(1)} %slice.254.refs_0_), channel_id=1, source_target_pairs={{0,2},{1,5},{2,0},{3,7},{4,6},{5,1},{6,4},{7,3},{8,10},{9,13},{10,... | collective-permute-start | bytes 1179656 | tf_op jit(solution)/shard_map/ppermute | solution.py:30
  84.7 8.0 %collective-permute-start.10 = (bf16[4,128,512]{2,1,0:T(8,128)(2,1)S(1)}, bf16[4,128,512]{2,1,0:T(8,128)(2,1)S(1)}, u32[]{:S(2)}, u32[]{:S(2)}) collective-permute-start(bf16[4,128,512]{2,1,0:T(8,128)(2,1)S(1)} %slice.255.refs_0_), channel_id=1, source_target_pairs={{0,1},{1,0},{2,3},{3,2},{4,5},{5,4},{6,7},{7,6},{8,9},{9,8},{10,11... | collective-permute-start | bytes 1572872 | tf_op jit(solution)/shard_map/ppermute | solution.py:30
  86.6 6.2 %collective-permute-start.11 = (bf16[4,128,512]{2,1,0:T(8,128)(2,1)S(1)}, bf16[4,128,512]{2,1,0:T(8,128)(2,1)S(1)}, u32[]{:S(2)}, u32[]{:S(2)}) collective-permute-start(bf16[4,128,512]{2,1,0:T(8,128)(2,1)S(1)} %collective-permute-done.9.refs_1_), channel_id=1, source_target_pairs={{0,1},{1,0},{2,3},{3,2},{4,5},{5,4},{6,7},{7,6},{8,9},{9,8},{10,11... | collective-permute-start | bytes 1572872 | tf_op jit(solution)/shard_map/ppermute | solution.py:30
  96.4 14.0 %collective-permute-start.25 = (bf16[256,1024]{1,0:T(8,128)(2,1)S(1)}, bf16[256,1024]{1,0:T(8,128)(2,1)S(1)}, u32[]{:S(2)}, u32[]{:S(2)}) collective-permute-start(bf16[256,1024]{1,0:T(8,128)(2,1)S(1)} %get-tuple-element.21), channel_id=1, source_target_pairs={{0,8},{16,24},{8,0},{24,16},{1,9},{17,25},{9,1},{25,17},{2,10},{18... | collective-permute-start | bytes 1572872 | tf_op jit(solution)/shard_map/ppermute | solution.py:21
  96.4 17.0 %collective-permute-start.24 = (bf16[256,1024]{1,0:T(8,128)(2,1)S(1)}, bf16[256,1024]{1,0:T(8,128)(2,1)S(1)}, u32[]{:S(2)}, u32[]{:S(2)}) collective-permute-start(bf16[256,1024]{1,0:T(8,128)(2,1)S(1)} %get-tuple-element.22), channel_id=1, source_target_pairs={{8,16},{16,8},{9,17},{17,9},{10,18},{18,10},{11,19},{19,11},{12,20... | collective-permute-start | bytes 1572872 | tf_op jit(solution)/shard_map/ppermute | solution.py:21
  (8 other events, 35.2 us)

commit v17 on v13

--- a/solution.py
+++ b/solution.py
@@ -289,16 +289,18 @@
     middle_one, middle_two = list(range(1, wins - 1)), list(range(wins, crossing))
     order = [crossing, crossing, 0, wins - 1] + middle_one + middle_two
     spread = Spread(slot, owners[:, row_block], order)
-    streams = []
+    streams, opening = [], None
     for r in range(rounds):
         across = ([r + 1] if r + 1 < rounds else []) + ([r] if r == 0 else [])
         first = 2 - len(across)
         if r == 0:
             streams.append(spread.middle(spread.begin(across + [r, r], slice(first, 4))))
-            streams.append(spread.middle(spread.begin([r] * (len(order) - 4), slice(4, len(order)))))
+            opening = spread.begin([r] * (len(order) - 4), slice(4, len(order)))
+            streams.append(spread.middle(opening))
         else:
-            begun = spread.begin(across + [r] * crossing, slice(first, len(order)), streams[r - 1][2])
+            begun = spread.begin(across + [r] * crossing, slice(first, len(order)), opening[2])
             streams.append(spread.middle(begun))
+            opening = begun
     pairs = [spread.last(stream) for stream in streams[:2]]
     for r in range(1, rounds):
         pairs += spread.last_two(streams[r + 1], 3 if r + 1 < rounds else 2)

time: 114 us -> 115 us (level)
  starting transfers between devices: 28.1 us -> 24.6 us
  waiting for transfers between devices: 45.7 us -> 48.5 us
    ppermute x21, starting transfers between devices: 16.9 us -> 14.3 us  [flip(): lax.ppermute(value, 'cols', [(d, d ^ 1 << bits[d & 1]) for d in range(cou...]
    ppermute x21, waiting for transfers between devices: 28.3 us -> 30.6 us  [flip(): lax.ppermute(value, 'cols', [(d, d ^ 1 << bits[d & 1]) for d in range(cou...]
    another operation x1, local copies, waits for them, and re-layouts: 0.17 us -> 1.49 us  [local(): jnp.stack([matrix[:window], matrix[local_rows - window:]])]
    slice x3, local copies, waits for them, and re-layouts: 1.49 us -> 0.18 us  [local(): matrix[window:local_rows - window].reshape(wins - 2, window, local_cols)]
    unnamed x10 -> x12, local copies, waits for them, and re-layouts: 3.01 us -> 2.23 us
  transfers between devices with their start and end apart: 26 -> 26, of which waited for: 11 -> 11; matrix products, arithmetic and copies ran while one was open for 17% -> 19% of each run, Pallas kernels for 3% -> 4%
where the time goes in v17:
time: 115 us; the launch traced here: 114 us
  waiting for transfers between devices  48.5 us (42%)
  starting transfers between devices  24.6 us (21%)
  matrix products  11.9 us (10%)
  other arithmetic  10.2 us (9%)
  Pallas kernels  8.72 us (8%)
  local copies, waits for them, and re-layouts  6.05 us (5%)
  between operations  4.26 us (4%)
    ppermute x21, waiting for transfers between devices, flip(): lax.ppermute(value, 'cols', [(d, d ^ 1 << bits[d & 1]) for d in range(cou...  30.6 us
    ppermute x21, starting transfers between devices, flip(): lax.ppermute(value, 'cols', [(d, d ^ 1 << bits[d & 1]) for d in range(cou...  14.3 us
    ppermute x4, waiting for transfers between devices, swap(): return lax.ppermute(value, 'rows', pairs + [(b, a) for a, b in pairs])  13.8 us
    dot_general x6, matrix products, apply_many(): jnp.einsum('nab,nac->nbc', q, x, preferred_element_type=jnp.float32)  10.1 us
    select_n x9, other arithmetic, choose(): return jnp.where(mask, yes, no)  8.84 us
    ppermute x4, starting transfers between devices, swap(): return lax.ppermute(value, 'rows', pairs + [(b, a) for a, b in pairs])  6.78 us
    ppermute x1, waiting for transfers between devices, shifted(): lax.ppermute(value, axis, [(source, source + steps) for source in range(i...  4.12 us
    ppermute x1, starting transfers between devices, shifted(): lax.ppermute(value, axis, [(source, source + steps) for source in range(i...  3.48 us
  transfers between devices with their start and end apart: 26, of which 11 were waited for; matrix products, arithmetic and copies ran while one was open for 19% of the time, Pallas kernels for 4%

profile of v17, /device:TPU:8, one launch (start us, length us, event | category | flops | bytes accessed | tf_op | source)
XLA Modules:
  0.0 114.2 jit_solution(15796807075234756755)
XLA Ops:
  0.0 2.2 %copy-done.2 = bf16[1,4096,512]{2,1,0:T(8,128)(2,1)S(1)} copy-done((bf16[1,4096,512]{2,1,0:T(8,128)(2,1)S(1)}, bf16[1,4096,512]{2,1,0:T(8,128)(2,1)}, u32[]{:S(2)}) %copy-start.2) | copy-done | bytes 4194328
  3.1 1.9 %cut_slot.2 = (bf16[9,128,512]{2,1,0:T(8,128)(2,1)S(1)}, bf16[9,128,512]{2,1,0:T(8,128)(2,1)}, bf16[9,128,512]{2,1,0:T(8,128)(2,1)S(1)}) custom-call(bf16[8,2,2,128,512]{4,3,2,1,0:T(8,128)(2,1)S(1)} %bitcast.84), custom_call_target="tpu_custom_call" | custom-call | bytes 6291456 | tf_op jit(solution)/shard_map/cut_slot/pallas_call | solution.py:105
  8.7 1.6 %collective-permute-start.11 = (bf16[4,128,512]{2,1,0:T(8,128)(2,1)S(1)}, bf16[4,128,512]{2,1,0:T(8,128)(2,1)S(1)}, u32[]{:S(2)}, u32[]{:S(2)}) collective-permute-start(bf16[4,128,512]{2,1,0:T(8,128)(2,1)S(1)} %slice_select_fusion.4), channel_id=1, source_target_pairs={{0,2},{1,5},{2,0},{3,7},{4,6},{5,1},{6,4},{7,3},{8,10},{9,13},{10,... | collective-permute-start | bytes 1572872 | tf_op jit(solution)/shard_map/ppermute | solution.py:30
  14.5 3.4 %collective-permute-done.11 = bf16[4,128,512]{2,1,0:T(8,128)(2,1)S(1)} collective-permute-done((bf16[4,128,512]{2,1,0:T(8,128)(2,1)S(1)}, bf16[4,128,512]{2,1,0:T(8,128)(2,1)S(1)}, u32[]{:S(2)}, u32[]{:S(2)}) %collective-permute-start.11) | collective-permute-done | bytes 524320 | tf_op jit(solution)/shard_map/ppermute | solution.py:30
  19.1 1.6 %collective-permute-start.12 = (bf16[4,128,512]{2,1,0:T(8,128)(2,1)S(1)}, bf16[4,128,512]{2,1,0:T(8,128)(2,1)S(1)}, u32[]{:S(2)}, u32[]{:S(2)}) collective-permute-start(bf16[4,128,512]{2,1,0:T(8,128)(2,1)S(1)} %fusion.34), channel_id=1, source_target_pairs={{0,4},{1,3},{2,6},{3,1},{4,0},{5,7},{6,2},{7,5},{8,12},{9,11},{10,... | collective-permute-start | bytes 1572872 | tf_op jit(solution)/shard_map/ppermute | solution.py:30
  22.0 6.8 %collective-permute-done.2.refs_0_ = bf16[5,128,512]{2,1,0:T(8,128)(2,1)S(1)} collective-permute-done((bf16[5,128,512]{2,1,0:T(8,128)(2,1)S(1)}, bf16[5,128,512]{2,1,0:T(8,128)(2,1)S(1)}, u32[]{:S(2)}, u32[]{:S(2)}) %collective-permute-start.2) | collective-permute-done | bytes 655392 | tf_op jit(solution)/shard_map/ppermute | solution.py:30
  29.0 1.6 %collective-permute-start.3 = (bf16[7,128,512]{2,1,0:T(8,128)(2,1)S(1)}, bf16[7,128,512]{2,1,0:T(8,128)(2,1)}, u32[]{:S(2)}, u32[]{:S(2)}) collective-permute-start(bf16[7,128,512]{2,1,0:T(8,128)(2,1)S(1)} %after.1), channel_id=1, source_target_pairs={{0,2},{1,5},{2,0},{3,7},{4,6},{5,1},{6,4},{7,3},{8,10},{9,13},{10,... | collective-permute-start | bytes 2752520 | tf_op jit(solution)/shard_map/ppermute | solution.py:30
  31.9 1.6 %collective-permute-start.20 = (bf16[5,128,512]{2,1,0:T(8,128)(2,1)S(1)}, bf16[5,128,512]{2,1,0:T(8,128)(2,1)}, u32[]{:S(2)}, u32[]{:S(2)}) collective-permute-start(bf16[5,128,512]{2,1,0:T(8,128)(2,1)S(1)} %fusion.33), channel_id=1, source_target_pairs={{0,4},{1,3},{2,6},{3,1},{4,0},{5,7},{6,2},{7,5},{8,12},{9,11},{10,... | collective-permute-start | bytes 1966088 | tf_op jit(solution)/shard_map/ppermute | solution.py:30
  36.0 13.7 %collective-permute-done.20 = bf16[5,128,512]{2,1,0:T(8,128)(2,1)} collective-permute-done((bf16[5,128,512]{2,1,0:T(8,128)(2,1)S(1)}, bf16[5,128,512]{2,1,0:T(8,128)(2,1)}, u32[]{:S(2)}, u32[]{:S(2)}) %collective-permute-start.20) | collective-permute-done | bytes 655392 | tf_op jit(solution)/shard_map/ppermute | solution.py:30
  51.8 1.5 %collective-permute-done.13.refs_1_ = bf16[4,128,512]{2,1,0:T(8,128)(2,1)} collective-permute-done((bf16[4,128,512]{2,1,0:T(8,128)(2,1)S(1)}, bf16[4,128,512]{2,1,0:T(8,128)(2,1)}, u32[]{:S(2)}, u32[]{:S(2)}) %collective-permute-start.13) | collective-permute-done | bytes 524320 | tf_op jit(solution)/shard_map/ppermute | solution.py:30
  54.3 3.5 %collective-permute-start.16 = (bf16[2,2,128,256]{3,2,1,0:T(8,128)(2,1)S(1)}, bf16[2,2,128,256]{3,2,1,0:T(8,128)(2,1)S(1)}, u32[]{:S(2)}, u32[]{:S(2)}) collective-permute-start(bf16[2,2,128,256]{3,2,1,0:T(8,128)(2,1)S(1)} %pad_maximum_fusion.4), channel_id=1, source_target_pairs={{0,8},{8,16},{16,24},{1,9},{9,17},{17,25},{2,10},{10,18},{18,26},{... | collective-permute-start | bytes 786440 | tf_op jit(solution)/shard_map/ppermute | solution.py:12
  59.3 4.1 %collective-permute-done.16 = bf16[2,2,128,256]{3,2,1,0:T(8,128)(2,1)S(1)} collective-permute-done((bf16[2,2,128,256]{3,2,1,0:T(8,128)(2,1)S(1)}, bf16[2,2,128,256]{3,2,1,0:T(8,128)(2,1)S(1)}, u32[]{:S(2)}, u32[]{:S(2)}) %collective-permute-start.16) | collective-permute-done | bytes 262176 | tf_op jit(solution)/shard_map/ppermute | solution.py:12
  63.4 1.5 %collective-permute-start.4 = (bf16[7,128,512]{2,1,0:T(8,128)(2,1)S(1)}, bf16[7,128,512]{2,1,0:T(8,128)(2,1)S(1)}, u32[]{:S(2)}, u32[]{:S(2)}) collective-permute-start(bf16[7,128,512]{2,1,0:T(8,128)(2,1)S(1)} %fusion.32), channel_id=1, source_target_pairs={{0,4},{1,3},{2,6},{3,1},{4,0},{5,7},{6,2},{7,5},{8,12},{9,11},{10,... | collective-permute-start | bytes 2752520 | tf_op jit(solution)/shard_map/ppermute | solution.py:30
  68.3 3.5 %collective-permute-start.18 = (bf16[256,1024]{1,0:T(8,128)(2,1)S(1)}, bf16[256,1024]{1,0:T(8,128)(2,1)S(1)}, u32[]{:S(2)}, u32[]{:S(2)}) collective-permute-start(bf16[256,1024]{1,0:T(8,128)(2,1)S(1)} %get-tuple-element.27), channel_id=1, source_target_pairs={{8,16},{16,8},{9,17},{17,9},{10,18},{18,10},{11,19},{19,11},{12,20... | collective-permute-start | bytes 1572872 | tf_op jit(solution)/shard_map/ppermute | solution.py:21
  72.6 4.2 %collective-permute-done.4 = bf16[7,128,512]{2,1,0:T(8,128)(2,1)S(1)} collective-permute-done((bf16[7,128,512]{2,1,0:T(8,128)(2,1)S(1)}, bf16[7,128,512]{2,1,0:T(8,128)(2,1)S(1)}, u32[]{:S(2)}, u32[]{:S(2)}) %collective-permute-start.4) | collective-permute-done | bytes 917536 | tf_op jit(solution)/shard_map/ppermute | solution.py:30
  77.1 1.6 %collective-permute-start.8 = (bf16[2,128,512]{2,1,0:T(8,128)(2,1)S(1)}, bf16[2,128,512]{2,1,0:T(8,128)(2,1)S(1)}, u32[]{:S(2)}, u32[]{:S(2)}) collective-permute-start(bf16[2,128,512]{2,1,0:T(8,128)(2,1)S(1)} %slice.254.refs_0_), channel_id=1, source_target_pairs={{0,2},{1,5},{2,0},{3,7},{4,6},{5,1},{6,4},{7,3},{8,10},{9,13},{10,... | collective-permute-start | bytes 786440 | tf_op jit(solution)/shard_map/ppermute | solution.py:30
  79.4 1.5 %convolution_convert_fusion.3 = bf16[2,512,1024]{2,1,0:T(8,128)(2,1)S(1)} fusion(bf16[5,512,512]{2,1,0:T(8,128)(2,1)S(1)} %place.9, bf16[2,512,1024]{2,1,0:T(8,128)(2,1)S(1)} %bitcast.88), kind=kOutput, calls=%fused_computation.13 | convolution fusion | flops 1074790400 | bytes 6815744 | tf_op jit(solution)/shard_map/nab,nac->nbc/dot_general | solution.py:230
  81.3 2.1 %convolution_convert_fusion.1 = bf16[3,512,1024]{2,1,0:T(8,128)(2,1)S(1)} fusion(bf16[5,512,512]{2,1,0:T(8,128)(2,1)S(1)} %place.9, bf16[3,512,1024]{2,1,0:T(8,128)(2,1)S(1)} %bitcast.89), kind=kOutput, calls=%fused_computation.3 | convolution fusion | flops 1612185600 | bytes 8912896 | tf_op jit(solution)/shard_map/nab,nac->nbc/dot_general | solution.py:230
  89.6 2.9 %collective-permute-start.24 = (bf16[256,1024]{1,0:T(8,128)(2,1)S(1)}, bf16[256,1024]{1,0:T(8,128)(2,1)S(1)}, u32[]{:S(2)}, u32[]{:S(2)}) collective-permute-start(bf16[256,1024]{1,0:T(8,128)(2,1)S(1)} %get-tuple-element.22), channel_id=1, source_target_pairs={{8,16},{16,8},{9,17},{17,9},{10,18},{18,10},{11,19},{19,11},{12,20... | collective-permute-start | bytes 1572872 | tf_op jit(solution)/shard_map/ppermute | solution.py:21
  93.5 9.8 %collective-permute-done.25 = bf16[256,1024]{1,0:T(8,128)(2,1)S(1)} collective-permute-done((bf16[256,1024]{1,0:T(8,128)(2,1)S(1)}, bf16[256,1024]{1,0:T(8,128)(2,1)S(1)}, u32[]{:S(2)}, u32[]{:S(2)}) %collective-permute-start.25) | collective-permute-done | bytes 524320 | tf_op jit(solution)/shard_map/ppermute | solution.py:21
  103.3 1.9 %collective-permute-done.24 = bf16[256,1024]{1,0:T(8,128)(2,1)S(1)} collective-permute-done((bf16[256,1024]{1,0:T(8,128)(2,1)S(1)}, bf16[256,1024]{1,0:T(8,128)(2,1)S(1)}, u32[]{:S(2)}, u32[]{:S(2)}) %collective-permute-start.24) | collective-permute-done | bytes 524320 | tf_op jit(solution)/shard_map/ppermute | solution.py:21
  106.5 1.5 %convolution_convert_fusion.2 = bf16[2,512,1024]{2,1,0:T(8,128)(2,1)S(1)} fusion(bf16[5,512,512]{2,1,0:T(8,128)(2,1)S(1)} %place.5, bf16[2,512,1024]{2,1,0:T(8,128)(2,1)S(1)} %bitcast.93), kind=kOutput, calls=%fused_computation.12 | convolution fusion | flops 1074790400 | bytes 6815744 | tf_op jit(solution)/shard_map/nab,nac->nbc/dot_general | solution.py:230
  108.4 2.1 %convolution_convert_fusion = bf16[3,512,1024]{2,1,0:T(8,128)(2,1)S(1)} fusion(bf16[5,512,512]{2,1,0:T(8,128)(2,1)S(1)} %place.5, bf16[3,512,1024]{2,1,0:T(8,128)(2,1)S(1)} %bitcast.90), kind=kOutput, calls=%fused_computation.2 | convolution fusion | flops 1612185600 | bytes 8912896 | tf_op jit(solution)/shard_map/nab,nac->nbc/dot_general | solution.py:230
  110.5 2.7 %write_inner.1._ = bf16[2048,1024]{1,0:T(8,128)(2,1)} custom-call(bf16[1536,1024]{1,0:T(8,128)(2,1)S(1)} %bitcast.85), custom_call_target="tpu_custom_call" | custom-call | bytes 6291456 | tf_op jit(solution)/shard_map/write_inner/pallas_call | solution.py:240
  (95 shorter events, 31.2 us)
Async XLA Ops:
  5.0 9.5 %collective-permute-start = (bf16[9,128,512]{2,1,0:T(8,128)(2,1)}, bf16[9,128,512]{2,1,0:T(8,128)(2,1)}, u32[]{:S(2)}, u32[]{:S(2)}) collective-permute-start(bf16[9,128,512]{2,1,0:T(8,128)(2,1)} %get-tuple-element.9), channel_id=1, source_target_pairs={{0,1},{1,0},{2,3},{3,2},{4,5},{5,4},{6,7},{7,6},{8,9},{9,8},{10,11... | collective-permute-start | bytes 3538952 | tf_op jit(solution)/shard_map/ppermute | solution.py:30
  8.7 9.2 %collective-permute-start.11 = (bf16[4,128,512]{2,1,0:T(8,128)(2,1)S(1)}, bf16[4,128,512]{2,1,0:T(8,128)(2,1)S(1)}, u32[]{:S(2)}, u32[]{:S(2)}) collective-permute-start(bf16[4,128,512]{2,1,0:T(8,128)(2,1)S(1)} %slice_select_fusion.4), channel_id=1, source_target_pairs={{0,2},{1,5},{2,0},{3,7},{4,6},{5,1},{6,4},{7,3},{8,10},{9,13},{10,... | collective-permute-start | bytes 1572872 | tf_op jit(solution)/shard_map/ppermute | solution.py:30
  13.9 14.9 %collective-permute-start.2 = (bf16[5,128,512]{2,1,0:T(8,128)(2,1)S(1)}, bf16[5,128,512]{2,1,0:T(8,128)(2,1)S(1)}, u32[]{:S(2)}, u32[]{:S(2)}) collective-permute-start(bf16[5,128,512]{2,1,0:T(8,128)(2,1)S(1)} %slice_select_fusion.3), channel_id=1, source_target_pairs={{0,2},{1,5},{2,0},{3,7},{4,6},{5,1},{6,4},{7,3},{8,10},{9,13},{10,... | collective-permute-start | bytes 1966088 | tf_op jit(solution)/shard_map/ppermute | solution.py:30
  19.1 14.3 %collective-permute-start.12 = (bf16[4,128,512]{2,1,0:T(8,128)(2,1)S(1)}, bf16[4,128,512]{2,1,0:T(8,128)(2,1)S(1)}, u32[]{:S(2)}, u32[]{:S(2)}) collective-permute-start(bf16[4,128,512]{2,1,0:T(8,128)(2,1)S(1)} %fusion.34), channel_id=1, source_target_pairs={{0,4},{1,3},{2,6},{3,1},{4,0},{5,7},{6,2},{7,5},{8,12},{9,11},{10,... | collective-permute-start | bytes 1572872 | tf_op jit(solution)/shard_map/ppermute | solution.py:30
  29.0 28.8 %collective-permute-start.3 = (bf16[7,128,512]{2,1,0:T(8,128)(2,1)S(1)}, bf16[7,128,512]{2,1,0:T(8,128)(2,1)}, u32[]{:S(2)}, u32[]{:S(2)}) collective-permute-start(bf16[7,128,512]{2,1,0:T(8,128)(2,1)S(1)} %after.1), channel_id=1, source_target_pairs={{0,2},{1,5},{2,0},{3,7},{4,6},{5,1},{6,4},{7,3},{8,10},{9,13},{10,... | collective-permute-start | bytes 2752520 | tf_op jit(solution)/shard_map/ppermute | solution.py:30
  31.9 17.8 %collective-permute-start.20 = (bf16[5,128,512]{2,1,0:T(8,128)(2,1)S(1)}, bf16[5,128,512]{2,1,0:T(8,128)(2,1)}, u32[]{:S(2)}, u32[]{:S(2)}) collective-permute-start(bf16[5,128,512]{2,1,0:T(8,128)(2,1)S(1)} %fusion.33), channel_id=1, source_target_pairs={{0,4},{1,3},{2,6},{3,1},{4,0},{5,7},{6,2},{7,5},{8,12},{9,11},{10,... | collective-permute-start | bytes 1966088 | tf_op jit(solution)/shard_map/ppermute | solution.py:30
  33.6 19.8 %collective-permute-start.13 = (bf16[4,128,512]{2,1,0:T(8,128)(2,1)S(1)}, bf16[4,128,512]{2,1,0:T(8,128)(2,1)}, u32[]{:S(2)}, u32[]{:S(2)}) collective-permute-start(bf16[4,128,512]{2,1,0:T(8,128)(2,1)S(1)} %broadcast_select_fusion.2.refs_0_), channel_id=1, source_target_pairs={{0,2},{1,5},{2,0},{3,7},{4,6},{5,1},{6,4},{7,3},{8,10},{9,13},{10,... | collective-permute-start | bytes 1572872 | tf_op jit(solution)/shard_map/ppermute | solution.py:30
  36.0 29.0 %collective-permute-start.14 = (bf16[4,128,512]{2,1,0:T(8,128)(2,1)S(1)}, bf16[4,128,512]{2,1,0:T(8,128)(2,1)S(1)}, u32[]{:S(2)}, u32[]{:S(2)}) collective-permute-start(bf16[4,128,512]{2,1,0:T(8,128)(2,1)S(1)} %broadcast_select_fusion.2.refs_0_), channel_id=1, source_target_pairs={{0,1},{1,0},{2,3},{3,2},{4,5},{5,4},{6,7},{7,6},{8,9},{9,8},{10,11... | collective-permute-start | bytes 1572872 | tf_op jit(solution)/shard_map/ppermute | solution.py:30
  50.9 26.2 %collective-permute-start.22 = (bf16[5,128,512]{2,1,0:T(8,128)(2,1)S(1)}, bf16[5,128,512]{2,1,0:T(8,128)(2,1)S(1)}, u32[]{:S(2)}, u32[]{:S(2)}) collective-permute-start(bf16[5,128,512]{2,1,0:T(8,128)(2,1)S(1)} %broadcast_select_fusion.1.refs_0_), channel_id=1, source_target_pairs={{0,1},{1,0},{2,3},{3,2},{4,5},{5,4},{6,7},{7,6},{8,9},{9,8},{10,11... | collective-permute-start | bytes 1966088 | tf_op jit(solution)/shard_map/ppermute | solution.py:30
  50.9 14.1 %collective-permute-start.21 = (bf16[5,128,512]{2,1,0:T(8,128)(2,1)S(1)}, bf16[5,128,512]{2,1,0:T(8,128)(2,1)S(1)}, u32[]{:S(2)}, u32[]{:S(2)}) collective-permute-start(bf16[5,128,512]{2,1,0:T(8,128)(2,1)S(1)} %broadcast_select_fusion.1.refs_0_), channel_id=1, source_target_pairs={{0,2},{1,5},{2,0},{3,7},{4,6},{5,1},{6,4},{7,3},{8,10},{9,13},{10,... | collective-permute-start | bytes 1966088 | tf_op jit(solution)/shard_map/ppermute | solution.py:30
  54.3 9.1 %collective-permute-start.16 = (bf16[2,2,128,256]{3,2,1,0:T(8,128)(2,1)S(1)}, bf16[2,2,128,256]{3,2,1,0:T(8,128)(2,1)S(1)}, u32[]{:S(2)}, u32[]{:S(2)}) collective-permute-start(bf16[2,2,128,256]{3,2,1,0:T(8,128)(2,1)S(1)} %pad_maximum_fusion.4), channel_id=1, source_target_pairs={{0,8},{8,16},{16,24},{1,9},{9,17},{17,25},{2,10},{10,18},{18,26},{... | collective-permute-start | bytes 786440 | tf_op jit(solution)/shard_map/ppermute | solution.py:12
  57.8 7.7 %collective-permute-start.15 = (bf16[4,128,512]{2,1,0:T(8,128)(2,1)}, bf16[4,128,512]{2,1,0:T(8,128)(2,1)S(1)}, u32[]{:S(2)}, u32[]{:S(2)}) collective-permute-start(bf16[4,128,512]{2,1,0:T(8,128)(2,1)} %collective-permute-done.13.refs_1_), channel_id=1, source_target_pairs={{0,1},{1,0},{2,3},{3,2},{4,5},{5,4},{6,7},{7,6},{8,9},{9,8},{10,11... | collective-permute-start | bytes 1572872 | tf_op jit(solution)/shard_map/ppermute | solution.py:30
  63.4 13.4 %collective-permute-start.4 = (bf16[7,128,512]{2,1,0:T(8,128)(2,1)S(1)}, bf16[7,128,512]{2,1,0:T(8,128)(2,1)S(1)}, u32[]{:S(2)}, u32[]{:S(2)}) collective-permute-start(bf16[7,128,512]{2,1,0:T(8,128)(2,1)S(1)} %fusion.32), channel_id=1, source_target_pairs={{0,4},{1,3},{2,6},{3,1},{4,0},{5,7},{6,2},{7,5},{8,12},{9,11},{10,... | collective-permute-start | bytes 2752520 | tf_op jit(solution)/shard_map/ppermute | solution.py:30
  65.0 6.9 %collective-permute-start.17 = (bf16[2,2,128,256]{3,2,1,0:T(8,128)(2,1)S(1)}, bf16[2,2,128,256]{3,2,1,0:T(8,128)(2,1)S(1)}, u32[]{:S(2)}, u32[]{:S(2)}) collective-permute-start(bf16[2,2,128,256]{3,2,1,0:T(8,128)(2,1)S(1)} %collective-permute-done.16), channel_id=1, source_target_pairs={{0,1},{1,0},{2,3},{3,2},{4,5},{5,4},{6,7},{7,6},{8,9},{9,8},{10,11... | collective-permute-start | bytes 786440 | tf_op jit(solution)/shard_map/ppermute | solution.py:30
  65.0 13.6 %collective-permute-start.23 = (bf16[5,128,512]{2,1,0:T(8,128)(2,1)S(1)}, bf16[5,128,512]{2,1,0:T(8,128)(2,1)S(1)}, u32[]{:S(2)}, u32[]{:S(2)}) collective-permute-start(bf16[5,128,512]{2,1,0:T(8,128)(2,1)S(1)} %collective-permute-done.21.refs_1_), channel_id=1, source_target_pairs={{0,1},{1,0},{2,3},{3,2},{4,5},{5,4},{6,7},{7,6},{8,9},{9,8},{10,11... | collective-permute-start | bytes 1966088 | tf_op jit(solution)/shard_map/ppermute | solution.py:30
  68.3 15.8 %collective-permute-start.18 = (bf16[256,1024]{1,0:T(8,128)(2,1)S(1)}, bf16[256,1024]{1,0:T(8,128)(2,1)S(1)}, u32[]{:S(2)}, u32[]{:S(2)}) collective-permute-start(bf16[256,1024]{1,0:T(8,128)(2,1)S(1)} %get-tuple-element.27), channel_id=1, source_target_pairs={{8,16},{16,8},{9,17},{17,9},{10,18},{18,10},{11,19},{19,11},{12,20... | collective-permute-start | bytes 1572872 | tf_op jit(solution)/shard_map/ppermute | solution.py:21
  71.9 13.7 %collective-permute-start.19 = (bf16[256,1024]{1,0:T(8,128)(2,1)S(1)}, bf16[256,1024]{1,0:T(8,128)(2,1)S(1)}, u32[]{:S(2)}, u32[]{:S(2)}) collective-permute-start(bf16[256,1024]{1,0:T(8,128)(2,1)S(1)} %get-tuple-element.28), channel_id=1, source_target_pairs={{0,8},{16,24},{8,0},{24,16},{1,9},{17,25},{9,1},{25,17},{2,10},{18... | collective-permute-start | bytes 1572872 | tf_op jit(solution)/shard_map/ppermute | solution.py:21
  77.0 9.9 %collective-permute-start.9 = (bf16[2,128,512]{2,1,0:T(8,128)(2,1)S(1)}, bf16[2,128,512]{2,1,0:T(8,128)(2,1)S(1)}, u32[]{:S(2)}, u32[]{:S(2)}) collective-permute-start(bf16[2,128,512]{2,1,0:T(8,128)(2,1)S(1)} %slice.254.refs_0_), channel_id=1, source_target_pairs={{0,1},{1,0},{2,3},{3,2},{4,5},{5,4},{6,7},{7,6},{8,9},{9,8},{10,11... | collective-permute-start | bytes 786440 | tf_op jit(solution)/shard_map/ppermute | solution.py:30
  77.1 9.1 %collective-permute-start.8 = (bf16[2,128,512]{2,1,0:T(8,128)(2,1)S(1)}, bf16[2,128,512]{2,1,0:T(8,128)(2,1)S(1)}, u32[]{:S(2)}, u32[]{:S(2)}) collective-permute-start(bf16[2,128,512]{2,1,0:T(8,128)(2,1)S(1)} %slice.254.refs_0_), channel_id=1, source_target_pairs={{0,2},{1,5},{2,0},{3,7},{4,6},{5,1},{6,4},{7,3},{8,10},{9,13},{10,... | collective-permute-start | bytes 786440 | tf_op jit(solution)/shard_map/ppermute | solution.py:30
  78.6 14.3 %collective-permute-start.5 = (bf16[5,128,512]{2,1,0:T(8,128)(2,1)S(1)}, bf16[5,128,512]{2,1,0:T(8,128)(2,1)S(1)}, u32[]{:S(2)}, u32[]{:S(2)}) collective-permute-start(bf16[5,128,512]{2,1,0:T(8,128)(2,1)S(1)} %slice.253.refs_0_), channel_id=1, source_target_pairs={{0,2},{1,5},{2,0},{3,7},{4,6},{5,1},{6,4},{7,3},{8,10},{9,13},{10,... | collective-permute-start | bytes 1966088 | tf_op jit(solution)/shard_map/ppermute | solution.py:30
  89.2 14.0 %collective-permute-start.25 = (bf16[256,1024]{1,0:T(8,128)(2,1)S(1)}, bf16[256,1024]{1,0:T(8,128)(2,1)S(1)}, u32[]{:S(2)}, u32[]{:S(2)}) collective-permute-start(bf16[256,1024]{1,0:T(8,128)(2,1)S(1)} %get-tuple-element.21), channel_id=1, source_target_pairs={{0,8},{16,24},{8,0},{24,16},{1,9},{17,25},{9,1},{25,17},{2,10},{18... | collective-permute-start | bytes 1572872 | tf_op jit(solution)/shard_map/ppermute | solution.py:21
  89.6 15.6 %collective-permute-start.24 = (bf16[256,1024]{1,0:T(8,128)(2,1)S(1)}, bf16[256,1024]{1,0:T(8,128)(2,1)S(1)}, u32[]{:S(2)}, u32[]{:S(2)}) collective-permute-start(bf16[256,1024]{1,0:T(8,128)(2,1)S(1)} %get-tuple-element.22), channel_id=1, source_target_pairs={{8,16},{16,8},{9,17},{17,9},{10,18},{18,10},{11,19},{19,11},{12,20... | collective-permute-start | bytes 1572872 | tf_op jit(solution)/shard_map/ppermute | solution.py:21
  92.5 13.7 %collective-permute-start.6 = (bf16[5,128,512]{2,1,0:T(8,128)(2,1)S(1)}, bf16[5,128,512]{2,1,0:T(8,128)(2,1)S(1)}, u32[]{:S(2)}, u32[]{:S(2)}) collective-permute-start(bf16[5,128,512]{2,1,0:T(8,128)(2,1)S(1)} %slice.253.refs_0_), channel_id=1, source_target_pairs={{0,1},{1,0},{2,3},{3,2},{4,5},{5,4},{6,7},{7,6},{8,9},{9,8},{10,11... | collective-permute-start | bytes 1966088 | tf_op jit(solution)/shard_map/ppermute | solution.py:30
  92.9 13.3 %collective-permute-start.7 = (bf16[5,128,512]{2,1,0:T(8,128)(2,1)S(1)}, bf16[5,128,512]{2,1,0:T(8,128)(2,1)S(1)}, u32[]{:S(2)}, u32[]{:S(2)}) collective-permute-start(bf16[5,128,512]{2,1,0:T(8,128)(2,1)S(1)} %collective-permute-done.5.refs_1_), channel_id=1, source_target_pairs={{0,1},{1,0},{2,3},{3,2},{4,5},{5,4},{6,7},{7,6},{8,9},{9,8},{10,11... | collective-permute-start | bytes 1966088 | tf_op jit(solution)/shard_map/ppermute | solution.py:30
  (9 other events, 26.2 us)
